TPU v7x, 32 devices: a whole 2x2x4 slice. The times are simulated.
32 devices in a mesh: groups: 2 (over x), cols: 16 (over z, y, core).
Axes of the slice: x: 2, y: 2, z: 4, core: 2. Of those that a mesh axis runs over, the one named last changes fastest.
Arguments:
- image_feats: bfloat16 [64, 16384], P('groups', 'cols'), parts along dimension 0, may hold values from -6 to 6
- teacher: bfloat16 [64, 256, 512], P('groups', 'cols'), parts along dimension 0, may hold values from -40 to 40
- w_first: bfloat16 [128, 576], P('cols'), may hold values from -0.25 to 0.25
- w_middle: bfloat16 [128, 1152], P('cols'), may hold values from -0.1875 to 0.1875
- w_last: bfloat16 [512, 1152], P('cols'), may hold values from -0.1875 to 0.1875
Outputs:
- grad_first: float32 [256, 576], P(('groups', 'cols')), parts along dimension 0
- grad_middle: float32 [256, 1152], P(('groups', 'cols')), parts along dimension 0
- grad_last: float32 [1024, 1152], P(('groups', 'cols')), parts along dimension 0
There are 2 independent parts, one for each index of `groups`. A program takes and returns all parts, laid end to end along the dimension named above; an argument that names none is the same for every part. Nothing has to cross between parts.
All inputs are finite; a program needn't handle non-finite values.
Results may differ from a plain program's by a relative error of at most 0.012.
Values may be sent and summed in bfloat16 or wider, within the bound.
No kernel may reach another device: no remote copies, remote signals or barrier semaphores. Data moves between devices by JAX's collectives and lax.ppermute only.
A program may use at most 64 MiB of HBM per device.

v0:
```python
import jax
import jax.numpy as jnp
from jax import lax
from jax.sharding import PartitionSpec as P

epsilon = 1e-06


def padded_2(array, sides, width):
    for axis, dim in sides:
        count, length = (lax.axis_size(axis), array.shape[dim])
        up = [(i, (i + 1) % count) for i in range(count - 1)]
        down = [(j, i) for i, j in up]
        last = lax.slice_in_dim(array, length - width, length, axis=dim)
        initial = lax.slice_in_dim(array, 0, width, axis=dim)
        before = lax.ppermute(last, axis, up)
        after = lax.ppermute(initial, axis, down)
        array = jnp.concatenate([before, array, after], axis=dim)
    return array


def silu_slope(pre):
    sigma = jax.nn.sigmoid(pre)
    return sigma * (1.0 + pre * (1.0 - sigma))


def pad_rows(field, spread):
    return jnp.pad(field, ((spread, spread), (0, 0), (0, 0)))


def window_at(padded, row_at, col_at, height, breadth):
    depth = padded.shape[2]
    piece = lax.slice(padded, (row_at, col_at, 0), (row_at + height, col_at + breadth, depth))
    return piece.reshape(height * breadth, depth)


def conv_forward(padded, kernel, spread, height, breadth):
    depth = padded.shape[2]
    summed = jnp.zeros((height * breadth, kernel.shape[0]), jnp.float32)
    for tap_row in range(3):
        for tap_col in range(3):
            window = window_at(padded, tap_row * spread, tap_col * spread, height, breadth)
            offset = (3 * tap_row + tap_col) * depth
            summed = summed + lax.dot_general(
                window,
                kernel[:, offset : offset + depth],
                (((1,), (1,)), ((), ())),
                preferred_element_type=jnp.float32,
            )
    return summed.reshape(height, breadth, kernel.shape[0])


def conv_transpose(padded_slope, kernel, spread, height, breadth, depth):
    summed = jnp.zeros((height * breadth, depth), jnp.float32)
    for tap_row in range(3):
        for tap_col in range(3):
            window = window_at(
                padded_slope, (2 - tap_row) * spread, (2 - tap_col) * spread, height, breadth
            )
            offset = (3 * tap_row + tap_col) * depth
            summed = summed + jnp.dot(
                window, kernel[:, offset : offset + depth], preferred_element_type=jnp.float32
            )
    return summed.reshape(height, breadth, depth)


def weight_term(padded, slope, spread, height, breadth):
    flat_slope = slope.reshape(height * breadth, slope.shape[2])
    blocks = []
    for tap_row in range(3):
        for tap_col in range(3):
            window = window_at(padded, tap_row * spread, tap_col * spread, height, breadth)
            blocks.append(
                lax.dot_general(
                    flat_slope, window, (((0,), (0,)), ((), ())), preferred_element_type=jnp.float32
                )
            )
    return jnp.concatenate(blocks, 1)


def on_device(image_feats, teacher, w_first, w_middle, w_last):
    in_depth = w_first.shape[1] // 9
    hidden_depth = w_middle.shape[1] // 9
    kernel_first, kernel_middle, kernel_last = (
        lax.all_gather(w_first, "cols", axis=0, tiled=True),
        lax.all_gather(w_middle, "cols", axis=0, tiled=True),
        lax.all_gather(w_last, "cols", axis=0, tiled=True),
    )
    height, breadth = (teacher.shape[0], teacher.shape[1])
    wide_input = pad_rows(
        padded_2(image_feats, (("cols", 1),), 2 * in_depth).reshape(height, breadth + 4, in_depth),
        2,
    )
    first_pre = conv_forward(wide_input, kernel_first, 2, height, breadth)
    first_act = jax.nn.silu(first_pre).astype(jnp.bfloat16)
    wide_first = pad_rows(padded_2(first_act, (("cols", 1),), 4), 4)
    second_pre = conv_forward(wide_first, kernel_middle, 4, height, breadth)
    second_act = jax.nn.silu(second_pre).astype(jnp.bfloat16)
    wide_second = pad_rows(padded_2(second_act, (("cols", 1),), 8), 8)
    student = conv_forward(wide_second, kernel_last, 8, height, breadth)
    s_norm = jnp.sqrt(jnp.sum(student * student, -1, keepdims=True) + epsilon)
    target = teacher.astype(jnp.float32)
    t_norm = jnp.sqrt(jnp.sum(target * target, -1, keepdims=True) + epsilon)
    s_unit = student / s_norm
    differ = s_unit - target / t_norm
    slope = ((differ - s_unit * jnp.sum(s_unit * differ, -1, keepdims=True)) / s_norm).astype(
        jnp.bfloat16
    )
    grad_last = lax.psum_scatter(
        weight_term(wide_second, slope, 8, height, breadth), "cols", scatter_dimension=0, tiled=True
    )
    wide_slope = pad_rows(padded_2(slope, (("cols", 1),), 8), 8)
    back_second = conv_transpose(wide_slope, kernel_last, 8, height, breadth, hidden_depth)
    slope_second = (back_second * silu_slope(second_pre)).astype(jnp.bfloat16)
    grad_middle = lax.psum_scatter(
        weight_term(wide_first, slope_second, 4, height, breadth),
        "cols",
        scatter_dimension=0,
        tiled=True,
    )
    wide_slope_second = pad_rows(padded_2(slope_second, (("cols", 1),), 4), 4)
    back_first = conv_transpose(wide_slope_second, kernel_middle, 4, height, breadth, hidden_depth)
    slope_first = (back_first * silu_slope(first_pre)).astype(jnp.bfloat16)
    grad_first = lax.psum_scatter(
        weight_term(wide_input, slope_first, 2, height, breadth),
        "cols",
        scatter_dimension=0,
        tiled=True,
    )
    return (grad_first, grad_middle, grad_last)


def solution(mesh):
    placed = (
        P("groups", "cols"),
        P("groups", "cols", None),
        P("cols", None),
        P("cols", None),
        P("cols", None),
    )
    return jax.shard_map(
        on_device,
        mesh=mesh,
        in_specs=placed,
        out_specs=(
            P(("groups", "cols"), None),
            P(("groups", "cols"), None),
            P(("groups", "cols"), None),
        ),
        check_vma=False,
    )
```

profile of v0, /device:TPU:0, one launch (start us, length us, event | category | flops | bytes accessed | tf_op | source)
XLA Modules:
  0.0 292.2 jit_solution(16077987380912446101)
XLA Ops:
  7.9 2.3 collective-permute-start
  10.3 1.3 collective-permute-start.1
  11.7 1.2 fusion.43
  12.9 25.7 %all_gather.9 = bf16[128,576]{1,0:T(8,128)(2,1)S(1)} all-gather(bf16[8,576]{1,0:T(8,128)(2,1)} %param.7), channel_id=1, replica_groups=mesh['groups'=2,'cols'=16] {'cols'}, dimensions={0}, use_global_device_ids=true | all-gather | bytes 156672 | tf_op jit(solution)/shard_map/all_gather | solution.py:85
  38.6 0.9 pad_maximum_fusion.8
  42.6 2.2 collective-permute-start.2
  44.9 1.3 collective-permute-start.3
  46.2 20.2 %all_gather.10 = bf16[128,1152]{1,0:T(8,128)(2,1)S(1)} all-gather(bf16[8,1152]{1,0:T(8,128)(2,1)S(1)} %copy-done.21), channel_id=1, replica_groups=mesh['groups'=2,'cols'=16] {'cols'}, dimensions={0}, use_global_device_ids=true | all-gather | bytes 313344 | tf_op jit(solution)/shard_map/all_gather | solution.py:86
  69.7 2.3 collective-permute-start.4
  71.9 1.3 collective-permute-start.5
  73.3 1.8 collective-permute-done.5
  79.0 1.4 fusion.89
  80.4 1.3 convolution_add_fusion.7
  84.1 1.3 multiply_reduce_fusion
  85.5 4.8 %fusion.10 = bf16[32,16,512]{2,1,0:T(8,128)(2,1)S(1)} fusion(bf16[32,16,512]{2,1,0:T(8,128)(2,1)} %param.6, f32[32,16]{1,0:T(8,128)S(1)} %add_sqrt_fusion, f32[32,16]{1,0:T(8,128)S(1)} %sqrt.20, f32[32,16,512]{2,1,0:T(8,128)} %bitcast.244), kind=kOutput, calls=%fused_computation.22 | output fusion | flops 3408895 | bytes 2101248 | tf_op jit(solution)/shard_map/mul | solution.py:106
  92.7 4.4 %collective-permute-start.6 = (bf16[32,8,512]{2,1,0:T(8,128)(2,1)S(1)}, bf16[32,8,512]{2,1,0:T(8,128)(2,1)S(1)}, u32[]{:S(2)}, u32[]{:S(2)}) collective-permute-start(bf16[32,8,512]{2,1,0:T(8,128)(2,1)S(1)} %get-tuple-element.22), channel_id=1, source_target_pairs={{0,1},{1,2},{2,3},{3,4},{4,5},{5,6},{6,7},{7,8},{8,9},{9,10},{10,1... | collective-permute-start | bytes 786440 | tf_op jit(solution)/shard_map/ppermute | solution.py:16
  97.1 1.5 collective-permute-start.7
  99.1 1.1 copy-done.1
  105.9 6.2 %collective-permute-start.8 = (bf16[32,4,128]{2,0,1:T(8,128)(2,1)S(1)}, bf16[32,4,128]{2,0,1:T(8,128)(2,1)S(1)}, u32[]{:S(2)}, u32[]{:S(2)}) collective-permute-start(bf16[32,4,128]{2,0,1:T(8,128)(2,1)S(1)} %get-tuple-element.53), channel_id=1, source_target_pairs={{0,1},{1,2},{2,3},{3,4},{4,5},{5,6},{6,7},{7,8},{8,9},{9,10},{10,1... | collective-permute-start | bytes 98312 | tf_op jit(solution)/shard_map/ppermute | solution.py:16
  112.1 1.3 collective-permute-start.9
  113.6 1.5 collective-permute-done.9
  117.7 0.8 fusion.42
  118.5 0.8 fusion.41
  120.2 0.8 fusion.39
  121.8 0.8 fusion.37
  122.7 0.8 fusion.36
  123.5 0.8 fusion.35
  125.8 2.0 copy.146
  129.7 89.7 %all-reduce.10.cloned.1.call-done = (f32[128,576]{0,1:T(8,128)}, f32[128,1152]{0,1:T(8,128)}) async-done(((f32[128,576]{0,1:T(8,128)}, f32[128,1152]{0,1:T(8,128)}), (f32[128,576]{0,1:T(8,128)}, f32[128,1152]{0,1:T(8,128)})) %all-reduce.10.cloned.1.call-update) | async-done | bytes 884752
  219.3 1.3 constant_dynamic-slice_fusion
  220.7 0.8 copy.140
  222.4 63.3 %reduce-scatter.6.cloned.1.call-done = f32[32,1152]{1,0:T(8,128)} async-done(((f32[512,1152]{1,0:T(8,128)}), f32[32,1152]{1,0:T(8,128)}) %reduce-scatter.6.cloned.1.call-update) | async-done | bytes 147472
  (186 shorter events, 29.4 us)
Async XLA Ops:
  7.2 71.8 %all-gather.2.cloned.1.call-start = ((), (), s32[]{:S(2)}) async-start(), calls=%async_computation.1 | async-start | bytes 1253376 | tf_op jit(solution)/shard_map/all_gather | solution.py:87
  7.9 30.6 %collective-permute-start = (bf16[32,128]{1,0:T(8,128)(2,1)S(1)}, bf16[32,128]{1,0:T(8,128)(2,1)S(1)}, u32[]{:S(2)}, u32[]{:S(2)}) collective-permute-start(bf16[32,128]{1,0:T(8,128)(2,1)S(1)} %get-tuple-element.63), channel_id=1, source_target_pairs={{0,1},{1,2},{2,3},{3,4},{4,5},{5,6},{6,7},{7,8},{8,9},{9,10},{10,1... | collective-permute-start | bytes 24584 | tf_op jit(solution)/shard_map/ppermute | solution.py:16
  10.3 28.3 %collective-permute-start.1 = (bf16[32,128]{1,0:T(8,128)(2,1)S(1)}, bf16[32,128]{1,0:T(8,128)(2,1)S(1)}, u32[]{:S(2)}, u32[]{:S(2)}) collective-permute-start(bf16[32,128]{1,0:T(8,128)(2,1)S(1)} %get-tuple-element.64), channel_id=1, source_target_pairs={{1,0},{2,1},{3,2},{4,3},{5,4},{6,5},{7,6},{8,7},{9,8},{10,9},{11,1... | collective-permute-start | bytes 24584 | tf_op jit(solution)/shard_map/ppermute | solution.py:17
  11.6 207.7 %all-reduce.10.cloned.1.call-start = ((), (), s32[]{:S(2)}) async-start(), calls=%async_computation.3 | async-start | bytes 1769472
  41.5 4.7 %copy-start.21 = (bf16[8,1152]{1,0:T(8,128)(2,1)S(1)}, bf16[8,1152]{1,0:T(8,128)(2,1)}, u32[]{:S(2)}) copy-start(bf16[8,1152]{1,0:T(8,128)(2,1)} %param.8) | copy-start | bytes 55300
  42.6 23.8 %collective-permute-start.2 = (bf16[32,4,128]{2,0,1:T(8,128)(2,1)S(1)}, bf16[32,4,128]{2,0,1:T(8,128)(2,1)S(1)}, u32[]{:S(2)}, u32[]{:S(2)}) collective-permute-start(bf16[32,4,128]{2,0,1:T(8,128)(2,1)S(1)} %get-tuple-element.61), channel_id=1, source_target_pairs={{0,1},{1,2},{2,3},{3,4},{4,5},{5,6},{6,7},{7,8},{8,9},{9,10},{10,1... | collective-permute-start | bytes 98312 | tf_op jit(solution)/shard_map/ppermute | solution.py:16
  44.9 21.6 %collective-permute-start.3 = (bf16[32,4,128]{2,0,1:T(8,128)(2,1)S(1)}, bf16[32,4,128]{2,0,1:T(8,128)(2,1)S(1)}, u32[]{:S(2)}, u32[]{:S(2)}) collective-permute-start(bf16[32,4,128]{2,0,1:T(8,128)(2,1)S(1)} %get-tuple-element.62), channel_id=1, source_target_pairs={{1,0},{2,1},{3,2},{4,3},{5,4},{6,5},{7,6},{8,7},{9,8},{10,9},{11,1... | collective-permute-start | bytes 98312 | tf_op jit(solution)/shard_map/ppermute | solution.py:17
  66.5 2.1 copy-start.9
  69.7 3.6 %collective-permute-start.4 = (bf16[32,8,128]{2,0,1:T(8,128)(2,1)S(1)}, bf16[32,8,128]{2,0,1:T(8,128)(2,1)S(1)}, u32[]{:S(2)}, u32[]{:S(2)}) collective-permute-start(bf16[32,8,128]{2,0,1:T(8,128)(2,1)S(1)} %get-tuple-element.57), channel_id=1, source_target_pairs={{0,1},{1,2},{2,3},{3,4},{4,5},{5,6},{6,7},{7,8},{8,9},{9,10},{10,1... | collective-permute-start | bytes 196616 | tf_op jit(solution)/shard_map/ppermute | solution.py:16
  71.9 3.1 %collective-permute-start.5 = (bf16[32,8,128]{2,0,1:T(8,128)(2,1)S(1)}, bf16[32,8,128]{2,0,1:T(8,128)(2,1)S(1)}, u32[]{:S(2)}, u32[]{:S(2)}) collective-permute-start(bf16[32,8,128]{2,0,1:T(8,128)(2,1)S(1)} %get-tuple-element.58), channel_id=1, source_target_pairs={{1,0},{2,1},{3,2},{4,3},{5,4},{6,5},{7,6},{8,7},{9,8},{10,9},{11,1... | collective-permute-start | bytes 196616 | tf_op jit(solution)/shard_map/ppermute | solution.py:17
  75.1 3.0 %copy-start.13 = (bf16[32,16,128]{2,0,1:T(8,128)(2,1)}, bf16[32,16,128]{2,0,1:T(8,128)(2,1)S(1)}, u32[]{:S(2)}) copy-start(bf16[32,16,128]{2,0,1:T(8,128)(2,1)S(1)} %get-tuple-element.55) | copy-start | bytes 393220
  75.9 3.1 %copy-start.3 = (bf16[32,16,128]{2,0,1:T(8,128)(2,1)}, bf16[32,16,128]{2,0,1:T(8,128)(2,1)S(1)}, u32[]{:S(2)}) copy-start(bf16[32,16,128]{2,0,1:T(8,128)(2,1)S(1)} %get-tuple-element.27) | copy-start | bytes 393220
  75.9 3.0 %copy-start.5 = (bf16[32,16,128]{2,0,1:T(8,128)(2,1)}, bf16[32,16,128]{2,0,1:T(8,128)(2,1)S(1)}, u32[]{:S(2)}) copy-start(bf16[32,16,128]{2,0,1:T(8,128)(2,1)S(1)} %get-tuple-element.28) | copy-start | bytes 393220
  75.9 3.0 %copy-start.7 = (bf16[32,16,128]{2,0,1:T(8,128)(2,1)}, bf16[32,16,128]{2,0,1:T(8,128)(2,1)S(1)}, u32[]{:S(2)}) copy-start(bf16[32,16,128]{2,0,1:T(8,128)(2,1)S(1)} %get-tuple-element.29) | copy-start | bytes 393220
  79.0 2.7 copy-start
  79.0 2.7 copy-start.18
  83.2 0.9 copy-start.19
  85.5 4.8 %copy-start.8 = (bf16[32,16,128]{2,0,1:T(8,128)(2,1)S(1)}, bf16[32,16,128]{2,0,1:T(8,128)(2,1)}, u32[]{:S(2)}) copy-start(bf16[32,16,128]{2,0,1:T(8,128)(2,1)} %copy-done.7) | copy-start | bytes 393220
  90.3 1.2 copy-start.4
  90.6 1.2 copy-start.16
  91.5 0.9 copy-start.14
  92.7 6.4 %collective-permute-start.6 = (bf16[32,8,512]{2,1,0:T(8,128)(2,1)S(1)}, bf16[32,8,512]{2,1,0:T(8,128)(2,1)S(1)}, u32[]{:S(2)}, u32[]{:S(2)}) collective-permute-start(bf16[32,8,512]{2,1,0:T(8,128)(2,1)S(1)} %get-tuple-element.22), channel_id=1, source_target_pairs={{0,1},{1,2},{2,3},{3,4},{4,5},{5,6},{6,7},{7,8},{8,9},{9,10},{10,1... | collective-permute-start | bytes 786440 | tf_op jit(solution)/shard_map/ppermute | solution.py:16
  97.1 3.4 %collective-permute-start.7 = (bf16[32,8,512]{2,1,0:T(8,128)(2,1)S(1)}, bf16[32,8,512]{2,1,0:T(8,128)(2,1)S(1)}, u32[]{:S(2)}, u32[]{:S(2)}) collective-permute-start(bf16[32,8,512]{2,1,0:T(8,128)(2,1)S(1)} %get-tuple-element.23), channel_id=1, source_target_pairs={{1,0},{2,1},{3,2},{4,3},{5,4},{6,5},{7,6},{8,7},{9,8},{10,9},{11,1... | collective-permute-start | bytes 786440 | tf_op jit(solution)/shard_map/ppermute | solution.py:17
  98.8 1.4 copy-start.1
  103.4 1.3 copy-start.12
  103.7 1.5 copy-start.10
  105.9 7.7 %collective-permute-start.8 = (bf16[32,4,128]{2,0,1:T(8,128)(2,1)S(1)}, bf16[32,4,128]{2,0,1:T(8,128)(2,1)S(1)}, u32[]{:S(2)}, u32[]{:S(2)}) collective-permute-start(bf16[32,4,128]{2,0,1:T(8,128)(2,1)S(1)} %get-tuple-element.53), channel_id=1, source_target_pairs={{0,1},{1,2},{2,3},{3,4},{4,5},{5,6},{6,7},{7,8},{8,9},{9,10},{10,1... | collective-permute-start | bytes 98312 | tf_op jit(solution)/shard_map/ppermute | solution.py:16
  112.1 3.1 %collective-permute-start.9 = (bf16[32,4,128]{2,0,1:T(8,128)(2,1)S(1)}, bf16[32,4,128]{2,0,1:T(8,128)(2,1)S(1)}, u32[]{:S(2)}, u32[]{:S(2)}) collective-permute-start(bf16[32,4,128]{2,0,1:T(8,128)(2,1)S(1)} %get-tuple-element.54), channel_id=1, source_target_pairs={{1,0},{2,1},{3,2},{4,3},{5,4},{6,5},{7,6},{8,7},{9,8},{10,9},{11,1... | collective-permute-start | bytes 98312 | tf_op jit(solution)/shard_map/ppermute | solution.py:17
  113.6 2.1 copy-start.17
  119.4 5.8 %copy-start.2 = (f32[512,1152]{0,1:T(8,128)S(1)}, f32[512,1152]{0,1:T(8,128)}, u32[]{:S(2)}) copy-start(f32[512,1152]{0,1:T(8,128)} %copy-done.1) | copy-start | bytes 7077892
  125.2 160.5 %reduce-scatter.6.cloned.1.call-start = ((), (), s32[]{:S(2)}) async-start(), calls=%async_computation.2 | async-start | bytes 2506752
  219.3 2.2 copy-start.20
  (4 other events, 2.9 us)
Sparse Core Ops, SparseCore 0:
  11.7 43.5 all-gather.1
  125.3 94.0 all-reduce.9
  223.7 61.9 reduce-scatter.5
where the time goes:
time: 293 us; the launch traced here: 292 us
  waiting for transfers between devices  157 us (54%)
  blocking collectives  45.9 us (16%)
  matrix products  25.6 us (9%)
  starting transfers between devices  24.1 us (8%)
  local copies, waits for them, and re-layouts  16.3 us (6%)
  between operations  15.5 us (5%)
  other arithmetic  8.07 us (3%)
    unnamed x5, waiting for transfers between devices  153 us
    all_gather x1, blocking collectives, on_device(): lax.all_gather(w_first, 'cols', axis=0, tiled=True)  25.7 us
    all_gather x1, blocking collectives, on_device(): lax.all_gather(w_middle, 'cols', axis=0, tiled=True)  20.2 us
    ppermute x5, starting transfers between devices, padded_2(): before = lax.ppermute(last, axis, up)  17.4 us
    dot_general x27, matrix products, weight_term(): lax.dot_general(flat_slope, window, (((0,), (0,)), ((), ())), preferred_e...  12 us
    unnamed x52, local copies, waits for them, and re-layouts  9.84 us
    dot_general x27, matrix products, conv_forward(): lax.dot_general(window, kernel[:, offset:offset + depth], (((1,), (1,)),...  9.41 us
    ppermute x5, starting transfers between devices, padded_2(): after = lax.ppermute(initial, axis, down)  6.64 us
  transfers between devices with their start and end apart: 13, of which 5 were waited for; matrix products, arithmetic and copies ran while one was open for 6% of the time, Pallas kernels for 0%

commit v1 on v0

v1 whole, which is shorter than its diff:
```python
import functools

import jax
import jax.numpy as jnp
from jax import lax
from jax.experimental import pallas as pl
from jax.experimental.pallas import tpu as pltpu
from jax.sharding import PartitionSpec as P

epsilon = 1e-06
bf16, f32 = jnp.bfloat16, jnp.float32
VMEM_LIMIT = 48 * 1024 * 1024
HALO_X, HALO_FIRST, HALO_SECOND, HALO_SLOPE, HALO_BACK = 13, 12, 10, 6, 2


def swap(array, mask):
    size = lax.axis_size("cols")
    return lax.ppermute(array, "cols", [(i, i ^ mask) for i in range(size)])


def shift(array, step):
    size = lax.axis_size("cols")
    return lax.ppermute(
        array, "cols", [(i, i + step) for i in range(size) if 0 <= i + step < size]
    )


def in_order(pieces, at):
    count = len(pieces)
    if count == 1:
        return pieces[0]
    half = count // 2
    low = in_order(pieces[:half], at % half)
    high = in_order(pieces[half:], at % half)
    return jnp.where(
        at < half, jnp.concatenate([low, high], 0), jnp.concatenate([high, low], 0)
    )


def pick(array, at):
    return lax.dynamic_index_in_dim(array, at, 0, keepdims=False)


def gather_rows(shard, me):
    size = lax.axis_size("cols")
    far = size // 4
    held = in_order([shard[None]] + [swap(shard, 4 * k)[None] for k in range(1, far)], me // 4)
    other = swap(held, 2)
    held = jnp.where(
        (me // 2) % 2 == 0, jnp.stack([held, other], 1), jnp.stack([other, held], 1)
    )
    other = swap(held, 1)
    held = jnp.where(me % 2 == 0, jnp.stack([held, other], 2), jnp.stack([other, held], 2))
    return held.reshape(size * shard.shape[0], shard.shape[1])


def scatter_rows(terms, me):
    size = lax.axis_size("cols")
    far = size // 4
    rows = terms.shape[0] // size
    held = terms.reshape(far, 2, 2, rows, terms.shape[1])
    core = me % 2
    mine = lax.dynamic_index_in_dim(held, core, 2, keepdims=False)
    theirs = lax.dynamic_index_in_dim(held, 1 - core, 2, keepdims=False)
    held = mine.astype(f32) + swap(theirs.astype(bf16), 1).astype(f32)
    row = (me // 2) % 2
    mine = lax.dynamic_index_in_dim(held, row, 1, keepdims=False)
    theirs = lax.dynamic_index_in_dim(held, 1 - row, 1, keepdims=False)
    held = mine + swap(theirs.astype(bf16), 2).astype(f32)
    place = me // 4
    sent = held.astype(bf16)
    total = pick(held, place)
    for k in range(1, far):
        total = total + swap(pick(sent, place ^ k), 4 * k).astype(f32)
    return total


def row_shifted(value, step, rows):
    count = value.shape[0]
    if step == 0:
        return value
    row = lax.broadcasted_iota(jnp.int32, (count, 1), 0) % rows + step
    rolled = pltpu.roll(value, (-step) % count, 0)
    return jnp.where((row >= 0) & (row < rows), rolled, 0.0)


def inside(count, rows, first, total):
    col = lax.broadcasted_iota(jnp.int32, (count, 1), 0) // rows + first
    return (col >= 0) & (col < total)


def dot(a, b, contract):
    return lax.dot_general(a, b, (contract, ((), ())), preferred_element_type=f32)


def put_patch(patch_ref, value, step, rows, out_cols):
    depth = value.shape[1]
    for ky in range(3):
        moved = row_shifted(value, (ky - 1) * step, rows).astype(bf16)
        for kx in range(3):
            tap = 3 * ky + kx
            start = kx * step * rows
            patch_ref[:, tap * depth : (tap + 1) * depth] = moved[start : start + out_cols * rows]


def front_kernel(
    own,
    rows,
    total,
    band_ref,
    xcol_ref,
    teacher_ref,
    w_first_ref,
    w_middle_ref,
    w_last_ref,
    grad_last_ref,
    slope_ref,
    tilt_first_ref,
    tilt_second_ref,
    patch_middle_ref,
    patch_last_ref,
    student_ref,
):
    first_col = band_ref[0] * own
    n_first, n_second, n_slope = (
        own + 2 * HALO_FIRST,
        own + 2 * HALO_SECOND,
        own + 2 * HALO_SLOPE,
    )
    pre = dot(xcol_ref[...], w_first_ref[...], ((1,), (1,)))
    sigma = 1.0 / (1.0 + jnp.exp(-pre))
    act = jnp.where(
        inside(n_first * rows, rows, first_col - HALO_FIRST, total), pre * sigma, 0.0
    )
    lo = HALO_FIRST * rows
    pre_own, sigma_own = pre[lo : lo + own * rows], sigma[lo : lo + own * rows]
    tilt_first_ref[...] = sigma_own * (1.0 + pre_own * (1.0 - sigma_own))
    put_patch(patch_middle_ref, act, 2, rows, n_second)

    pre = dot(patch_middle_ref[...], w_middle_ref[...], ((1,), (1,)))
    sigma = 1.0 / (1.0 + jnp.exp(-pre))
    act = jnp.where(
        inside(n_second * rows, rows, first_col - HALO_SECOND, total), pre * sigma, 0.0
    )
    lo, n_back = (HALO_SECOND - HALO_BACK) * rows, (own + 2 * HALO_BACK) * rows
    pre_back, sigma_back = pre[lo : lo + n_back], sigma[lo : lo + n_back]
    tilt_second_ref[...] = jnp.where(
        inside(n_back, rows, first_col - HALO_BACK, total),
        sigma_back * (1.0 + pre_back * (1.0 - sigma_back)),
        0.0,
    )
    put_patch(patch_last_ref, act, 4, rows, n_slope)

    student_ref[...] = dot(patch_last_ref[...], w_last_ref[...], ((1,), (1,)))
    block = 4 * rows

    def slopes(step, carry):
        at = pl.ds(pl.multiple_of(step * block, block), block)
        student = student_ref[at, :]
        s_inv = lax.rsqrt(jnp.sum(student * student, -1, keepdims=True) + epsilon)
        target = teacher_ref[at, :].astype(f32)
        t_inv = lax.rsqrt(jnp.sum(target * target, -1, keepdims=True) + epsilon)
        s_unit = student * s_inv
        differ = s_unit - target * t_inv
        slope = (differ - s_unit * jnp.sum(s_unit * differ, -1, keepdims=True)) * s_inv
        ok = inside(block, rows, first_col - HALO_SLOPE + step * (block // rows), total)
        slope_ref[at, :] = jnp.where(ok, slope, 0.0).astype(bf16)
        return carry

    lax.fori_loop(0, n_slope * rows // block, slopes, 0)
    lo, n_own = HALO_SLOPE * rows, own * rows
    grad_last_ref[...] = dot(
        slope_ref[lo : lo + n_own, :], patch_last_ref[lo : lo + n_own, :], ((0,), (0,))
    ).astype(bf16)


def spread_back(parts_ref, step, rows, out_cols):
    depth = parts_ref.shape[1] // 9
    total = None
    for ky in range(3):
        line = None
        for kx in range(3):
            tap = 3 * ky + kx
            start = (2 - kx) * step * rows
            piece = parts_ref[start : start + out_cols * rows, tap * depth : (tap + 1) * depth]
            line = piece if line is None else line + piece
        line = row_shifted(line, (1 - ky) * step, rows)
        total = line if total is None else total + line
    return total


def back_kernel(
    own,
    rows,
    xcol_ref,
    slope_ref,
    tilt_first_ref,
    tilt_second_ref,
    patch_middle_ref,
    w_middle_ref,
    w_last_ref,
    grad_first_ref,
    grad_middle_ref,
    parts_last_ref,
    parts_middle_ref,
):
    n_own, n_back = own * rows, (own + 2 * HALO_BACK) * rows
    parts_last_ref[...] = dot(slope_ref[...], w_last_ref[...], ((1,), (0,)))
    back_second = spread_back(parts_last_ref, 4, rows, own + 2 * HALO_BACK)
    slope_second = (back_second * tilt_second_ref[...]).astype(bf16)
    lo, hi = HALO_BACK * rows, HALO_SECOND * rows
    grad_middle_ref[...] = dot(
        slope_second[lo : lo + n_own], patch_middle_ref[hi : hi + n_own, :], ((0,), (0,))
    ).astype(bf16)
    parts_middle_ref[...] = dot(slope_second, w_middle_ref[...], ((1,), (0,)))
    back_first = spread_back(parts_middle_ref, 2, rows, own)
    slope_first = (back_first * tilt_first_ref[...]).astype(bf16)
    hi = HALO_FIRST * rows
    grad_first_ref[...] = dot(slope_first, xcol_ref[hi : hi + n_own, :], ((0,), (0,))).astype(bf16)


def on_device(image_feats, teacher, w_first, w_middle, w_last):
    size = lax.axis_size("cols")
    me = lax.axis_index("cols")
    height, breadth, channels = teacher.shape
    in_depth = w_first.shape[1] // 9
    hidden = w_middle.shape[1] // 9
    rows, piece = height // 2, breadth // 2
    own = 4 * piece
    total = own * (size // 4)

    small = gather_rows(jnp.concatenate([w_first, w_middle], 1), me)
    kernel_last = gather_rows(w_last, me)
    kernel_first, kernel_middle = small[:, : 9 * in_depth], small[:, 9 * in_depth :]

    cells = jnp.concatenate([teacher, image_feats.reshape(height, breadth, in_depth)], 2)
    classes = cells.reshape(rows, 2, piece, 2, -1).transpose(3, 1, 2, 0, 4)
    classes = classes.reshape(4, piece, rows, -1)
    low = me % 4
    band = in_order([pick(classes, low)] + [swap(pick(classes, low ^ k), k) for k in (1, 2, 3)], low)
    x_band, t_band = band[:, :, channels:], band[:, :, :channels]

    def widen(array, halo):
        before = shift(array[own - halo :], 4)
        after = shift(array[:halo], -4)
        return jnp.concatenate([before, array, after], 0)

    x_wide = jnp.pad(widen(x_band, HALO_X), ((0, 0), (1, 1), (0, 0)))
    t_wide = widen(t_band, HALO_SLOPE)
    n_first, n_slope, n_back = own + 2 * HALO_FIRST, own + 2 * HALO_SLOPE, own + 2 * HALO_BACK
    xcol = jnp.concatenate(
        [x_wide[kx : kx + n_first, ky : ky + rows] for ky in range(3) for kx in range(3)], 2
    ).reshape(n_first * rows, 9 * in_depth)
    t_wide = t_wide.reshape(n_slope * rows, channels)

    vmem = pl.BlockSpec(memory_space=pltpu.VMEM)
    n_second = own + 2 * HALO_SECOND
    grad_last, slope, tilt_first, tilt_second, patch_middle = pl.pallas_call(
        functools.partial(front_kernel, own, rows, total),
        in_specs=[pl.BlockSpec(memory_space=pltpu.SMEM)] + [vmem] * 5,
        out_specs=[vmem] * 5,
        out_shape=[
            jax.ShapeDtypeStruct((channels, 9 * hidden), bf16),
            jax.ShapeDtypeStruct((n_slope * rows, channels), bf16),
            jax.ShapeDtypeStruct((own * rows, hidden), f32),
            jax.ShapeDtypeStruct((n_back * rows, hidden), f32),
            jax.ShapeDtypeStruct((n_second * rows, 9 * hidden), bf16),
        ],
        scratch_shapes=[
            pltpu.VMEM((n_slope * rows, 9 * hidden), bf16),
            pltpu.VMEM((n_slope * rows, channels), f32),
        ],
        compiler_params=pltpu.CompilerParams(vmem_limit_bytes=VMEM_LIMIT),
        name="front",
    )((me // 4).astype(jnp.int32).reshape(1), xcol, t_wide, kernel_first, kernel_middle, kernel_last)
    out_last = scatter_rows(grad_last, me)
    grad_first, grad_middle = pl.pallas_call(
        functools.partial(back_kernel, own, rows),
        in_specs=[vmem] * 7,
        out_specs=[vmem] * 2,
        out_shape=[
            jax.ShapeDtypeStruct((hidden, 9 * in_depth), bf16),
            jax.ShapeDtypeStruct((hidden, 9 * hidden), bf16),
        ],
        scratch_shapes=[
            pltpu.VMEM((n_slope * rows, 9 * hidden), f32),
            pltpu.VMEM((n_back * rows, 9 * hidden), f32),
        ],
        compiler_params=pltpu.CompilerParams(vmem_limit_bytes=VMEM_LIMIT),
        name="back",
    )(xcol, slope, tilt_first, tilt_second, patch_middle, kernel_middle, kernel_last)
    out_small = scatter_rows(jnp.concatenate([grad_first, grad_middle], 1), me)
    return (out_small[:, : 9 * in_depth], out_small[:, 9 * in_depth :], out_last)


def solution(mesh):
    placed = (
        P("groups", "cols"),
        P("groups", "cols", None),
        P("cols", None),
        P("cols", None),
        P("cols", None),
    )
    return jax.shard_map(
        on_device,
        mesh=mesh,
        in_specs=placed,
        out_specs=(
            P(("groups", "cols"), None),
            P(("groups", "cols"), None),
            P(("groups", "cols"), None),
        ),
        check_vma=False,
    )
```

time: 293 us -> 85 us (0.29)
  waiting for transfers between devices: 157 us -> 15.5 us
  blocking collectives: 45.9 us -> 0 us
  matrix products: 25.6 us -> 0 us
  starting transfers between devices: 24.1 us -> 39.4 us
  between operations: 15.5 us -> 1.24 us
  Pallas kernels: 0 us -> 10.4 us
  local copies, waits for them, and re-layouts: 16.3 us -> 9.81 us
    unnamed x5 -> x0, waiting for transfers between devices: 153 us -> none
    all_gather x2 -> x0, blocking collectives: 45.9 us -> none  [the longest x1 25.7 us: on_device(): lax.all_gather(w_first, 'cols', axis=0, tiled=True)]
    dot_general x72 -> x0, matrix products: 25.6 us -> none  [the longest x27 12 us: weight_term(): lax.dot_general(flat_slope, window, (((0,), (0,)), ((), ())), preferred_e...]
    ppermute x10 -> x27, starting transfers between devices: 24 us -> 39.4 us  [the longest x23 27.1 us: swap(): return lax.ppermute(array, 'cols', [(i, i ^ mask) for i in range(size)])]
    ppermute x10 -> x27, waiting for transfers between devices: 3.6 us -> 15.5 us  [the longest x23 15.4 us: swap(): return lax.ppermute(array, 'cols', [(i, i ^ mask) for i in range(size)])]
    pallas_call x0 -> x2, Pallas kernels: none -> 10.4 us  [the longest x1 6.72 us: on_device(): pl.pallas_call(functools.partial(front_kernel, own, rows, total), in_spec...]
    unnamed x52 -> x6, local copies, waits for them, and re-layouts: 9.84 us -> 0.44 us
    mul x1 -> x0, other arithmetic: 4.79 us -> none  [on_device(): s_unit * jnp.sum(s_unit * differ, -1, keepdims=True)]
  transfers between devices with their start and end apart: 13 -> 27, of which waited for: 5 -> 6; matrix products, arithmetic and copies ran while one was open for 6% -> 17% of each run, Pallas kernels for 0% -> 0%
where the time goes in v1:
time: 85 us; the launch traced here: 84.4 us
  starting transfers between devices  39.4 us (46%)
  waiting for transfers between devices  15.5 us (18%)
  Pallas kernels  10.4 us (12%)
  local copies, waits for them, and re-layouts  9.81 us (12%)
  other arithmetic  8.1 us (10%)
  between operations  1.24 us (1%)
    ppermute x23, starting transfers between devices, swap(): return lax.ppermute(array, 'cols', [(i, i ^ mask) for i in range(size)])  27.1 us
    ppermute x23, waiting for transfers between devices, swap(): return lax.ppermute(array, 'cols', [(i, i ^ mask) for i in range(size)])  15.4 us
    ppermute x4, starting transfers between devices, shift(): lax.ppermute(array, 'cols', [(i, i + step) for i in range(size) if 0 <= i...  12.3 us
    pallas_call x1, Pallas kernels, on_device(): pl.pallas_call(functools.partial(front_kernel, own, rows, total), in_spec...  6.72 us
    pallas_call x1, Pallas kernels, on_device(): pl.pallas_call(functools.partial(back_kernel, own, rows), in_specs=[vmem]...  3.65 us
    concatenate x1, local copies, waits for them, and re-layouts, on_device(): jnp.concatenate([x_wide[kx:kx + n_first, ky:ky + rows] for ky in range(3)...  2.42 us
    concatenate x2, local copies, waits for them, and re-layouts, on_device(): jnp.concatenate([teacher, image_feats.reshape(height, breadth, in_depth)]...  2.24 us
  transfers between devices with their start and end apart: 27, of which 6 were waited for; matrix products, arithmetic and copies ran while one was open for 17% of the time, Pallas kernels for 0%

profile of v1, /device:TPU:0, one launch (start us, length us, event | category | flops | bytes accessed | tf_op | source)
XLA Modules:
  0.0 84.4 jit_solution(8796254145474177610)
XLA Ops:
  0.6 0.8 fusion.6
  1.4 5.1 %collective-permute-start.9 = (bf16[8,1728]{1,0:T(8,128)(2,1)S(1)}, bf16[8,1728]{1,0:T(8,128)(2,1)S(1)}, u32[]{:S(2)}, u32[]{:S(2)}) collective-permute-start(bf16[8,1728]{1,0:T(8,128)(2,1)S(1)} %get-tuple-element.45), channel_id=1, source_target_pairs={{0,12},{1,13},{2,14},{3,15},{4,8},{5,9},{6,10},{7,11},{8,4},{9,5},... | collective-permute-start | bytes 82952 | tf_op jit(solution)/shard_map/ppermute | solution.py:18
  7.1 3.7 %collective-permute-start.14 = (bf16[32,1152]{1,0:T(8,128)(2,1)}, bf16[32,1152]{1,0:T(8,128)(2,1)S(1)}, u32[]{:S(2)}, u32[]{:S(2)}) collective-permute-start(bf16[32,1152]{1,0:T(8,128)(2,1)} %param.9), channel_id=1, source_target_pairs={{0,12},{1,13},{2,14},{3,15},{4,8},{5,9},{6,10},{7,11},{8,4},{9,5},... | collective-permute-start | bytes 221192 | tf_op jit(solution)/shard_map/ppermute | solution.py:18
  10.9 1.0 %concatenate.274 = bf16[16,2,8,2,64]{4,3,2,1,0:T(2,128)(2,1)S(1)} reshape(bf16[32,1024]{1,0:T(8,128)(2,1)} %param.5) | data formatting | bytes 131072 | tf_op jit(solution)/shard_map/concatenate | solution.py:236
  11.9 1.2 %concatenate.273 = bf16[16,2,8,2,512]{4,3,2,1,0:T(2,128)(2,1)S(1)} reshape(bf16[32,16,512]{2,1,0:T(8,128)(2,1)} %param.6) | data formatting | bytes 1048576 | tf_op jit(solution)/shard_map/concatenate | solution.py:236
  15.4 1.7 %collective-permute-start.1 = (bf16[8,16,576]{2,1,0:T(8,128)(2,1)S(1)}, bf16[8,16,576]{2,1,0:T(8,128)(2,1)S(1)}, u32[]{:S(2)}, u32[]{:S(2)}) collective-permute-start(bf16[8,16,576]{2,1,0:T(8,128)(2,1)S(1)} %get-tuple-element.27), channel_id=1, source_target_pairs={{0,2},{1,3},{2,0},{3,1},{4,6},{5,7},{6,4},{7,5},{8,10},{9,11},{10,... | collective-permute-start | bytes 442376 | tf_op jit(solution)/shard_map/ppermute | solution.py:18
  17.5 1.7 %collective-permute-start.10 = (bf16[4,8,1728]{2,1,0:T(8,128)(2,1)S(1)}, bf16[4,8,1728]{2,1,0:T(8,128)(2,1)S(1)}, u32[]{:S(2)}, u32[]{:S(2)}) collective-permute-start(bf16[4,8,1728]{2,1,0:T(8,128)(2,1)S(1)} %maximum_select_fusion.14), channel_id=1, source_target_pairs={{0,2},{1,3},{2,0},{3,1},{4,6},{5,7},{6,4},{7,5},{8,10},{9,11},{10,... | collective-permute-start | bytes 331784 | tf_op jit(solution)/shard_map/ppermute | solution.py:18
  19.3 0.8 maximum_select_fusion.8
  20.1 1.4 %collective-permute-start.15 = (bf16[4,32,1152]{2,1,0:T(8,128)(2,1)}, bf16[4,32,1152]{2,1,0:T(8,128)(2,1)S(1)}, u32[]{:S(2)}, u32[]{:S(2)}) collective-permute-start(bf16[4,32,1152]{2,1,0:T(8,128)(2,1)} %maximum_select_fusion.8), channel_id=1, source_target_pairs={{0,2},{1,3},{2,0},{3,1},{4,6},{5,7},{6,4},{7,5},{8,10},{9,11},{10,... | collective-permute-start | bytes 884744 | tf_op jit(solution)/shard_map/ppermute | solution.py:18
  21.4 6.6 %collective-permute-done.10 = bf16[4,8,1728]{2,1,0:T(8,128)(2,1)S(1)} collective-permute-done((bf16[4,8,1728]{2,1,0:T(8,128)(2,1)S(1)}, bf16[4,8,1728]{2,1,0:T(8,128)(2,1)S(1)}, u32[]{:S(2)}, u32[]{:S(2)}) %collective-permute-start.10) | collective-permute-done | bytes 110624 | tf_op jit(solution)/shard_map/ppermute | solution.py:18
  29.9 1.3 %collective-permute-start.4 = (bf16[13,16,64]{2,1,0:T(8,128)(2,1)S(1)}, bf16[13,16,64]{2,1,0:T(8,128)(2,1)S(1)}, u32[]{:S(2)}, u32[]{:S(2)}) collective-permute-start(bf16[13,16,64]{2,1,0:T(8,128)(2,1)S(1)} %get-tuple-element.24), channel_id=1, source_target_pairs={{4,0},{5,1},{6,2},{7,3},{8,4},{9,5},{10,6},{11,7},{12,8},{13,9},{1... | collective-permute-start | bytes 79880 | tf_op jit(solution)/shard_map/ppermute | solution.py:23
  31.2 4.5 %collective-permute-start.3 = (bf16[13,16,64]{2,1,0:T(8,128)(2,1)S(1)}, bf16[13,16,64]{2,1,0:T(8,128)(2,1)S(1)}, u32[]{:S(2)}, u32[]{:S(2)}) collective-permute-start(bf16[13,16,64]{2,1,0:T(8,128)(2,1)S(1)} %get-tuple-element.23), channel_id=1, source_target_pairs={{0,4},{1,5},{2,6},{3,7},{4,8},{5,9},{6,10},{7,11},{8,12},{9,13},{1... | collective-permute-start | bytes 79880 | tf_op jit(solution)/shard_map/ppermute | solution.py:23
  36.5 1.3 %collective-permute-start.6 = (bf16[6,16,512]{2,1,0:T(8,128)(2,1)}, bf16[6,16,512]{2,1,0:T(8,128)(2,1)}, u32[]{:S(2)}, u32[]{:S(2)}) collective-permute-start(bf16[6,16,512]{2,1,0:T(8,128)(2,1)} %get-tuple-element.22), channel_id=1, source_target_pairs={{4,0},{5,1},{6,2},{7,3},{8,4},{9,5},{10,6},{11,7},{12,8},{13,9},{1... | collective-permute-start | bytes 294920 | tf_op jit(solution)/shard_map/ppermute | solution.py:23
  37.8 5.2 %collective-permute-start.5 = (bf16[6,16,512]{2,1,0:T(8,128)(2,1)}, bf16[6,16,512]{2,1,0:T(8,128)(2,1)}, u32[]{:S(2)}, u32[]{:S(2)}) collective-permute-start(bf16[6,16,512]{2,1,0:T(8,128)(2,1)} %get-tuple-element.21), channel_id=1, source_target_pairs={{0,4},{1,5},{2,6},{3,7},{4,8},{5,9},{6,10},{7,11},{8,12},{9,13},{1... | collective-permute-start | bytes 294920 | tf_op jit(solution)/shard_map/ppermute | solution.py:23
  43.1 1.1 %pad_slice_fusion = (bf16[56,16,64]{2,1,0:T(8,128)(2,1)S(1)}, bf16[56,16,64]{2,1,0:T(8,128)(2,1)S(1)}, bf16[56,16,64]{2,1,0:T(8,128)(2,1)S(1)}, bf16[56,16,64]{2...) fusion(bf16[58,16,64]{2,1,0:T(8,128)(2,1)S(1)} %pad_maximum_fus, ...), kind=kLoop, calls=%fused_computation.13 | loop fusion | bytes 1957888 | tf_op jit(solution)/shard_map/slice | solution.py:252
  44.1 2.4 %concatenate.283 = bf16[56,16,576]{2,1,0:T(8,128)(2,1)S(1)} concatenate(bf16[56,16,64]{2,1,0:T(8,128)(2,1)} %get-tuple-element.40, bf16[56,16,64]{2,1,0:T(8,128)(2,1)S(1)} %get-tuple-element.33, bf16[56,16,64]{2,1,0:T(8,128)(2,1)S(1)} %get-tuple-element.34, bf16[56,16,64]{2,1,0:T(8,128)(2,1)} %get-tuple-element.39, bf16[56,16,64]{2,1,0:T(8,128)(2,1)} %get-tuple-element.38, ...), dimensions={2} | concatenate | bytes 2064384 | tf_op jit(solution)/shard_map/concatenate | solution.py:251
  46.8 0.8 slice-done
  47.6 1.0 %pad_maximum_fusion = bf16[44,16,512]{2,1,0:T(8,128)(2,1)S(1)} fusion(bf16[6,16,512]{2,1,0:T(8,128)(2,1)} %collective-permute-done.6, bf16[32,16,512]{2,1,0:T(8,128)(2,1)S(1)} %slice-done, bf16[6,16,512]{2,1,0:T(8,128)(2,1)} %collective-permute-done.5), kind=kLoop, calls=%fused_computation.2 | loop fusion | flops 720896 | bytes 1441792 | tf_op jit(solution)/shard_map/concatenate | solution.py:246
  48.7 1.1 %maximum_select_fusion.4 = bf16[4,2,2,8,1728]{4,3,0,1,2:T(8,128)(2,1)S(1)} fusion(bf16[4,2,1,8,1728]{4,3,0,1,2:T(8,128)(2,1)} %bitcast.18, bf16[4,2,1,8,1728]{4,3,0,1,2:T(8,128)(2,1)S(1)} %copy-done.1, pred[]{:T(512)S(6)} %eq.24), kind=kLoop, calls=%fused_computation.10 | loop fusion | flops 663552 | bytes 884737 | tf_op jit(solution)/shard_map/jit(_where)/select_n | solution.py:53
  50.5 6.7 %front.1 = (bf16[512,1152]{1,0:T(8,128)(2,1)S(1)}, bf16[704,512]{1,0:T(8,128)(2,1)S(1)}, f32[512,128]{1,0:T(8,128)S(1)}, f32[576,128]{1,0:T(8,128)S(1)}, bf16[832,1152]{1,0:T(8,128)(2,1)}) custom-call(s32[1]{0:T(128)} %bitcast.7.band_ref, bf16[896,576]{1,0:T(8,128)(2,1)S(1)} %bitcast.89, bf16[704,512]{1,0:T(8,128)(2,1)S(1)} %bitcast.91, ...), custom_call_target="tpu_custom_call" | custom-call | tf_op jit(solution)/shard_map/front/pallas_call | solution.py:258
  57.2 3.6 %back.1 = (bf16[128,576]{1,0:T(8,128)(2,1)S(1)}, bf16[128,1152]{1,0:T(8,128)(2,1)S(1)}) custom-call(bf16[896,576]{1,0:T(8,128)(2,1)S(1)} %bitcast.90, bf16[704,512]{1,0:T(8,128)(2,1)S(1)} %get-tuple-element.10.slope_ref, f32[512,128]{1,0:T(8,128)S(1)} %get-tuple-element.11.tilt_first_ref, f32[576,128]{1,0:T(8,128)S(1)} %get-tuple-element.12.tilt_second_ref, ...), custom_call_target="tpu_custom_call" | custom-call | tf_op jit(solution)/shard_map/back/pallas_call | solution.py:277
  61.8 0.9 %collective-permute-done.17 = bf16[4,2,8,1728]{3,2,1,0:T(8,128)(2,1)S(1)} collective-permute-done((bf16[4,2,8,1728]{3,2,1,0:T(8,128)(2,1)S(1)}, bf16[4,2,8,1728]{3,2,1,0:T(8,128)(2,1)S(1)}, u32[]{:S(2)}, u32[]{:S(2)}) %collective-permute-start.17) | collective-permute-done | bytes 221216 | tf_op jit(solution)/shard_map/ppermute | solution.py:18
  62.7 1.6 %collective-permute-start.18 = (bf16[4,8,1728]{2,1,0:T(8,128)(2,1)S(1)}, bf16[4,8,1728]{2,1,0:T(8,128)(2,1)S(1)}, u32[]{:S(2)}, u32[]{:S(2)}) collective-permute-start(bf16[4,8,1728]{2,1,0:T(8,128)(2,1)S(1)} %fusion.3), channel_id=1, source_target_pairs={{0,2},{1,3},{2,0},{3,1},{4,6},{5,7},{6,4},{7,5},{8,10},{9,11},{10,... | collective-permute-start | bytes 331784 | tf_op jit(solution)/shard_map/ppermute | solution.py:18
  64.5 0.8 collective-permute-start.23
  65.3 3.5 %collective-permute-done.18 = bf16[4,8,1728]{2,1,0:T(8,128)(2,1)S(1)} collective-permute-done((bf16[4,8,1728]{2,1,0:T(8,128)(2,1)S(1)}, bf16[4,8,1728]{2,1,0:T(8,128)(2,1)S(1)}, u32[]{:S(2)}, u32[]{:S(2)}) %collective-permute-start.18) | collective-permute-done | bytes 110624 | tf_op jit(solution)/shard_map/ppermute | solution.py:18
  68.8 1.9 %collective-permute-start.21 = (bf16[8,1728]{1,0:T(8,128)(2,1)S(1)}, bf16[8,1728]{1,0:T(8,128)(2,1)S(1)}, u32[]{:S(2)}, u32[]{:S(2)}) collective-permute-start(bf16[8,1728]{1,0:T(8,128)(2,1)S(1)} %get-tuple-element.42), channel_id=1, source_target_pairs={{0,12},{1,13},{2,14},{3,15},{4,8},{5,9},{6,10},{7,11},{8,4},{9,5},... | collective-permute-start | bytes 82952 | tf_op jit(solution)/shard_map/ppermute | solution.py:18
  71.1 2.2 %collective-permute-start.19 = (bf16[8,1728]{1,0:T(8,128)(2,1)S(1)}, bf16[8,1728]{1,0:T(8,128)(2,1)S(1)}, u32[]{:S(2)}, u32[]{:S(2)}) collective-permute-start(bf16[8,1728]{1,0:T(8,128)(2,1)S(1)} %get-tuple-element.41), channel_id=1, source_target_pairs={{0,4},{1,5},{2,6},{3,7},{4,0},{5,1},{6,2},{7,3},{8,12},{9,13},{10,... | collective-permute-start | bytes 82952 | tf_op jit(solution)/shard_map/ppermute | solution.py:18
  73.3 1.0 %collective-permute-done.23 = bf16[4,32,1152]{2,1,0:T(8,128)(2,1)S(1)} collective-permute-done((bf16[4,32,1152]{2,1,0:T(8,128)(2,1)S(1)}, bf16[4,32,1152]{2,1,0:T(8,128)(2,1)S(1)}, u32[]{:S(2)}, u32[]{:S(2)}) %collective-permute-start.23) | collective-permute-done | bytes 294944 | tf_op jit(solution)/shard_map/ppermute | solution.py:18
  74.4 1.9 %collective-permute-start.26 = (bf16[32,1152]{1,0:T(8,128)(2,1)S(1)}, bf16[32,1152]{1,0:T(8,128)(2,1)S(1)}, u32[]{:S(2)}, u32[]{:S(2)}) collective-permute-start(bf16[32,1152]{1,0:T(8,128)(2,1)S(1)} %get-tuple-element.30), channel_id=1, source_target_pairs={{0,12},{1,13},{2,14},{3,15},{4,8},{5,9},{6,10},{7,11},{8,4},{9,5},... | collective-permute-start | bytes 221192 | tf_op jit(solution)/shard_map/ppermute | solution.py:18
  76.7 2.2 %collective-permute-start.24 = (bf16[32,1152]{1,0:T(8,128)(2,1)S(1)}, bf16[32,1152]{1,0:T(8,128)(2,1)S(1)}, u32[]{:S(2)}, u32[]{:S(2)}) collective-permute-start(bf16[32,1152]{1,0:T(8,128)(2,1)S(1)} %get-tuple-element.29), channel_id=1, source_target_pairs={{0,4},{1,5},{2,6},{3,7},{4,0},{5,1},{6,2},{7,3},{8,12},{9,13},{10,... | collective-permute-start | bytes 221192 | tf_op jit(solution)/shard_map/ppermute | solution.py:18
  80.2 1.2 %collective-permute-done.26 = bf16[32,1152]{1,0:T(8,128)(2,1)S(1)} collective-permute-done((bf16[32,1152]{1,0:T(8,128)(2,1)S(1)}, bf16[32,1152]{1,0:T(8,128)(2,1)S(1)}, u32[]{:S(2)}, u32[]{:S(2)}) %collective-permute-start.26) | collective-permute-done | bytes 73760 | tf_op jit(solution)/shard_map/ppermute | solution.py:18
  81.3 2.3 %collective-permute-done.25 = bf16[32,1152]{1,0:T(8,128)(2,1)S(1)} collective-permute-done((bf16[32,1152]{1,0:T(8,128)(2,1)S(1)}, bf16[32,1152]{1,0:T(8,128)(2,1)S(1)}, u32[]{:S(2)}, u32[]{:S(2)}) %collective-permute-start.25) | collective-permute-done | bytes 73760 | tf_op jit(solution)/shard_map/ppermute | solution.py:18
  (85 shorter events, 10.7 us)
Async XLA Ops:
  1.4 12.8 %collective-permute-start.9 = (bf16[8,1728]{1,0:T(8,128)(2,1)S(1)}, bf16[8,1728]{1,0:T(8,128)(2,1)S(1)}, u32[]{:S(2)}, u32[]{:S(2)}) collective-permute-start(bf16[8,1728]{1,0:T(8,128)(2,1)S(1)} %get-tuple-element.45), channel_id=1, source_target_pairs={{0,12},{1,13},{2,14},{3,15},{4,8},{5,9},{6,10},{7,11},{8,4},{9,5},... | collective-permute-start | bytes 82952 | tf_op jit(solution)/shard_map/ppermute | solution.py:18
  6.5 8.9 %collective-permute-start.8 = (bf16[8,1728]{1,0:T(8,128)(2,1)S(1)}, bf16[8,1728]{1,0:T(8,128)(2,1)S(1)}, u32[]{:S(2)}, u32[]{:S(2)}) collective-permute-start(bf16[8,1728]{1,0:T(8,128)(2,1)S(1)} %get-tuple-element.45), channel_id=1, source_target_pairs={{0,8},{1,9},{2,10},{3,11},{4,12},{5,13},{6,14},{7,15},{8,0},{9,1},... | collective-permute-start | bytes 82952 | tf_op jit(solution)/shard_map/ppermute | solution.py:18
  6.5 8.9 %collective-permute-start.7 = (bf16[8,1728]{1,0:T(8,128)(2,1)S(1)}, bf16[8,1728]{1,0:T(8,128)(2,1)S(1)}, u32[]{:S(2)}, u32[]{:S(2)}) collective-permute-start(bf16[8,1728]{1,0:T(8,128)(2,1)S(1)} %get-tuple-element.45), channel_id=1, source_target_pairs={{0,4},{1,5},{2,6},{3,7},{4,0},{5,1},{6,2},{7,3},{8,12},{9,13},{10,... | collective-permute-start | bytes 82952 | tf_op jit(solution)/shard_map/ppermute | solution.py:18
  7.1 10.1 %collective-permute-start.14 = (bf16[32,1152]{1,0:T(8,128)(2,1)}, bf16[32,1152]{1,0:T(8,128)(2,1)S(1)}, u32[]{:S(2)}, u32[]{:S(2)}) collective-permute-start(bf16[32,1152]{1,0:T(8,128)(2,1)} %param.9), channel_id=1, source_target_pairs={{0,12},{1,13},{2,14},{3,15},{4,8},{5,9},{6,10},{7,11},{8,4},{9,5},... | collective-permute-start | bytes 221192 | tf_op jit(solution)/shard_map/ppermute | solution.py:18
  10.9 6.6 %collective-permute-start.13 = (bf16[32,1152]{1,0:T(8,128)(2,1)}, bf16[32,1152]{1,0:T(8,128)(2,1)S(1)}, u32[]{:S(2)}, u32[]{:S(2)}) collective-permute-start(bf16[32,1152]{1,0:T(8,128)(2,1)} %param.9), channel_id=1, source_target_pairs={{0,8},{1,9},{2,10},{3,11},{4,12},{5,13},{6,14},{7,15},{8,0},{9,1},... | collective-permute-start | bytes 221192 | tf_op jit(solution)/shard_map/ppermute | solution.py:18
  13.8 0.9 %copy-start.2 = (bf16[32,1152]{1,0:T(8,128)(2,1)S(1)}, bf16[32,1152]{1,0:T(8,128)(2,1)}, u32[]{:S(2)}) copy-start(bf16[32,1152]{1,0:T(8,128)(2,1)} %param.9) | copy-start | bytes 221188
  14.7 4.5 %collective-permute-start.12 = (bf16[32,1152]{1,0:T(8,128)(2,1)S(1)}, bf16[32,1152]{1,0:T(8,128)(2,1)S(1)}, u32[]{:S(2)}, u32[]{:S(2)}) collective-permute-start(bf16[32,1152]{1,0:T(8,128)(2,1)S(1)} %copy-done.2), channel_id=1, source_target_pairs={{0,4},{1,5},{2,6},{3,7},{4,0},{5,1},{6,2},{7,3},{8,12},{9,13},{10,... | collective-permute-start | bytes 221192 | tf_op jit(solution)/shard_map/ppermute | solution.py:18
  15.3 14.1 %collective-permute-start.2 = (bf16[8,16,576]{2,1,0:T(8,128)(2,1)S(1)}, bf16[8,16,576]{2,1,0:T(8,128)(2,1)S(1)}, u32[]{:S(2)}, u32[]{:S(2)}) collective-permute-start(bf16[8,16,576]{2,1,0:T(8,128)(2,1)S(1)} %get-tuple-element.26), channel_id=1, source_target_pairs={{0,3},{1,2},{2,1},{3,0},{4,7},{5,6},{6,5},{7,4},{8,11},{9,10},{10,... | collective-permute-start | bytes 442376 | tf_op jit(solution)/shard_map/ppermute | solution.py:18
  15.4 14.1 %collective-permute-start.1 = (bf16[8,16,576]{2,1,0:T(8,128)(2,1)S(1)}, bf16[8,16,576]{2,1,0:T(8,128)(2,1)S(1)}, u32[]{:S(2)}, u32[]{:S(2)}) collective-permute-start(bf16[8,16,576]{2,1,0:T(8,128)(2,1)S(1)} %get-tuple-element.27), channel_id=1, source_target_pairs={{0,2},{1,3},{2,0},{3,1},{4,6},{5,7},{6,4},{7,5},{8,10},{9,11},{10,... | collective-permute-start | bytes 442376 | tf_op jit(solution)/shard_map/ppermute | solution.py:18
  17.2 12.4 %collective-permute-start = (bf16[8,16,576]{2,1,0:T(8,128)(2,1)S(1)}, bf16[8,16,576]{2,1,0:T(8,128)(2,1)S(1)}, u32[]{:S(2)}, u32[]{:S(2)}) collective-permute-start(bf16[8,16,576]{2,1,0:T(8,128)(2,1)S(1)} %get-tuple-element.28), channel_id=1, source_target_pairs={{0,1},{1,0},{2,3},{3,2},{4,5},{5,4},{6,7},{7,6},{8,9},{9,8},{10,11... | collective-permute-start | bytes 442376 | tf_op jit(solution)/shard_map/ppermute | solution.py:18
  17.5 10.5 %collective-permute-start.10 = (bf16[4,8,1728]{2,1,0:T(8,128)(2,1)S(1)}, bf16[4,8,1728]{2,1,0:T(8,128)(2,1)S(1)}, u32[]{:S(2)}, u32[]{:S(2)}) collective-permute-start(bf16[4,8,1728]{2,1,0:T(8,128)(2,1)S(1)} %maximum_select_fusion.14), channel_id=1, source_target_pairs={{0,2},{1,3},{2,0},{3,1},{4,6},{5,7},{6,4},{7,5},{8,10},{9,11},{10,... | collective-permute-start | bytes 331784 | tf_op jit(solution)/shard_map/ppermute | solution.py:18
  20.1 26.5 %collective-permute-start.15 = (bf16[4,32,1152]{2,1,0:T(8,128)(2,1)}, bf16[4,32,1152]{2,1,0:T(8,128)(2,1)S(1)}, u32[]{:S(2)}, u32[]{:S(2)}) collective-permute-start(bf16[4,32,1152]{2,1,0:T(8,128)(2,1)} %maximum_select_fusion.8), channel_id=1, source_target_pairs={{0,2},{1,3},{2,0},{3,1},{4,6},{5,7},{6,4},{7,5},{8,10},{9,11},{10,... | collective-permute-start | bytes 884744 | tf_op jit(solution)/shard_map/ppermute | solution.py:18
  28.7 19.9 %collective-permute-start.11 = (bf16[4,2,8,1728]{3,2,0,1:T(8,128)(2,1)}, bf16[4,2,8,1728]{3,2,0,1:T(8,128)(2,1)}, u32[]{:S(2)}, u32[]{:S(2)}) collective-permute-start(bf16[4,2,8,1728]{3,2,0,1:T(8,128)(2,1)} %maximum_select_fusion.10), channel_id=1, source_target_pairs={{0,1},{1,0},{2,3},{3,2},{4,5},{5,4},{6,7},{7,6},{8,9},{9,8},{10,11... | collective-permute-start | bytes 663560 | tf_op jit(solution)/shard_map/ppermute | solution.py:18
  29.9 13.2 %copy-start = (bf16[32,16,576]{2,1,0:T(8,128)(2,1)}, bf16[32,16,576]{2,1,0:T(8,128)(2,1)S(1)}, u32[]{:S(2)}) copy-start(bf16[32,16,576]{2,1,0:T(8,128)(2,1)S(1)} %maximum_select_fusion.1) | copy-start | bytes 1769476
  29.9 7.9 %collective-permute-start.4 = (bf16[13,16,64]{2,1,0:T(8,128)(2,1)S(1)}, bf16[13,16,64]{2,1,0:T(8,128)(2,1)S(1)}, u32[]{:S(2)}, u32[]{:S(2)}) collective-permute-start(bf16[13,16,64]{2,1,0:T(8,128)(2,1)S(1)} %get-tuple-element.24), channel_id=1, source_target_pairs={{4,0},{5,1},{6,2},{7,3},{8,4},{9,5},{10,6},{11,7},{12,8},{13,9},{1... | collective-permute-start | bytes 79880 | tf_op jit(solution)/shard_map/ppermute | solution.py:23
  31.2 11.8 %collective-permute-start.3 = (bf16[13,16,64]{2,1,0:T(8,128)(2,1)S(1)}, bf16[13,16,64]{2,1,0:T(8,128)(2,1)S(1)}, u32[]{:S(2)}, u32[]{:S(2)}) collective-permute-start(bf16[13,16,64]{2,1,0:T(8,128)(2,1)S(1)} %get-tuple-element.23), channel_id=1, source_target_pairs={{0,4},{1,5},{2,6},{3,7},{4,8},{5,9},{6,10},{7,11},{8,12},{9,13},{1... | collective-permute-start | bytes 79880 | tf_op jit(solution)/shard_map/ppermute | solution.py:23
  36.5 10.3 %collective-permute-start.6 = (bf16[6,16,512]{2,1,0:T(8,128)(2,1)}, bf16[6,16,512]{2,1,0:T(8,128)(2,1)}, u32[]{:S(2)}, u32[]{:S(2)}) collective-permute-start(bf16[6,16,512]{2,1,0:T(8,128)(2,1)} %get-tuple-element.22), channel_id=1, source_target_pairs={{4,0},{5,1},{6,2},{7,3},{8,4},{9,5},{10,6},{11,7},{12,8},{13,9},{1... | collective-permute-start | bytes 294920 | tf_op jit(solution)/shard_map/ppermute | solution.py:23
  37.8 9.0 %collective-permute-start.5 = (bf16[6,16,512]{2,1,0:T(8,128)(2,1)}, bf16[6,16,512]{2,1,0:T(8,128)(2,1)}, u32[]{:S(2)}, u32[]{:S(2)}) collective-permute-start(bf16[6,16,512]{2,1,0:T(8,128)(2,1)} %get-tuple-element.21), channel_id=1, source_target_pairs={{0,4},{1,5},{2,6},{3,7},{4,8},{5,9},{6,10},{7,11},{8,12},{9,13},{1... | collective-permute-start | bytes 294920 | tf_op jit(solution)/shard_map/ppermute | solution.py:23
  46.6 1.0 %slice-start = ((bf16[32,16,576]{2,1,0:T(8,128)(2,1)}), bf16[32,16,512]{2,1,0:T(8,128)(2,1)S(1)}, s32[]{:S(2)}) async-start(bf16[32,16,576]{2,1,0:T(8,128)(2,1)} %copy-done), calls=%async_computation | async-start | bytes 1048576 | tf_op jit(solution)/shard_map/slice | solution.py:241
  46.6 2.1 %copy-start.1 = (bf16[4,2,1,8,1728]{4,3,0,1,2:T(8,128)(2,1)S(1)}, bf16[4,2,1,8,1728]{4,3,0,1,2:T(8,128)(2,1)}, u32[]{:S(2)}) copy-start(bf16[4,2,1,8,1728]{4,3,0,1,2:T(8,128)(2,1)} %maximum_select_fusion.9) | copy-start | bytes 663556
  46.7 3.4 %collective-permute-start.16 = (bf16[4,2,32,1152]{3,2,0,1:T(8,128)(2,1)S(1)}, bf16[4,2,32,1152]{3,2,0,1:T(8,128)(2,1)S(1)}, u32[]{:S(2)}, u32[]{:S(2)}) collective-permute-start(bf16[4,2,32,1152]{3,2,0,1:T(8,128)(2,1)S(1)} %maximum_select_fusion.3), channel_id=1, source_target_pairs={{0,1},{1,0},{2,3},{3,2},{4,5},{5,4},{6,7},{7,6},{8,9},{9,8},{10,11... | collective-permute-start | bytes 1769480 | tf_op jit(solution)/shard_map/ppermute | solution.py:18
  61.1 1.6 %collective-permute-start.17 = (bf16[4,2,8,1728]{3,2,1,0:T(8,128)(2,1)S(1)}, bf16[4,2,8,1728]{3,2,1,0:T(8,128)(2,1)S(1)}, u32[]{:S(2)}, u32[]{:S(2)}) collective-permute-start(bf16[4,2,8,1728]{3,2,1,0:T(8,128)(2,1)S(1)} %dynamic-slice_bitcast_fusion.1), channel_id=1, source_target_pairs={{0,1},{1,0},{2,3},{3,2},{4,5},{5,4},{6,7},{7,6},{8,9},{9,8},{10,11... | collective-permute-start | bytes 663560 | tf_op jit(solution)/shard_map/ppermute | solution.py:18
  61.2 3.1 %collective-permute-start.22 = (bf16[4,2,32,1152]{3,2,1,0:T(8,128)(2,1)S(1)}, bf16[4,2,32,1152]{3,2,1,0:T(8,128)(2,1)S(1)}, u32[]{:S(2)}, u32[]{:S(2)}) collective-permute-start(bf16[4,2,32,1152]{3,2,1,0:T(8,128)(2,1)S(1)} %dynamic-slice_bitcast_fusion), channel_id=1, source_target_pairs={{0,1},{1,0},{2,3},{3,2},{4,5},{5,4},{6,7},{7,6},{8,9},{9,8},{10,11... | collective-permute-start | bytes 1769480 | tf_op jit(solution)/shard_map/ppermute | solution.py:18
  62.7 6.1 %collective-permute-start.18 = (bf16[4,8,1728]{2,1,0:T(8,128)(2,1)S(1)}, bf16[4,8,1728]{2,1,0:T(8,128)(2,1)S(1)}, u32[]{:S(2)}, u32[]{:S(2)}) collective-permute-start(bf16[4,8,1728]{2,1,0:T(8,128)(2,1)S(1)} %fusion.3), channel_id=1, source_target_pairs={{0,2},{1,3},{2,0},{3,1},{4,6},{5,7},{6,4},{7,5},{8,10},{9,11},{10,... | collective-permute-start | bytes 331784 | tf_op jit(solution)/shard_map/ppermute | solution.py:18
  64.5 9.7 %collective-permute-start.23 = (bf16[4,32,1152]{2,1,0:T(8,128)(2,1)S(1)}, bf16[4,32,1152]{2,1,0:T(8,128)(2,1)S(1)}, u32[]{:S(2)}, u32[]{:S(2)}) collective-permute-start(bf16[4,32,1152]{2,1,0:T(8,128)(2,1)S(1)} %fusion), channel_id=1, source_target_pairs={{0,2},{1,3},{2,0},{3,1},{4,6},{5,7},{6,4},{7,5},{8,10},{9,11},{10,... | collective-permute-start | bytes 884744 | tf_op jit(solution)/shard_map/ppermute | solution.py:18
  68.8 7.9 %collective-permute-start.21 = (bf16[8,1728]{1,0:T(8,128)(2,1)S(1)}, bf16[8,1728]{1,0:T(8,128)(2,1)S(1)}, u32[]{:S(2)}, u32[]{:S(2)}) collective-permute-start(bf16[8,1728]{1,0:T(8,128)(2,1)S(1)} %get-tuple-element.42), channel_id=1, source_target_pairs={{0,12},{1,13},{2,14},{3,15},{4,8},{5,9},{6,10},{7,11},{8,4},{9,5},... | collective-permute-start | bytes 82952 | tf_op jit(solution)/shard_map/ppermute | solution.py:18
  70.8 8.1 %collective-permute-start.20 = (bf16[8,1728]{1,0:T(8,128)(2,1)S(1)}, bf16[8,1728]{1,0:T(8,128)(2,1)S(1)}, u32[]{:S(2)}, u32[]{:S(2)}) collective-permute-start(bf16[8,1728]{1,0:T(8,128)(2,1)S(1)} %get-tuple-element.43), channel_id=1, source_target_pairs={{0,8},{1,9},{2,10},{3,11},{4,12},{5,13},{6,14},{7,15},{8,0},{9,1},... | collective-permute-start | bytes 82952 | tf_op jit(solution)/shard_map/ppermute | solution.py:18
  71.1 7.7 %collective-permute-start.19 = (bf16[8,1728]{1,0:T(8,128)(2,1)S(1)}, bf16[8,1728]{1,0:T(8,128)(2,1)S(1)}, u32[]{:S(2)}, u32[]{:S(2)}) collective-permute-start(bf16[8,1728]{1,0:T(8,128)(2,1)S(1)} %get-tuple-element.41), channel_id=1, source_target_pairs={{0,4},{1,5},{2,6},{3,7},{4,0},{5,1},{6,2},{7,3},{8,12},{9,13},{10,... | collective-permute-start | bytes 82952 | tf_op jit(solution)/shard_map/ppermute | solution.py:18
  74.4 7.0 %collective-permute-start.26 = (bf16[32,1152]{1,0:T(8,128)(2,1)S(1)}, bf16[32,1152]{1,0:T(8,128)(2,1)S(1)}, u32[]{:S(2)}, u32[]{:S(2)}) collective-permute-start(bf16[32,1152]{1,0:T(8,128)(2,1)S(1)} %get-tuple-element.30), channel_id=1, source_target_pairs={{0,12},{1,13},{2,14},{3,15},{4,8},{5,9},{6,10},{7,11},{8,4},{9,5},... | collective-permute-start | bytes 221192 | tf_op jit(solution)/shard_map/ppermute | solution.py:18
  76.3 7.3 %collective-permute-start.25 = (bf16[32,1152]{1,0:T(8,128)(2,1)S(1)}, bf16[32,1152]{1,0:T(8,128)(2,1)S(1)}, u32[]{:S(2)}, u32[]{:S(2)}) collective-permute-start(bf16[32,1152]{1,0:T(8,128)(2,1)S(1)} %get-tuple-element.31), channel_id=1, source_target_pairs={{0,8},{1,9},{2,10},{3,11},{4,12},{5,13},{6,14},{7,15},{8,0},{9,1},... | collective-permute-start | bytes 221192 | tf_op jit(solution)/shard_map/ppermute | solution.py:18
  76.7 7.0 %collective-permute-start.24 = (bf16[32,1152]{1,0:T(8,128)(2,1)S(1)}, bf16[32,1152]{1,0:T(8,128)(2,1)S(1)}, u32[]{:S(2)}, u32[]{:S(2)}) collective-permute-start(bf16[32,1152]{1,0:T(8,128)(2,1)S(1)} %get-tuple-element.29), channel_id=1, source_target_pairs={{0,4},{1,5},{2,6},{3,7},{4,0},{5,1},{6,2},{7,3},{8,12},{9,13},{10,... | collective-permute-start | bytes 221192 | tf_op jit(solution)/shard_map/ppermute | solution.py:18

commit v2 on v1

v2 whole, which is shorter than its diff:
```python
import functools

import jax
import jax.numpy as jnp
from jax import lax
from jax.experimental import pallas as pl
from jax.experimental.pallas import tpu as pltpu
from jax.sharding import PartitionSpec as P

epsilon = 1e-06
bf16, f32 = jnp.bfloat16, jnp.float32
MIB = 1024 * 1024
HALO_X, HALO_FIRST, HALO_SECOND, HALO_SLOPE, HALO_BACK = 13, 12, 10, 6, 2
BLOCKS, FAR = 16, 4


def swap(array, mask):
    size = lax.axis_size("cols")
    return lax.ppermute(array, "cols", [(i, i ^ mask) for i in range(size)])


def shift(array, step):
    size = lax.axis_size("cols")
    return lax.ppermute(
        array, "cols", [(i, i + step) for i in range(size) if 0 <= i + step < size]
    )


def neighbours(fold):
    size = lax.axis_size("cols")
    return [list(range(i, i + fold)) for i in range(0, size, fold)]


def dot(a, b, contract):
    return lax.dot_general(a, b, (contract, ((), ())), preferred_element_type=f32)


def iota(shape, axis):
    return lax.broadcasted_iota(jnp.int32, shape, axis)


def row_shifted(value, step, rows):
    count = value.shape[0]
    if step == 0:
        return value
    row = iota((count, 1), 0) % rows + step
    rolled = pltpu.roll(value, (-step) % count, 0)
    return jnp.where((row >= 0) & (row < rows), rolled, 0.0)


def inside(count, rows, first, total):
    col = iota((count, 1), 0) // rows + first
    return (col >= 0) & (col < total)


def put_patch(patch_ref, value, step, rows, out_cols):
    depth = value.shape[1]
    for ky in range(3):
        moved = row_shifted(value, (ky - 1) * step, rows).astype(bf16)
        for kx in range(3):
            tap = 3 * ky + kx
            start = kx * step * rows
            patch_ref[:, tap * depth : (tap + 1) * depth] = moved[start : start + out_cols * rows]


def spread_back(parts_ref, step, rows, out_cols):
    depth = parts_ref.shape[1] // 9
    total = None
    for ky in range(3):
        line = None
        for kx in range(3):
            tap = 3 * ky + kx
            start = (2 - kx) * step * rows
            piece = parts_ref[start : start + out_cols * rows, tap * depth : (tap + 1) * depth]
            line = piece if line is None else line + piece
        line = row_shifted(line, (1 - ky) * step, rows)
        total = line if total is None else total + line
    return total


def deal_kernel(
    at_ref,
    x_hbm,
    teacher_hbm,
    w_first_hbm,
    w_middle_hbm,
    w_last_hbm,
    kept_ref,
    sent_ref,
    shard_ref,
    x_ref,
    teacher_ref,
    w_first_ref,
    w_middle_ref,
    w_last_ref,
    arrived,
):
    copies = [
        pltpu.make_async_copy(source, target, arrived.at[i])
        for i, (source, target) in enumerate(
            (
                (teacher_hbm, teacher_ref),
                (x_hbm, x_ref),
                (w_last_hbm, w_last_ref),
                (w_middle_hbm, w_middle_ref),
                (w_first_hbm, w_first_ref),
            )
        )
    ]
    for copy in copies:
        copy.start()
    height, breadth, channels = teacher_ref.shape
    depth = x_ref.shape[1] // breadth
    rows, piece = height // 2, breadth // 2
    cells = rows * piece
    core, row = at_ref[1] % 2, at_ref[1] // 2
    out = iota((cells, 1), 0)
    col, line = out // rows, out % rows
    for copy in copies:
        copy.wait()
    r_last, r_small, taps = w_last_ref.shape[0], w_middle_ref.shape[0], w_first_ref.shape[1]
    shard_ref[:r_last] = w_last_ref[...]
    shard_ref[r_last : r_last + r_small] = w_middle_ref[...]
    shard_ref[r_last + r_small :, :taps] = w_first_ref[...]
    shard_ref[r_last + r_small :, taps:] = jnp.zeros(
        (r_small, shard_ref.shape[1] - taps), shard_ref.dtype
    )
    field = teacher_ref[...].reshape(height * breadth, channels)
    pairs = jnp.concatenate(
        [x_ref[:, 2 * depth * i : 2 * depth * (i + 1)] for i in range(piece)], 0
    )
    for rc, out_ref in ((1, sent_ref), (0, kept_ref)):
        row_parity = core ^ rc
        source = col * height + 2 * line + row_parity
        pick = (iota((cells, piece * height), 1) == source).astype(f32).astype(bf16)
        both = dot(pick, pairs, ((1,), (0,)))
        low, high = both[:, :depth], both[:, depth:]
        for ry in range(2):
            col_parity = row ^ ry
            source = (2 * line + row_parity) * breadth + 2 * col + col_parity
            pick = (iota((cells, height * breadth), 1) == source).astype(f32).astype(bf16)
            out_ref[ry, :, :channels] = dot(pick, field, ((1,), (0,))).astype(bf16)
            out_ref[ry, :, channels:] = jnp.where(col_parity == 0, low, high).astype(bf16)


def collect_kernel(
    halo,
    at_ref,
    kept_ref,
    near_ref,
    far_ref,
    shard_ref,
    far1_ref,
    far2_ref,
    far3_ref,
    h_ref,
    band_ref,
    low_ref,
    high_ref,
):
    for far, ref in enumerate((shard_ref, far1_ref, far2_ref, far3_ref)):
        h_ref[far] = ref[...]
    cells = kept_ref.shape[1]
    low = at_ref[1]
    for k, piece in enumerate((kept_ref.at[0], near_ref.at[0], far_ref.at[0], far_ref.at[1])):
        band_ref[pl.ds(pl.multiple_of((low ^ k) * cells, cells), cells), :] = piece[...]
    low_ref[...] = band_ref[:halo]
    high_ref[...] = band_ref[band_ref.shape[0] - halo :]


def early_kernel(rows, channels, cols, before_ref, band_ref, after_ref, patch_ref):
    wide = jnp.concatenate([ref[:, channels:] for ref in (before_ref, band_ref, after_ref)], 0)
    put_patch(patch_ref, wide.astype(f32), 1, rows, cols)


def front_kernel(
    own,
    rows,
    total,
    at_ref,
    before_ref,
    band_ref,
    after_ref,
    patch_first_ref,
    h_ref,
    hy_ref,
    hc_ref,
    hyc_ref,
    keep_ref,
    send_ref,
    slope_ref,
    tilt_first_ref,
    tilt_second_ref,
    patch_middle_ref,
    w_middle_ref,
    w_last_ref,
    small_ref,
    patch_last_ref,
    student_ref,
    terms_ref,
):
    first_col, place = at_ref[0] * own, at_ref[2]
    r_last = w_last_ref.shape[1]
    r_small = small_ref.shape[1] // 2
    hidden = tilt_first_ref.shape[1]
    channels = slope_ref.shape[1]
    in_taps = patch_first_ref.shape[1]
    for near, ref in enumerate((h_ref, hc_ref, hy_ref, hyc_ref)):
        for far in range(FAR):
            at = place ^ (4 * far + near)
            w_last_ref[at] = ref[far, :r_last]
            small_ref[at] = ref[far, r_last:].astype(f32)
    small = small_ref[...]
    w_middle_ref[...] = small[:, :r_small].reshape(-1, 9 * hidden).astype(bf16)
    w_first = small[:, r_small:, :in_taps].reshape(-1, in_taps).astype(bf16)

    n_first, n_second, n_slope = (
        own + 2 * HALO_FIRST,
        own + 2 * HALO_SECOND,
        own + 2 * HALO_SLOPE,
    )
    pre = dot(patch_first_ref[...], w_first, ((1,), (1,)))
    sigma = 1.0 / (1.0 + jnp.exp(-pre))
    act = jnp.where(
        inside(n_first * rows, rows, first_col - HALO_FIRST, total), pre * sigma, 0.0
    )
    lo = HALO_FIRST * rows
    pre_own, sigma_own = pre[lo : lo + own * rows], sigma[lo : lo + own * rows]
    tilt_first_ref[...] = sigma_own * (1.0 + pre_own * (1.0 - sigma_own))
    put_patch(patch_middle_ref, act, 2, rows, n_second)

    pre = dot(patch_middle_ref[...], w_middle_ref[...], ((1,), (1,)))
    sigma = 1.0 / (1.0 + jnp.exp(-pre))
    act = jnp.where(
        inside(n_second * rows, rows, first_col - HALO_SECOND, total), pre * sigma, 0.0
    )
    lo, n_back = (HALO_SECOND - HALO_BACK) * rows, (own + 2 * HALO_BACK) * rows
    pre_back, sigma_back = pre[lo : lo + n_back], sigma[lo : lo + n_back]
    tilt_second_ref[...] = jnp.where(
        inside(n_back, rows, first_col - HALO_BACK, total),
        sigma_back * (1.0 + pre_back * (1.0 - sigma_back)),
        0.0,
    )
    put_patch(patch_last_ref, act, 4, rows, n_slope)

    w_last = w_last_ref[...].reshape(-1, 9 * hidden)
    student_ref[...] = dot(patch_last_ref[...], w_last, ((1,), (1,)))

    def slopes(start, count, target, col):
        at = pl.ds(start, count)
        student = student_ref[at, :]
        s_inv = lax.rsqrt(jnp.sum(student * student, -1, keepdims=True) + epsilon)
        target = target.astype(f32)
        t_inv = lax.rsqrt(jnp.sum(target * target, -1, keepdims=True) + epsilon)
        s_unit = student * s_inv
        differ = s_unit - target * t_inv
        slope = (differ - s_unit * jnp.sum(s_unit * differ, -1, keepdims=True)) * s_inv
        slope_ref[at, :] = jnp.where(inside(count, rows, col, total), slope, 0.0).astype(bf16)

    edge, block = HALO_SLOPE * rows, 4 * rows
    lo, n_own = edge, own * rows
    slopes(0, edge, before_ref[(HALO_X - HALO_SLOPE) * rows :, :channels], first_col - HALO_SLOPE)
    slopes(edge + n_own, edge, after_ref[:edge, :channels], first_col + own)

    def step(i, carry):
        at = pl.multiple_of(i * block, block)
        target = band_ref[pl.ds(at, block), :channels]
        slopes(pl.multiple_of(edge + at, rows), block, target, first_col + i * 4)
        return carry

    lax.fori_loop(0, own // 4, step, 0)
    terms = dot(
        slope_ref[lo : lo + n_own, :], patch_last_ref[lo : lo + n_own, :], ((0,), (0,))
    )
    terms_ref[...] = terms.reshape(terms_ref.shape)
    for ry in range(2):
        for far in range(FAR):
            at = place ^ (4 * far + 2 * ry)
            keep_ref[ry, far] = terms_ref[at]
            send_ref[ry, far] = terms_ref[at ^ 1].astype(bf16)


def back_kernel(
    own,
    rows,
    at_ref,
    slope_ref,
    tilt_second_ref,
    w_last_ref,
    tilt_first_ref,
    patch_first_ref,
    patch_middle_ref,
    w_middle_ref,
    keep_ref,
    send_ref,
    parts_last_ref,
    parts_ref,
    terms_ref,
):
    place = at_ref[2]
    n_own = own * rows
    w_last = w_last_ref[...].reshape(-1, w_last_ref.shape[2])
    parts_last_ref[...] = dot(slope_ref[...], w_last, ((1,), (0,)))
    back_second = spread_back(parts_last_ref, 4, rows, own + 2 * HALO_BACK)
    slope_second = (back_second * tilt_second_ref[...]).astype(bf16)
    lo, hi = HALO_BACK * rows, HALO_SECOND * rows
    r_small, middle = terms_ref.shape[1], patch_middle_ref.shape[1]
    grad_middle = dot(
        slope_second[lo : lo + n_own], patch_middle_ref[hi : hi + n_own, :], ((0,), (0,))
    )
    terms_ref[:, :, :middle] = grad_middle.reshape(-1, r_small, middle)
    parts_ref[...] = dot(slope_second, w_middle_ref[...], ((1,), (0,)))
    back_first = spread_back(parts_ref, 2, rows, own)
    slope_first = (back_first * tilt_first_ref[...]).astype(bf16)
    hi = HALO_FIRST * rows
    grad_first = dot(slope_first, patch_first_ref[hi : hi + n_own, :], ((0,), (0,)))
    terms_ref[:, :, middle:] = grad_first.reshape(-1, r_small, grad_first.shape[1])
    for ry in range(2):
        for far in range(FAR):
            at = place ^ (4 * far + 2 * ry)
            keep_ref[ry, far] = terms_ref[at]
            send_ref[ry, far] = terms_ref[at ^ 1].astype(bf16)


def merge_kernel(
    last_ref, last_got_ref, small_ref, small_got_ref, kept_ref, send1_ref, send2_ref, send3_ref
):
    r_last, middle = last_ref.shape[1], last_ref.shape[2]
    r_small = small_ref.shape[1]
    taps = small_ref.shape[2] - middle
    for far, ref in enumerate((kept_ref, send1_ref, send2_ref, send3_ref)):
        small = small_ref[far] + small_got_ref[far].astype(f32)
        ref[:r_last] = (last_ref[far] + last_got_ref[far].astype(f32)).astype(ref.dtype)
        pad = jnp.zeros((r_small, middle - taps), f32)
        tail = jnp.concatenate(
            [small[:, :middle], jnp.concatenate([small[:, middle:], pad], 1)], 0
        )
        ref[r_last:] = tail.astype(ref.dtype)


def finish_kernel(kept_ref, got1_ref, got2_ref, got3_ref, first_ref, middle_ref, last_ref):
    total = kept_ref[...]
    for ref in (got1_ref, got2_ref, got3_ref):
        total = total + ref[...].astype(f32)
    r_last, r_small, taps = last_ref.shape[0], middle_ref.shape[0], first_ref.shape[1]
    last_ref[...] = total[:r_last]
    middle_ref[...] = total[r_last : r_last + r_small]
    first_ref[...] = total[r_last + r_small :, :taps]


def call(kernel, name, inputs, outs, scratch, flops, spaces=None, semaphores=(), vmem_mib=24):
    vmem = pl.BlockSpec(memory_space=pltpu.VMEM)
    spaces = spaces or {}
    return pl.pallas_call(
        kernel,
        in_specs=[spaces.get(i, vmem) for i in range(len(inputs))],
        out_specs=[vmem] * len(outs),
        out_shape=[jax.ShapeDtypeStruct(shape, kind) for shape, kind in outs],
        scratch_shapes=[pltpu.VMEM(shape, kind) for shape, kind in scratch] + list(semaphores),
        compiler_params=pltpu.CompilerParams(vmem_limit_bytes=vmem_mib * MIB),
        cost_estimate=pl.CostEstimate(flops=flops, bytes_accessed=1_000_000, transcendentals=0),
        name=name,
    )(*inputs)


SMEM = {0: pl.BlockSpec(memory_space=pltpu.SMEM)}


def on_device(image_feats, teacher, w_first, w_middle, w_last):
    size = lax.axis_size("cols")
    me = lax.axis_index("cols")
    fold = size // BLOCKS
    height, breadth, channels = teacher.shape
    in_depth = w_first.shape[1] // 9
    hidden = w_middle.shape[1] // 9
    rows, piece = height // 2, breadth // 2
    own = 4 * piece
    total = own * (size // 4)
    at = jnp.stack([me // 4, me % 4, me // fold]).astype(jnp.int32)

    if fold > 1:
        w_first, w_middle, w_last = (
            lax.all_gather(w, "cols", axis_index_groups=neighbours(fold), axis=0, tiled=True)
            for w in (w_first, w_middle, w_last)
        )
    r_last, r_small = w_last.shape[0], w_first.shape[0]
    cells, deep = piece * rows, channels + in_depth
    hbm = pl.BlockSpec(memory_space=pltpu.HBM)
    kept, sent, shard = call(
        deal_kernel,
        "deal",
        (at, image_feats, teacher, w_first, w_middle, w_last),
        [
            ((2, cells, deep), bf16),
            ((2, cells, deep), bf16),
            ((r_last + 2 * r_small, 9 * hidden), bf16),
        ],
        [(a.shape, a.dtype) for a in (image_feats, teacher, w_first, w_middle, w_last)],
        600_000_000,
        SMEM | {i: hbm for i in range(1, 6)},
        [pltpu.SemaphoreType.DMA((5,))],
        60,
    )
    near = swap(sent, 1)
    pair = jnp.stack([kept[1], near[1]], 0)
    far = {k: swap(shard, 4 * k * fold) for k in (3, 2, 1)}
    pair = swap(pair, 2)
    halo = HALO_X * rows
    h, band, low_edge, high_edge = call(
        functools.partial(collect_kernel, halo),
        "collect",
        (at, kept, near, pair, shard, far[1], far[2], far[3]),
        [
            ((FAR,) + shard.shape, bf16),
            ((own * rows, deep), bf16),
            ((halo, deep), bf16),
            ((halo, deep), bf16),
        ],
        [],
        1_000_000,
        SMEM,
    )
    hy = swap(h, 2 * fold)
    hc = swap(h, fold)
    before = shift(high_edge, 4)
    after = shift(low_edge, -4)
    hyc = swap(hy, fold)

    n_first, n_second, n_slope, n_back = (
        (own + 2 * halo) * rows for halo in (HALO_FIRST, HALO_SECOND, HALO_SLOPE, HALO_BACK)
    )
    (patch_first,) = call(
        functools.partial(early_kernel, rows, channels, own + 2 * HALO_FIRST),
        "early",
        (before, band, after),
        [((n_first, 9 * in_depth), bf16)],
        [],
        6_000_000_000,
    )
    keep, send, slope, tilt_first, tilt_second, patch_middle, all_middle, all_last = call(
        functools.partial(front_kernel, own, rows, total),
        "front",
        (at, before, band, after, patch_first, h, hy, hc, hyc),
        [
            ((2, FAR, r_last, 9 * hidden), f32),
            ((2, FAR, r_last, 9 * hidden), bf16),
            ((n_slope, channels), bf16),
            ((own * rows, hidden), f32),
            ((n_back, hidden), f32),
            ((n_second, 9 * hidden), bf16),
            ((hidden, 9 * hidden), bf16),
            ((BLOCKS, r_last, 9 * hidden), bf16),
        ],
        [
            ((BLOCKS, 2 * r_small, 9 * hidden), f32),
            ((n_slope, 9 * hidden), bf16),
            ((n_slope, channels), f32),
            ((BLOCKS, r_last, 9 * hidden), f32),
        ],
        6_000_000_000,
        SMEM,
    )
    got = swap(send, fold)
    small_keep, small_send = call(
        functools.partial(back_kernel, own, rows),
        "back",
        (at, slope, tilt_second, all_last, tilt_first, patch_first, patch_middle, all_middle),
        [
            ((2, FAR, r_small, 9 * (hidden + in_depth)), f32),
            ((2, FAR, r_small, 9 * (hidden + in_depth)), bf16),
        ],
        [
            ((n_slope, 9 * hidden), f32),
            ((n_back, 9 * hidden), f32),
            ((BLOCKS, r_small, 9 * (hidden + in_depth)), f32),
        ],
        4_000_000_000,
        SMEM,
    )
    last_kept = keep[0] + got[0].astype(f32)
    last_sent = (keep[1] + got[1].astype(f32)).astype(bf16)
    last_got = swap(last_sent, 2 * fold)
    got = swap(small_send, fold)
    small_kept = small_keep[0] + got[0].astype(f32)
    small_sent = (small_keep[1] + got[1].astype(f32)).astype(bf16)
    small_got = swap(small_sent, 2 * fold)
    merged = call(
        merge_kernel,
        "merge",
        (last_kept, last_got, small_kept, small_got),
        [(shard.shape, f32)] + [(shard.shape, bf16)] * 3,
        [],
        1_000_000,
    )
    got = {k: swap(merged[k], 4 * k * fold) for k in (3, 2, 1)}
    out_first, out_middle, out_last = call(
        finish_kernel,
        "finish",
        (merged[0], got[1], got[2], got[3]),
        [(w.shape, f32) for w in (w_first, w_middle, w_last)],
        [],
        1_000_000,
    )
    if fold > 1:
        out_first, out_middle, out_last = (
            lax.psum_scatter(
                out, "cols", scatter_dimension=0, axis_index_groups=neighbours(fold), tiled=True
            )
            for out in (out_first, out_middle, out_last)
        )
    return (out_first, out_middle, out_last)


def solution(mesh):
    placed = (
        P("groups", "cols"),
        P("groups", "cols", None),
        P("cols", None),
        P("cols", None),
        P("cols", None),
    )
    return jax.shard_map(
        on_device,
        mesh=mesh,
        in_specs=placed,
        out_specs=(
            P(("groups", "cols"), None),
            P(("groups", "cols"), None),
            P(("groups", "cols"), None),
        ),
        check_vma=False,
    )
```

time: 85 us -> 70.3 us (0.83)
  starting transfers between devices: 39.4 us -> 18.8 us
  waiting for transfers between devices: 15.5 us -> 34.2 us
  local copies, waits for them, and re-layouts: 9.81 us -> 0.96 us
  other arithmetic: 8.1 us -> 0.88 us
  Pallas kernels: 10.4 us -> 14.5 us
    ppermute x23 -> x15, waiting for transfers between devices: 15.4 us -> 34.1 us  [swap(): return lax.ppermute(array, 'cols', [(i, i ^ mask) for i in range(size)])]
    ppermute x23 -> x15, starting transfers between devices: 27.1 us -> 15.4 us  [swap(): return lax.ppermute(array, 'cols', [(i, i ^ mask) for i in range(size)])]
    ppermute x4 -> x2, starting transfers between devices: 12.3 us -> 3.45 us  [shift(): lax.ppermute(array, 'cols', [(i, i + step) for i in range(size) if 0 <= i...]
    concatenate x3 -> x0, local copies, waits for them, and re-layouts: 4.66 us -> none  [the longest x1 2.42 us: on_device(): jnp.concatenate([x_wide[kx:kx + n_first, ky:ky + rows] for ky in range(3)...]
    select_n x17 -> x0, other arithmetic: 4.29 us -> none  [the longest x4 1.66 us: gather_rows(): jnp.where(me // 2 % 2 == 0, jnp.stack([held, other], 1), jnp.stack([other...]
    pallas_call x2 -> x7, Pallas kernels: 10.4 us -> 14.5 us  [call(): pl.pallas_call(kernel, in_specs=[spaces.get(i, vmem) for i in range(len(i...]
    slice x10 -> x2, local copies, waits for them, and re-layouts: 4.1 us -> 0.94 us  [on_device(): pair = jnp.stack([kept[1], near[1]], 0)]
    concatenate x8 -> x0, other arithmetic: 2.12 us -> none  [the longest x2 1.09 us: widen(): return jnp.concatenate([before, array, after], 0)]
  transfers between devices with their start and end apart: 27 -> 17, of which waited for: 6 -> 10; matrix products, arithmetic and copies ran while one was open for 17% -> 2% of each run, Pallas kernels for 0% -> 5%
where the time goes in v2:
time: 70.3 us; the launch traced here: 70.1 us
  waiting for transfers between devices  34.2 us (49%)
  starting transfers between devices  18.8 us (27%)
  Pallas kernels  14.5 us (21%)
  local copies, waits for them, and re-layouts  0.96 us (1%)
  other arithmetic  0.88 us (1%)
  between operations  0.79 us (1%)
    ppermute x15, waiting for transfers between devices, swap(): return lax.ppermute(array, 'cols', [(i, i ^ mask) for i in range(size)])  34.1 us
    ppermute x15, starting transfers between devices, swap(): return lax.ppermute(array, 'cols', [(i, i ^ mask) for i in range(size)])  15.4 us
    pallas_call x7, Pallas kernels, call(): pl.pallas_call(kernel, in_specs=[spaces.get(i, vmem) for i in range(len(i...  14.5 us
    ppermute x2, starting transfers between devices, shift(): lax.ppermute(array, 'cols', [(i, i + step) for i in range(size) if 0 <= i...  3.45 us
  transfers between devices with their start and end apart: 17, of which 10 were waited for; matrix products, arithmetic and copies ran while one was open for 2% of the time, Pallas kernels for 5%

profile of v2, /device:TPU:0, one launch (start us, length us, event | category | flops | bytes accessed | tf_op | source)
XLA Modules:
  0.0 70.1 jit_solution(15026314192848358432)
XLA Ops:
  0.6 0.7 pad_add_fusion.at_ref
  1.3 3.0 %deal.1 = (bf16[2,128,576]{2,1,0:T(8,128)(2,1)}, bf16[2,128,576]{2,1,0:T(8,128)(2,1)}, bf16[48,1152]{1,0:T(8,128)(2,1)}) custom-call(s32[3]{0:T(128)} %pad_add_fusion.at_ref, bf16[32,1024]{1,0:T(8,128)(2,1)} %x_hbm.1, bf16[32,16,512]{2,1,0:T(8,128)(2,1)} %teacher_hbm.1, bf16[8,576]{1,0:T(8,128)(2,1)} %w_first_hbm.1, bf16[8,1152]{1,0:T(8,128)(2,1)} %w_middle_hbm.1, ...), custom_call_target="tpu_custom_call" | custom-call | flops 600000000 | bytes 1000000 | tf_op jit(solution)/shard_map/deal/pallas_call | solution.py:354
  4.3 0.5 collective-permute-start
  4.8 0.9 %slice.30 = bf16[1,128,576]{2,1,0:T(8,128)(2,1)S(1)} slice(bf16[2,128,576]{2,1,0:T(8,128)(2,1)} %get-tuple-element.24.kept_ref), slice={[1:2], [0:128], [0:576]} | slice | bytes 294912 | tf_op jit(solution)/shard_map/slice | solution.py:405
  5.8 0.5 collective-permute-done.near_ref
  6.4 3.0 %collective-permute-start.1 = (bf16[2,128,576]{2,1,0:T(8,128)(2,1)S(1)}, bf16[2,128,576]{2,1,0:T(8,128)(2,1)S(1)}, u32[]{:S(2)}, u32[]{:S(2)}) collective-permute-start(bf16[2,128,576]{2,1,0:T(8,128)(2,1)S(1)} %pad_maximum_fusion), channel_id=1, source_target_pairs={{0,2},{1,3},{2,0},{3,1},{4,6},{5,7},{6,4},{7,5},{8,10},{9,11},{10,... | collective-permute-start | bytes 884744 | tf_op jit(solution)/shard_map/ppermute | solution.py:19
  9.3 3.6 %collective-permute-start.4 = (bf16[48,1152]{1,0:T(8,128)(2,1)S(1)}, bf16[48,1152]{1,0:T(8,128)(2,1)S(1)}, u32[]{:S(2)}, u32[]{:S(2)}) collective-permute-start(bf16[48,1152]{1,0:T(8,128)(2,1)S(1)} %copy-done.1), channel_id=1, source_target_pairs={{0,12},{1,13},{2,14},{3,15},{4,8},{5,9},{6,10},{7,11},{8,4},{9,5},... | collective-permute-start | bytes 331784 | tf_op jit(solution)/shard_map/ppermute | solution.py:19
  12.9 0.8 %collective-permute-start.2 = (bf16[48,1152]{1,0:T(8,128)(2,1)S(1)}, bf16[48,1152]{1,0:T(8,128)(2,1)S(1)}, u32[]{:S(2)}, u32[]{:S(2)}) collective-permute-start(bf16[48,1152]{1,0:T(8,128)(2,1)S(1)} %copy-done.1), channel_id=1, source_target_pairs={{0,4},{1,5},{2,6},{3,7},{4,0},{5,1},{6,2},{7,3},{8,12},{9,13},{10,... | collective-permute-start | bytes 331784 | tf_op jit(solution)/shard_map/ppermute | solution.py:19
  13.7 3.4 %collective-permute-done.4.far3_ref = bf16[48,1152]{1,0:T(8,128)(2,1)S(1)} collective-permute-done((bf16[48,1152]{1,0:T(8,128)(2,1)S(1)}, bf16[48,1152]{1,0:T(8,128)(2,1)S(1)}, u32[]{:S(2)}, u32[]{:S(2)}) %collective-permute-start.4) | collective-permute-done | bytes 110624 | tf_op jit(solution)/shard_map/ppermute | solution.py:19
  17.1 5.1 %collective-permute-done.3.far2_ref = bf16[48,1152]{1,0:T(8,128)(2,1)S(1)} collective-permute-done((bf16[48,1152]{1,0:T(8,128)(2,1)S(1)}, bf16[48,1152]{1,0:T(8,128)(2,1)S(1)}, u32[]{:S(2)}, u32[]{:S(2)}) %collective-permute-start.3) | collective-permute-done | bytes 110624 | tf_op jit(solution)/shard_map/ppermute | solution.py:19
  22.3 0.7 collect.1
  23.0 0.6 collective-permute-start.7
  23.6 2.2 %collective-permute-start.5 = (bf16[208,576]{1,0:T(8,128)(2,1)S(1)}, bf16[208,576]{1,0:T(8,128)(2,1)S(1)}, u32[]{:S(2)}, u32[]{:S(2)}) collective-permute-start(bf16[208,576]{1,0:T(8,128)(2,1)S(1)} %get-tuple-element.27), channel_id=1, source_target_pairs={{0,4},{1,5},{2,6},{3,7},{4,8},{5,9},{6,10},{7,11},{8,12},{9,13},{1... | collective-permute-start | bytes 718856 | tf_op jit(solution)/shard_map/ppermute | solution.py:24
  25.7 1.3 %collective-permute-start.6 = (bf16[208,576]{1,0:T(8,128)(2,1)S(1)}, bf16[208,576]{1,0:T(8,128)(2,1)S(1)}, u32[]{:S(2)}, u32[]{:S(2)}) collective-permute-start(bf16[208,576]{1,0:T(8,128)(2,1)S(1)} %get-tuple-element.29), channel_id=1, source_target_pairs={{4,0},{5,1},{6,2},{7,3},{8,4},{9,5},{10,6},{11,7},{12,8},{13,9},{1... | collective-permute-start | bytes 718856 | tf_op jit(solution)/shard_map/ppermute | solution.py:24
  27.1 7.2 %collective-permute-done.7.hy_ref = bf16[4,48,1152]{2,1,0:T(8,128)(2,1)S(1)} collective-permute-done((bf16[4,48,1152]{2,1,0:T(8,128)(2,1)S(1)}, bf16[4,48,1152]{2,1,0:T(8,128)(2,1)S(1)}, u32[]{:S(2)}, u32[]{:S(2)}) %collective-permute-start.7) | collective-permute-done | bytes 442400 | tf_op jit(solution)/shard_map/ppermute | solution.py:19
  34.4 0.4 early.1.patch_first_ref
  34.8 1.2 %collective-permute-done.9.hyc_ref = bf16[4,48,1152]{2,1,0:T(8,128)(2,1)S(1)} collective-permute-done((bf16[4,48,1152]{2,1,0:T(8,128)(2,1)S(1)}, bf16[4,48,1152]{2,1,0:T(8,128)(2,1)S(1)}, u32[]{:S(2)}, u32[]{:S(2)}) %collective-permute-start.9) | collective-permute-done | bytes 442400 | tf_op jit(solution)/shard_map/ppermute | solution.py:19
  36.1 6.9 %front.1 = (f32[2,4,32,1152]{3,2,1,0:T(8,128)S(1)}, bf16[2,4,32,1152]{3,2,1,0:T(8,128)(2,1)S(1)}, bf16[704,512]{1,0:T(8,128)(2,1)S(1)}, f32[512,128]{1,0:T(8,128...) custom-call(s32[3]{0:T(128)S(1)} %copy-done.2, ...), custom_call_target="tpu_custom_call" | custom-call | flops 6000000000 | bytes 1000000 | tf_op jit(solution)/shard_map/front/pallas_call | solution.py:354
  42.9 0.2 collective-permute-start.10
  43.1 2.7 %back.1 = (f32[2,4,8,1728]{3,2,1,0:T(8,128)S(1)}, bf16[2,4,8,1728]{3,2,1,0:T(8,128)(2,1)S(1)}) custom-call(s32[3]{0:T(128)S(1)} %copy-done.2, bf16[704,512]{1,0:T(8,128)(2,1)S(1)} %get-tuple-element.33.slope_ref, f32[576,128]{1,0:T(8,128)S(1)} %get-tuple-element.34.tilt_second_ref, bf16[16,32,1152]{2,1,0:T(8,128)(2,1)S(1)} %get-tuple-element.35.w_last_ref, ...), custom_call_target="tpu_custom_call" | custom-call | flops 4000000000 | bytes 1000000 | tf_op jit(solution)/shard_map/back/pallas_call | solution.py:354
  45.9 0.4 collective-permute-start.12
  46.3 0.1 fusion
  46.4 0.6 collective-permute-start.11
  47.0 0.4 collective-permute-done.12
  47.5 1.2 %collective-permute-start.13 = (bf16[4,8,1728]{2,1,0:T(8,128)(2,1)S(1)}, bf16[4,8,1728]{2,1,0:T(8,128)(2,1)S(1)}, u32[]{:S(2)}, u32[]{:S(2)}) collective-permute-start(bf16[4,8,1728]{2,1,0:T(8,128)(2,1)S(1)} %get-tuple-element.47), channel_id=1, source_target_pairs={{0,2},{1,3},{2,0},{3,1},{4,6},{5,7},{6,4},{7,5},{8,10},{9,11},{10,... | collective-permute-start | bytes 331784 | tf_op jit(solution)/shard_map/ppermute | solution.py:19
  48.7 9.4 %collective-permute-done.13.small_got_ref = bf16[4,8,1728]{2,1,0:T(8,128)(2,1)S(1)} collective-permute-done((bf16[4,8,1728]{2,1,0:T(8,128)(2,1)S(1)}, bf16[4,8,1728]{2,1,0:T(8,128)(2,1)S(1)}, u32[]{:S(2)}, u32[]{:S(2)}) %collective-permute-start.13) | collective-permute-done | bytes 110624 | tf_op jit(solution)/shard_map/ppermute | solution.py:19
  58.1 0.3 collective-permute-start.14
  58.4 2.6 %collective-permute-start.15 = (bf16[48,1152]{1,0:T(8,128)(2,1)S(1)}, bf16[48,1152]{1,0:T(8,128)(2,1)S(1)}, u32[]{:S(2)}, u32[]{:S(2)}) collective-permute-start(bf16[48,1152]{1,0:T(8,128)(2,1)S(1)} %get-tuple-element.43), channel_id=1, source_target_pairs={{0,8},{1,9},{2,10},{3,11},{4,12},{5,13},{6,14},{7,15},{8,0},{9,1},... | collective-permute-start | bytes 331784 | tf_op jit(solution)/shard_map/ppermute | solution.py:19
  61.1 1.5 %collective-permute-start.16 = (bf16[48,1152]{1,0:T(8,128)(2,1)S(1)}, bf16[48,1152]{1,0:T(8,128)(2,1)S(1)}, u32[]{:S(2)}, u32[]{:S(2)}) collective-permute-start(bf16[48,1152]{1,0:T(8,128)(2,1)S(1)} %get-tuple-element.44), channel_id=1, source_target_pairs={{0,12},{1,13},{2,14},{3,15},{4,8},{5,9},{6,10},{7,11},{8,4},{9,5},... | collective-permute-start | bytes 331784 | tf_op jit(solution)/shard_map/ppermute | solution.py:19
  62.6 1.3 %collective-permute-done.14.got1_ref = bf16[48,1152]{1,0:T(8,128)(2,1)S(1)} collective-permute-done((bf16[48,1152]{1,0:T(8,128)(2,1)S(1)}, bf16[48,1152]{1,0:T(8,128)(2,1)S(1)}, u32[]{:S(2)}, u32[]{:S(2)}) %collective-permute-start.14) | collective-permute-done | bytes 110624 | tf_op jit(solution)/shard_map/ppermute | solution.py:19
  63.8 5.6 %collective-permute-done.15.got2_ref = bf16[48,1152]{1,0:T(8,128)(2,1)S(1)} collective-permute-done((bf16[48,1152]{1,0:T(8,128)(2,1)S(1)}, bf16[48,1152]{1,0:T(8,128)(2,1)S(1)}, u32[]{:S(2)}, u32[]{:S(2)}) %collective-permute-start.15) | collective-permute-done | bytes 110624 | tf_op jit(solution)/shard_map/ppermute | solution.py:19
  69.4 0.7 %finish.1 = (f32[8,576]{1,0:T(8,128)}, f32[8,1152]{1,0:T(8,128)}, f32[32,1152]{1,0:T(8,128)}) custom-call(f32[48,1152]{1,0:T(8,128)S(1)} %get-tuple-element.41.kept_ref, bf16[48,1152]{1,0:T(8,128)(2,1)S(1)} %collective-permute-done.14.got1_ref, bf16[48,1152]{1,0:T(8,128)(2,1)S(1)} %collective-permute-done.15.got2_ref, ...), custom_call_target="tpu_custom_call" | custom-call | flops 1000000 | bytes 1000000 | tf_op jit(solution)/shard_map/finish/pallas_call | solution.py:354
  (21 shorter events, 0.4 us)
Async XLA Ops:
  4.3 5.0 %copy-start.1 = (bf16[48,1152]{1,0:T(8,128)(2,1)S(1)}, bf16[48,1152]{1,0:T(8,128)(2,1)}, u32[]{:S(2)}) copy-start(bf16[48,1152]{1,0:T(8,128)(2,1)} %get-tuple-element.26.shard_ref) | copy-start | bytes 331780
  4.3 18.0 %copy-start = (bf16[2,128,576]{2,1,0:T(8,128)(2,1)S(1)}, bf16[2,128,576]{2,1,0:T(8,128)(2,1)}, u32[]{:S(2)}) copy-start(bf16[2,128,576]{2,1,0:T(8,128)(2,1)} %get-tuple-element.24.kept_ref) | copy-start | bytes 884740
  4.3 18.0 %copy-start.2 = (s32[3]{0:T(128)S(1)}, s32[3]{0:T(128)}, u32[]{:S(2)}) copy-start(s32[3]{0:T(128)} %pad_add_fusion.at_ref) | copy-start | bytes 40
  4.3 2.0 %collective-permute-start = (bf16[2,128,576]{2,1,0:T(8,128)(2,1)}, bf16[2,128,576]{2,1,0:T(8,128)(2,1)S(1)}, u32[]{:S(2)}, u32[]{:S(2)}) collective-permute-start(bf16[2,128,576]{2,1,0:T(8,128)(2,1)} %get-tuple-element.25), channel_id=1, source_target_pairs={{0,1},{1,0},{2,3},{3,2},{4,5},{5,4},{6,7},{7,6},{8,9},{9,8},{10,11... | collective-permute-start | bytes 884744 | tf_op jit(solution)/shard_map/ppermute | solution.py:19
  6.4 15.9 %collective-permute-start.1 = (bf16[2,128,576]{2,1,0:T(8,128)(2,1)S(1)}, bf16[2,128,576]{2,1,0:T(8,128)(2,1)S(1)}, u32[]{:S(2)}, u32[]{:S(2)}) collective-permute-start(bf16[2,128,576]{2,1,0:T(8,128)(2,1)S(1)} %pad_maximum_fusion), channel_id=1, source_target_pairs={{0,2},{1,3},{2,0},{3,1},{4,6},{5,7},{6,4},{7,5},{8,10},{9,11},{10,... | collective-permute-start | bytes 884744 | tf_op jit(solution)/shard_map/ppermute | solution.py:19
  9.3 7.8 %collective-permute-start.4 = (bf16[48,1152]{1,0:T(8,128)(2,1)S(1)}, bf16[48,1152]{1,0:T(8,128)(2,1)S(1)}, u32[]{:S(2)}, u32[]{:S(2)}) collective-permute-start(bf16[48,1152]{1,0:T(8,128)(2,1)S(1)} %copy-done.1), channel_id=1, source_target_pairs={{0,12},{1,13},{2,14},{3,15},{4,8},{5,9},{6,10},{7,11},{8,4},{9,5},... | collective-permute-start | bytes 331784 | tf_op jit(solution)/shard_map/ppermute | solution.py:19
  12.9 9.3 %collective-permute-start.3 = (bf16[48,1152]{1,0:T(8,128)(2,1)S(1)}, bf16[48,1152]{1,0:T(8,128)(2,1)S(1)}, u32[]{:S(2)}, u32[]{:S(2)}) collective-permute-start(bf16[48,1152]{1,0:T(8,128)(2,1)S(1)} %copy-done.1), channel_id=1, source_target_pairs={{0,8},{1,9},{2,10},{3,11},{4,12},{5,13},{6,14},{7,15},{8,0},{9,1},... | collective-permute-start | bytes 331784 | tf_op jit(solution)/shard_map/ppermute | solution.py:19
  12.9 9.3 %collective-permute-start.2 = (bf16[48,1152]{1,0:T(8,128)(2,1)S(1)}, bf16[48,1152]{1,0:T(8,128)(2,1)S(1)}, u32[]{:S(2)}, u32[]{:S(2)}) collective-permute-start(bf16[48,1152]{1,0:T(8,128)(2,1)S(1)} %copy-done.1), channel_id=1, source_target_pairs={{0,4},{1,5},{2,6},{3,7},{4,0},{5,1},{6,2},{7,3},{8,12},{9,13},{10,... | collective-permute-start | bytes 331784 | tf_op jit(solution)/shard_map/ppermute | solution.py:19
  23.0 11.3 %collective-permute-start.7 = (bf16[4,48,1152]{2,1,0:T(8,128)(2,1)S(1)}, bf16[4,48,1152]{2,1,0:T(8,128)(2,1)S(1)}, u32[]{:S(2)}, u32[]{:S(2)}) collective-permute-start(bf16[4,48,1152]{2,1,0:T(8,128)(2,1)S(1)} %get-tuple-element.30.h_ref), channel_id=1, source_target_pairs={{0,2},{1,3},{2,0},{3,1},{4,6},{5,7},{6,4},{7,5},{8,10},{9,11},{10,... | collective-permute-start | bytes 1327112 | tf_op jit(solution)/shard_map/ppermute | solution.py:19
  23.6 10.7 %collective-permute-start.5 = (bf16[208,576]{1,0:T(8,128)(2,1)S(1)}, bf16[208,576]{1,0:T(8,128)(2,1)S(1)}, u32[]{:S(2)}, u32[]{:S(2)}) collective-permute-start(bf16[208,576]{1,0:T(8,128)(2,1)S(1)} %get-tuple-element.27), channel_id=1, source_target_pairs={{0,4},{1,5},{2,6},{3,7},{4,8},{5,9},{6,10},{7,11},{8,12},{9,13},{1... | collective-permute-start | bytes 718856 | tf_op jit(solution)/shard_map/ppermute | solution.py:24
  25.7 8.7 %collective-permute-start.6 = (bf16[208,576]{1,0:T(8,128)(2,1)S(1)}, bf16[208,576]{1,0:T(8,128)(2,1)S(1)}, u32[]{:S(2)}, u32[]{:S(2)}) collective-permute-start(bf16[208,576]{1,0:T(8,128)(2,1)S(1)} %get-tuple-element.29), channel_id=1, source_target_pairs={{4,0},{5,1},{6,2},{7,3},{8,4},{9,5},{10,6},{11,7},{12,8},{13,9},{1... | collective-permute-start | bytes 718856 | tf_op jit(solution)/shard_map/ppermute | solution.py:24
  27.0 7.8 %collective-permute-start.8 = (bf16[4,48,1152]{2,1,0:T(8,128)(2,1)S(1)}, bf16[4,48,1152]{2,1,0:T(8,128)(2,1)S(1)}, u32[]{:S(2)}, u32[]{:S(2)}) collective-permute-start(bf16[4,48,1152]{2,1,0:T(8,128)(2,1)S(1)} %get-tuple-element.30.h_ref), channel_id=1, source_target_pairs={{0,1},{1,0},{2,3},{3,2},{4,5},{5,4},{6,7},{7,6},{8,9},{9,8},{10,11... | collective-permute-start | bytes 1327112 | tf_op jit(solution)/shard_map/ppermute | solution.py:19
  34.3 1.8 %collective-permute-start.9 = (bf16[4,48,1152]{2,1,0:T(8,128)(2,1)S(1)}, bf16[4,48,1152]{2,1,0:T(8,128)(2,1)S(1)}, u32[]{:S(2)}, u32[]{:S(2)}) collective-permute-start(bf16[4,48,1152]{2,1,0:T(8,128)(2,1)S(1)} %collective-permute-done.7.hy_ref), channel_id=1, source_target_pairs={{0,1},{1,0},{2,3},{3,2},{4,5},{5,4},{6,7},{7,6},{8,9},{9,8},{10,11... | collective-permute-start | bytes 1327112 | tf_op jit(solution)/shard_map/ppermute | solution.py:19
  42.9 3.4 %collective-permute-start.10 = (bf16[2,4,32,1152]{3,2,1,0:T(8,128)(2,1)S(1)}, bf16[2,4,32,1152]{3,2,1,0:T(8,128)(2,1)S(1)}, u32[]{:S(2)}, u32[]{:S(2)}) collective-permute-start(bf16[2,4,32,1152]{3,2,1,0:T(8,128)(2,1)S(1)} %get-tuple-element.32), channel_id=1, source_target_pairs={{0,1},{1,0},{2,3},{3,2},{4,5},{5,4},{6,7},{7,6},{8,9},{9,8},{10,11... | collective-permute-start | bytes 1769480 | tf_op jit(solution)/shard_map/ppermute | solution.py:19
  45.9 1.6 %collective-permute-start.12 = (bf16[2,4,8,1728]{3,2,1,0:T(8,128)(2,1)S(1)}, bf16[2,4,8,1728]{3,2,1,0:T(8,128)(2,1)S(1)}, u32[]{:S(2)}, u32[]{:S(2)}) collective-permute-start(bf16[2,4,8,1728]{3,2,1,0:T(8,128)(2,1)S(1)} %get-tuple-element.40), channel_id=1, source_target_pairs={{0,1},{1,0},{2,3},{3,2},{4,5},{5,4},{6,7},{7,6},{8,9},{9,8},{10,11... | collective-permute-start | bytes 663560 | tf_op jit(solution)/shard_map/ppermute | solution.py:19
  46.4 11.6 %collective-permute-start.11 = (bf16[4,32,1152]{2,1,0:T(8,128)(2,1)S(1)}, bf16[4,32,1152]{2,1,0:T(8,128)(2,1)S(1)}, u32[]{:S(2)}, u32[]{:S(2)}) collective-permute-start(bf16[4,32,1152]{2,1,0:T(8,128)(2,1)S(1)} %get-tuple-element.45), channel_id=1, source_target_pairs={{0,2},{1,3},{2,0},{3,1},{4,6},{5,7},{6,4},{7,5},{8,10},{9,11},{10,... | collective-permute-start | bytes 884744 | tf_op jit(solution)/shard_map/ppermute | solution.py:19
  47.5 10.5 %collective-permute-start.13 = (bf16[4,8,1728]{2,1,0:T(8,128)(2,1)S(1)}, bf16[4,8,1728]{2,1,0:T(8,128)(2,1)S(1)}, u32[]{:S(2)}, u32[]{:S(2)}) collective-permute-start(bf16[4,8,1728]{2,1,0:T(8,128)(2,1)S(1)} %get-tuple-element.47), channel_id=1, source_target_pairs={{0,2},{1,3},{2,0},{3,1},{4,6},{5,7},{6,4},{7,5},{8,10},{9,11},{10,... | collective-permute-start | bytes 331784 | tf_op jit(solution)/shard_map/ppermute | solution.py:19
  58.1 5.7 %collective-permute-start.14 = (bf16[48,1152]{1,0:T(8,128)(2,1)S(1)}, bf16[48,1152]{1,0:T(8,128)(2,1)S(1)}, u32[]{:S(2)}, u32[]{:S(2)}) collective-permute-start(bf16[48,1152]{1,0:T(8,128)(2,1)S(1)} %get-tuple-element.42), channel_id=1, source_target_pairs={{0,4},{1,5},{2,6},{3,7},{4,0},{5,1},{6,2},{7,3},{8,12},{9,13},{10,... | collective-permute-start | bytes 331784 | tf_op jit(solution)/shard_map/ppermute | solution.py:19
  58.4 11.0 %collective-permute-start.15 = (bf16[48,1152]{1,0:T(8,128)(2,1)S(1)}, bf16[48,1152]{1,0:T(8,128)(2,1)S(1)}, u32[]{:S(2)}, u32[]{:S(2)}) collective-permute-start(bf16[48,1152]{1,0:T(8,128)(2,1)S(1)} %get-tuple-element.43), channel_id=1, source_target_pairs={{0,8},{1,9},{2,10},{3,11},{4,12},{5,13},{6,14},{7,15},{8,0},{9,1},... | collective-permute-start | bytes 331784 | tf_op jit(solution)/shard_map/ppermute | solution.py:19
  61.1 8.4 %collective-permute-start.16 = (bf16[48,1152]{1,0:T(8,128)(2,1)S(1)}, bf16[48,1152]{1,0:T(8,128)(2,1)S(1)}, u32[]{:S(2)}, u32[]{:S(2)}) collective-permute-start(bf16[48,1152]{1,0:T(8,128)(2,1)S(1)} %get-tuple-element.44), channel_id=1, source_target_pairs={{0,12},{1,13},{2,14},{3,15},{4,8},{5,9},{6,10},{7,11},{8,4},{9,5},... | collective-permute-start | bytes 331784 | tf_op jit(solution)/shard_map/ppermute | solution.py:19

commit v3 on v2

--- a/solution.py
+++ b/solution.py
@@ -12,6 +12,7 @@
 MIB = 1024 * 1024
 HALO_X, HALO_FIRST, HALO_SECOND, HALO_SLOPE, HALO_BACK = 13, 12, 10, 6, 2
 BLOCKS, FAR = 16, 4
+STACK_COST = 3_000_000_000
 
 
 def swap(array, mask):
@@ -29,6 +30,11 @@
 def neighbours(fold):
     size = lax.axis_size("cols")
     return [list(range(i, i + fold)) for i in range(0, size, fold)]
+
+
+def position(blocks):
+    me = lax.axis_index("cols")
+    return me // 4, me % 4, me // (lax.axis_size("cols") // blocks)
 
 
 def dot(a, b, contract):
@@ -79,7 +85,6 @@
 
 
 def deal_kernel(
-    at_ref,
     x_hbm,
     teacher_hbm,
     w_first_hbm,
@@ -93,6 +98,8 @@
     w_first_ref,
     w_middle_ref,
     w_last_ref,
+    pick_x_ref,
+    pick_t_ref,
     arrived,
 ):
     copies = [
@@ -113,9 +120,16 @@
     depth = x_ref.shape[1] // breadth
     rows, piece = height // 2, breadth // 2
     cells = rows * piece
-    core, row = at_ref[1] % 2, at_ref[1] // 2
+    low = position(BLOCKS)[1]
+    core, row = low % 2, low // 2
     out = iota((cells, 1), 0)
     col, line = out // rows, out % rows
+    for rc in range(2):
+        line_of = 2 * line + (core ^ rc)
+        pick_x_ref[rc] = (iota((cells, piece * height), 1) == col * height + line_of).astype(f32).astype(bf16)
+        for ry in range(2):
+            source = line_of * breadth + 2 * col + (row ^ ry)
+            pick_t_ref[rc, ry] = (iota((cells, height * breadth), 1) == source).astype(f32).astype(bf16)
     for copy in copies:
         copy.wait()
     r_last, r_small, taps = w_last_ref.shape[0], w_middle_ref.shape[0], w_first_ref.shape[1]
@@ -130,38 +144,21 @@
         [x_ref[:, 2 * depth * i : 2 * depth * (i + 1)] for i in range(piece)], 0
     )
     for rc, out_ref in ((1, sent_ref), (0, kept_ref)):
-        row_parity = core ^ rc
-        source = col * height + 2 * line + row_parity
-        pick = (iota((cells, piece * height), 1) == source).astype(f32).astype(bf16)
-        both = dot(pick, pairs, ((1,), (0,)))
+        both = dot(pick_x_ref[rc], pairs, ((1,), (0,)))
         low, high = both[:, :depth], both[:, depth:]
         for ry in range(2):
-            col_parity = row ^ ry
-            source = (2 * line + row_parity) * breadth + 2 * col + col_parity
-            pick = (iota((cells, height * breadth), 1) == source).astype(f32).astype(bf16)
-            out_ref[ry, :, :channels] = dot(pick, field, ((1,), (0,))).astype(bf16)
-            out_ref[ry, :, channels:] = jnp.where(col_parity == 0, low, high).astype(bf16)
-
-
-def collect_kernel(
-    halo,
-    at_ref,
-    kept_ref,
-    near_ref,
-    far_ref,
-    shard_ref,
-    far1_ref,
-    far2_ref,
-    far3_ref,
-    h_ref,
-    band_ref,
-    low_ref,
-    high_ref,
-):
-    for far, ref in enumerate((shard_ref, far1_ref, far2_ref, far3_ref)):
-        h_ref[far] = ref[...]
+            out_ref[ry, :, :channels] = dot(pick_t_ref[rc, ry], field, ((1,), (0,))).astype(bf16)
+            out_ref[ry, :, channels:] = jnp.where((row ^ ry) == 0, low, high).astype(bf16)
+
+
+def stack_kernel(*refs):
+    for i, ref in enumerate(refs[:-1]):
+        refs[-1][i] = ref[...]
+
+
+def collect_kernel(halo, kept_ref, near_ref, far_ref, h_ref, band_ref, low_ref, high_ref, same_ref):
     cells = kept_ref.shape[1]
-    low = at_ref[1]
+    low = position(BLOCKS)[1]
     for k, piece in enumerate((kept_ref.at[0], near_ref.at[0], far_ref.at[0], far_ref.at[1])):
         band_ref[pl.ds(pl.multiple_of((low ^ k) * cells, cells), cells), :] = piece[...]
     low_ref[...] = band_ref[:halo]
@@ -177,7 +174,6 @@
     own,
     rows,
     total,
-    at_ref,
     before_ref,
     band_ref,
     after_ref,
@@ -199,7 +195,8 @@
     student_ref,
     terms_ref,
 ):
-    first_col, place = at_ref[0] * own, at_ref[2]
+    group, _, place = position(BLOCKS)
+    first_col = group * own
     r_last = w_last_ref.shape[1]
     r_small = small_ref.shape[1] // 2
     hidden = tilt_first_ref.shape[1]
@@ -283,7 +280,6 @@
 def back_kernel(
     own,
     rows,
-    at_ref,
     slope_ref,
     tilt_second_ref,
     w_last_ref,
@@ -297,7 +293,7 @@
     parts_ref,
     terms_ref,
 ):
-    place = at_ref[2]
+    place = position(BLOCKS)[2]
     n_own = own * rows
     w_last = w_last_ref[...].reshape(-1, w_last_ref.shape[2])
     parts_last_ref[...] = dot(slope_ref[...], w_last, ((1,), (0,)))
@@ -318,43 +314,43 @@
     for ry in range(2):
         for far in range(FAR):
             at = place ^ (4 * far + 2 * ry)
-            keep_ref[ry, far] = terms_ref[at]
-            send_ref[ry, far] = terms_ref[at ^ 1].astype(bf16)
-
-
-def merge_kernel(
-    last_ref, last_got_ref, small_ref, small_got_ref, kept_ref, send1_ref, send2_ref, send3_ref
-):
-    r_last, middle = last_ref.shape[1], last_ref.shape[2]
-    r_small = small_ref.shape[1]
-    taps = small_ref.shape[2] - middle
-    for far, ref in enumerate((kept_ref, send1_ref, send2_ref, send3_ref)):
-        small = small_ref[far] + small_got_ref[far].astype(f32)
-        ref[:r_last] = (last_ref[far] + last_got_ref[far].astype(f32)).astype(ref.dtype)
-        pad = jnp.zeros((r_small, middle - taps), f32)
-        tail = jnp.concatenate(
-            [small[:, :middle], jnp.concatenate([small[:, middle:], pad], 1)], 0
-        )
-        ref[r_last:] = tail.astype(ref.dtype)
-
-
-def finish_kernel(kept_ref, got1_ref, got2_ref, got3_ref, first_ref, middle_ref, last_ref):
-    total = kept_ref[...]
+            keep_ref[far, ry] = terms_ref[at]
+            send_ref[far, ry] = terms_ref[at ^ 1].astype(bf16)
+
+
+def split_kernel(keep_ref, got_ref, kept_ref, *send_refs):
+    for i, ref in enumerate((kept_ref,) + send_refs):
+        ref[...] = (keep_ref[i] + got_ref[i].astype(f32)).astype(ref.dtype)
+
+
+def add_kernel(keep_ref, got1_ref, got2_ref, got3_ref, kept_ref, send_ref):
+    total = keep_ref[...]
     for ref in (got1_ref, got2_ref, got3_ref):
         total = total + ref[...].astype(f32)
-    r_last, r_small, taps = last_ref.shape[0], middle_ref.shape[0], first_ref.shape[1]
-    last_ref[...] = total[:r_last]
-    middle_ref[...] = total[r_last : r_last + r_small]
-    first_ref[...] = total[r_last + r_small :, :taps]
-
-
-def call(kernel, name, inputs, outs, scratch, flops, spaces=None, semaphores=(), vmem_mib=24):
+    kept_ref[...] = total[0]
+    send_ref[...] = total[1].astype(bf16)
+
+
+def finish_kernel(
+    last_ref, got1_ref, got2_ref, got3_ref, small_ref, got_ref, first_ref, middle_ref, out_ref
+):
+    total = last_ref[...]
+    for ref in (got1_ref, got2_ref, got3_ref):
+        total = total + ref[...].astype(f32)
+    out_ref[...] = total
+    small = small_ref[...] + got_ref[...].astype(f32)
+    middle_ref[...] = small[:, : middle_ref.shape[1]]
+    first_ref[...] = small[:, middle_ref.shape[1] :]
+
+
+def call(kernel, name, inputs, outs, scratch, flops, spaces=None, semaphores=(), vmem_mib=24, out_spaces=None, aliases=None):
     vmem = pl.BlockSpec(memory_space=pltpu.VMEM)
     spaces = spaces or {}
     return pl.pallas_call(
         kernel,
         in_specs=[spaces.get(i, vmem) for i in range(len(inputs))],
-        out_specs=[vmem] * len(outs),
+        out_specs=[(out_spaces or {}).get(i, vmem) for i in range(len(outs))],
+        input_output_aliases=aliases or {},
         out_shape=[jax.ShapeDtypeStruct(shape, kind) for shape, kind in outs],
         scratch_shapes=[pltpu.VMEM(shape, kind) for shape, kind in scratch] + list(semaphores),
         compiler_params=pltpu.CompilerParams(vmem_limit_bytes=vmem_mib * MIB),
@@ -363,12 +359,8 @@
     )(*inputs)
 
 
-SMEM = {0: pl.BlockSpec(memory_space=pltpu.SMEM)}
-
-
 def on_device(image_feats, teacher, w_first, w_middle, w_last):
     size = lax.axis_size("cols")
-    me = lax.axis_index("cols")
     fold = size // BLOCKS
     height, breadth, channels = teacher.shape
     in_depth = w_first.shape[1] // 9
@@ -376,7 +368,6 @@
     rows, piece = height // 2, breadth // 2
     own = 4 * piece
     total = own * (size // 4)
-    at = jnp.stack([me // 4, me % 4, me // fold]).astype(jnp.int32)
 
     if fold > 1:
         w_first, w_middle, w_last = (
@@ -389,15 +380,16 @@
     kept, sent, shard = call(
         deal_kernel,
         "deal",
-        (at, image_feats, teacher, w_first, w_middle, w_last),
+        (image_feats, teacher, w_first, w_middle, w_last),
         [
             ((2, cells, deep), bf16),
             ((2, cells, deep), bf16),
             ((r_last + 2 * r_small, 9 * hidden), bf16),
         ],
-        [(a.shape, a.dtype) for a in (image_feats, teacher, w_first, w_middle, w_last)],
+        [(a.shape, a.dtype) for a in (image_feats, teacher, w_first, w_middle, w_last)]
+        + [((2, cells, piece * height), bf16), ((2, 2, cells, height * breadth), bf16)],
         600_000_000,
-        SMEM | {i: hbm for i in range(1, 6)},
+        {i: hbm for i in range(5)},
         [pltpu.SemaphoreType.DMA((5,))],
         60,
     )
@@ -406,19 +398,29 @@
     far = {k: swap(shard, 4 * k * fold) for k in (3, 2, 1)}
     pair = swap(pair, 2)
     halo = HALO_X * rows
-    h, band, low_edge, high_edge = call(
+    (h,) = call(
+        stack_kernel,
+        "stack",
+        (shard, far[1], far[2], far[3]),
+        [((FAR,) + shard.shape, bf16)],
+        [],
+        STACK_COST,
+    )
+    band, low_edge, high_edge, h = call(
         functools.partial(collect_kernel, halo),
         "collect",
-        (at, kept, near, pair, shard, far[1], far[2], far[3]),
+        (kept, near, pair, h),
         [
-            ((FAR,) + shard.shape, bf16),
             ((own * rows, deep), bf16),
             ((halo, deep), bf16),
             ((halo, deep), bf16),
+            (h.shape, bf16),
         ],
         [],
         1_000_000,
-        SMEM,
+        {3: pl.BlockSpec(memory_space=pl.ANY)},
+        out_spaces={3: pl.BlockSpec(memory_space=pl.ANY)},
+        aliases={3: 3},
     )
     hy = swap(h, 2 * fold)
     hc = swap(h, fold)
@@ -440,7 +442,7 @@
     keep, send, slope, tilt_first, tilt_second, patch_middle, all_middle, all_last = call(
         functools.partial(front_kernel, own, rows, total),
         "front",
-        (at, before, band, after, patch_first, h, hy, hc, hyc),
+        (before, band, after, patch_first, h, hy, hc, hyc),
         [
             ((2, FAR, r_last, 9 * hidden), f32),
             ((2, FAR, r_last, 9 * hidden), bf16),
@@ -458,45 +460,48 @@
             ((BLOCKS, r_last, 9 * hidden), f32),
         ],
         6_000_000_000,
-        SMEM,
-    )
+    )
+    both = 9 * (hidden + in_depth)
     got = swap(send, fold)
     small_keep, small_send = call(
         functools.partial(back_kernel, own, rows),
         "back",
-        (at, slope, tilt_second, all_last, tilt_first, patch_first, patch_middle, all_middle),
+        (slope, tilt_second, all_last, tilt_first, patch_first, patch_middle, all_middle),
         [
-            ((2, FAR, r_small, 9 * (hidden + in_depth)), f32),
-            ((2, FAR, r_small, 9 * (hidden + in_depth)), bf16),
+            ((FAR, 2, r_small, both), f32),
+            ((FAR, 2, r_small, both), bf16),
         ],
         [
             ((n_slope, 9 * hidden), f32),
             ((n_back, 9 * hidden), f32),
-            ((BLOCKS, r_small, 9 * (hidden + in_depth)), f32),
+            ((BLOCKS, r_small, both), f32),
         ],
         4_000_000_000,
-        SMEM,
-    )
-    last_kept = keep[0] + got[0].astype(f32)
-    last_sent = (keep[1] + got[1].astype(f32)).astype(bf16)
+    )
+    def split(keep, got, count):
+        shape = keep.shape[1:]
+        outs = [(shape, f32)] + [(shape, bf16)] * (count - 1)
+        return call(split_kernel, "split", (keep, got), outs, [], 1_000_000)
+
+    last_kept, last_sent = split(keep, got, 2)
     last_got = swap(last_sent, 2 * fold)
-    got = swap(small_send, fold)
-    small_kept = small_keep[0] + got[0].astype(f32)
-    small_sent = (small_keep[1] + got[1].astype(f32)).astype(bf16)
-    small_got = swap(small_sent, 2 * fold)
-    merged = call(
-        merge_kernel,
-        "merge",
-        (last_kept, last_got, small_kept, small_got),
-        [(shard.shape, f32)] + [(shard.shape, bf16)] * 3,
+    parts = split(small_keep, swap(small_send, fold), FAR)
+    small_got = {k: swap(parts[k], 4 * k * fold) for k in (3, 2, 1)}
+    last = split(last_kept, last_got, FAR)
+    last_got = {k: swap(last[k], 4 * k * fold) for k in (3, 2, 1)}
+    small_kept, small_sent = call(
+        add_kernel,
+        "add",
+        (parts[0], small_got[1], small_got[2], small_got[3]),
+        [((r_small, both), f32), ((r_small, both), bf16)],
         [],
         1_000_000,
     )
-    got = {k: swap(merged[k], 4 * k * fold) for k in (3, 2, 1)}
+    small_got = swap(small_sent, 2 * fold)
     out_first, out_middle, out_last = call(
         finish_kernel,
         "finish",
-        (merged[0], got[1], got[2], got[3]),
+        (last[0], last_got[1], last_got[2], last_got[3], small_kept, small_got),
         [(w.shape, f32) for w in (w_first, w_middle, w_last)],
         [],
         1_000_000,

time: 70.3 us -> 62.6 us (0.89)
  waiting for transfers between devices: 34.2 us -> 23.4 us
  starting transfers between devices: 18.8 us -> 24.5 us
  Pallas kernels: 14.5 us -> 12.4 us
  other arithmetic: 0.88 us -> 0.05 us
    ppermute x15 -> x18, waiting for transfers between devices: 34.1 us -> 20.8 us  [swap(): return lax.ppermute(array, 'cols', [(i, i ^ mask) for i in range(size)])]
    ppermute x15 -> x18, starting transfers between devices: 15.4 us -> 19.8 us  [swap(): return lax.ppermute(array, 'cols', [(i, i ^ mask) for i in range(size)])]
    ppermute x2, waiting for transfers between devices: 0.11 us -> 2.58 us  [shift(): lax.ppermute(array, 'cols', [(i, i + step) for i in range(size) if 0 <= i...]
    pallas_call x7 -> x11, Pallas kernels: 14.5 us -> 12.4 us  [call(): pl.pallas_call(kernel, in_specs=[spaces.get(i, vmem) for i in range(len(i...]
    ppermute x2, starting transfers between devices: 3.45 us -> 4.68 us  [shift(): lax.ppermute(array, 'cols', [(i, i + step) for i in range(size) if 0 <= i...]
  transfers between devices with their start and end apart: 17 -> 20, of which waited for: 10 -> 11; matrix products, arithmetic and copies ran while one was open for 2% -> 2% of each run, Pallas kernels for 5% -> 5%
where the time goes in v3:
time: 62.6 us; the launch traced here: 62.1 us
  starting transfers between devices  24.5 us (39%)
  waiting for transfers between devices  23.4 us (37%)
  Pallas kernels  12.4 us (20%)
  local copies, waits for them, and re-layouts  0.96 us (2%)
  between operations  0.79 us (1%)
    ppermute x18, waiting for transfers between devices, swap(): return lax.ppermute(array, 'cols', [(i, i ^ mask) for i in range(size)])  20.8 us
    ppermute x18, starting transfers between devices, swap(): return lax.ppermute(array, 'cols', [(i, i ^ mask) for i in range(size)])  19.8 us
    pallas_call x11, Pallas kernels, call(): pl.pallas_call(kernel, in_specs=[spaces.get(i, vmem) for i in range(len(i...  12.4 us
    ppermute x2, starting transfers between devices, shift(): lax.ppermute(array, 'cols', [(i, i + step) for i in range(size) if 0 <= i...  4.68 us
    ppermute x2, waiting for transfers between devices, shift(): lax.ppermute(array, 'cols', [(i, i + step) for i in range(size) if 0 <= i...  2.58 us
  transfers between devices with their start and end apart: 20, of which 11 were waited for; matrix products, arithmetic and copies ran while one was open for 2% of the time, Pallas kernels for 5%

profile of v3, /device:TPU:0, one launch (start us, length us, event | category | flops | bytes accessed | tf_op | source)
XLA Modules:
  0.0 62.1 jit_solution(13194240741286656307)
XLA Ops:
  0.6 2.3 %deal.1 = (bf16[2,128,576]{2,1,0:T(8,128)(2,1)}, bf16[2,128,576]{2,1,0:T(8,128)(2,1)}, bf16[48,1152]{1,0:T(8,128)(2,1)}) custom-call(bf16[32,1024]{1,0:T(8,128)(2,1)} %x_hbm.1, bf16[32,16,512]{2,1,0:T(8,128)(2,1)} %teacher_hbm.1, bf16[8,576]{1,0:T(8,128)(2,1)} %w_first_hbm.1, bf16[8,1152]{1,0:T(8,128)(2,1)} %w_middle_hbm.1, bf16[32,1152]{1,0:T(8,128)(2,1)} %w_last_hbm.1), custom_call_target="tpu_custom_call" | custom-call | flops 600000000 | bytes 1000000 | tf_op jit(solution)/shard_map/deal/pallas_call | solution.py:349
  2.9 0.5 collective-permute-start
  3.5 4.7 %collective-permute-start.4 = (bf16[48,1152]{1,0:T(8,128)(2,1)}, bf16[48,1152]{1,0:T(8,128)(2,1)S(1)}, u32[]{:S(2)}, u32[]{:S(2)}) collective-permute-start(bf16[48,1152]{1,0:T(8,128)(2,1)} %get-tuple-element.34.refs_0_), channel_id=1, source_target_pairs={{0,12},{1,13},{2,14},{3,15},{4,8},{5,9},{6,10},{7,11},{8,4},{9,5},... | collective-permute-start | bytes 331784 | tf_op jit(solution)/shard_map/ppermute | solution.py:20
  8.1 0.7 %collective-permute-start.2 = (bf16[48,1152]{1,0:T(8,128)(2,1)}, bf16[48,1152]{1,0:T(8,128)(2,1)S(1)}, u32[]{:S(2)}, u32[]{:S(2)}) collective-permute-start(bf16[48,1152]{1,0:T(8,128)(2,1)} %get-tuple-element.34.refs_0_), channel_id=1, source_target_pairs={{0,4},{1,5},{2,6},{3,7},{4,0},{5,1},{6,2},{7,3},{8,12},{9,13},{10,... | collective-permute-start | bytes 331784 | tf_op jit(solution)/shard_map/ppermute | solution.py:20
  8.8 0.9 %slice.6 = bf16[1,128,576]{2,1,0:T(8,128)(2,1)S(1)} slice(bf16[2,128,576]{2,1,0:T(8,128)(2,1)} %get-tuple-element.32.kept_ref), slice={[1:2], [0:128], [0:576]} | slice | bytes 294912 | tf_op jit(solution)/shard_map/slice | solution.py:397
  9.8 1.7 %collective-permute-start.1 = (bf16[2,128,576]{2,1,0:T(8,128)(2,1)S(1)}, bf16[2,128,576]{2,1,0:T(8,128)(2,1)S(1)}, u32[]{:S(2)}, u32[]{:S(2)}) collective-permute-start(bf16[2,128,576]{2,1,0:T(8,128)(2,1)S(1)} %pad_maximum_fusion), channel_id=1, source_target_pairs={{0,2},{1,3},{2,0},{3,1},{4,6},{5,7},{6,4},{7,5},{8,10},{9,11},{10,... | collective-permute-start | bytes 884744 | tf_op jit(solution)/shard_map/ppermute | solution.py:20
  11.5 0.8 %collective-permute-done.4.refs_3_ = bf16[48,1152]{1,0:T(8,128)(2,1)S(1)} collective-permute-done((bf16[48,1152]{1,0:T(8,128)(2,1)}, bf16[48,1152]{1,0:T(8,128)(2,1)S(1)}, u32[]{:S(2)}, u32[]{:S(2)}) %collective-permute-start.4) | collective-permute-done | bytes 110624 | tf_op jit(solution)/shard_map/ppermute | solution.py:20
  12.4 5.9 %collective-permute-done.3.refs_2_ = bf16[48,1152]{1,0:T(8,128)(2,1)S(1)} collective-permute-done((bf16[48,1152]{1,0:T(8,128)(2,1)}, bf16[48,1152]{1,0:T(8,128)(2,1)S(1)}, u32[]{:S(2)}, u32[]{:S(2)}) %collective-permute-start.3) | collective-permute-done | bytes 110624 | tf_op jit(solution)/shard_map/ppermute | solution.py:20
  18.3 1.0 %collective-permute-done.1.far_ref = bf16[2,128,576]{2,1,0:T(8,128)(2,1)S(1)} collective-permute-done((bf16[2,128,576]{2,1,0:T(8,128)(2,1)S(1)}, bf16[2,128,576]{2,1,0:T(8,128)(2,1)S(1)}, u32[]{:S(2)}, u32[]{:S(2)}) %collective-permute-start.1) | collective-permute-done | bytes 294944 | tf_op jit(solution)/shard_map/ppermute | solution.py:20
  19.4 1.6 %collective-permute-start.7 = (bf16[4,48,1152]{2,1,0:T(8,128)(2,1)S(1)}, bf16[4,48,1152]{2,1,0:T(8,128)(2,1)S(1)}, u32[]{:S(2)}, u32[]{:S(2)}) collective-permute-start(bf16[4,48,1152]{2,1,0:T(8,128)(2,1)S(1)} %get-tuple-element.38.h_ref), channel_id=1, source_target_pairs={{0,2},{1,3},{2,0},{3,1},{4,6},{5,7},{6,4},{7,5},{8,10},{9,11},{10,... | collective-permute-start | bytes 1327112 | tf_op jit(solution)/shard_map/ppermute | solution.py:20
  21.0 3.4 %collective-permute-start.5 = (bf16[208,576]{1,0:T(8,128)(2,1)S(1)}, bf16[208,576]{1,0:T(8,128)(2,1)S(1)}, u32[]{:S(2)}, u32[]{:S(2)}) collective-permute-start(bf16[208,576]{1,0:T(8,128)(2,1)S(1)} %get-tuple-element.35), channel_id=1, source_target_pairs={{0,4},{1,5},{2,6},{3,7},{4,8},{5,9},{6,10},{7,11},{8,12},{9,13},{1... | collective-permute-start | bytes 718856 | tf_op jit(solution)/shard_map/ppermute | solution.py:25
  24.4 1.3 %collective-permute-start.6 = (bf16[208,576]{1,0:T(8,128)(2,1)S(1)}, bf16[208,576]{1,0:T(8,128)(2,1)S(1)}, u32[]{:S(2)}, u32[]{:S(2)}) collective-permute-start(bf16[208,576]{1,0:T(8,128)(2,1)S(1)} %get-tuple-element.37), channel_id=1, source_target_pairs={{4,0},{5,1},{6,2},{7,3},{8,4},{9,5},{10,6},{11,7},{12,8},{13,9},{1... | collective-permute-start | bytes 718856 | tf_op jit(solution)/shard_map/ppermute | solution.py:25
  25.8 4.7 %collective-permute-done.7.hy_ref = bf16[4,48,1152]{2,1,0:T(8,128)(2,1)S(1)} collective-permute-done((bf16[4,48,1152]{2,1,0:T(8,128)(2,1)S(1)}, bf16[4,48,1152]{2,1,0:T(8,128)(2,1)S(1)}, u32[]{:S(2)}, u32[]{:S(2)}) %collective-permute-start.7) | collective-permute-done | bytes 442400 | tf_op jit(solution)/shard_map/ppermute | solution.py:20
  30.5 2.6 %collective-permute-done.6.after_ref = bf16[208,576]{1,0:T(8,128)(2,1)S(1)} collective-permute-done((bf16[208,576]{1,0:T(8,128)(2,1)S(1)}, bf16[208,576]{1,0:T(8,128)(2,1)S(1)}, u32[]{:S(2)}, u32[]{:S(2)}) %collective-permute-start.6) | collective-permute-done | bytes 239648 | tf_op jit(solution)/shard_map/ppermute | solution.py:25
  33.0 0.4 early.1.patch_first_ref
  33.5 6.3 %front.1 = (f32[2,4,32,1152]{3,2,1,0:T(8,128)S(1)}, bf16[2,4,32,1152]{3,2,1,0:T(8,128)(2,1)S(1)}, bf16[704,512]{1,0:T(8,128)(2,1)S(1)}, f32[512,128]{1,0:T(8,128...) custom-call(bf16[208,576]{1,0:T(8,128)(2,1)S(1)} %collective-permute, ...), custom_call_target="tpu_custom_call" | custom-call | flops 6000000000 | bytes 1000000 | tf_op jit(solution)/shard_map/front/pallas_call | solution.py:349
  39.9 2.0 %collective-permute-done.10.got_ref = bf16[2,4,32,1152]{3,2,1,0:T(8,128)(2,1)S(1)} collective-permute-done((bf16[2,4,32,1152]{3,2,1,0:T(8,128)(2,1)S(1)}, bf16[2,4,32,1152]{3,2,1,0:T(8,128)(2,1)S(1)}, u32[]{:S(2)}, u32[]{:S(2)}) %collective-permute-start.10) | collective-permute-done | bytes 589856 | tf_op jit(solution)/shard_map/ppermute | solution.py:20
  42.1 0.6 collective-permute-start.11
  42.6 2.2 %back.1 = (f32[4,2,8,1728]{3,2,1,0:T(8,128)S(1)}, bf16[4,2,8,1728]{3,2,1,0:T(8,128)(2,1)S(1)}) custom-call(bf16[704,512]{1,0:T(8,128)(2,1)S(1)} %get-tuple-element.47.slope_ref, f32[576,128]{1,0:T(8,128)S(1)} %get-tuple-element.48.tilt_second_ref, bf16[16,32,1152]{2,1,0:T(8,128)(2,1)S(1)} %get-tuple-element.49.w_last_ref, ...), custom_call_target="tpu_custom_call" | custom-call | flops 4000000000 | bytes 1000000 | tf_op jit(solution)/shard_map/back/pallas_call | solution.py:349
  44.9 1.5 %collective-permute-done.15.got_ref = bf16[4,2,8,1728]{3,2,1,0:T(8,128)(2,1)S(1)} collective-permute-done((bf16[4,2,8,1728]{3,2,1,0:T(8,128)(2,1)S(1)}, bf16[4,2,8,1728]{3,2,1,0:T(8,128)(2,1)S(1)}, u32[]{:S(2)}, u32[]{:S(2)}) %collective-permute-start.15) | collective-permute-done | bytes 221216 | tf_op jit(solution)/shard_map/ppermute | solution.py:20
  46.4 1.5 %collective-permute-start.16 = (bf16[2,8,1728]{2,1,0:T(8,128)(2,1)S(1)}, bf16[2,8,1728]{2,1,0:T(8,128)(2,1)S(1)}, u32[]{:S(2)}, u32[]{:S(2)}) collective-permute-start(bf16[2,8,1728]{2,1,0:T(8,128)(2,1)S(1)} %get-tuple-element.56), channel_id=1, source_target_pairs={{0,4},{1,5},{2,6},{3,7},{4,0},{5,1},{6,2},{7,3},{8,12},{9,13},{10,... | collective-permute-start | bytes 165896 | tf_op jit(solution)/shard_map/ppermute | solution.py:20
  48.0 2.2 %collective-permute-start.17 = (bf16[2,8,1728]{2,1,0:T(8,128)(2,1)S(1)}, bf16[2,8,1728]{2,1,0:T(8,128)(2,1)S(1)}, u32[]{:S(2)}, u32[]{:S(2)}) collective-permute-start(bf16[2,8,1728]{2,1,0:T(8,128)(2,1)S(1)} %get-tuple-element.57), channel_id=1, source_target_pairs={{0,8},{1,9},{2,10},{3,11},{4,12},{5,13},{6,14},{7,15},{8,0},{9,1},... | collective-permute-start | bytes 165896 | tf_op jit(solution)/shard_map/ppermute | solution.py:20
  50.2 0.7 %collective-permute-start.18 = (bf16[2,8,1728]{2,1,0:T(8,128)(2,1)S(1)}, bf16[2,8,1728]{2,1,0:T(8,128)(2,1)S(1)}, u32[]{:S(2)}, u32[]{:S(2)}) collective-permute-start(bf16[2,8,1728]{2,1,0:T(8,128)(2,1)S(1)} %get-tuple-element.58), channel_id=1, source_target_pairs={{0,12},{1,13},{2,14},{3,15},{4,8},{5,9},{6,10},{7,11},{8,4},{9,5},... | collective-permute-start | bytes 165896 | tf_op jit(solution)/shard_map/ppermute | solution.py:20
  50.9 0.3 collective-permute-done.11.got_ref
  51.2 1.5 %collective-permute-start.12 = (bf16[32,1152]{1,0:T(8,128)(2,1)S(1)}, bf16[32,1152]{1,0:T(8,128)(2,1)S(1)}, u32[]{:S(2)}, u32[]{:S(2)}) collective-permute-start(bf16[32,1152]{1,0:T(8,128)(2,1)S(1)} %get-tuple-element.44), channel_id=1, source_target_pairs={{0,4},{1,5},{2,6},{3,7},{4,0},{5,1},{6,2},{7,3},{8,12},{9,13},{10,... | collective-permute-start | bytes 221192 | tf_op jit(solution)/shard_map/ppermute | solution.py:20
  52.8 1.9 %collective-permute-start.13 = (bf16[32,1152]{1,0:T(8,128)(2,1)S(1)}, bf16[32,1152]{1,0:T(8,128)(2,1)S(1)}, u32[]{:S(2)}, u32[]{:S(2)}) collective-permute-start(bf16[32,1152]{1,0:T(8,128)(2,1)S(1)} %get-tuple-element.45), channel_id=1, source_target_pairs={{0,8},{1,9},{2,10},{3,11},{4,12},{5,13},{6,14},{7,15},{8,0},{9,1},... | collective-permute-start | bytes 221192 | tf_op jit(solution)/shard_map/ppermute | solution.py:20
  54.7 1.0 %collective-permute-start.14 = (bf16[32,1152]{1,0:T(8,128)(2,1)S(1)}, bf16[32,1152]{1,0:T(8,128)(2,1)S(1)}, u32[]{:S(2)}, u32[]{:S(2)}) collective-permute-start(bf16[32,1152]{1,0:T(8,128)(2,1)S(1)} %get-tuple-element.46), channel_id=1, source_target_pairs={{0,12},{1,13},{2,14},{3,15},{4,8},{5,9},{6,10},{7,11},{8,4},{9,5},... | collective-permute-start | bytes 221192 | tf_op jit(solution)/shard_map/ppermute | solution.py:20
  55.7 1.0 %collective-permute-done.18.got3_ref = bf16[2,8,1728]{2,1,0:T(8,128)(2,1)S(1)} collective-permute-done((bf16[2,8,1728]{2,1,0:T(8,128)(2,1)S(1)}, bf16[2,8,1728]{2,1,0:T(8,128)(2,1)S(1)}, u32[]{:S(2)}, u32[]{:S(2)}) %collective-permute-start.18) | collective-permute-done | bytes 55328 | tf_op jit(solution)/shard_map/ppermute | solution.py:20
  56.8 1.0 %collective-permute-start.19 = (bf16[8,1728]{1,0:T(8,128)(2,1)S(1)}, bf16[8,1728]{1,0:T(8,128)(2,1)S(1)}, u32[]{:S(2)}, u32[]{:S(2)}) collective-permute-start(bf16[8,1728]{1,0:T(8,128)(2,1)S(1)} %get-tuple-element.60), channel_id=1, source_target_pairs={{0,2},{1,3},{2,0},{3,1},{4,6},{5,7},{6,4},{7,5},{8,10},{9,11},{10,... | collective-permute-start | bytes 82952 | tf_op jit(solution)/shard_map/ppermute | solution.py:20
  57.7 2.9 %collective-permute-done.19.got_ref = bf16[8,1728]{1,0:T(8,128)(2,1)S(1)} collective-permute-done((bf16[8,1728]{1,0:T(8,128)(2,1)S(1)}, bf16[8,1728]{1,0:T(8,128)(2,1)S(1)}, u32[]{:S(2)}, u32[]{:S(2)}) %collective-permute-start.19) | collective-permute-done | bytes 27680 | tf_op jit(solution)/shard_map/ppermute | solution.py:20
  60.7 0.7 %collective-permute-done.13.got2_ref = bf16[32,1152]{1,0:T(8,128)(2,1)S(1)} collective-permute-done((bf16[32,1152]{1,0:T(8,128)(2,1)S(1)}, bf16[32,1152]{1,0:T(8,128)(2,1)S(1)}, u32[]{:S(2)}, u32[]{:S(2)}) %collective-permute-start.13) | collective-permute-done | bytes 73760 | tf_op jit(solution)/shard_map/ppermute | solution.py:20
  61.4 0.7 %finish.1 = (f32[8,576]{1,0:T(8,128)}, f32[8,1152]{1,0:T(8,128)}, f32[32,1152]{1,0:T(8,128)}) custom-call(f32[32,1152]{1,0:T(8,128)S(1)} %get-tuple-element.43.last_ref, bf16[32,1152]{1,0:T(8,128)(2,1)S(1)} %collective-permute-done.12.got1_ref, bf16[32,1152]{1,0:T(8,128)(2,1)S(1)} %collective-permute-done.13.got2_ref, ...), custom_call_target="tpu_custom_call" | custom-call | flops 1000000 | bytes 1000000 | tf_op jit(solution)/shard_map/finish/pallas_call | solution.py:349
  (26 shorter events, 0.7 us)
Async XLA Ops:
  2.9 15.4 %copy-start.1 = (bf16[48,1152]{1,0:T(8,128)(2,1)S(1)}, bf16[48,1152]{1,0:T(8,128)(2,1)}, u32[]{:S(2)}) copy-start(bf16[48,1152]{1,0:T(8,128)(2,1)} %get-tuple-element.34.refs_0_) | copy-start | bytes 331780
  2.9 6.8 %collective-permute-start = (bf16[2,128,576]{2,1,0:T(8,128)(2,1)}, bf16[2,128,576]{2,1,0:T(8,128)(2,1)S(1)}, u32[]{:S(2)}, u32[]{:S(2)}) collective-permute-start(bf16[2,128,576]{2,1,0:T(8,128)(2,1)} %get-tuple-element.33), channel_id=1, source_target_pairs={{0,1},{1,0},{2,3},{3,2},{4,5},{5,4},{6,7},{7,6},{8,9},{9,8},{10,11... | collective-permute-start | bytes 884744 | tf_op jit(solution)/shard_map/ppermute | solution.py:20
  3.5 8.9 %collective-permute-start.4 = (bf16[48,1152]{1,0:T(8,128)(2,1)}, bf16[48,1152]{1,0:T(8,128)(2,1)S(1)}, u32[]{:S(2)}, u32[]{:S(2)}) collective-permute-start(bf16[48,1152]{1,0:T(8,128)(2,1)} %get-tuple-element.34.refs_0_), channel_id=1, source_target_pairs={{0,12},{1,13},{2,14},{3,15},{4,8},{5,9},{6,10},{7,11},{8,4},{9,5},... | collective-permute-start | bytes 331784 | tf_op jit(solution)/shard_map/ppermute | solution.py:20
  8.1 10.1 %collective-permute-start.3 = (bf16[48,1152]{1,0:T(8,128)(2,1)}, bf16[48,1152]{1,0:T(8,128)(2,1)S(1)}, u32[]{:S(2)}, u32[]{:S(2)}) collective-permute-start(bf16[48,1152]{1,0:T(8,128)(2,1)} %get-tuple-element.34.refs_0_), channel_id=1, source_target_pairs={{0,8},{1,9},{2,10},{3,11},{4,12},{5,13},{6,14},{7,15},{8,0},{9,1},... | collective-permute-start | bytes 331784 | tf_op jit(solution)/shard_map/ppermute | solution.py:20
  8.1 10.1 %collective-permute-start.2 = (bf16[48,1152]{1,0:T(8,128)(2,1)}, bf16[48,1152]{1,0:T(8,128)(2,1)S(1)}, u32[]{:S(2)}, u32[]{:S(2)}) collective-permute-start(bf16[48,1152]{1,0:T(8,128)(2,1)} %get-tuple-element.34.refs_0_), channel_id=1, source_target_pairs={{0,4},{1,5},{2,6},{3,7},{4,0},{5,1},{6,2},{7,3},{8,12},{9,13},{10,... | collective-permute-start | bytes 331784 | tf_op jit(solution)/shard_map/ppermute | solution.py:20
  9.8 9.5 %copy-start = (bf16[2,128,576]{2,1,0:T(8,128)(2,1)S(1)}, bf16[2,128,576]{2,1,0:T(8,128)(2,1)}, u32[]{:S(2)}) copy-start(bf16[2,128,576]{2,1,0:T(8,128)(2,1)} %get-tuple-element.32.kept_ref) | copy-start | bytes 884740
  9.8 9.5 %collective-permute-start.1 = (bf16[2,128,576]{2,1,0:T(8,128)(2,1)S(1)}, bf16[2,128,576]{2,1,0:T(8,128)(2,1)S(1)}, u32[]{:S(2)}, u32[]{:S(2)}) collective-permute-start(bf16[2,128,576]{2,1,0:T(8,128)(2,1)S(1)} %pad_maximum_fusion), channel_id=1, source_target_pairs={{0,2},{1,3},{2,0},{3,1},{4,6},{5,7},{6,4},{7,5},{8,10},{9,11},{10,... | collective-permute-start | bytes 884744 | tf_op jit(solution)/shard_map/ppermute | solution.py:20
  19.4 11.0 %collective-permute-start.7 = (bf16[4,48,1152]{2,1,0:T(8,128)(2,1)S(1)}, bf16[4,48,1152]{2,1,0:T(8,128)(2,1)S(1)}, u32[]{:S(2)}, u32[]{:S(2)}) collective-permute-start(bf16[4,48,1152]{2,1,0:T(8,128)(2,1)S(1)} %get-tuple-element.38.h_ref), channel_id=1, source_target_pairs={{0,2},{1,3},{2,0},{3,1},{4,6},{5,7},{6,4},{7,5},{8,10},{9,11},{10,... | collective-permute-start | bytes 1327112 | tf_op jit(solution)/shard_map/ppermute | solution.py:20
  21.0 9.5 %collective-permute-start.5 = (bf16[208,576]{1,0:T(8,128)(2,1)S(1)}, bf16[208,576]{1,0:T(8,128)(2,1)S(1)}, u32[]{:S(2)}, u32[]{:S(2)}) collective-permute-start(bf16[208,576]{1,0:T(8,128)(2,1)S(1)} %get-tuple-element.35), channel_id=1, source_target_pairs={{0,4},{1,5},{2,6},{3,7},{4,8},{5,9},{6,10},{7,11},{8,12},{9,13},{1... | collective-permute-start | bytes 718856 | tf_op jit(solution)/shard_map/ppermute | solution.py:25
  24.4 8.7 %collective-permute-start.6 = (bf16[208,576]{1,0:T(8,128)(2,1)S(1)}, bf16[208,576]{1,0:T(8,128)(2,1)S(1)}, u32[]{:S(2)}, u32[]{:S(2)}) collective-permute-start(bf16[208,576]{1,0:T(8,128)(2,1)S(1)} %get-tuple-element.37), channel_id=1, source_target_pairs={{4,0},{5,1},{6,2},{7,3},{8,4},{9,5},{10,6},{11,7},{12,8},{13,9},{1... | collective-permute-start | bytes 718856 | tf_op jit(solution)/shard_map/ppermute | solution.py:25
  25.7 7.8 %collective-permute-start.8 = (bf16[4,48,1152]{2,1,0:T(8,128)(2,1)S(1)}, bf16[4,48,1152]{2,1,0:T(8,128)(2,1)S(1)}, u32[]{:S(2)}, u32[]{:S(2)}) collective-permute-start(bf16[4,48,1152]{2,1,0:T(8,128)(2,1)S(1)} %get-tuple-element.38.h_ref), channel_id=1, source_target_pairs={{0,1},{1,0},{2,3},{3,2},{4,5},{5,4},{6,7},{7,6},{8,9},{9,8},{10,11... | collective-permute-start | bytes 1327112 | tf_op jit(solution)/shard_map/ppermute | solution.py:20
  30.5 3.0 %collective-permute-start.9 = (bf16[4,48,1152]{2,1,0:T(8,128)(2,1)S(1)}, bf16[4,48,1152]{2,1,0:T(8,128)(2,1)S(1)}, u32[]{:S(2)}, u32[]{:S(2)}) collective-permute-start(bf16[4,48,1152]{2,1,0:T(8,128)(2,1)S(1)} %collective-permute-done.7.hy_ref), channel_id=1, source_target_pairs={{0,1},{1,0},{2,3},{3,2},{4,5},{5,4},{6,7},{7,6},{8,9},{9,8},{10,11... | collective-permute-start | bytes 1327112 | tf_op jit(solution)/shard_map/ppermute | solution.py:20
  39.9 2.1 %collective-permute-start.10 = (bf16[2,4,32,1152]{3,2,1,0:T(8,128)(2,1)S(1)}, bf16[2,4,32,1152]{3,2,1,0:T(8,128)(2,1)S(1)}, u32[]{:S(2)}, u32[]{:S(2)}) collective-permute-start(bf16[2,4,32,1152]{3,2,1,0:T(8,128)(2,1)S(1)} %get-tuple-element.40), channel_id=1, source_target_pairs={{0,1},{1,0},{2,3},{3,2},{4,5},{5,4},{6,7},{7,6},{8,9},{9,8},{10,11... | collective-permute-start | bytes 1769480 | tf_op jit(solution)/shard_map/ppermute | solution.py:20
  42.1 9.1 %collective-permute-start.11 = (bf16[4,32,1152]{2,1,0:T(8,128)(2,1)S(1)}, bf16[4,32,1152]{2,1,0:T(8,128)(2,1)S(1)}, u32[]{:S(2)}, u32[]{:S(2)}) collective-permute-start(bf16[4,32,1152]{2,1,0:T(8,128)(2,1)S(1)} %get-tuple-element.42), channel_id=1, source_target_pairs={{0,2},{1,3},{2,0},{3,1},{4,6},{5,7},{6,4},{7,5},{8,10},{9,11},{10,... | collective-permute-start | bytes 884744 | tf_op jit(solution)/shard_map/ppermute | solution.py:20
  44.8 1.6 %collective-permute-start.15 = (bf16[4,2,8,1728]{3,2,1,0:T(8,128)(2,1)S(1)}, bf16[4,2,8,1728]{3,2,1,0:T(8,128)(2,1)S(1)}, u32[]{:S(2)}, u32[]{:S(2)}) collective-permute-start(bf16[4,2,8,1728]{3,2,1,0:T(8,128)(2,1)S(1)} %get-tuple-element.54), channel_id=1, source_target_pairs={{0,1},{1,0},{2,3},{3,2},{4,5},{5,4},{6,7},{7,6},{8,9},{9,8},{10,11... | collective-permute-start | bytes 663560 | tf_op jit(solution)/shard_map/ppermute | solution.py:20
  46.4 8.3 %collective-permute-start.16 = (bf16[2,8,1728]{2,1,0:T(8,128)(2,1)S(1)}, bf16[2,8,1728]{2,1,0:T(8,128)(2,1)S(1)}, u32[]{:S(2)}, u32[]{:S(2)}) collective-permute-start(bf16[2,8,1728]{2,1,0:T(8,128)(2,1)S(1)} %get-tuple-element.56), channel_id=1, source_target_pairs={{0,4},{1,5},{2,6},{3,7},{4,0},{5,1},{6,2},{7,3},{8,12},{9,13},{10,... | collective-permute-start | bytes 165896 | tf_op jit(solution)/shard_map/ppermute | solution.py:20
  48.0 7.7 %collective-permute-start.17 = (bf16[2,8,1728]{2,1,0:T(8,128)(2,1)S(1)}, bf16[2,8,1728]{2,1,0:T(8,128)(2,1)S(1)}, u32[]{:S(2)}, u32[]{:S(2)}) collective-permute-start(bf16[2,8,1728]{2,1,0:T(8,128)(2,1)S(1)} %get-tuple-element.57), channel_id=1, source_target_pairs={{0,8},{1,9},{2,10},{3,11},{4,12},{5,13},{6,14},{7,15},{8,0},{9,1},... | collective-permute-start | bytes 165896 | tf_op jit(solution)/shard_map/ppermute | solution.py:20
  50.2 6.5 %collective-permute-start.18 = (bf16[2,8,1728]{2,1,0:T(8,128)(2,1)S(1)}, bf16[2,8,1728]{2,1,0:T(8,128)(2,1)S(1)}, u32[]{:S(2)}, u32[]{:S(2)}) collective-permute-start(bf16[2,8,1728]{2,1,0:T(8,128)(2,1)S(1)} %get-tuple-element.58), channel_id=1, source_target_pairs={{0,12},{1,13},{2,14},{3,15},{4,8},{5,9},{6,10},{7,11},{8,4},{9,5},... | collective-permute-start | bytes 165896 | tf_op jit(solution)/shard_map/ppermute | solution.py:20
  51.2 9.4 %collective-permute-start.12 = (bf16[32,1152]{1,0:T(8,128)(2,1)S(1)}, bf16[32,1152]{1,0:T(8,128)(2,1)S(1)}, u32[]{:S(2)}, u32[]{:S(2)}) collective-permute-start(bf16[32,1152]{1,0:T(8,128)(2,1)S(1)} %get-tuple-element.44), channel_id=1, source_target_pairs={{0,4},{1,5},{2,6},{3,7},{4,0},{5,1},{6,2},{7,3},{8,12},{9,13},{10,... | collective-permute-start | bytes 221192 | tf_op jit(solution)/shard_map/ppermute | solution.py:20
  52.8 8.7 %collective-permute-start.13 = (bf16[32,1152]{1,0:T(8,128)(2,1)S(1)}, bf16[32,1152]{1,0:T(8,128)(2,1)S(1)}, u32[]{:S(2)}, u32[]{:S(2)}) collective-permute-start(bf16[32,1152]{1,0:T(8,128)(2,1)S(1)} %get-tuple-element.45), channel_id=1, source_target_pairs={{0,8},{1,9},{2,10},{3,11},{4,12},{5,13},{6,14},{7,15},{8,0},{9,1},... | collective-permute-start | bytes 221192 | tf_op jit(solution)/shard_map/ppermute | solution.py:20
  54.7 6.7 %collective-permute-start.14 = (bf16[32,1152]{1,0:T(8,128)(2,1)S(1)}, bf16[32,1152]{1,0:T(8,128)(2,1)S(1)}, u32[]{:S(2)}, u32[]{:S(2)}) collective-permute-start(bf16[32,1152]{1,0:T(8,128)(2,1)S(1)} %get-tuple-element.46), channel_id=1, source_target_pairs={{0,12},{1,13},{2,14},{3,15},{4,8},{5,9},{6,10},{7,11},{8,4},{9,5},... | collective-permute-start | bytes 221192 | tf_op jit(solution)/shard_map/ppermute | solution.py:20
  56.8 3.9 %collective-permute-start.19 = (bf16[8,1728]{1,0:T(8,128)(2,1)S(1)}, bf16[8,1728]{1,0:T(8,128)(2,1)S(1)}, u32[]{:S(2)}, u32[]{:S(2)}) collective-permute-start(bf16[8,1728]{1,0:T(8,128)(2,1)S(1)} %get-tuple-element.60), channel_id=1, source_target_pairs={{0,2},{1,3},{2,0},{3,1},{4,6},{5,7},{6,4},{7,5},{8,10},{9,11},{10,... | collective-permute-start | bytes 82952 | tf_op jit(solution)/shard_map/ppermute | solution.py:20

commit v4 on v3

--- a/solution.py
+++ b/solution.py
@@ -12,7 +12,9 @@
 MIB = 1024 * 1024
 HALO_X, HALO_FIRST, HALO_SECOND, HALO_SLOPE, HALO_BACK = 13, 12, 10, 6, 2
 BLOCKS, FAR = 16, 4
+LANES = 128
 STACK_COST = 3_000_000_000
+EARLY_COST = 1_500_000_000
 
 
 def swap(array, mask):
@@ -20,11 +22,11 @@
     return lax.ppermute(array, "cols", [(i, i ^ mask) for i in range(size)])
 
 
-def shift(array, step):
+def bands_beside(low_pairs, high_pairs):
     size = lax.axis_size("cols")
-    return lax.ppermute(
-        array, "cols", [(i, i + step) for i in range(size) if 0 <= i + step < size]
-    )
+    pairs = [(i, i + 4) for i in range(4, size - 4) if (i // 4) % 2]
+    across = lax.ppermute(high_pairs, "cols", pairs + [(j, i) for i, j in pairs])
+    return swap(low_pairs, 4), across
 
 
 def neighbours(fold):
@@ -90,8 +92,9 @@
     w_first_hbm,
     w_middle_hbm,
     w_last_hbm,
-    kept_ref,
-    sent_ref,
+    own_ref,
+    near_ref,
+    across_ref,
     shard_ref,
     x_ref,
     teacher_ref,
@@ -132,52 +135,210 @@
             pick_t_ref[rc, ry] = (iota((cells, height * breadth), 1) == source).astype(f32).astype(bf16)
     for copy in copies:
         copy.wait()
-    r_last, r_small, taps = w_last_ref.shape[0], w_middle_ref.shape[0], w_first_ref.shape[1]
-    shard_ref[:r_last] = w_last_ref[...]
-    shard_ref[r_last : r_last + r_small] = w_middle_ref[...]
-    shard_ref[r_last + r_small :, :taps] = w_first_ref[...]
-    shard_ref[r_last + r_small :, taps:] = jnp.zeros(
-        (r_small, shard_ref.shape[1] - taps), shard_ref.dtype
-    )
+    at = put_tiles(shard_ref, 0, w_last_ref[...])
+    at = put_tiles(shard_ref, at, w_middle_ref[...])
+    put_tiles(shard_ref, at, w_first_ref[...])
+    own_ref[: shard_ref.shape[0]] = shard_ref[...]
     field = teacher_ref[...].reshape(height * breadth, channels)
     pairs = jnp.concatenate(
         [x_ref[:, 2 * depth * i : 2 * depth * (i + 1)] for i in range(piece)], 0
     )
-    for rc, out_ref in ((1, sent_ref), (0, kept_ref)):
-        both = dot(pick_x_ref[rc], pairs, ((1,), (0,)))
+    x_parts = []
+    for rc, out_ref in ((0, own_ref), (1, near_ref)):
+        both = dot(pick_x_ref[rc], pairs, ((1,), (0,))).astype(bf16)
         low, high = both[:, :depth], both[:, depth:]
-        for ry in range(2):
-            out_ref[ry, :, :channels] = dot(pick_t_ref[rc, ry], field, ((1,), (0,))).astype(bf16)
-            out_ref[ry, :, channels:] = jnp.where((row ^ ry) == 0, low, high).astype(bf16)
-
-
-def stack_kernel(*refs):
-    for i, ref in enumerate(refs[:-1]):
-        refs[-1][i] = ref[...]
-
-
-def collect_kernel(halo, kept_ref, near_ref, far_ref, h_ref, band_ref, low_ref, high_ref, same_ref):
-    cells = kept_ref.shape[1]
+        x_parts.append(jnp.where(row == 0, high, low))
+        across = dot(pick_t_ref[rc, 1], field, ((1,), (0,))).astype(bf16)
+        put_tiles(across_ref, rc * cells * len(tiles(channels)), across)
+        value = dot(pick_t_ref[rc, 0], field, ((1,), (0,))).astype(bf16)
+        at = put_tiles(out_ref, out_ref.shape[0] - near_ref.shape[0], value)
+        x = jnp.where(row == 0, low, high)
+        out_ref[at:, :] = jnp.concatenate([x, jnp.zeros_like(x)], 1)
+    across_ref[across_ref.shape[0] - cells :, :] = jnp.concatenate(x_parts, 1)
+
+
+def tiles(width):
+    return [(start, min(LANES, width - start)) for start in range(0, width, LANES)]
+
+
+def put_tiles(ref, at, value):
+    rows, width = value.shape
+    for start, size in tiles(width):
+        ref[at : at + rows, :size] = value[:, start : start + size]
+        at += rows
+    return at
+
+
+def take_tiles(value, at, rows, width):
+    return jnp.concatenate(
+        [
+            value[at + i * rows : at + (i + 1) * rows, :size]
+            for i, (_, size) in enumerate(tiles(width))
+        ],
+        1,
+    )
+
+
+def hold_kernel(own_ref, across_ref, held_ref, same_ref):
+    held_ref[...] = own_ref[...]
+
+
+def stack_kernel(own_ref, far1_ref, far2_ref, far3_ref, last_ref, small_ref):
+    cut, end = last_ref.shape[1], last_ref.shape[1] + small_ref.shape[1]
+    for far, ref in enumerate((own_ref, far1_ref, far2_ref, far3_ref)):
+        last_ref[far] = ref[:cut]
+        small_ref[far] = ref[cut:end]
+
+
+def after_kernel(value_ref, first_ref, same_ref):
+    pass
+
+
+def collect_kernel(
+    cells,
+    edge_t,
+    edge_x,
+    own_ref,
+    near_ref,
+    across_ref,
+    diagonal_ref,
+    last_ref,
+    small_ref,
+    x_ref,
+    teacher_ref,
+    edge_a_ref,
+    edge_b_ref,
+    same_last_ref,
+    same_small_ref,
+):
+    depth, channels = x_ref.shape[1], teacher_ref.shape[1]
     low = position(BLOCKS)[1]
-    for k, piece in enumerate((kept_ref.at[0], near_ref.at[0], far_ref.at[0], far_ref.at[1])):
-        band_ref[pl.ds(pl.multiple_of((low ^ k) * cells, cells), cells), :] = piece[...]
-    low_ref[...] = band_ref[:halo]
-    high_ref[...] = band_ref[band_ref.shape[0] - halo :]
-
-
-def early_kernel(rows, channels, cols, before_ref, band_ref, after_ref, patch_ref):
-    wide = jnp.concatenate([ref[:, channels:] for ref in (before_ref, band_ref, after_ref)], 0)
-    put_patch(patch_ref, wide.astype(f32), 1, rows, cols)
+    part = cells * len(tiles(channels))
+    skip = own_ref.shape[0] - near_ref.shape[0]
+    pieces = ((own_ref, skip, 0), (near_ref, 0, 0), (across_ref, 0, 0), (diagonal_ref, part, depth))
+    for k, (ref, row, lane) in enumerate(pieces):
+        at = pl.ds(pl.multiple_of((low ^ k) * cells, cells), cells)
+        x_ref[at, :] = ref[ref.shape[0] - cells :, lane : lane + depth]
+        for lanes, size in tiles(channels):
+            teacher_ref[at, lanes : lanes + size] = ref[row : row + cells, :]
+            row += cells
+    own = teacher_ref.shape[0]
+    half = edge_x - edge_t
+    odd = position(BLOCKS)[0] % 2
+    for ref, high in ((edge_a_ref, 1 - odd), (edge_b_ref, odd)):
+        at = pl.ds(pl.multiple_of(high * (own - edge_t), 16), edge_t)
+        row = put_tiles(ref, 0, teacher_ref[at, :])
+        at = high * (own - edge_x)
+        ref[row:, :] = jnp.concatenate(
+            [
+                x_ref[pl.ds(pl.multiple_of(at, 16), half), :],
+                x_ref[pl.ds(pl.multiple_of(at + edge_t, 16), half), :],
+            ],
+            1,
+        )
+
+
+def sides(edge_a_ref, edge_b_ref):
+    a, b = edge_a_ref[...], edge_b_ref[...]
+    odd = position(BLOCKS)[0] % 2 == 1
+    return jnp.where(odd, a, b), jnp.where(odd, b, a)
+
+
+def edge_x_cells(edge, edge_t, channels):
+    packed = edge[edge_t * len(tiles(channels)) :, :]
+    depth = LANES // 2
+    overlap = packed.shape[0] - edge_t
+    return jnp.concatenate([packed[:, :depth], packed[overlap:, depth:]], 0)
+
+
+def early_kernel(
+    own,
+    rows,
+    total,
+    channels,
+    edge_t,
+    x_ref,
+    edge_a_ref,
+    edge_b_ref,
+    h_ref,
+    hy_ref,
+    hc_ref,
+    hyc_ref,
+    tilt_first_ref,
+    tilt_second_ref,
+    patch_first_ref,
+    patch_middle_ref,
+    patch_last_ref,
+    w_middle_ref,
+    small_ref,
+):
+    group, _, place = position(BLOCKS)
+    first_col = group * own
+    r_small = small_ref.shape[1] // 2
+    in_taps, taps = patch_first_ref.shape[1], patch_middle_ref.shape[1]
+    for near, ref in enumerate((h_ref, hc_ref, hy_ref, hyc_ref)):
+        for far in range(FAR):
+            at = place ^ (4 * far + near)
+            small = ref[far].astype(f32)
+            row = 0
+            for first, width in ((0, taps), (r_small, in_taps)):
+                for start, size in tiles(width):
+                    small_ref[at, first : first + r_small, start : start + size] = small[
+                        row : row + r_small, :size
+                    ]
+                    row += r_small
+    small = small_ref[...]
+    w_middle_ref[...] = small[:, :r_small].reshape(-1, taps).astype(bf16)
+    w_first = small[:, r_small:, :in_taps].reshape(-1, in_taps).astype(bf16)
+
+    n_first, n_second, n_slope = (
+        own + 2 * HALO_FIRST,
+        own + 2 * HALO_SECOND,
+        own + 2 * HALO_SLOPE,
+    )
+    before, after = sides(edge_a_ref, edge_b_ref)
+    wide = jnp.concatenate(
+        [
+            edge_x_cells(before, edge_t, channels),
+            x_ref[...],
+            edge_x_cells(after, edge_t, channels),
+        ],
+        0,
+    )
+    put_patch(patch_first_ref, wide.astype(f32), 1, rows, n_first)
+    pre = dot(patch_first_ref[...], w_first, ((1,), (1,)))
+    sigma = 1.0 / (1.0 + jnp.exp(-pre))
+    act = jnp.where(
+        inside(n_first * rows, rows, first_col - HALO_FIRST, total), pre * sigma, 0.0
+    )
+    lo = HALO_FIRST * rows
+    pre_own, sigma_own = pre[lo : lo + own * rows], sigma[lo : lo + own * rows]
+    tilt_first_ref[...] = sigma_own * (1.0 + pre_own * (1.0 - sigma_own))
+    put_patch(patch_middle_ref, act, 2, rows, n_second)
+
+    pre = dot(patch_middle_ref[...], w_middle_ref[...], ((1,), (1,)))
+    sigma = 1.0 / (1.0 + jnp.exp(-pre))
+    act = jnp.where(
+        inside(n_second * rows, rows, first_col - HALO_SECOND, total), pre * sigma, 0.0
+    )
+    lo, n_back = (HALO_SECOND - HALO_BACK) * rows, (own + 2 * HALO_BACK) * rows
+    pre_back, sigma_back = pre[lo : lo + n_back], sigma[lo : lo + n_back]
+    tilt_second_ref[...] = jnp.where(
+        inside(n_back, rows, first_col - HALO_BACK, total),
+        sigma_back * (1.0 + pre_back * (1.0 - sigma_back)),
+        0.0,
+    )
+    put_patch(patch_last_ref, act, 4, rows, n_slope)
 
 
 def front_kernel(
     own,
     rows,
     total,
-    before_ref,
-    band_ref,
-    after_ref,
-    patch_first_ref,
+    teacher_ref,
+    edge_a_ref,
+    edge_b_ref,
+    patch_last_ref,
     h_ref,
     hy_ref,
     hc_ref,
@@ -185,62 +346,21 @@
     keep_ref,
     send_ref,
     slope_ref,
-    tilt_first_ref,
-    tilt_second_ref,
-    patch_middle_ref,
-    w_middle_ref,
     w_last_ref,
-    small_ref,
-    patch_last_ref,
     student_ref,
     terms_ref,
 ):
     group, _, place = position(BLOCKS)
     first_col = group * own
-    r_last = w_last_ref.shape[1]
-    r_small = small_ref.shape[1] // 2
-    hidden = tilt_first_ref.shape[1]
+    r_last, taps = w_last_ref.shape[1:]
     channels = slope_ref.shape[1]
-    in_taps = patch_first_ref.shape[1]
     for near, ref in enumerate((h_ref, hc_ref, hy_ref, hyc_ref)):
         for far in range(FAR):
             at = place ^ (4 * far + near)
-            w_last_ref[at] = ref[far, :r_last]
-            small_ref[at] = ref[far, r_last:].astype(f32)
-    small = small_ref[...]
-    w_middle_ref[...] = small[:, :r_small].reshape(-1, 9 * hidden).astype(bf16)
-    w_first = small[:, r_small:, :in_taps].reshape(-1, in_taps).astype(bf16)
-
-    n_first, n_second, n_slope = (
-        own + 2 * HALO_FIRST,
-        own + 2 * HALO_SECOND,
-        own + 2 * HALO_SLOPE,
-    )
-    pre = dot(patch_first_ref[...], w_first, ((1,), (1,)))
-    sigma = 1.0 / (1.0 + jnp.exp(-pre))
-    act = jnp.where(
-        inside(n_first * rows, rows, first_col - HALO_FIRST, total), pre * sigma, 0.0
-    )
-    lo = HALO_FIRST * rows
-    pre_own, sigma_own = pre[lo : lo + own * rows], sigma[lo : lo + own * rows]
-    tilt_first_ref[...] = sigma_own * (1.0 + pre_own * (1.0 - sigma_own))
-    put_patch(patch_middle_ref, act, 2, rows, n_second)
-
-    pre = dot(patch_middle_ref[...], w_middle_ref[...], ((1,), (1,)))
-    sigma = 1.0 / (1.0 + jnp.exp(-pre))
-    act = jnp.where(
-        inside(n_second * rows, rows, first_col - HALO_SECOND, total), pre * sigma, 0.0
-    )
-    lo, n_back = (HALO_SECOND - HALO_BACK) * rows, (own + 2 * HALO_BACK) * rows
-    pre_back, sigma_back = pre[lo : lo + n_back], sigma[lo : lo + n_back]
-    tilt_second_ref[...] = jnp.where(
-        inside(n_back, rows, first_col - HALO_BACK, total),
-        sigma_back * (1.0 + pre_back * (1.0 - sigma_back)),
-        0.0,
-    )
-    put_patch(patch_last_ref, act, 4, rows, n_slope)
-
-    w_last = w_last_ref[...].reshape(-1, 9 * hidden)
+            for i, (start, size) in enumerate(tiles(taps)):
+                w_last_ref[at, :, start : start + size] = ref[far, i * r_last : (i + 1) * r_last]
+
+    w_last = w_last_ref[...].reshape(-1, taps)
     student_ref[...] = dot(patch_last_ref[...], w_last, ((1,), (1,)))
 
     def slopes(start, count, target, col):
@@ -256,12 +376,13 @@
 
     edge, block = HALO_SLOPE * rows, 4 * rows
     lo, n_own = edge, own * rows
-    slopes(0, edge, before_ref[(HALO_X - HALO_SLOPE) * rows :, :channels], first_col - HALO_SLOPE)
-    slopes(edge + n_own, edge, after_ref[:edge, :channels], first_col + own)
+    before, after = sides(edge_a_ref, edge_b_ref)
+    slopes(0, edge, take_tiles(before, 0, edge, channels), first_col - HALO_SLOPE)
+    slopes(edge + n_own, edge, take_tiles(after, 0, edge, channels), first_col + own)
 
     def step(i, carry):
         at = pl.multiple_of(i * block, block)
-        target = band_ref[pl.ds(at, block), :channels]
+        target = teacher_ref[pl.ds(at, block), :]
         slopes(pl.multiple_of(edge + at, rows), block, target, first_col + i * 4)
         return carry
 
@@ -353,7 +474,7 @@
         input_output_aliases=aliases or {},
         out_shape=[jax.ShapeDtypeStruct(shape, kind) for shape, kind in outs],
         scratch_shapes=[pltpu.VMEM(shape, kind) for shape, kind in scratch] + list(semaphores),
-        compiler_params=pltpu.CompilerParams(vmem_limit_bytes=vmem_mib * MIB),
+        compiler_params=pltpu.CompilerParams(vmem_limit_bytes=int(vmem_mib * MIB)),
         cost_estimate=pl.CostEstimate(flops=flops, bytes_accessed=1_000_000, transcendentals=0),
         name=name,
     )(*inputs)
@@ -375,16 +496,20 @@
             for w in (w_first, w_middle, w_last)
         )
     r_last, r_small = w_last.shape[0], w_first.shape[0]
-    cells, deep = piece * rows, channels + in_depth
+    cells = piece * rows
+    dealt = cells * len(tiles(channels)) + cells
+    packed = r_last * len(tiles(9 * hidden))
+    packed += r_small * (len(tiles(9 * hidden)) + len(tiles(9 * in_depth)))
     hbm = pl.BlockSpec(memory_space=pltpu.HBM)
-    kept, sent, shard = call(
+    own_class, near, across, shard = call(
         deal_kernel,
         "deal",
         (image_feats, teacher, w_first, w_middle, w_last),
         [
-            ((2, cells, deep), bf16),
-            ((2, cells, deep), bf16),
-            ((r_last + 2 * r_small, 9 * hidden), bf16),
+            ((packed + dealt, LANES), bf16),
+            ((dealt, LANES), bf16),
+            ((2 * dealt - cells, LANES), bf16),
+            ((packed, LANES), bf16),
         ],
         [(a.shape, a.dtype) for a in (image_feats, teacher, w_first, w_middle, w_last)]
         + [((2, cells, piece * height), bf16), ((2, 2, cells, height * breadth), bf16)],
@@ -393,69 +518,98 @@
         [pltpu.SemaphoreType.DMA((5,))],
         60,
     )
-    near = swap(sent, 1)
-    pair = jnp.stack([kept[1], near[1]], 0)
+    across = swap(across, 2)
     far = {k: swap(shard, 4 * k * fold) for k in (3, 2, 1)}
-    pair = swap(pair, 2)
-    halo = HALO_X * rows
-    (h,) = call(
+    near = swap(near, 1)
+    anywhere = pl.BlockSpec(memory_space=pl.ANY)
+    held, across = call(
+        hold_kernel,
+        "hold",
+        (own_class, across),
+        [(own_class.shape, bf16), (across.shape, bf16)],
+        [],
+        1_000_000,
+        {1: anywhere},
+        out_spaces={1: anywhere},
+        aliases={1: 1},
+    )
+    diagonal = swap(across, 1)
+    edge_t, edge_x = HALO_SLOPE * rows, HALO_X * rows
+    edge = edge_t * len(tiles(channels)) + edge_x - edge_t
+    part_last = r_last * len(tiles(9 * hidden))
+    held_last, held_small = call(
         stack_kernel,
         "stack",
-        (shard, far[1], far[2], far[3]),
-        [((FAR,) + shard.shape, bf16)],
+        (held, far[1], far[2], far[3]),
+        [((FAR, part_last, LANES), bf16), ((FAR, packed - part_last, LANES), bf16)],
         [],
         STACK_COST,
     )
-    band, low_edge, high_edge, h = call(
-        functools.partial(collect_kernel, halo),
+    x_band, t_band, edge_a, edge_b, held_last, held_small = call(
+        functools.partial(collect_kernel, cells, edge_t, edge_x),
         "collect",
-        (kept, near, pair, h),
-        [
-            ((own * rows, deep), bf16),
-            ((halo, deep), bf16),
-            ((halo, deep), bf16),
-            (h.shape, bf16),
+        (held, near, across, diagonal, held_last, held_small),
+        [
+            ((own * rows, in_depth), bf16),
+            ((own * rows, channels), bf16),
+            ((edge, LANES), bf16),
+            ((edge, LANES), bf16),
+            (held_last.shape, bf16),
+            (held_small.shape, bf16),
         ],
         [],
         1_000_000,
-        {3: pl.BlockSpec(memory_space=pl.ANY)},
-        out_spaces={3: pl.BlockSpec(memory_space=pl.ANY)},
-        aliases={3: 3},
-    )
-    hy = swap(h, 2 * fold)
-    hc = swap(h, fold)
-    before = shift(high_edge, 4)
-    after = shift(low_edge, -4)
-    hyc = swap(hy, fold)
+        {4: anywhere, 5: anywhere},
+        out_spaces={4: anywhere, 5: anywhere},
+        aliases={4: 4, 5: 5},
+    )
+
+    small_y = swap(held_small, 2 * fold)
+    last_y = swap(held_last, 2 * fold)
+    all_small = held_small, small_y, swap(held_small, fold), swap(small_y, fold)
+    edge_a, edge_b = bands_beside(edge_a, edge_b)
 
     n_first, n_second, n_slope, n_back = (
         (own + 2 * halo) * rows for halo in (HALO_FIRST, HALO_SECOND, HALO_SLOPE, HALO_BACK)
     )
-    (patch_first,) = call(
-        functools.partial(early_kernel, rows, channels, own + 2 * HALO_FIRST),
+    tilt_first, tilt_second, patch_first, patch_middle, patch_last, all_middle = call(
+        functools.partial(early_kernel, own, rows, total, channels, edge_t),
         "early",
-        (before, band, after),
-        [((n_first, 9 * in_depth), bf16)],
+        (x_band, edge_a, edge_b, *all_small),
+        [
+            ((own * rows, hidden), f32),
+            ((n_back, hidden), f32),
+            ((n_first, 9 * in_depth), bf16),
+            ((n_second, 9 * hidden), bf16),
+            ((n_slope, 9 * hidden), bf16),
+            ((hidden, 9 * hidden), bf16),
+        ],
+        [((BLOCKS, 2 * r_small, 9 * hidden), f32)],
+        EARLY_COST,
+    )
+    (last_y,) = call(
+        after_kernel,
+        "after",
+        (last_y, patch_last),
+        [(last_y.shape, bf16)],
         [],
-        6_000_000_000,
-    )
-    keep, send, slope, tilt_first, tilt_second, patch_middle, all_middle, all_last = call(
+        1_000_000,
+        {0: anywhere, 1: anywhere},
+        out_spaces={0: anywhere},
+        aliases={0: 0},
+    )
+    all_last = held_last, last_y, swap(held_last, fold), swap(last_y, fold)
+    keep, send, slope, all_last = call(
         functools.partial(front_kernel, own, rows, total),
         "front",
-        (before, band, after, patch_first, h, hy, hc, hyc),
+        (t_band, edge_a, edge_b, patch_last, *all_last),
         [
             ((2, FAR, r_last, 9 * hidden), f32),
             ((2, FAR, r_last, 9 * hidden), bf16),
             ((n_slope, channels), bf16),
-            ((own * rows, hidden), f32),
-            ((n_back, hidden), f32),
-            ((n_second, 9 * hidden), bf16),
-            ((hidden, 9 * hidden), bf16),
             ((BLOCKS, r_last, 9 * hidden), bf16),
         ],
         [
-            ((BLOCKS, 2 * r_small, 9 * hidden), f32),
-            ((n_slope, 9 * hidden), bf16),
             ((n_slope, channels), f32),
             ((BLOCKS, r_last, 9 * hidden), f32),
         ],

time: 62.6 us -> 58.9 us (0.941)
  waiting for transfers between devices: 23.4 us -> 21 us
  starting transfers between devices: 24.5 us -> 23.5 us
    ppermute x2 -> x1, starting transfers between devices: 4.68 us -> 0.66 us  [bands_beside(): lax.ppermute(high_pairs, 'cols', pairs + [(j, i) for i, j in pairs])]
    ppermute x18 -> x23, starting transfers between devices: 19.8 us -> 22.9 us  [swap(): return lax.ppermute(array, 'cols', [(i, i ^ mask) for i in range(size)])]
    ppermute x2 -> x1, waiting for transfers between devices: 2.58 us -> 0.01 us  [bands_beside(): lax.ppermute(high_pairs, 'cols', pairs + [(j, i) for i, j in pairs])]
    slice x2 -> x0, local copies, waits for them, and re-layouts: 0.95 us -> none  [on_device(): pair = jnp.stack([kept[1], near[1]], 0)]
    unnamed x4 -> x2, local copies, waits for them, and re-layouts: 0.01 us -> 0.95 us
    ppermute x18 -> x23, waiting for transfers between devices: 20.8 us -> 21 us  [swap(): return lax.ppermute(array, 'cols', [(i, i ^ mask) for i in range(size)])]
    pallas_call x11 -> x13, Pallas kernels: 12.4 us -> 12.4 us  [call(): pl.pallas_call(kernel, in_specs=[spaces.get(i, vmem) for i in range(len(i...]
  transfers between devices with their start and end apart: 20 -> 24, of which waited for: 11 -> 12; matrix products, arithmetic and copies ran while one was open for 2% -> 0% of each run, Pallas kernels for 5% -> 8%
where the time goes in v4:
time: 58.9 us; the launch traced here: 58.7 us
  starting transfers between devices  23.5 us (40%)
  waiting for transfers between devices  21 us (36%)
  Pallas kernels  12.4 us (21%)
  local copies, waits for them, and re-layouts  0.95 us (2%)
  between operations  0.76 us (1%)
    ppermute x23, starting transfers between devices, swap(): return lax.ppermute(array, 'cols', [(i, i ^ mask) for i in range(size)])  22.9 us
    ppermute x23, waiting for transfers between devices, swap(): return lax.ppermute(array, 'cols', [(i, i ^ mask) for i in range(size)])  21 us
    pallas_call x13, Pallas kernels, call(): pl.pallas_call(kernel, in_specs=[spaces.get(i, vmem) for i in range(len(i...  12.4 us
  transfers between devices with their start and end apart: 24, of which 12 were waited for; matrix products, arithmetic and copies ran while one was open for 0% of the time, Pallas kernels for 8%

profile of v4, /device:TPU:0, one launch (start us, length us, event | category | flops | bytes accessed | tf_op | source)
XLA Modules:
  0.0 58.7 jit_solution(5330836610858811726)
XLA Ops:
  0.6 2.4 %deal.1 = (bf16[1040,128]{1,0:T(8,128)(2,1)}, bf16[640,128]{1,0:T(8,128)(2,1)}, bf16[1152,128]{1,0:T(8,128)(2,1)}, bf16[400,128]{1,0:T(8,128)(2,1)}) custom-call(bf16[32,1024]{1,0:T(8,128)(2,1)} %x_hbm.1, bf16[32,16,512]{2,1,0:T(8,128)(2,1)} %teacher_hbm.1, bf16[8,576]{1,0:T(8,128)(2,1)} %w_first_hbm.1, bf16[8,1152]{1,0:T(8,128)(2,1)} %w_middle_hbm.1, ...), custom_call_target="tpu_custom_call" | custom-call | flops 600000000 | bytes 1000000 | tf_op jit(solution)/shard_map/deal/pallas_call | solution.py:470
  3.0 3.0 %collective-permute-start = (bf16[1152,128]{1,0:T(8,128)(2,1)}, bf16[1152,128]{1,0:T(8,128)(2,1)S(1)}, u32[]{:S(2)}, u32[]{:S(2)}) collective-permute-start(bf16[1152,128]{1,0:T(8,128)(2,1)} %get-tuple-element.42), channel_id=1, source_target_pairs={{0,2},{1,3},{2,0},{3,1},{4,6},{5,7},{6,4},{7,5},{8,10},{9,11},{10,... | collective-permute-start | bytes 884744 | tf_op jit(solution)/shard_map/ppermute | solution.py:22
  6.1 3.6 %collective-permute-start.5 = (bf16[400,128]{1,0:T(8,128)(2,1)}, bf16[400,128]{1,0:T(8,128)(2,1)S(1)}, u32[]{:S(2)}, u32[]{:S(2)}) collective-permute-start(bf16[400,128]{1,0:T(8,128)(2,1)} %get-tuple-element.46), channel_id=1, source_target_pairs={{0,12},{1,13},{2,14},{3,15},{4,8},{5,9},{6,10},{7,11},{8,4},{9,5},... | collective-permute-start | bytes 307208 | tf_op jit(solution)/shard_map/ppermute | solution.py:22
  9.7 0.8 %collective-permute-start.3 = (bf16[400,128]{1,0:T(8,128)(2,1)}, bf16[400,128]{1,0:T(8,128)(2,1)S(1)}, u32[]{:S(2)}, u32[]{:S(2)}) collective-permute-start(bf16[400,128]{1,0:T(8,128)(2,1)} %get-tuple-element.46), channel_id=1, source_target_pairs={{0,4},{1,5},{2,6},{3,7},{4,0},{5,1},{6,2},{7,3},{8,12},{9,13},{10,... | collective-permute-start | bytes 307208 | tf_op jit(solution)/shard_map/ppermute | solution.py:22
  10.5 2.8 %collective-permute-done.across_ref = bf16[1152,128]{1,0:T(8,128)(2,1)S(1)} collective-permute-done((bf16[1152,128]{1,0:T(8,128)(2,1)}, bf16[1152,128]{1,0:T(8,128)(2,1)S(1)}, u32[]{:S(2)}, u32[]{:S(2)}) %collective-permute-start) | collective-permute-done | bytes 294944 | tf_op jit(solution)/shard_map/ppermute | solution.py:22
  13.3 0.9 %copy-done = bf16[1040,128]{1,0:T(8,128)(2,1)S(1)} copy-done((bf16[1040,128]{1,0:T(8,128)(2,1)S(1)}, bf16[1040,128]{1,0:T(8,128)(2,1)}, u32[]{:S(2)}) %copy-start) | copy-done | bytes 266264
  14.3 0.5 collective-permute-start.1
  14.8 3.4 %collective-permute-done.4.far2_ref = bf16[400,128]{1,0:T(8,128)(2,1)S(1)} collective-permute-done((bf16[400,128]{1,0:T(8,128)(2,1)}, bf16[400,128]{1,0:T(8,128)(2,1)S(1)}, u32[]{:S(2)}, u32[]{:S(2)}) %collective-permute-start.4) | collective-permute-done | bytes 102432 | tf_op jit(solution)/shard_map/ppermute | solution.py:22
  18.5 0.6 collective-permute-start.8
  19.1 1.5 %collective-permute-start.11 = (bf16[4,288,128]{2,1,0:T(8,128)(2,1)S(1)}, bf16[4,288,128]{2,1,0:T(8,128)(2,1)S(1)}, u32[]{:S(2)}, u32[]{:S(2)}) collective-permute-start(bf16[4,288,128]{2,1,0:T(8,128)(2,1)S(1)} %get-tuple-element.55.h_ref), channel_id=1, source_target_pairs={{0,2},{1,3},{2,0},{3,1},{4,6},{5,7},{6,4},{7,5},{8,10},{9,11},{10,... | collective-permute-start | bytes 884744 | tf_op jit(solution)/shard_map/ppermute | solution.py:22
  21.0 0.7 %collective-permute-start.7 = (bf16[496,128]{1,0:T(8,128)(2,1)S(1)}, bf16[496,128]{1,0:T(8,128)(2,1)S(1)}, u32[]{:S(2)}, u32[]{:S(2)}) collective-permute-start(bf16[496,128]{1,0:T(8,128)(2,1)S(1)} %get-tuple-element.51), channel_id=1, source_target_pairs={{4,8},{5,9},{6,10},{7,11},{8,4},{9,5},{10,6},{11,7},{20,24},{21,25... | collective-permute-start | bytes 380936 | tf_op jit(solution)/shard_map/ppermute | solution.py:28
  21.8 2.9 %collective-permute-done.8.hy_ref = bf16[4,112,128]{2,1,0:T(8,128)(2,1)S(1)} collective-permute-done((bf16[4,112,128]{2,1,0:T(8,128)(2,1)S(1)}, bf16[4,112,128]{2,1,0:T(8,128)(2,1)S(1)}, u32[]{:S(2)}, u32[]{:S(2)}) %collective-permute-start.8) | collective-permute-done | bytes 114720 | tf_op jit(solution)/shard_map/ppermute | solution.py:22
  24.7 0.5 collective-permute-start.12
  26.0 2.2 %early.1 = (f32[512,128]{1,0:T(8,128)S(1)}, f32[576,128]{1,0:T(8,128)S(1)}, bf16[896,576]{1,0:T(8,128)(2,1)S(1)}, bf16[832,1152]{1,0:T(8,128)(2,1)S(1)}, bf16[70...) custom-call(bf16[512,64]{1,0:T(8,128)(2,1)S(1)} %get-tuple-element.52.x_ref, ...), custom_call_target="tpu_custom_call" | custom-call | flops 1500000000 | bytes 1000000 | tf_op jit(solution)/shard_map/early/pallas_call | solution.py:470
  28.2 0.9 %collective-permute-done.11.value_ref = bf16[4,288,128]{2,1,0:T(8,128)(2,1)S(1)} collective-permute-done((bf16[4,288,128]{2,1,0:T(8,128)(2,1)S(1)}, bf16[4,288,128]{2,1,0:T(8,128)(2,1)S(1)}, u32[]{:S(2)}, u32[]{:S(2)}) %collective-permute-start.11) | collective-permute-done | bytes 294944 | tf_op jit(solution)/shard_map/ppermute | solution.py:22
  29.1 1.6 %collective-permute-done.13.hyc_ref = bf16[4,288,128]{2,1,0:T(8,128)(2,1)S(1)} collective-permute-done((bf16[4,288,128]{2,1,0:T(8,128)(2,1)S(1)}, bf16[4,288,128]{2,1,0:T(8,128)(2,1)S(1)}, u32[]{:S(2)}, u32[]{:S(2)}) %collective-permute-start.13) | collective-permute-done | bytes 294944 | tf_op jit(solution)/shard_map/ppermute | solution.py:22
  30.6 4.4 %front.1 = (f32[2,4,32,1152]{3,2,1,0:T(8,128)S(1)}, bf16[2,4,32,1152]{3,2,1,0:T(8,128)(2,1)S(1)}, bf16[704,512]{1,0:T(8,128)(2,1)S(1)}, bf16[16,32,1152]{2,1,0:T(8,128)(2,1)S(1)}) custom-call(bf16[512,512]{1,0:T(8,128)(2,1)S(1)} %get-tuple-element.49.teacher_ref, bf16[496,128]{1,0:T(8,128)(2,1)S(1)} %collective-permute-done.6.edge_a_ref, ...), custom_call_target="tpu_custom_call" | custom-call | flops 6000000000 | bytes 1000000 | tf_op jit(solution)/shard_map/front/pallas_call | solution.py:470
  35.2 1.9 %collective-permute-done.14.got_ref = bf16[2,4,32,1152]{3,2,1,0:T(8,128)(2,1)S(1)} collective-permute-done((bf16[2,4,32,1152]{3,2,1,0:T(8,128)(2,1)S(1)}, bf16[2,4,32,1152]{3,2,1,0:T(8,128)(2,1)S(1)}, u32[]{:S(2)}, u32[]{:S(2)}) %collective-permute-start.14) | collective-permute-done | bytes 589856 | tf_op jit(solution)/shard_map/ppermute | solution.py:22
  37.3 0.9 %collective-permute-start.15 = (bf16[4,32,1152]{2,1,0:T(8,128)(2,1)S(1)}, bf16[4,32,1152]{2,1,0:T(8,128)(2,1)S(1)}, u32[]{:S(2)}, u32[]{:S(2)}) collective-permute-start(bf16[4,32,1152]{2,1,0:T(8,128)(2,1)S(1)} %get-tuple-element.59), channel_id=1, source_target_pairs={{0,2},{1,3},{2,0},{3,1},{4,6},{5,7},{6,4},{7,5},{8,10},{9,11},{10,... | collective-permute-start | bytes 884744 | tf_op jit(solution)/shard_map/ppermute | solution.py:22
  38.2 2.2 %back.1 = (f32[4,2,8,1728]{3,2,1,0:T(8,128)S(1)}, bf16[4,2,8,1728]{3,2,1,0:T(8,128)(2,1)S(1)}) custom-call(bf16[704,512]{1,0:T(8,128)(2,1)S(1)} %get-tuple-element.64.slope_ref, f32[576,128]{1,0:T(8,128)S(1)} %get-tuple-element.65.tilt_second_ref, bf16[16,32,1152]{2,1,0:T(8,128)(2,1)S(1)} %get-tuple-element.66.w_last_ref, ...), custom_call_target="tpu_custom_call" | custom-call | flops 4000000000 | bytes 1000000 | tf_op jit(solution)/shard_map/back/pallas_call | solution.py:470
  40.4 1.5 %collective-permute-done.19.got_ref = bf16[4,2,8,1728]{3,2,1,0:T(8,128)(2,1)S(1)} collective-permute-done((bf16[4,2,8,1728]{3,2,1,0:T(8,128)(2,1)S(1)}, bf16[4,2,8,1728]{3,2,1,0:T(8,128)(2,1)S(1)}, u32[]{:S(2)}, u32[]{:S(2)}) %collective-permute-start.19) | collective-permute-done | bytes 221216 | tf_op jit(solution)/shard_map/ppermute | solution.py:22
  42.0 2.4 %collective-permute-start.20 = (bf16[2,8,1728]{2,1,0:T(8,128)(2,1)S(1)}, bf16[2,8,1728]{2,1,0:T(8,128)(2,1)S(1)}, u32[]{:S(2)}, u32[]{:S(2)}) collective-permute-start(bf16[2,8,1728]{2,1,0:T(8,128)(2,1)S(1)} %get-tuple-element.74), channel_id=1, source_target_pairs={{0,4},{1,5},{2,6},{3,7},{4,0},{5,1},{6,2},{7,3},{8,12},{9,13},{10,... | collective-permute-start | bytes 165896 | tf_op jit(solution)/shard_map/ppermute | solution.py:22
  44.4 1.8 %collective-permute-start.21 = (bf16[2,8,1728]{2,1,0:T(8,128)(2,1)S(1)}, bf16[2,8,1728]{2,1,0:T(8,128)(2,1)S(1)}, u32[]{:S(2)}, u32[]{:S(2)}) collective-permute-start(bf16[2,8,1728]{2,1,0:T(8,128)(2,1)S(1)} %get-tuple-element.75), channel_id=1, source_target_pairs={{0,8},{1,9},{2,10},{3,11},{4,12},{5,13},{6,14},{7,15},{8,0},{9,1},... | collective-permute-start | bytes 165896 | tf_op jit(solution)/shard_map/ppermute | solution.py:22
  46.2 1.1 %collective-permute-start.22 = (bf16[2,8,1728]{2,1,0:T(8,128)(2,1)S(1)}, bf16[2,8,1728]{2,1,0:T(8,128)(2,1)S(1)}, u32[]{:S(2)}, u32[]{:S(2)}) collective-permute-start(bf16[2,8,1728]{2,1,0:T(8,128)(2,1)S(1)} %get-tuple-element.76), channel_id=1, source_target_pairs={{0,12},{1,13},{2,14},{3,15},{4,8},{5,9},{6,10},{7,11},{8,4},{9,5},... | collective-permute-start | bytes 165896 | tf_op jit(solution)/shard_map/ppermute | solution.py:22
  47.4 1.8 %collective-permute-start.16 = (bf16[32,1152]{1,0:T(8,128)(2,1)S(1)}, bf16[32,1152]{1,0:T(8,128)(2,1)S(1)}, u32[]{:S(2)}, u32[]{:S(2)}) collective-permute-start(bf16[32,1152]{1,0:T(8,128)(2,1)S(1)} %get-tuple-element.61), channel_id=1, source_target_pairs={{0,4},{1,5},{2,6},{3,7},{4,0},{5,1},{6,2},{7,3},{8,12},{9,13},{10,... | collective-permute-start | bytes 221192 | tf_op jit(solution)/shard_map/ppermute | solution.py:22
  49.2 1.5 %collective-permute-start.17 = (bf16[32,1152]{1,0:T(8,128)(2,1)S(1)}, bf16[32,1152]{1,0:T(8,128)(2,1)S(1)}, u32[]{:S(2)}, u32[]{:S(2)}) collective-permute-start(bf16[32,1152]{1,0:T(8,128)(2,1)S(1)} %get-tuple-element.62), channel_id=1, source_target_pairs={{0,8},{1,9},{2,10},{3,11},{4,12},{5,13},{6,14},{7,15},{8,0},{9,1},... | collective-permute-start | bytes 221192 | tf_op jit(solution)/shard_map/ppermute | solution.py:22
  50.7 1.1 %collective-permute-start.18 = (bf16[32,1152]{1,0:T(8,128)(2,1)S(1)}, bf16[32,1152]{1,0:T(8,128)(2,1)S(1)}, u32[]{:S(2)}, u32[]{:S(2)}) collective-permute-start(bf16[32,1152]{1,0:T(8,128)(2,1)S(1)} %get-tuple-element.63), channel_id=1, source_target_pairs={{0,12},{1,13},{2,14},{3,15},{4,8},{5,9},{6,10},{7,11},{8,4},{9,5},... | collective-permute-start | bytes 221192 | tf_op jit(solution)/shard_map/ppermute | solution.py:22
  51.8 1.0 %collective-permute-done.22.got3_ref = bf16[2,8,1728]{2,1,0:T(8,128)(2,1)S(1)} collective-permute-done((bf16[2,8,1728]{2,1,0:T(8,128)(2,1)S(1)}, bf16[2,8,1728]{2,1,0:T(8,128)(2,1)S(1)}, u32[]{:S(2)}, u32[]{:S(2)}) %collective-permute-start.22) | collective-permute-done | bytes 55328 | tf_op jit(solution)/shard_map/ppermute | solution.py:22
  52.8 0.8 %collective-permute-start.23 = (bf16[8,1728]{1,0:T(8,128)(2,1)S(1)}, bf16[8,1728]{1,0:T(8,128)(2,1)S(1)}, u32[]{:S(2)}, u32[]{:S(2)}) collective-permute-start(bf16[8,1728]{1,0:T(8,128)(2,1)S(1)} %get-tuple-element.78), channel_id=1, source_target_pairs={{0,2},{1,3},{2,0},{3,1},{4,6},{5,7},{6,4},{7,5},{8,10},{9,11},{10,... | collective-permute-start | bytes 82952 | tf_op jit(solution)/shard_map/ppermute | solution.py:22
  53.6 3.1 %collective-permute-done.23.got_ref = bf16[8,1728]{1,0:T(8,128)(2,1)S(1)} collective-permute-done((bf16[8,1728]{1,0:T(8,128)(2,1)S(1)}, bf16[8,1728]{1,0:T(8,128)(2,1)S(1)}, u32[]{:S(2)}, u32[]{:S(2)}) %collective-permute-start.23) | collective-permute-done | bytes 27680 | tf_op jit(solution)/shard_map/ppermute | solution.py:22
  56.8 1.2 %collective-permute-done.17.got2_ref = bf16[32,1152]{1,0:T(8,128)(2,1)S(1)} collective-permute-done((bf16[32,1152]{1,0:T(8,128)(2,1)S(1)}, bf16[32,1152]{1,0:T(8,128)(2,1)S(1)}, u32[]{:S(2)}, u32[]{:S(2)}) %collective-permute-start.17) | collective-permute-done | bytes 73760 | tf_op jit(solution)/shard_map/ppermute | solution.py:22
  58.0 0.7 %finish.1 = (f32[8,576]{1,0:T(8,128)}, f32[8,1152]{1,0:T(8,128)}, f32[32,1152]{1,0:T(8,128)}) custom-call(f32[32,1152]{1,0:T(8,128)S(1)} %get-tuple-element.60.last_ref, bf16[32,1152]{1,0:T(8,128)(2,1)S(1)} %collective-permute-done.16.got1_ref, bf16[32,1152]{1,0:T(8,128)(2,1)S(1)} %collective-permute-done.17.got2_ref, ...), custom_call_target="tpu_custom_call" | custom-call | flops 1000000 | bytes 1000000 | tf_op jit(solution)/shard_map/finish/pallas_call | solution.py:470
  (31 shorter events, 2.2 us)
Async XLA Ops:
  3.0 10.3 %collective-permute-start = (bf16[1152,128]{1,0:T(8,128)(2,1)}, bf16[1152,128]{1,0:T(8,128)(2,1)S(1)}, u32[]{:S(2)}, u32[]{:S(2)}) collective-permute-start(bf16[1152,128]{1,0:T(8,128)(2,1)} %get-tuple-element.42), channel_id=1, source_target_pairs={{0,2},{1,3},{2,0},{3,1},{4,6},{5,7},{6,4},{7,5},{8,10},{9,11},{10,... | collective-permute-start | bytes 884744 | tf_op jit(solution)/shard_map/ppermute | solution.py:22
  6.1 8.8 %collective-permute-start.5 = (bf16[400,128]{1,0:T(8,128)(2,1)}, bf16[400,128]{1,0:T(8,128)(2,1)S(1)}, u32[]{:S(2)}, u32[]{:S(2)}) collective-permute-start(bf16[400,128]{1,0:T(8,128)(2,1)} %get-tuple-element.46), channel_id=1, source_target_pairs={{0,12},{1,13},{2,14},{3,15},{4,8},{5,9},{6,10},{7,11},{8,4},{9,5},... | collective-permute-start | bytes 307208 | tf_op jit(solution)/shard_map/ppermute | solution.py:22
  9.7 8.5 %collective-permute-start.4 = (bf16[400,128]{1,0:T(8,128)(2,1)}, bf16[400,128]{1,0:T(8,128)(2,1)S(1)}, u32[]{:S(2)}, u32[]{:S(2)}) collective-permute-start(bf16[400,128]{1,0:T(8,128)(2,1)} %get-tuple-element.46), channel_id=1, source_target_pairs={{0,8},{1,9},{2,10},{3,11},{4,12},{5,13},{6,14},{7,15},{8,0},{9,1},... | collective-permute-start | bytes 307208 | tf_op jit(solution)/shard_map/ppermute | solution.py:22
  9.7 8.5 %collective-permute-start.3 = (bf16[400,128]{1,0:T(8,128)(2,1)}, bf16[400,128]{1,0:T(8,128)(2,1)S(1)}, u32[]{:S(2)}, u32[]{:S(2)}) collective-permute-start(bf16[400,128]{1,0:T(8,128)(2,1)} %get-tuple-element.46), channel_id=1, source_target_pairs={{0,4},{1,5},{2,6},{3,7},{4,0},{5,1},{6,2},{7,3},{8,12},{9,13},{10,... | collective-permute-start | bytes 307208 | tf_op jit(solution)/shard_map/ppermute | solution.py:22
  13.3 1.0 %copy-start = (bf16[1040,128]{1,0:T(8,128)(2,1)S(1)}, bf16[1040,128]{1,0:T(8,128)(2,1)}, u32[]{:S(2)}) copy-start(bf16[1040,128]{1,0:T(8,128)(2,1)} %get-tuple-element.41.own_ref) | copy-start | bytes 798724
  14.3 4.0 %collective-permute-start.2 = (bf16[1152,128]{1,0:T(8,128)(2,1)S(1)}, bf16[1152,128]{1,0:T(8,128)(2,1)S(1)}, u32[]{:S(2)}, u32[]{:S(2)}) collective-permute-start(bf16[1152,128]{1,0:T(8,128)(2,1)S(1)} %get-tuple-element.45.across_ref), channel_id=1, source_target_pairs={{0,1},{1,0},{2,3},{3,2},{4,5},{5,4},{6,7},{7,6},{8,9},{9,8},{10,11... | collective-permute-start | bytes 884744 | tf_op jit(solution)/shard_map/ppermute | solution.py:22
  14.3 3.9 %collective-permute-start.1 = (bf16[640,128]{1,0:T(8,128)(2,1)}, bf16[640,128]{1,0:T(8,128)(2,1)S(1)}, u32[]{:S(2)}, u32[]{:S(2)}) collective-permute-start(bf16[640,128]{1,0:T(8,128)(2,1)} %get-tuple-element.44), channel_id=1, source_target_pairs={{0,1},{1,0},{2,3},{3,2},{4,5},{5,4},{6,7},{7,6},{8,9},{9,8},{10,11... | collective-permute-start | bytes 491528 | tf_op jit(solution)/shard_map/ppermute | solution.py:22
  18.5 6.1 %collective-permute-start.8 = (bf16[4,112,128]{2,1,0:T(8,128)(2,1)S(1)}, bf16[4,112,128]{2,1,0:T(8,128)(2,1)S(1)}, u32[]{:S(2)}, u32[]{:S(2)}) collective-permute-start(bf16[4,112,128]{2,1,0:T(8,128)(2,1)S(1)} %get-tuple-element.53.h_ref), channel_id=1, source_target_pairs={{0,2},{1,3},{2,0},{3,1},{4,6},{5,7},{6,4},{7,5},{8,10},{9,11},{10,... | collective-permute-start | bytes 344072 | tf_op jit(solution)/shard_map/ppermute | solution.py:22
  19.1 10.0 %collective-permute-start.11 = (bf16[4,288,128]{2,1,0:T(8,128)(2,1)S(1)}, bf16[4,288,128]{2,1,0:T(8,128)(2,1)S(1)}, u32[]{:S(2)}, u32[]{:S(2)}) collective-permute-start(bf16[4,288,128]{2,1,0:T(8,128)(2,1)S(1)} %get-tuple-element.55.h_ref), channel_id=1, source_target_pairs={{0,2},{1,3},{2,0},{3,1},{4,6},{5,7},{6,4},{7,5},{8,10},{9,11},{10,... | collective-permute-start | bytes 884744 | tf_op jit(solution)/shard_map/ppermute | solution.py:22
  20.6 4.9 %collective-permute-start.6 = (bf16[496,128]{1,0:T(8,128)(2,1)S(1)}, bf16[496,128]{1,0:T(8,128)(2,1)S(1)}, u32[]{:S(2)}, u32[]{:S(2)}) collective-permute-start(bf16[496,128]{1,0:T(8,128)(2,1)S(1)} %get-tuple-element.50), channel_id=1, source_target_pairs={{0,4},{1,5},{2,6},{3,7},{4,0},{5,1},{6,2},{7,3},{8,12},{9,13},{10,... | collective-permute-start | bytes 380936 | tf_op jit(solution)/shard_map/ppermute | solution.py:22
  21.0 4.5 %collective-permute-start.7 = (bf16[496,128]{1,0:T(8,128)(2,1)S(1)}, bf16[496,128]{1,0:T(8,128)(2,1)S(1)}, u32[]{:S(2)}, u32[]{:S(2)}) collective-permute-start(bf16[496,128]{1,0:T(8,128)(2,1)S(1)} %get-tuple-element.51), channel_id=1, source_target_pairs={{4,8},{5,9},{6,10},{7,11},{8,4},{9,5},{10,6},{11,7},{20,24},{21,25... | collective-permute-start | bytes 380936 | tf_op jit(solution)/shard_map/ppermute | solution.py:28
  21.7 3.0 %collective-permute-start.9 = (bf16[4,112,128]{2,1,0:T(8,128)(2,1)S(1)}, bf16[4,112,128]{2,1,0:T(8,128)(2,1)S(1)}, u32[]{:S(2)}, u32[]{:S(2)}) collective-permute-start(bf16[4,112,128]{2,1,0:T(8,128)(2,1)S(1)} %get-tuple-element.53.h_ref), channel_id=1, source_target_pairs={{0,1},{1,0},{2,3},{3,2},{4,5},{5,4},{6,7},{7,6},{8,9},{9,8},{10,11... | collective-permute-start | bytes 344072 | tf_op jit(solution)/shard_map/ppermute | solution.py:22
  24.7 1.3 %collective-permute-start.10 = (bf16[4,112,128]{2,1,0:T(8,128)(2,1)S(1)}, bf16[4,112,128]{2,1,0:T(8,128)(2,1)S(1)}, u32[]{:S(2)}, u32[]{:S(2)}) collective-permute-start(bf16[4,112,128]{2,1,0:T(8,128)(2,1)S(1)} %collective-permute-done.8.hy_ref), channel_id=1, source_target_pairs={{0,1},{1,0},{2,3},{3,2},{4,5},{5,4},{6,7},{7,6},{8,9},{9,8},{10,11... | collective-permute-start | bytes 344072 | tf_op jit(solution)/shard_map/ppermute | solution.py:22
  24.7 4.4 %collective-permute-start.12 = (bf16[4,288,128]{2,1,0:T(8,128)(2,1)S(1)}, bf16[4,288,128]{2,1,0:T(8,128)(2,1)S(1)}, u32[]{:S(2)}, u32[]{:S(2)}) collective-permute-start(bf16[4,288,128]{2,1,0:T(8,128)(2,1)S(1)} %get-tuple-element.55.h_ref), channel_id=1, source_target_pairs={{0,1},{1,0},{2,3},{3,2},{4,5},{5,4},{6,7},{7,6},{8,9},{9,8},{10,11... | collective-permute-start | bytes 884744 | tf_op jit(solution)/shard_map/ppermute | solution.py:22
  29.1 1.6 %collective-permute-start.13 = (bf16[4,288,128]{2,1,0:T(8,128)(2,1)S(1)}, bf16[4,288,128]{2,1,0:T(8,128)(2,1)S(1)}, u32[]{:S(2)}, u32[]{:S(2)}) collective-permute-start(bf16[4,288,128]{2,1,0:T(8,128)(2,1)S(1)} %after.1.hy_ref), channel_id=1, source_target_pairs={{0,1},{1,0},{2,3},{3,2},{4,5},{5,4},{6,7},{7,6},{8,9},{9,8},{10,11... | collective-permute-start | bytes 884744 | tf_op jit(solution)/shard_map/ppermute | solution.py:22
  35.0 2.1 %collective-permute-start.14 = (bf16[2,4,32,1152]{3,2,1,0:T(8,128)(2,1)S(1)}, bf16[2,4,32,1152]{3,2,1,0:T(8,128)(2,1)S(1)}, u32[]{:S(2)}, u32[]{:S(2)}) collective-permute-start(bf16[2,4,32,1152]{3,2,1,0:T(8,128)(2,1)S(1)} %get-tuple-element.57), channel_id=1, source_target_pairs={{0,1},{1,0},{2,3},{3,2},{4,5},{5,4},{6,7},{7,6},{8,9},{9,8},{10,11... | collective-permute-start | bytes 1769480 | tf_op jit(solution)/shard_map/ppermute | solution.py:22
  37.3 10.0 %collective-permute-start.15 = (bf16[4,32,1152]{2,1,0:T(8,128)(2,1)S(1)}, bf16[4,32,1152]{2,1,0:T(8,128)(2,1)S(1)}, u32[]{:S(2)}, u32[]{:S(2)}) collective-permute-start(bf16[4,32,1152]{2,1,0:T(8,128)(2,1)S(1)} %get-tuple-element.59), channel_id=1, source_target_pairs={{0,2},{1,3},{2,0},{3,1},{4,6},{5,7},{6,4},{7,5},{8,10},{9,11},{10,... | collective-permute-start | bytes 884744 | tf_op jit(solution)/shard_map/ppermute | solution.py:22
  40.4 1.6 %collective-permute-start.19 = (bf16[4,2,8,1728]{3,2,1,0:T(8,128)(2,1)S(1)}, bf16[4,2,8,1728]{3,2,1,0:T(8,128)(2,1)S(1)}, u32[]{:S(2)}, u32[]{:S(2)}) collective-permute-start(bf16[4,2,8,1728]{3,2,1,0:T(8,128)(2,1)S(1)} %get-tuple-element.72), channel_id=1, source_target_pairs={{0,1},{1,0},{2,3},{3,2},{4,5},{5,4},{6,7},{7,6},{8,9},{9,8},{10,11... | collective-permute-start | bytes 663560 | tf_op jit(solution)/shard_map/ppermute | solution.py:22
  42.0 8.7 %collective-permute-start.20 = (bf16[2,8,1728]{2,1,0:T(8,128)(2,1)S(1)}, bf16[2,8,1728]{2,1,0:T(8,128)(2,1)S(1)}, u32[]{:S(2)}, u32[]{:S(2)}) collective-permute-start(bf16[2,8,1728]{2,1,0:T(8,128)(2,1)S(1)} %get-tuple-element.74), channel_id=1, source_target_pairs={{0,4},{1,5},{2,6},{3,7},{4,0},{5,1},{6,2},{7,3},{8,12},{9,13},{10,... | collective-permute-start | bytes 165896 | tf_op jit(solution)/shard_map/ppermute | solution.py:22
  44.4 7.4 %collective-permute-start.21 = (bf16[2,8,1728]{2,1,0:T(8,128)(2,1)S(1)}, bf16[2,8,1728]{2,1,0:T(8,128)(2,1)S(1)}, u32[]{:S(2)}, u32[]{:S(2)}) collective-permute-start(bf16[2,8,1728]{2,1,0:T(8,128)(2,1)S(1)} %get-tuple-element.75), channel_id=1, source_target_pairs={{0,8},{1,9},{2,10},{3,11},{4,12},{5,13},{6,14},{7,15},{8,0},{9,1},... | collective-permute-start | bytes 165896 | tf_op jit(solution)/shard_map/ppermute | solution.py:22
  46.2 6.6 %collective-permute-start.22 = (bf16[2,8,1728]{2,1,0:T(8,128)(2,1)S(1)}, bf16[2,8,1728]{2,1,0:T(8,128)(2,1)S(1)}, u32[]{:S(2)}, u32[]{:S(2)}) collective-permute-start(bf16[2,8,1728]{2,1,0:T(8,128)(2,1)S(1)} %get-tuple-element.76), channel_id=1, source_target_pairs={{0,12},{1,13},{2,14},{3,15},{4,8},{5,9},{6,10},{7,11},{8,4},{9,5},... | collective-permute-start | bytes 165896 | tf_op jit(solution)/shard_map/ppermute | solution.py:22
  47.4 9.4 %collective-permute-start.16 = (bf16[32,1152]{1,0:T(8,128)(2,1)S(1)}, bf16[32,1152]{1,0:T(8,128)(2,1)S(1)}, u32[]{:S(2)}, u32[]{:S(2)}) collective-permute-start(bf16[32,1152]{1,0:T(8,128)(2,1)S(1)} %get-tuple-element.61), channel_id=1, source_target_pairs={{0,4},{1,5},{2,6},{3,7},{4,0},{5,1},{6,2},{7,3},{8,12},{9,13},{10,... | collective-permute-start | bytes 221192 | tf_op jit(solution)/shard_map/ppermute | solution.py:22
  49.2 8.8 %collective-permute-start.17 = (bf16[32,1152]{1,0:T(8,128)(2,1)S(1)}, bf16[32,1152]{1,0:T(8,128)(2,1)S(1)}, u32[]{:S(2)}, u32[]{:S(2)}) collective-permute-start(bf16[32,1152]{1,0:T(8,128)(2,1)S(1)} %get-tuple-element.62), channel_id=1, source_target_pairs={{0,8},{1,9},{2,10},{3,11},{4,12},{5,13},{6,14},{7,15},{8,0},{9,1},... | collective-permute-start | bytes 221192 | tf_op jit(solution)/shard_map/ppermute | solution.py:22
  50.7 7.2 %collective-permute-start.18 = (bf16[32,1152]{1,0:T(8,128)(2,1)S(1)}, bf16[32,1152]{1,0:T(8,128)(2,1)S(1)}, u32[]{:S(2)}, u32[]{:S(2)}) collective-permute-start(bf16[32,1152]{1,0:T(8,128)(2,1)S(1)} %get-tuple-element.63), channel_id=1, source_target_pairs={{0,12},{1,13},{2,14},{3,15},{4,8},{5,9},{6,10},{7,11},{8,4},{9,5},... | collective-permute-start | bytes 221192 | tf_op jit(solution)/shard_map/ppermute | solution.py:22
  52.8 3.9 %collective-permute-start.23 = (bf16[8,1728]{1,0:T(8,128)(2,1)S(1)}, bf16[8,1728]{1,0:T(8,128)(2,1)S(1)}, u32[]{:S(2)}, u32[]{:S(2)}) collective-permute-start(bf16[8,1728]{1,0:T(8,128)(2,1)S(1)} %get-tuple-element.78), channel_id=1, source_target_pairs={{0,2},{1,3},{2,0},{3,1},{4,6},{5,7},{6,4},{7,5},{8,10},{9,11},{10,... | collective-permute-start | bytes 82952 | tf_op jit(solution)/shard_map/ppermute | solution.py:22

commit v5 on v4

--- a/solution.py
+++ b/solution.py
@@ -15,6 +15,7 @@
 LANES = 128
 STACK_COST = 3_000_000_000
 EARLY_COST = 1_500_000_000
+HALF_COST = 1_500_000_000
 
 
 def swap(array, mask):
@@ -183,7 +184,7 @@
     held_ref[...] = own_ref[...]
 
 
-def stack_kernel(own_ref, far1_ref, far2_ref, far3_ref, last_ref, small_ref):
+def stack_kernel(own_ref, far3_ref, far1_ref, far2_ref, last_ref, small_ref):
     cut, end = last_ref.shape[1], last_ref.shape[1] + small_ref.shape[1]
     for far, ref in enumerate((own_ref, far1_ref, far2_ref, far3_ref)):
         last_ref[far] = ref[:cut]
@@ -331,71 +332,96 @@
     put_patch(patch_last_ref, act, 4, rows, n_slope)
 
 
-def front_kernel(
-    own,
+def put_blocks(w_ref, blocks, r_last):
+    taps = w_ref.shape[1]
+    for i, (ref, far) in enumerate(blocks):
+        for j, (start, size) in enumerate(tiles(taps)):
+            w_ref[i * r_last : (i + 1) * r_last, start : start + size] = ref[
+                far, j * r_last : (j + 1) * r_last
+            ]
+
+
+def half_kernel(
     rows,
-    total,
+    edge_t,
     teacher_ref,
     edge_a_ref,
     edge_b_ref,
     patch_last_ref,
     h_ref,
     hy_ref,
+    w_own_ref,
+    student_ref,
+    target_ref,
+):
+    place = position(BLOCKS)[2]
+    channels = teacher_ref.shape[1]
+    r_last = channels // BLOCKS
+    put_blocks(w_own_ref, [(ref, far) for ref in (h_ref, hy_ref) for far in range(FAR)], r_last)
+    student_ref[...] = dot(patch_last_ref[...], w_own_ref[...], ((1,), (1,)))
+    before, after = sides(edge_a_ref, edge_b_ref)
+    wide = jnp.concatenate(
+        [
+            take_tiles(before, 0, edge_t, channels),
+            teacher_ref[...],
+            take_tiles(after, 0, edge_t, channels),
+        ],
+        0,
+    )
+    out = iota((1, channels), 1)
+    block = out // r_last
+    key = 4 * (block % FAR) + 2 * (block // FAR % 2) + block // (2 * FAR)
+    source = (key ^ place) * r_last + out % r_last
+    pick = (iota((channels, channels), 0) == source).astype(f32).astype(bf16)
+    target_ref[...] = dot(wide, pick, ((1,), (0,))).astype(bf16)
+
+
+def front_kernel(
+    own,
+    rows,
+    total,
+    target_ref,
+    patch_last_ref,
+    student_own_ref,
     hc_ref,
     hyc_ref,
-    keep_ref,
     send_ref,
     slope_ref,
-    w_last_ref,
+    w_other_ref,
     student_ref,
-    terms_ref,
 ):
-    group, _, place = position(BLOCKS)
-    first_col = group * own
-    r_last, taps = w_last_ref.shape[1:]
+    first_col = position(BLOCKS)[0] * own
     channels = slope_ref.shape[1]
-    for near, ref in enumerate((h_ref, hc_ref, hy_ref, hyc_ref)):
-        for far in range(FAR):
-            at = place ^ (4 * far + near)
-            for i, (start, size) in enumerate(tiles(taps)):
-                w_last_ref[at, :, start : start + size] = ref[far, i * r_last : (i + 1) * r_last]
-
-    w_last = w_last_ref[...].reshape(-1, taps)
-    student_ref[...] = dot(patch_last_ref[...], w_last, ((1,), (1,)))
-
-    def slopes(start, count, target, col):
-        at = pl.ds(start, count)
-        student = student_ref[at, :]
-        s_inv = lax.rsqrt(jnp.sum(student * student, -1, keepdims=True) + epsilon)
-        target = target.astype(f32)
-        t_inv = lax.rsqrt(jnp.sum(target * target, -1, keepdims=True) + epsilon)
-        s_unit = student * s_inv
-        differ = s_unit - target * t_inv
-        slope = (differ - s_unit * jnp.sum(s_unit * differ, -1, keepdims=True)) * s_inv
-        slope_ref[at, :] = jnp.where(inside(count, rows, col, total), slope, 0.0).astype(bf16)
-
-    edge, block = HALO_SLOPE * rows, 4 * rows
-    lo, n_own = edge, own * rows
-    before, after = sides(edge_a_ref, edge_b_ref)
-    slopes(0, edge, take_tiles(before, 0, edge, channels), first_col - HALO_SLOPE)
-    slopes(edge + n_own, edge, take_tiles(after, 0, edge, channels), first_col + own)
-
-    def step(i, carry):
-        at = pl.multiple_of(i * block, block)
-        target = teacher_ref[pl.ds(at, block), :]
-        slopes(pl.multiple_of(edge + at, rows), block, target, first_col + i * 4)
-        return carry
-
-    lax.fori_loop(0, own // 4, step, 0)
+    half = channels // 2
+    put_blocks(
+        w_other_ref, [(ref, far) for ref in (hc_ref, hyc_ref) for far in range(FAR)], channels // BLOCKS
+    )
+    student_ref[...] = dot(patch_last_ref[...], w_other_ref[...], ((1,), (1,)))
+    block = 4 * rows
+    for step in range(slope_ref.shape[0] // block):
+        at = pl.ds(step * block, block)
+        parts = [
+            (student, target_ref[at, lane : lane + half].astype(f32), lane)
+            for student, lane in ((student_own_ref[at, :], 0), (student_ref[at, :], half))
+        ]
+
+        def total_of(product):
+            return sum(jnp.sum(product(s, t), -1, keepdims=True) for s, t, _ in parts)
+
+        s_inv = lax.rsqrt(total_of(lambda s, t: s * s) + epsilon)
+        t_inv = lax.rsqrt(total_of(lambda s, t: t * t) + epsilon)
+        cosine = total_of(lambda s, t: s * t) * (s_inv * t_inv)
+        ok = inside(block, rows, first_col - HALO_SLOPE + step * (block // rows), total)
+        s_part = jnp.where(ok, s_inv * s_inv * (cosine + epsilon * (s_inv * s_inv)), 0.0)
+        t_part = jnp.where(ok, s_inv * t_inv, 0.0)
+        for student, target, lane in parts:
+            slope_ref[at, lane : lane + half] = (student * s_part - target * t_part).astype(bf16)
+
+    lo, n_own = HALO_SLOPE * rows, own * rows
     terms = dot(
-        slope_ref[lo : lo + n_own, :], patch_last_ref[lo : lo + n_own, :], ((0,), (0,))
-    )
-    terms_ref[...] = terms.reshape(terms_ref.shape)
-    for ry in range(2):
-        for far in range(FAR):
-            at = place ^ (4 * far + 2 * ry)
-            keep_ref[ry, far] = terms_ref[at]
-            send_ref[ry, far] = terms_ref[at ^ 1].astype(bf16)
+        slope_ref[lo : lo + n_own, half:], patch_last_ref[lo : lo + n_own, :], ((0,), (0,))
+    )
+    send_ref[...] = terms.astype(bf16).reshape(send_ref.shape)
 
 
 def back_kernel(
@@ -403,23 +429,42 @@
     rows,
     slope_ref,
     tilt_second_ref,
-    w_last_ref,
+    w_own_ref,
+    w_other_ref,
+    patch_last_ref,
+    keep_ref,
+    slope_second_ref,
+    parts_ref,
+):
+    half = w_own_ref.shape[0]
+    lo, n_own = HALO_SLOPE * rows, own * rows
+    terms = dot(
+        slope_ref[lo : lo + n_own, :half], patch_last_ref[lo : lo + n_own, :], ((0,), (0,))
+    )
+    keep_ref[...] = terms.reshape(keep_ref.shape)
+    parts_ref[...] = dot(slope_ref[:, :half], w_own_ref[...], ((1,), (0,))) + dot(
+        slope_ref[:, half:], w_other_ref[...], ((1,), (0,))
+    )
+    back_second = spread_back(parts_ref, 4, rows, own + 2 * HALO_BACK)
+    slope_second_ref[...] = (back_second * tilt_second_ref[...]).astype(bf16)
+
+
+def first_kernel(
+    own,
+    rows,
+    slope_second_ref,
     tilt_first_ref,
     patch_first_ref,
     patch_middle_ref,
     w_middle_ref,
     keep_ref,
     send_ref,
-    parts_last_ref,
     parts_ref,
     terms_ref,
 ):
     place = position(BLOCKS)[2]
     n_own = own * rows
-    w_last = w_last_ref[...].reshape(-1, w_last_ref.shape[2])
-    parts_last_ref[...] = dot(slope_ref[...], w_last, ((1,), (0,)))
-    back_second = spread_back(parts_last_ref, 4, rows, own + 2 * HALO_BACK)
-    slope_second = (back_second * tilt_second_ref[...]).astype(bf16)
+    slope_second = slope_second_ref[...]
     lo, hi = HALO_BACK * rows, HALO_SECOND * rows
     r_small, middle = terms_ref.shape[1], patch_middle_ref.shape[1]
     grad_middle = dot(
@@ -437,6 +482,10 @@
             at = place ^ (4 * far + 2 * ry)
             keep_ref[far, ry] = terms_ref[at]
             send_ref[far, ry] = terms_ref[at ^ 1].astype(bf16)
+
+
+def tied_split_kernel(keep_ref, got_ref, tie_ref, *out_refs):
+    split_kernel(keep_ref, got_ref, *out_refs)
 
 
 def split_kernel(keep_ref, got_ref, kept_ref, *send_refs):
@@ -519,7 +568,7 @@
         60,
     )
     across = swap(across, 2)
-    far = {k: swap(shard, 4 * k * fold) for k in (3, 2, 1)}
+    far = {k: swap(shard, 4 * k * fold) for k in (1, 2, 3)}
     near = swap(near, 1)
     anywhere = pl.BlockSpec(memory_space=pl.ANY)
     held, across = call(
@@ -540,7 +589,7 @@
     held_last, held_small = call(
         stack_kernel,
         "stack",
-        (held, far[1], far[2], far[3]),
+        (held, far[3], far[1], far[2]),
         [((FAR, part_last, LANES), bf16), ((FAR, packed - part_last, LANES), bf16)],
         [],
         STACK_COST,
@@ -598,55 +647,74 @@
         out_spaces={0: anywhere},
         aliases={0: 0},
     )
-    all_last = held_last, last_y, swap(held_last, fold), swap(last_y, fold)
-    keep, send, slope, all_last = call(
+    half = channels // 2
+    last_c, last_yc = swap(held_last, fold), swap(last_y, fold)
+    w_own, student_own, target = call(
+        functools.partial(half_kernel, rows, edge_t),
+        "half",
+        (t_band, edge_a, edge_b, patch_last, held_last, last_y),
+        [
+            ((half, 9 * hidden), bf16),
+            ((n_slope, half), f32),
+            ((n_slope, channels), bf16),
+        ],
+        [],
+        HALF_COST,
+    )
+    send, slope, w_other = call(
         functools.partial(front_kernel, own, rows, total),
         "front",
-        (t_band, edge_a, edge_b, patch_last, *all_last),
+        (target, patch_last, student_own, last_c, last_yc),
         [
-            ((2, FAR, r_last, 9 * hidden), f32),
             ((2, FAR, r_last, 9 * hidden), bf16),
             ((n_slope, channels), bf16),
-            ((BLOCKS, r_last, 9 * hidden), bf16),
+            ((half, 9 * hidden), bf16),
         ],
-        [
-            ((n_slope, channels), f32),
-            ((BLOCKS, r_last, 9 * hidden), f32),
-        ],
+        [((n_slope, half), f32)],
         6_000_000_000,
     )
-    both = 9 * (hidden + in_depth)
     got = swap(send, fold)
-    small_keep, small_send = call(
+    keep, slope_second = call(
         functools.partial(back_kernel, own, rows),
         "back",
-        (slope, tilt_second, all_last, tilt_first, patch_first, patch_middle, all_middle),
-        [
-            ((FAR, 2, r_small, both), f32),
-            ((FAR, 2, r_small, both), bf16),
-        ],
-        [
-            ((n_slope, 9 * hidden), f32),
-            ((n_back, 9 * hidden), f32),
-            ((BLOCKS, r_small, both), f32),
-        ],
+        (slope, tilt_second, w_own, w_other, patch_last),
+        [((2, FAR, r_last, 9 * hidden), f32), ((n_back, hidden), bf16)],
+        [((n_slope, 9 * hidden), f32)],
         4_000_000_000,
     )
+    both = 9 * (hidden + in_depth)
+    small_keep, small_send = call(
+        functools.partial(first_kernel, own, rows),
+        "first",
+        (slope_second, tilt_first, patch_first, patch_middle, all_middle),
+        [((FAR, 2, r_small, both), f32), ((FAR, 2, r_small, both), bf16)],
+        [((n_back, 9 * hidden), f32), ((BLOCKS, r_small, both), f32)],
+        2_000_000_000,
+    )
+
     def split(keep, got, count):
         shape = keep.shape[1:]
         outs = [(shape, f32)] + [(shape, bf16)] * (count - 1)
         return call(split_kernel, "split", (keep, got), outs, [], 1_000_000)
 
-    last_kept, last_sent = split(keep, got, 2)
+    last_kept, last_sent = call(
+        tied_split_kernel,
+        "split",
+        (keep, got, slope_second),
+        [(keep.shape[1:], f32), (keep.shape[1:], bf16)],
+        [],
+        1_000_000,
+        {2: anywhere},
+    )
     last_got = swap(last_sent, 2 * fold)
     parts = split(small_keep, swap(small_send, fold), FAR)
-    small_got = {k: swap(parts[k], 4 * k * fold) for k in (3, 2, 1)}
+    small_got = {k: swap(parts[k], 4 * k * fold) for k in (1, 2, 3)}
     last = split(last_kept, last_got, FAR)
-    last_got = {k: swap(last[k], 4 * k * fold) for k in (3, 2, 1)}
+    last_got = {k: swap(last[k], 4 * k * fold) for k in (1, 2, 3)}
     small_kept, small_sent = call(
         add_kernel,
         "add",
-        (parts[0], small_got[1], small_got[2], small_got[3]),
+        (parts[0], small_got[3], small_got[2], small_got[1]),
         [((r_small, both), f32), ((r_small, both), bf16)],
         [],
         1_000_000,
@@ -655,7 +723,7 @@
     out_first, out_middle, out_last = call(
         finish_kernel,
         "finish",
-        (last[0], last_got[1], last_got[2], last_got[3], small_kept, small_got),
+        (last[0], last_got[3], last_got[2], last_got[1], small_kept, small_got),
         [(w.shape, f32) for w in (w_first, w_middle, w_last)],
         [],
         1_000_000,

time: 58.9 us -> 55.4 us (0.941)
  waiting for transfers between devices: 21 us -> 17.7 us
  Pallas kernels: 12.4 us -> 11.6 us
  starting transfers between devices: 23.5 us -> 24.2 us
    ppermute x23, waiting for transfers between devices: 21 us -> 17.7 us  [swap(): return lax.ppermute(array, 'cols', [(i, i ^ mask) for i in range(size)])]
    pallas_call x13 -> x15, Pallas kernels: 12.4 us -> 11.6 us  [call(): pl.pallas_call(kernel, in_specs=[spaces.get(i, vmem) for i in range(len(i...]
    ppermute x23, starting transfers between devices: 22.9 us -> 23.5 us  [swap(): return lax.ppermute(array, 'cols', [(i, i ^ mask) for i in range(size)])]
  transfers between devices with their start and end apart: 24 -> 24, of which waited for: 12 -> 14; matrix products, arithmetic and copies ran while one was open for 0% -> 0% of each run, Pallas kernels for 8% -> 11%
where the time goes in v5:
time: 55.4 us; the launch traced here: 55.3 us
  starting transfers between devices  24.2 us (44%)
  waiting for transfers between devices  17.7 us (32%)
  Pallas kernels  11.6 us (21%)
  local copies, waits for them, and re-layouts  0.95 us (2%)
  between operations  0.78 us (1%)
    ppermute x23, starting transfers between devices, swap(): return lax.ppermute(array, 'cols', [(i, i ^ mask) for i in range(size)])  23.5 us
    ppermute x23, waiting for transfers between devices, swap(): return lax.ppermute(array, 'cols', [(i, i ^ mask) for i in range(size)])  17.7 us
    pallas_call x15, Pallas kernels, call(): pl.pallas_call(kernel, in_specs=[spaces.get(i, vmem) for i in range(len(i...  11.6 us
  transfers between devices with their start and end apart: 24, of which 14 were waited for; matrix products, arithmetic and copies ran while one was open for 0% of the time, Pallas kernels for 11%

profile of v5, /device:TPU:0, one launch (start us, length us, event | category | flops | bytes accessed | tf_op | source)
XLA Modules:
  0.0 55.3 jit_solution(12290709887829679454)
XLA Ops:
  0.6 2.4 %deal.1 = (bf16[1040,128]{1,0:T(8,128)(2,1)}, bf16[640,128]{1,0:T(8,128)(2,1)}, bf16[1152,128]{1,0:T(8,128)(2,1)}, bf16[400,128]{1,0:T(8,128)(2,1)}) custom-call(bf16[32,1024]{1,0:T(8,128)(2,1)} %x_hbm.1, bf16[32,16,512]{2,1,0:T(8,128)(2,1)} %teacher_hbm.1, bf16[8,576]{1,0:T(8,128)(2,1)} %w_first_hbm.1, bf16[8,1152]{1,0:T(8,128)(2,1)} %w_middle_hbm.1, ...), custom_call_target="tpu_custom_call" | custom-call | flops 600000000 | bytes 1000000 | tf_op jit(solution)/shard_map/deal/pallas_call | solution.py:519
  3.0 3.0 %collective-permute-start = (bf16[1152,128]{1,0:T(8,128)(2,1)}, bf16[1152,128]{1,0:T(8,128)(2,1)S(1)}, u32[]{:S(2)}, u32[]{:S(2)}) collective-permute-start(bf16[1152,128]{1,0:T(8,128)(2,1)} %get-tuple-element.46), channel_id=1, source_target_pairs={{0,2},{1,3},{2,0},{3,1},{4,6},{5,7},{6,4},{7,5},{8,10},{9,11},{10,... | collective-permute-start | bytes 884744 | tf_op jit(solution)/shard_map/ppermute | solution.py:23
  6.1 2.6 %collective-permute-start.5 = (bf16[400,128]{1,0:T(8,128)(2,1)}, bf16[400,128]{1,0:T(8,128)(2,1)S(1)}, u32[]{:S(2)}, u32[]{:S(2)}) collective-permute-start(bf16[400,128]{1,0:T(8,128)(2,1)} %get-tuple-element.50), channel_id=1, source_target_pairs={{0,8},{1,9},{2,10},{3,11},{4,12},{5,13},{6,14},{7,15},{8,0},{9,1},... | collective-permute-start | bytes 307208 | tf_op jit(solution)/shard_map/ppermute | solution.py:23
  8.7 1.6 %collective-permute-start.4 = (bf16[400,128]{1,0:T(8,128)(2,1)}, bf16[400,128]{1,0:T(8,128)(2,1)S(1)}, u32[]{:S(2)}, u32[]{:S(2)}) collective-permute-start(bf16[400,128]{1,0:T(8,128)(2,1)} %get-tuple-element.50), channel_id=1, source_target_pairs={{0,4},{1,5},{2,6},{3,7},{4,0},{5,1},{6,2},{7,3},{8,12},{9,13},{10,... | collective-permute-start | bytes 307208 | tf_op jit(solution)/shard_map/ppermute | solution.py:23
  10.5 2.8 %collective-permute-done.across_ref = bf16[1152,128]{1,0:T(8,128)(2,1)S(1)} collective-permute-done((bf16[1152,128]{1,0:T(8,128)(2,1)}, bf16[1152,128]{1,0:T(8,128)(2,1)S(1)}, u32[]{:S(2)}, u32[]{:S(2)}) %collective-permute-start) | collective-permute-done | bytes 294944 | tf_op jit(solution)/shard_map/ppermute | solution.py:23
  13.3 0.9 %copy-done = bf16[1040,128]{1,0:T(8,128)(2,1)S(1)} copy-done((bf16[1040,128]{1,0:T(8,128)(2,1)S(1)}, bf16[1040,128]{1,0:T(8,128)(2,1)}, u32[]{:S(2)}) %copy-start) | copy-done | bytes 266264
  14.3 0.5 collective-permute-start.1
  15.0 2.0 %collective-permute-done.3.far3_ref = bf16[400,128]{1,0:T(8,128)(2,1)S(1)} collective-permute-done((bf16[400,128]{1,0:T(8,128)(2,1)}, bf16[400,128]{1,0:T(8,128)(2,1)S(1)}, u32[]{:S(2)}, u32[]{:S(2)}) %collective-permute-start.3) | collective-permute-done | bytes 102432 | tf_op jit(solution)/shard_map/ppermute | solution.py:23
  17.3 1.1 %collective-permute-start.8 = (bf16[4,112,128]{2,1,0:T(8,128)(2,1)S(1)}, bf16[4,112,128]{2,1,0:T(8,128)(2,1)S(1)}, u32[]{:S(2)}, u32[]{:S(2)}) collective-permute-start(bf16[4,112,128]{2,1,0:T(8,128)(2,1)S(1)} %get-tuple-element.57.h_ref), channel_id=1, source_target_pairs={{0,2},{1,3},{2,0},{3,1},{4,6},{5,7},{6,4},{7,5},{8,10},{9,11},{10,... | collective-permute-start | bytes 344072 | tf_op jit(solution)/shard_map/ppermute | solution.py:23
  18.4 1.0 %collective-permute-start.11 = (bf16[4,288,128]{2,1,0:T(8,128)(2,1)S(1)}, bf16[4,288,128]{2,1,0:T(8,128)(2,1)S(1)}, u32[]{:S(2)}, u32[]{:S(2)}) collective-permute-start(bf16[4,288,128]{2,1,0:T(8,128)(2,1)S(1)} %get-tuple-element.59.h_ref), channel_id=1, source_target_pairs={{0,2},{1,3},{2,0},{3,1},{4,6},{5,7},{6,4},{7,5},{8,10},{9,11},{10,... | collective-permute-start | bytes 884744 | tf_op jit(solution)/shard_map/ppermute | solution.py:23
  19.4 1.9 %collective-permute-start.6 = (bf16[496,128]{1,0:T(8,128)(2,1)S(1)}, bf16[496,128]{1,0:T(8,128)(2,1)S(1)}, u32[]{:S(2)}, u32[]{:S(2)}) collective-permute-start(bf16[496,128]{1,0:T(8,128)(2,1)S(1)} %get-tuple-element.54), channel_id=1, source_target_pairs={{0,4},{1,5},{2,6},{3,7},{4,0},{5,1},{6,2},{7,3},{8,12},{9,13},{10,... | collective-permute-start | bytes 380936 | tf_op jit(solution)/shard_map/ppermute | solution.py:23
  21.3 0.7 %collective-permute-start.7 = (bf16[496,128]{1,0:T(8,128)(2,1)S(1)}, bf16[496,128]{1,0:T(8,128)(2,1)S(1)}, u32[]{:S(2)}, u32[]{:S(2)}) collective-permute-start(bf16[496,128]{1,0:T(8,128)(2,1)S(1)} %get-tuple-element.55), channel_id=1, source_target_pairs={{4,8},{5,9},{6,10},{7,11},{8,4},{9,5},{10,6},{11,7},{20,24},{21,25... | collective-permute-start | bytes 380936 | tf_op jit(solution)/shard_map/ppermute | solution.py:29
  22.0 1.4 %collective-permute-done.8.hy_ref = bf16[4,112,128]{2,1,0:T(8,128)(2,1)S(1)} collective-permute-done((bf16[4,112,128]{2,1,0:T(8,128)(2,1)S(1)}, bf16[4,112,128]{2,1,0:T(8,128)(2,1)S(1)}, u32[]{:S(2)}, u32[]{:S(2)}) %collective-permute-start.8) | collective-permute-done | bytes 114720 | tf_op jit(solution)/shard_map/ppermute | solution.py:23
  23.4 0.5 collective-permute-start.12
  23.9 0.4 collective-permute-done.6.edge_a_ref
  24.7 2.2 %early.1 = (f32[512,128]{1,0:T(8,128)S(1)}, f32[576,128]{1,0:T(8,128)S(1)}, bf16[896,576]{1,0:T(8,128)(2,1)S(1)}, bf16[832,1152]{1,0:T(8,128)(2,1)S(1)}, bf16[70...) custom-call(bf16[512,64]{1,0:T(8,128)(2,1)S(1)} %get-tuple-element.56.x_ref, ...), custom_call_target="tpu_custom_call" | custom-call | flops 1500000000 | bytes 1000000 | tf_op jit(solution)/shard_map/early/pallas_call | solution.py:519
  26.9 1.5 %collective-permute-done.11.value_ref = bf16[4,288,128]{2,1,0:T(8,128)(2,1)S(1)} collective-permute-done((bf16[4,288,128]{2,1,0:T(8,128)(2,1)S(1)}, bf16[4,288,128]{2,1,0:T(8,128)(2,1)S(1)}, u32[]{:S(2)}, u32[]{:S(2)}) %collective-permute-start.11) | collective-permute-done | bytes 294944 | tf_op jit(solution)/shard_map/ppermute | solution.py:23
  28.4 1.1 %half.1 = (bf16[256,1152]{1,0:T(8,128)(2,1)S(1)}, f32[704,256]{1,0:T(8,128)S(1)}, bf16[704,512]{1,0:T(8,128)(2,1)S(1)}) custom-call(bf16[512,512]{1,0:T(8,128)(2,1)S(1)} %get-tuple-element.53.teacher_ref, bf16[496,128]{1,0:T(8,128)(2,1)S(1)} %collective-permute-done.6.edge_a_ref, bf16[496,128]{1,0:T(8,128)(2,1)S(1)} %collective-permute-done.7.edge_b_ref, ...), custom_call_target="tpu_custom_call" | custom-call | flops 1500000000 | bytes 1000000 | tf_op jit(solution)/shard_map/half/pallas_call | solution.py:519
  29.5 0.5 collective-permute-done.13.hyc_ref
  30.0 2.2 %front.1 = (bf16[2,4,32,1152]{3,2,1,0:T(8,128)(2,1)S(1)}, bf16[704,512]{1,0:T(8,128)(2,1)S(1)}, bf16[256,1152]{1,0:T(8,128)(2,1)S(1)}) custom-call(bf16[704,512]{1,0:T(8,128)(2,1)S(1)} %get-tuple-element.60.target_ref, bf16[704,1152]{1,0:T(8,128)(2,1)S(1)} %get-tuple-element.58.first_ref.patch_last_ref, f32[704,256]{1,0:T(8,128)S(1)} %get-tuple-element.61.student_own_ref, ...), custom_call_target="tpu_custom_call" | custom-call | flops 6000000000 | bytes 1000000 | tf_op jit(solution)/shard_map/front/pallas_call | solution.py:519
  32.4 1.5 %back.1 = (f32[2,4,32,1152]{3,2,1,0:T(8,128)S(1)}, bf16[576,128]{1,0:T(8,128)(2,1)S(1)}) custom-call(bf16[704,512]{1,0:T(8,128)(2,1)S(1)} %get-tuple-element.62.slope_ref, f32[576,128]{1,0:T(8,128)S(1)} %get-tuple-element.63.tilt_second_ref, bf16[256,1152]{1,0:T(8,128)(2,1)S(1)} %get-tuple-element.64.w_own_ref, ...), custom_call_target="tpu_custom_call" | custom-call | flops 4000000000 | bytes 1000000 | tf_op jit(solution)/shard_map/back/pallas_call | solution.py:519
  34.3 1.6 %collective-permute-start.15 = (bf16[4,32,1152]{2,1,0:T(8,128)(2,1)S(1)}, bf16[4,32,1152]{2,1,0:T(8,128)(2,1)S(1)}, u32[]{:S(2)}, u32[]{:S(2)}) collective-permute-start(bf16[4,32,1152]{2,1,0:T(8,128)(2,1)S(1)} %get-tuple-element.70), channel_id=1, source_target_pairs={{0,2},{1,3},{2,0},{3,1},{4,6},{5,7},{6,4},{7,5},{8,10},{9,11},{10,... | collective-permute-start | bytes 884744 | tf_op jit(solution)/shard_map/ppermute | solution.py:23
  35.9 1.1 %first.1 = (f32[4,2,8,1728]{3,2,1,0:T(8,128)S(1)}, bf16[4,2,8,1728]{3,2,1,0:T(8,128)(2,1)S(1)}) custom-call(bf16[576,128]{1,0:T(8,128)(2,1)S(1)} %get-tuple-element.68.tie_ref.slope_second_ref, f32[512,128]{1,0:T(8,128)S(1)} %get-tuple-element.75.tilt_first_ref, bf16[896,576]{1,0:T(8,128)(2,1)S(1)} %get-tuple-element.76.patch_first_ref, ...), custom_call_target="tpu_custom_call" | custom-call | flops 2000000000 | bytes 1000000 | tf_op jit(solution)/shard_map/first/pallas_call | solution.py:519
  37.1 1.5 %collective-permute-done.19.got_ref = bf16[4,2,8,1728]{3,2,1,0:T(8,128)(2,1)S(1)} collective-permute-done((bf16[4,2,8,1728]{3,2,1,0:T(8,128)(2,1)S(1)}, bf16[4,2,8,1728]{3,2,1,0:T(8,128)(2,1)S(1)}, u32[]{:S(2)}, u32[]{:S(2)}) %collective-permute-start.19) | collective-permute-done | bytes 221216 | tf_op jit(solution)/shard_map/ppermute | solution.py:23
  38.6 3.7 %collective-permute-start.20 = (bf16[2,8,1728]{2,1,0:T(8,128)(2,1)S(1)}, bf16[2,8,1728]{2,1,0:T(8,128)(2,1)S(1)}, u32[]{:S(2)}, u32[]{:S(2)}) collective-permute-start(bf16[2,8,1728]{2,1,0:T(8,128)(2,1)S(1)} %get-tuple-element.82), channel_id=1, source_target_pairs={{0,12},{1,13},{2,14},{3,15},{4,8},{5,9},{6,10},{7,11},{8,4},{9,5},... | collective-permute-start | bytes 165896 | tf_op jit(solution)/shard_map/ppermute | solution.py:23
  42.6 0.5 collective-permute-start.22
  43.5 3.7 %collective-permute-start.16 = (bf16[32,1152]{1,0:T(8,128)(2,1)S(1)}, bf16[32,1152]{1,0:T(8,128)(2,1)S(1)}, u32[]{:S(2)}, u32[]{:S(2)}) collective-permute-start(bf16[32,1152]{1,0:T(8,128)(2,1)S(1)} %get-tuple-element.72), channel_id=1, source_target_pairs={{0,12},{1,13},{2,14},{3,15},{4,8},{5,9},{6,10},{7,11},{8,4},{9,5},... | collective-permute-start | bytes 221192 | tf_op jit(solution)/shard_map/ppermute | solution.py:23
  47.4 0.5 collective-permute-start.18
  48.0 1.3 %collective-permute-done.21.got2_ref = bf16[2,8,1728]{2,1,0:T(8,128)(2,1)S(1)} collective-permute-done((bf16[2,8,1728]{2,1,0:T(8,128)(2,1)S(1)}, bf16[2,8,1728]{2,1,0:T(8,128)(2,1)S(1)}, u32[]{:S(2)}, u32[]{:S(2)}) %collective-permute-start.21) | collective-permute-done | bytes 55328 | tf_op jit(solution)/shard_map/ppermute | solution.py:23
  49.6 3.7 %collective-permute-done.23.got_ref = bf16[8,1728]{1,0:T(8,128)(2,1)S(1)} collective-permute-done((bf16[8,1728]{1,0:T(8,128)(2,1)S(1)}, bf16[8,1728]{1,0:T(8,128)(2,1)S(1)}, u32[]{:S(2)}, u32[]{:S(2)}) %collective-permute-start.23) | collective-permute-done | bytes 27680 | tf_op jit(solution)/shard_map/ppermute | solution.py:23
  53.3 1.3 %collective-permute-done.17.got2_ref = bf16[32,1152]{1,0:T(8,128)(2,1)S(1)} collective-permute-done((bf16[32,1152]{1,0:T(8,128)(2,1)S(1)}, bf16[32,1152]{1,0:T(8,128)(2,1)S(1)}, u32[]{:S(2)}, u32[]{:S(2)}) %collective-permute-start.17) | collective-permute-done | bytes 73760 | tf_op jit(solution)/shard_map/ppermute | solution.py:23
  54.5 0.7 %finish.1 = (f32[8,576]{1,0:T(8,128)}, f32[8,1152]{1,0:T(8,128)}, f32[32,1152]{1,0:T(8,128)}) custom-call(f32[32,1152]{1,0:T(8,128)S(1)} %get-tuple-element.71.last_ref, bf16[32,1152]{1,0:T(8,128)(2,1)S(1)} %collective-permute-done.16.got1_ref, bf16[32,1152]{1,0:T(8,128)(2,1)S(1)} %collective-permute-done.17.got2_ref, ...), custom_call_target="tpu_custom_call" | custom-call | flops 1000000 | bytes 1000000 | tf_op jit(solution)/shard_map/finish/pallas_call | solution.py:519
  (33 shorter events, 3.3 us)
Async XLA Ops:
  3.0 10.3 %collective-permute-start = (bf16[1152,128]{1,0:T(8,128)(2,1)}, bf16[1152,128]{1,0:T(8,128)(2,1)S(1)}, u32[]{:S(2)}, u32[]{:S(2)}) collective-permute-start(bf16[1152,128]{1,0:T(8,128)(2,1)} %get-tuple-element.46), channel_id=1, source_target_pairs={{0,2},{1,3},{2,0},{3,1},{4,6},{5,7},{6,4},{7,5},{8,10},{9,11},{10,... | collective-permute-start | bytes 884744 | tf_op jit(solution)/shard_map/ppermute | solution.py:23
  6.1 9.0 %collective-permute-start.5 = (bf16[400,128]{1,0:T(8,128)(2,1)}, bf16[400,128]{1,0:T(8,128)(2,1)S(1)}, u32[]{:S(2)}, u32[]{:S(2)}) collective-permute-start(bf16[400,128]{1,0:T(8,128)(2,1)} %get-tuple-element.50), channel_id=1, source_target_pairs={{0,8},{1,9},{2,10},{3,11},{4,12},{5,13},{6,14},{7,15},{8,0},{9,1},... | collective-permute-start | bytes 307208 | tf_op jit(solution)/shard_map/ppermute | solution.py:23
  8.7 6.4 %collective-permute-start.4 = (bf16[400,128]{1,0:T(8,128)(2,1)}, bf16[400,128]{1,0:T(8,128)(2,1)S(1)}, u32[]{:S(2)}, u32[]{:S(2)}) collective-permute-start(bf16[400,128]{1,0:T(8,128)(2,1)} %get-tuple-element.50), channel_id=1, source_target_pairs={{0,4},{1,5},{2,6},{3,7},{4,0},{5,1},{6,2},{7,3},{8,12},{9,13},{10,... | collective-permute-start | bytes 307208 | tf_op jit(solution)/shard_map/ppermute | solution.py:23
  10.2 6.8 %collective-permute-start.3 = (bf16[400,128]{1,0:T(8,128)(2,1)}, bf16[400,128]{1,0:T(8,128)(2,1)S(1)}, u32[]{:S(2)}, u32[]{:S(2)}) collective-permute-start(bf16[400,128]{1,0:T(8,128)(2,1)} %get-tuple-element.50), channel_id=1, source_target_pairs={{0,12},{1,13},{2,14},{3,15},{4,8},{5,9},{6,10},{7,11},{8,4},{9,5},... | collective-permute-start | bytes 307208 | tf_op jit(solution)/shard_map/ppermute | solution.py:23
  13.3 1.0 %copy-start = (bf16[1040,128]{1,0:T(8,128)(2,1)S(1)}, bf16[1040,128]{1,0:T(8,128)(2,1)}, u32[]{:S(2)}) copy-start(bf16[1040,128]{1,0:T(8,128)(2,1)} %get-tuple-element.45.own_ref) | copy-start | bytes 798724
  14.3 2.8 %collective-permute-start.2 = (bf16[1152,128]{1,0:T(8,128)(2,1)S(1)}, bf16[1152,128]{1,0:T(8,128)(2,1)S(1)}, u32[]{:S(2)}, u32[]{:S(2)}) collective-permute-start(bf16[1152,128]{1,0:T(8,128)(2,1)S(1)} %get-tuple-element.49.across_ref), channel_id=1, source_target_pairs={{0,1},{1,0},{2,3},{3,2},{4,5},{5,4},{6,7},{7,6},{8,9},{9,8},{10,11... | collective-permute-start | bytes 884744 | tf_op jit(solution)/shard_map/ppermute | solution.py:23
  14.3 2.7 %collective-permute-start.1 = (bf16[640,128]{1,0:T(8,128)(2,1)}, bf16[640,128]{1,0:T(8,128)(2,1)S(1)}, u32[]{:S(2)}, u32[]{:S(2)}) collective-permute-start(bf16[640,128]{1,0:T(8,128)(2,1)} %get-tuple-element.48), channel_id=1, source_target_pairs={{0,1},{1,0},{2,3},{3,2},{4,5},{5,4},{6,7},{7,6},{8,9},{9,8},{10,11... | collective-permute-start | bytes 491528 | tf_op jit(solution)/shard_map/ppermute | solution.py:23
  17.3 6.1 %collective-permute-start.8 = (bf16[4,112,128]{2,1,0:T(8,128)(2,1)S(1)}, bf16[4,112,128]{2,1,0:T(8,128)(2,1)S(1)}, u32[]{:S(2)}, u32[]{:S(2)}) collective-permute-start(bf16[4,112,128]{2,1,0:T(8,128)(2,1)S(1)} %get-tuple-element.57.h_ref), channel_id=1, source_target_pairs={{0,2},{1,3},{2,0},{3,1},{4,6},{5,7},{6,4},{7,5},{8,10},{9,11},{10,... | collective-permute-start | bytes 344072 | tf_op jit(solution)/shard_map/ppermute | solution.py:23
  18.4 10.0 %collective-permute-start.11 = (bf16[4,288,128]{2,1,0:T(8,128)(2,1)S(1)}, bf16[4,288,128]{2,1,0:T(8,128)(2,1)S(1)}, u32[]{:S(2)}, u32[]{:S(2)}) collective-permute-start(bf16[4,288,128]{2,1,0:T(8,128)(2,1)S(1)} %get-tuple-element.59.h_ref), channel_id=1, source_target_pairs={{0,2},{1,3},{2,0},{3,1},{4,6},{5,7},{6,4},{7,5},{8,10},{9,11},{10,... | collective-permute-start | bytes 884744 | tf_op jit(solution)/shard_map/ppermute | solution.py:23
  19.4 4.9 %collective-permute-start.6 = (bf16[496,128]{1,0:T(8,128)(2,1)S(1)}, bf16[496,128]{1,0:T(8,128)(2,1)S(1)}, u32[]{:S(2)}, u32[]{:S(2)}) collective-permute-start(bf16[496,128]{1,0:T(8,128)(2,1)S(1)} %get-tuple-element.54), channel_id=1, source_target_pairs={{0,4},{1,5},{2,6},{3,7},{4,0},{5,1},{6,2},{7,3},{8,12},{9,13},{10,... | collective-permute-start | bytes 380936 | tf_op jit(solution)/shard_map/ppermute | solution.py:23
  21.3 3.1 %collective-permute-start.7 = (bf16[496,128]{1,0:T(8,128)(2,1)S(1)}, bf16[496,128]{1,0:T(8,128)(2,1)S(1)}, u32[]{:S(2)}, u32[]{:S(2)}) collective-permute-start(bf16[496,128]{1,0:T(8,128)(2,1)S(1)} %get-tuple-element.55), channel_id=1, source_target_pairs={{4,8},{5,9},{6,10},{7,11},{8,4},{9,5},{10,6},{11,7},{20,24},{21,25... | collective-permute-start | bytes 380936 | tf_op jit(solution)/shard_map/ppermute | solution.py:29
  21.9 1.5 %collective-permute-start.9 = (bf16[4,112,128]{2,1,0:T(8,128)(2,1)S(1)}, bf16[4,112,128]{2,1,0:T(8,128)(2,1)S(1)}, u32[]{:S(2)}, u32[]{:S(2)}) collective-permute-start(bf16[4,112,128]{2,1,0:T(8,128)(2,1)S(1)} %get-tuple-element.57.h_ref), channel_id=1, source_target_pairs={{0,1},{1,0},{2,3},{3,2},{4,5},{5,4},{6,7},{7,6},{8,9},{9,8},{10,11... | collective-permute-start | bytes 344072 | tf_op jit(solution)/shard_map/ppermute | solution.py:23
  23.4 1.3 %collective-permute-start.10 = (bf16[4,112,128]{2,1,0:T(8,128)(2,1)S(1)}, bf16[4,112,128]{2,1,0:T(8,128)(2,1)S(1)}, u32[]{:S(2)}, u32[]{:S(2)}) collective-permute-start(bf16[4,112,128]{2,1,0:T(8,128)(2,1)S(1)} %collective-permute-done.8.hy_ref), channel_id=1, source_target_pairs={{0,1},{1,0},{2,3},{3,2},{4,5},{5,4},{6,7},{7,6},{8,9},{9,8},{10,11... | collective-permute-start | bytes 344072 | tf_op jit(solution)/shard_map/ppermute | solution.py:23
  23.4 6.1 %collective-permute-start.12 = (bf16[4,288,128]{2,1,0:T(8,128)(2,1)S(1)}, bf16[4,288,128]{2,1,0:T(8,128)(2,1)S(1)}, u32[]{:S(2)}, u32[]{:S(2)}) collective-permute-start(bf16[4,288,128]{2,1,0:T(8,128)(2,1)S(1)} %get-tuple-element.59.h_ref), channel_id=1, source_target_pairs={{0,1},{1,0},{2,3},{3,2},{4,5},{5,4},{6,7},{7,6},{8,9},{9,8},{10,11... | collective-permute-start | bytes 884744 | tf_op jit(solution)/shard_map/ppermute | solution.py:23
  28.4 1.6 %collective-permute-start.13 = (bf16[4,288,128]{2,1,0:T(8,128)(2,1)S(1)}, bf16[4,288,128]{2,1,0:T(8,128)(2,1)S(1)}, u32[]{:S(2)}, u32[]{:S(2)}) collective-permute-start(bf16[4,288,128]{2,1,0:T(8,128)(2,1)S(1)} %after.1.hy_ref), channel_id=1, source_target_pairs={{0,1},{1,0},{2,3},{3,2},{4,5},{5,4},{6,7},{7,6},{8,9},{9,8},{10,11... | collective-permute-start | bytes 884744 | tf_op jit(solution)/shard_map/ppermute | solution.py:23
  32.2 2.1 %collective-permute-start.14 = (bf16[2,4,32,1152]{3,2,1,0:T(8,128)(2,1)S(1)}, bf16[2,4,32,1152]{3,2,1,0:T(8,128)(2,1)S(1)}, u32[]{:S(2)}, u32[]{:S(2)}) collective-permute-start(bf16[2,4,32,1152]{3,2,1,0:T(8,128)(2,1)S(1)} %get-tuple-element.67), channel_id=1, source_target_pairs={{0,1},{1,0},{2,3},{3,2},{4,5},{5,4},{6,7},{7,6},{8,9},{9,8},{10,11... | collective-permute-start | bytes 1769480 | tf_op jit(solution)/shard_map/ppermute | solution.py:23
  34.3 9.1 %collective-permute-start.15 = (bf16[4,32,1152]{2,1,0:T(8,128)(2,1)S(1)}, bf16[4,32,1152]{2,1,0:T(8,128)(2,1)S(1)}, u32[]{:S(2)}, u32[]{:S(2)}) collective-permute-start(bf16[4,32,1152]{2,1,0:T(8,128)(2,1)S(1)} %get-tuple-element.70), channel_id=1, source_target_pairs={{0,2},{1,3},{2,0},{3,1},{4,6},{5,7},{6,4},{7,5},{8,10},{9,11},{10,... | collective-permute-start | bytes 884744 | tf_op jit(solution)/shard_map/ppermute | solution.py:23
  37.0 1.6 %collective-permute-start.19 = (bf16[4,2,8,1728]{3,2,1,0:T(8,128)(2,1)S(1)}, bf16[4,2,8,1728]{3,2,1,0:T(8,128)(2,1)S(1)}, u32[]{:S(2)}, u32[]{:S(2)}) collective-permute-start(bf16[4,2,8,1728]{3,2,1,0:T(8,128)(2,1)S(1)} %get-tuple-element.80), channel_id=1, source_target_pairs={{0,1},{1,0},{2,3},{3,2},{4,5},{5,4},{6,7},{7,6},{8,9},{9,8},{10,11... | collective-permute-start | bytes 663560 | tf_op jit(solution)/shard_map/ppermute | solution.py:23
  38.6 8.8 %collective-permute-start.20 = (bf16[2,8,1728]{2,1,0:T(8,128)(2,1)S(1)}, bf16[2,8,1728]{2,1,0:T(8,128)(2,1)S(1)}, u32[]{:S(2)}, u32[]{:S(2)}) collective-permute-start(bf16[2,8,1728]{2,1,0:T(8,128)(2,1)S(1)} %get-tuple-element.82), channel_id=1, source_target_pairs={{0,12},{1,13},{2,14},{3,15},{4,8},{5,9},{6,10},{7,11},{8,4},{9,5},... | collective-permute-start | bytes 165896 | tf_op jit(solution)/shard_map/ppermute | solution.py:23
  42.3 7.0 %collective-permute-start.21 = (bf16[2,8,1728]{2,1,0:T(8,128)(2,1)S(1)}, bf16[2,8,1728]{2,1,0:T(8,128)(2,1)S(1)}, u32[]{:S(2)}, u32[]{:S(2)}) collective-permute-start(bf16[2,8,1728]{2,1,0:T(8,128)(2,1)S(1)} %get-tuple-element.83), channel_id=1, source_target_pairs={{0,8},{1,9},{2,10},{3,11},{4,12},{5,13},{6,14},{7,15},{8,0},{9,1},... | collective-permute-start | bytes 165896 | tf_op jit(solution)/shard_map/ppermute | solution.py:23
  42.6 6.7 %collective-permute-start.22 = (bf16[2,8,1728]{2,1,0:T(8,128)(2,1)S(1)}, bf16[2,8,1728]{2,1,0:T(8,128)(2,1)S(1)}, u32[]{:S(2)}, u32[]{:S(2)}) collective-permute-start(bf16[2,8,1728]{2,1,0:T(8,128)(2,1)S(1)} %get-tuple-element.84), channel_id=1, source_target_pairs={{0,4},{1,5},{2,6},{3,7},{4,0},{5,1},{6,2},{7,3},{8,12},{9,13},{10,... | collective-permute-start | bytes 165896 | tf_op jit(solution)/shard_map/ppermute | solution.py:23
  43.5 9.8 %collective-permute-start.16 = (bf16[32,1152]{1,0:T(8,128)(2,1)S(1)}, bf16[32,1152]{1,0:T(8,128)(2,1)S(1)}, u32[]{:S(2)}, u32[]{:S(2)}) collective-permute-start(bf16[32,1152]{1,0:T(8,128)(2,1)S(1)} %get-tuple-element.72), channel_id=1, source_target_pairs={{0,12},{1,13},{2,14},{3,15},{4,8},{5,9},{6,10},{7,11},{8,4},{9,5},... | collective-permute-start | bytes 221192 | tf_op jit(solution)/shard_map/ppermute | solution.py:23
  47.2 7.4 %collective-permute-start.17 = (bf16[32,1152]{1,0:T(8,128)(2,1)S(1)}, bf16[32,1152]{1,0:T(8,128)(2,1)S(1)}, u32[]{:S(2)}, u32[]{:S(2)}) collective-permute-start(bf16[32,1152]{1,0:T(8,128)(2,1)S(1)} %get-tuple-element.73), channel_id=1, source_target_pairs={{0,8},{1,9},{2,10},{3,11},{4,12},{5,13},{6,14},{7,15},{8,0},{9,1},... | collective-permute-start | bytes 221192 | tf_op jit(solution)/shard_map/ppermute | solution.py:23
  47.4 7.1 %collective-permute-start.18 = (bf16[32,1152]{1,0:T(8,128)(2,1)S(1)}, bf16[32,1152]{1,0:T(8,128)(2,1)S(1)}, u32[]{:S(2)}, u32[]{:S(2)}) collective-permute-start(bf16[32,1152]{1,0:T(8,128)(2,1)S(1)} %get-tuple-element.74), channel_id=1, source_target_pairs={{0,4},{1,5},{2,6},{3,7},{4,0},{5,1},{6,2},{7,3},{8,12},{9,13},{10,... | collective-permute-start | bytes 221192 | tf_op jit(solution)/shard_map/ppermute | solution.py:23
  49.3 3.9 %collective-permute-start.23 = (bf16[8,1728]{1,0:T(8,128)(2,1)S(1)}, bf16[8,1728]{1,0:T(8,128)(2,1)S(1)}, u32[]{:S(2)}, u32[]{:S(2)}) collective-permute-start(bf16[8,1728]{1,0:T(8,128)(2,1)S(1)} %get-tuple-element.86), channel_id=1, source_target_pairs={{0,2},{1,3},{2,0},{3,1},{4,6},{5,7},{6,4},{7,5},{8,10},{9,11},{10,... | collective-permute-start | bytes 82952 | tf_op jit(solution)/shard_map/ppermute | solution.py:23

commit v6 on v5

--- a/solution.py
+++ b/solution.py
@@ -25,9 +25,13 @@
 
 def bands_beside(low_pairs, high_pairs):
     size = lax.axis_size("cols")
-    pairs = [(i, i + 4) for i in range(4, size - 4) if (i // 4) % 2]
-    across = lax.ppermute(high_pairs, "cols", pairs + [(j, i) for i, j in pairs])
-    return swap(low_pairs, 4), across
+    bands = size // 4
+
+    def other(i):
+        band = i // 4 + (1 if i // 4 % 2 else -1)
+        return i ^ 1 if band < 0 or band >= bands else 4 * band + i % 4
+
+    return swap(low_pairs, 4), lax.ppermute(high_pairs, "cols", [(i, other(i)) for i in range(size)])
 
 
 def neighbours(fold):
@@ -241,8 +245,11 @@
 
 def sides(edge_a_ref, edge_b_ref):
     a, b = edge_a_ref[...], edge_b_ref[...]
-    odd = position(BLOCKS)[0] % 2 == 1
-    return jnp.where(odd, a, b), jnp.where(odd, b, a)
+    group, bands = position(BLOCKS)[0], lax.axis_size("cols") // 4
+    odd = group % 2 == 1
+    before, after = jnp.where(odd, a, b), jnp.where(odd, b, a)
+    zero = jnp.zeros_like(a)
+    return jnp.where(group == 0, zero, before), jnp.where(group == bands - 1, zero, after)
 
 
 def edge_x_cells(edge, edge_t, channels):

time: 55.4 us -> 54.8 us (0.989)
  waiting for transfers between devices: 17.7 us -> 16.6 us
    ppermute x23, starting transfers between devices: 23.5 us -> 24.7 us  [swap(): return lax.ppermute(array, 'cols', [(i, i ^ mask) for i in range(size)])]
    ppermute x23, waiting for transfers between devices: 17.7 us -> 16.6 us  [swap(): return lax.ppermute(array, 'cols', [(i, i ^ mask) for i in range(size)])]
    ppermute x1, starting transfers between devices: 0.66 us -> 0.01 us  [bands_beside(): lax.ppermute(high_pairs, 'cols', [(i, other(i)) for i in range(size)])]
where the time goes in v6:
time: 54.8 us; the launch traced here: 54.6 us
  starting transfers between devices  24.7 us (45%)
  waiting for transfers between devices  16.6 us (30%)
  Pallas kernels  11.6 us (21%)
  local copies, waits for them, and re-layouts  0.95 us (2%)
  between operations  0.76 us (1%)
    ppermute x23, starting transfers between devices, swap(): return lax.ppermute(array, 'cols', [(i, i ^ mask) for i in range(size)])  24.7 us
    ppermute x23, waiting for transfers between devices, swap(): return lax.ppermute(array, 'cols', [(i, i ^ mask) for i in range(size)])  16.6 us
    pallas_call x15, Pallas kernels, call(): pl.pallas_call(kernel, in_specs=[spaces.get(i, vmem) for i in range(len(i...  11.6 us
  transfers between devices with their start and end apart: 24, of which 14 were waited for; matrix products, arithmetic and copies ran while one was open for 0% of the time, Pallas kernels for 11%

profile of v6, /device:TPU:0, one launch (start us, length us, event | category | flops | bytes accessed | tf_op | source)
XLA Modules:
  0.0 54.6 jit_solution(8435894469490689908)
XLA Ops:
  0.6 2.4 %deal.1 = (bf16[1040,128]{1,0:T(8,128)(2,1)}, bf16[640,128]{1,0:T(8,128)(2,1)}, bf16[1152,128]{1,0:T(8,128)(2,1)}, bf16[400,128]{1,0:T(8,128)(2,1)}) custom-call(bf16[32,1024]{1,0:T(8,128)(2,1)} %x_hbm.1, bf16[32,16,512]{2,1,0:T(8,128)(2,1)} %teacher_hbm.1, bf16[8,576]{1,0:T(8,128)(2,1)} %w_first_hbm.1, bf16[8,1152]{1,0:T(8,128)(2,1)} %w_middle_hbm.1, ...), custom_call_target="tpu_custom_call" | custom-call | flops 600000000 | bytes 1000000 | tf_op jit(solution)/shard_map/deal/pallas_call | solution.py:526
  3.0 3.0 %collective-permute-start = (bf16[1152,128]{1,0:T(8,128)(2,1)}, bf16[1152,128]{1,0:T(8,128)(2,1)S(1)}, u32[]{:S(2)}, u32[]{:S(2)}) collective-permute-start(bf16[1152,128]{1,0:T(8,128)(2,1)} %get-tuple-element.46), channel_id=1, source_target_pairs={{0,2},{1,3},{2,0},{3,1},{4,6},{5,7},{6,4},{7,5},{8,10},{9,11},{10,... | collective-permute-start | bytes 884744 | tf_op jit(solution)/shard_map/ppermute | solution.py:23
  6.1 2.6 %collective-permute-start.5 = (bf16[400,128]{1,0:T(8,128)(2,1)}, bf16[400,128]{1,0:T(8,128)(2,1)S(1)}, u32[]{:S(2)}, u32[]{:S(2)}) collective-permute-start(bf16[400,128]{1,0:T(8,128)(2,1)} %get-tuple-element.50), channel_id=1, source_target_pairs={{0,8},{1,9},{2,10},{3,11},{4,12},{5,13},{6,14},{7,15},{8,0},{9,1},... | collective-permute-start | bytes 307208 | tf_op jit(solution)/shard_map/ppermute | solution.py:23
  8.7 1.6 %collective-permute-start.4 = (bf16[400,128]{1,0:T(8,128)(2,1)}, bf16[400,128]{1,0:T(8,128)(2,1)S(1)}, u32[]{:S(2)}, u32[]{:S(2)}) collective-permute-start(bf16[400,128]{1,0:T(8,128)(2,1)} %get-tuple-element.50), channel_id=1, source_target_pairs={{0,4},{1,5},{2,6},{3,7},{4,0},{5,1},{6,2},{7,3},{8,12},{9,13},{10,... | collective-permute-start | bytes 307208 | tf_op jit(solution)/shard_map/ppermute | solution.py:23
  10.5 2.8 %collective-permute-done.across_ref = bf16[1152,128]{1,0:T(8,128)(2,1)S(1)} collective-permute-done((bf16[1152,128]{1,0:T(8,128)(2,1)}, bf16[1152,128]{1,0:T(8,128)(2,1)S(1)}, u32[]{:S(2)}, u32[]{:S(2)}) %collective-permute-start) | collective-permute-done | bytes 294944 | tf_op jit(solution)/shard_map/ppermute | solution.py:23
  13.3 0.9 %copy-done = bf16[1040,128]{1,0:T(8,128)(2,1)S(1)} copy-done((bf16[1040,128]{1,0:T(8,128)(2,1)S(1)}, bf16[1040,128]{1,0:T(8,128)(2,1)}, u32[]{:S(2)}) %copy-start) | copy-done | bytes 266264
  14.3 0.5 collective-permute-start.1
  15.0 2.0 %collective-permute-done.3.far3_ref = bf16[400,128]{1,0:T(8,128)(2,1)S(1)} collective-permute-done((bf16[400,128]{1,0:T(8,128)(2,1)}, bf16[400,128]{1,0:T(8,128)(2,1)S(1)}, u32[]{:S(2)}, u32[]{:S(2)}) %collective-permute-start.3) | collective-permute-done | bytes 102432 | tf_op jit(solution)/shard_map/ppermute | solution.py:23
  17.3 1.1 %collective-permute-start.8 = (bf16[4,112,128]{2,1,0:T(8,128)(2,1)S(1)}, bf16[4,112,128]{2,1,0:T(8,128)(2,1)S(1)}, u32[]{:S(2)}, u32[]{:S(2)}) collective-permute-start(bf16[4,112,128]{2,1,0:T(8,128)(2,1)S(1)} %get-tuple-element.57.h_ref), channel_id=1, source_target_pairs={{0,2},{1,3},{2,0},{3,1},{4,6},{5,7},{6,4},{7,5},{8,10},{9,11},{10,... | collective-permute-start | bytes 344072 | tf_op jit(solution)/shard_map/ppermute | solution.py:23
  18.4 1.0 %collective-permute-start.11 = (bf16[4,288,128]{2,1,0:T(8,128)(2,1)S(1)}, bf16[4,288,128]{2,1,0:T(8,128)(2,1)S(1)}, u32[]{:S(2)}, u32[]{:S(2)}) collective-permute-start(bf16[4,288,128]{2,1,0:T(8,128)(2,1)S(1)} %get-tuple-element.59.h_ref), channel_id=1, source_target_pairs={{0,2},{1,3},{2,0},{3,1},{4,6},{5,7},{6,4},{7,5},{8,10},{9,11},{10,... | collective-permute-start | bytes 884744 | tf_op jit(solution)/shard_map/ppermute | solution.py:23
  19.4 1.9 %collective-permute-start.6 = (bf16[496,128]{1,0:T(8,128)(2,1)S(1)}, bf16[496,128]{1,0:T(8,128)(2,1)S(1)}, u32[]{:S(2)}, u32[]{:S(2)}) collective-permute-start(bf16[496,128]{1,0:T(8,128)(2,1)S(1)} %get-tuple-element.54), channel_id=1, source_target_pairs={{0,4},{1,5},{2,6},{3,7},{4,0},{5,1},{6,2},{7,3},{8,12},{9,13},{10,... | collective-permute-start | bytes 380936 | tf_op jit(solution)/shard_map/ppermute | solution.py:23
  21.3 0.5 collective-permute-start.9
  21.8 1.6 %collective-permute-done.8.hy_ref = bf16[4,112,128]{2,1,0:T(8,128)(2,1)S(1)} collective-permute-done((bf16[4,112,128]{2,1,0:T(8,128)(2,1)S(1)}, bf16[4,112,128]{2,1,0:T(8,128)(2,1)S(1)}, u32[]{:S(2)}, u32[]{:S(2)}) %collective-permute-start.8) | collective-permute-done | bytes 114720 | tf_op jit(solution)/shard_map/ppermute | solution.py:23
  23.4 0.5 collective-permute-start.12
  24.7 2.2 %early.1 = (f32[512,128]{1,0:T(8,128)S(1)}, f32[576,128]{1,0:T(8,128)S(1)}, bf16[896,576]{1,0:T(8,128)(2,1)S(1)}, bf16[832,1152]{1,0:T(8,128)(2,1)S(1)}, bf16[70...) custom-call(bf16[512,64]{1,0:T(8,128)(2,1)S(1)} %get-tuple-element.56.x_ref, ...), custom_call_target="tpu_custom_call" | custom-call | flops 1500000000 | bytes 1000000 | tf_op jit(solution)/shard_map/early/pallas_call | solution.py:526
  26.9 1.5 %collective-permute-done.11.value_ref = bf16[4,288,128]{2,1,0:T(8,128)(2,1)S(1)} collective-permute-done((bf16[4,288,128]{2,1,0:T(8,128)(2,1)S(1)}, bf16[4,288,128]{2,1,0:T(8,128)(2,1)S(1)}, u32[]{:S(2)}, u32[]{:S(2)}) %collective-permute-start.11) | collective-permute-done | bytes 294944 | tf_op jit(solution)/shard_map/ppermute | solution.py:23
  28.4 1.1 %half.1 = (bf16[256,1152]{1,0:T(8,128)(2,1)S(1)}, f32[704,256]{1,0:T(8,128)S(1)}, bf16[704,512]{1,0:T(8,128)(2,1)S(1)}) custom-call(bf16[512,512]{1,0:T(8,128)(2,1)S(1)} %get-tuple-element.53.teacher_ref, bf16[496,128]{1,0:T(8,128)(2,1)S(1)} %collective-permute-done.6.edge_a_ref, bf16[496,128]{1,0:T(8,128)(2,1)S(1)} %collective-permute-done.7.edge_b_ref, ...), custom_call_target="tpu_custom_call" | custom-call | flops 1500000000 | bytes 1000000 | tf_op jit(solution)/shard_map/half/pallas_call | solution.py:526
  29.5 0.5 collective-permute-done.13.hyc_ref
  30.0 2.2 %front.1 = (bf16[2,4,32,1152]{3,2,1,0:T(8,128)(2,1)S(1)}, bf16[704,512]{1,0:T(8,128)(2,1)S(1)}, bf16[256,1152]{1,0:T(8,128)(2,1)S(1)}) custom-call(bf16[704,512]{1,0:T(8,128)(2,1)S(1)} %get-tuple-element.60.target_ref, bf16[704,1152]{1,0:T(8,128)(2,1)S(1)} %get-tuple-element.58.first_ref.patch_last_ref, f32[704,256]{1,0:T(8,128)S(1)} %get-tuple-element.61.student_own_ref, ...), custom_call_target="tpu_custom_call" | custom-call | flops 6000000000 | bytes 1000000 | tf_op jit(solution)/shard_map/front/pallas_call | solution.py:526
  32.4 1.5 %back.1 = (f32[2,4,32,1152]{3,2,1,0:T(8,128)S(1)}, bf16[576,128]{1,0:T(8,128)(2,1)S(1)}) custom-call(bf16[704,512]{1,0:T(8,128)(2,1)S(1)} %get-tuple-element.62.slope_ref, f32[576,128]{1,0:T(8,128)S(1)} %get-tuple-element.63.tilt_second_ref, bf16[256,1152]{1,0:T(8,128)(2,1)S(1)} %get-tuple-element.64.w_own_ref, ...), custom_call_target="tpu_custom_call" | custom-call | flops 4000000000 | bytes 1000000 | tf_op jit(solution)/shard_map/back/pallas_call | solution.py:526
  34.3 1.6 %collective-permute-start.15 = (bf16[4,32,1152]{2,1,0:T(8,128)(2,1)S(1)}, bf16[4,32,1152]{2,1,0:T(8,128)(2,1)S(1)}, u32[]{:S(2)}, u32[]{:S(2)}) collective-permute-start(bf16[4,32,1152]{2,1,0:T(8,128)(2,1)S(1)} %get-tuple-element.70), channel_id=1, source_target_pairs={{0,2},{1,3},{2,0},{3,1},{4,6},{5,7},{6,4},{7,5},{8,10},{9,11},{10,... | collective-permute-start | bytes 884744 | tf_op jit(solution)/shard_map/ppermute | solution.py:23
  35.9 1.1 %first.1 = (f32[4,2,8,1728]{3,2,1,0:T(8,128)S(1)}, bf16[4,2,8,1728]{3,2,1,0:T(8,128)(2,1)S(1)}) custom-call(bf16[576,128]{1,0:T(8,128)(2,1)S(1)} %get-tuple-element.68.tie_ref.slope_second_ref, f32[512,128]{1,0:T(8,128)S(1)} %get-tuple-element.75.tilt_first_ref, bf16[896,576]{1,0:T(8,128)(2,1)S(1)} %get-tuple-element.76.patch_first_ref, ...), custom_call_target="tpu_custom_call" | custom-call | flops 2000000000 | bytes 1000000 | tf_op jit(solution)/shard_map/first/pallas_call | solution.py:526
  37.1 1.5 %collective-permute-done.19.got_ref = bf16[4,2,8,1728]{3,2,1,0:T(8,128)(2,1)S(1)} collective-permute-done((bf16[4,2,8,1728]{3,2,1,0:T(8,128)(2,1)S(1)}, bf16[4,2,8,1728]{3,2,1,0:T(8,128)(2,1)S(1)}, u32[]{:S(2)}, u32[]{:S(2)}) %collective-permute-start.19) | collective-permute-done | bytes 221216 | tf_op jit(solution)/shard_map/ppermute | solution.py:23
  38.6 3.7 %collective-permute-start.20 = (bf16[2,8,1728]{2,1,0:T(8,128)(2,1)S(1)}, bf16[2,8,1728]{2,1,0:T(8,128)(2,1)S(1)}, u32[]{:S(2)}, u32[]{:S(2)}) collective-permute-start(bf16[2,8,1728]{2,1,0:T(8,128)(2,1)S(1)} %get-tuple-element.82), channel_id=1, source_target_pairs={{0,12},{1,13},{2,14},{3,15},{4,8},{5,9},{6,10},{7,11},{8,4},{9,5},... | collective-permute-start | bytes 165896 | tf_op jit(solution)/shard_map/ppermute | solution.py:23
  42.3 0.8 %collective-permute-start.22 = (bf16[2,8,1728]{2,1,0:T(8,128)(2,1)S(1)}, bf16[2,8,1728]{2,1,0:T(8,128)(2,1)S(1)}, u32[]{:S(2)}, u32[]{:S(2)}) collective-permute-start(bf16[2,8,1728]{2,1,0:T(8,128)(2,1)S(1)} %get-tuple-element.84), channel_id=1, source_target_pairs={{0,4},{1,5},{2,6},{3,7},{4,0},{5,1},{6,2},{7,3},{8,12},{9,13},{10,... | collective-permute-start | bytes 165896 | tf_op jit(solution)/shard_map/ppermute | solution.py:23
  43.5 3.7 %collective-permute-start.16 = (bf16[32,1152]{1,0:T(8,128)(2,1)S(1)}, bf16[32,1152]{1,0:T(8,128)(2,1)S(1)}, u32[]{:S(2)}, u32[]{:S(2)}) collective-permute-start(bf16[32,1152]{1,0:T(8,128)(2,1)S(1)} %get-tuple-element.72), channel_id=1, source_target_pairs={{0,12},{1,13},{2,14},{3,15},{4,8},{5,9},{6,10},{7,11},{8,4},{9,5},... | collective-permute-start | bytes 221192 | tf_op jit(solution)/shard_map/ppermute | solution.py:23
  47.4 0.6 %collective-permute-start.18 = (bf16[32,1152]{1,0:T(8,128)(2,1)S(1)}, bf16[32,1152]{1,0:T(8,128)(2,1)S(1)}, u32[]{:S(2)}, u32[]{:S(2)}) collective-permute-start(bf16[32,1152]{1,0:T(8,128)(2,1)S(1)} %get-tuple-element.74), channel_id=1, source_target_pairs={{0,4},{1,5},{2,6},{3,7},{4,0},{5,1},{6,2},{7,3},{8,12},{9,13},{10,... | collective-permute-start | bytes 221192 | tf_op jit(solution)/shard_map/ppermute | solution.py:23
  48.0 0.6 %collective-permute-done.21.got2_ref = bf16[2,8,1728]{2,1,0:T(8,128)(2,1)S(1)} collective-permute-done((bf16[2,8,1728]{2,1,0:T(8,128)(2,1)S(1)}, bf16[2,8,1728]{2,1,0:T(8,128)(2,1)S(1)}, u32[]{:S(2)}, u32[]{:S(2)}) %collective-permute-start.21) | collective-permute-done | bytes 55328 | tf_op jit(solution)/shard_map/ppermute | solution.py:23
  48.6 1.0 %collective-permute-start.23 = (bf16[8,1728]{1,0:T(8,128)(2,1)S(1)}, bf16[8,1728]{1,0:T(8,128)(2,1)S(1)}, u32[]{:S(2)}, u32[]{:S(2)}) collective-permute-start(bf16[8,1728]{1,0:T(8,128)(2,1)S(1)} %get-tuple-element.86), channel_id=1, source_target_pairs={{0,2},{1,3},{2,0},{3,1},{4,6},{5,7},{6,4},{7,5},{8,10},{9,11},{10,... | collective-permute-start | bytes 82952 | tf_op jit(solution)/shard_map/ppermute | solution.py:23
  49.6 3.0 %collective-permute-done.23.got_ref = bf16[8,1728]{1,0:T(8,128)(2,1)S(1)} collective-permute-done((bf16[8,1728]{1,0:T(8,128)(2,1)S(1)}, bf16[8,1728]{1,0:T(8,128)(2,1)S(1)}, u32[]{:S(2)}, u32[]{:S(2)}) %collective-permute-start.23) | collective-permute-done | bytes 27680 | tf_op jit(solution)/shard_map/ppermute | solution.py:23
  52.6 1.4 %collective-permute-done.17.got2_ref = bf16[32,1152]{1,0:T(8,128)(2,1)S(1)} collective-permute-done((bf16[32,1152]{1,0:T(8,128)(2,1)S(1)}, bf16[32,1152]{1,0:T(8,128)(2,1)S(1)}, u32[]{:S(2)}, u32[]{:S(2)}) %collective-permute-start.17) | collective-permute-done | bytes 73760 | tf_op jit(solution)/shard_map/ppermute | solution.py:23
  53.9 0.7 %finish.1 = (f32[8,576]{1,0:T(8,128)}, f32[8,1152]{1,0:T(8,128)}, f32[32,1152]{1,0:T(8,128)}) custom-call(f32[32,1152]{1,0:T(8,128)S(1)} %get-tuple-element.71.last_ref, bf16[32,1152]{1,0:T(8,128)(2,1)S(1)} %collective-permute-done.16.got1_ref, bf16[32,1152]{1,0:T(8,128)(2,1)S(1)} %collective-permute-done.17.got2_ref, ...), custom_call_target="tpu_custom_call" | custom-call | flops 1000000 | bytes 1000000 | tf_op jit(solution)/shard_map/finish/pallas_call | solution.py:526
  (33 shorter events, 3.1 us)
Async XLA Ops:
  3.0 10.3 %collective-permute-start = (bf16[1152,128]{1,0:T(8,128)(2,1)}, bf16[1152,128]{1,0:T(8,128)(2,1)S(1)}, u32[]{:S(2)}, u32[]{:S(2)}) collective-permute-start(bf16[1152,128]{1,0:T(8,128)(2,1)} %get-tuple-element.46), channel_id=1, source_target_pairs={{0,2},{1,3},{2,0},{3,1},{4,6},{5,7},{6,4},{7,5},{8,10},{9,11},{10,... | collective-permute-start | bytes 884744 | tf_op jit(solution)/shard_map/ppermute | solution.py:23
  6.1 9.0 %collective-permute-start.5 = (bf16[400,128]{1,0:T(8,128)(2,1)}, bf16[400,128]{1,0:T(8,128)(2,1)S(1)}, u32[]{:S(2)}, u32[]{:S(2)}) collective-permute-start(bf16[400,128]{1,0:T(8,128)(2,1)} %get-tuple-element.50), channel_id=1, source_target_pairs={{0,8},{1,9},{2,10},{3,11},{4,12},{5,13},{6,14},{7,15},{8,0},{9,1},... | collective-permute-start | bytes 307208 | tf_op jit(solution)/shard_map/ppermute | solution.py:23
  8.7 6.4 %collective-permute-start.4 = (bf16[400,128]{1,0:T(8,128)(2,1)}, bf16[400,128]{1,0:T(8,128)(2,1)S(1)}, u32[]{:S(2)}, u32[]{:S(2)}) collective-permute-start(bf16[400,128]{1,0:T(8,128)(2,1)} %get-tuple-element.50), channel_id=1, source_target_pairs={{0,4},{1,5},{2,6},{3,7},{4,0},{5,1},{6,2},{7,3},{8,12},{9,13},{10,... | collective-permute-start | bytes 307208 | tf_op jit(solution)/shard_map/ppermute | solution.py:23
  10.2 6.8 %collective-permute-start.3 = (bf16[400,128]{1,0:T(8,128)(2,1)}, bf16[400,128]{1,0:T(8,128)(2,1)S(1)}, u32[]{:S(2)}, u32[]{:S(2)}) collective-permute-start(bf16[400,128]{1,0:T(8,128)(2,1)} %get-tuple-element.50), channel_id=1, source_target_pairs={{0,12},{1,13},{2,14},{3,15},{4,8},{5,9},{6,10},{7,11},{8,4},{9,5},... | collective-permute-start | bytes 307208 | tf_op jit(solution)/shard_map/ppermute | solution.py:23
  13.3 1.0 %copy-start = (bf16[1040,128]{1,0:T(8,128)(2,1)S(1)}, bf16[1040,128]{1,0:T(8,128)(2,1)}, u32[]{:S(2)}) copy-start(bf16[1040,128]{1,0:T(8,128)(2,1)} %get-tuple-element.45.own_ref) | copy-start | bytes 798724
  14.3 2.8 %collective-permute-start.2 = (bf16[1152,128]{1,0:T(8,128)(2,1)S(1)}, bf16[1152,128]{1,0:T(8,128)(2,1)S(1)}, u32[]{:S(2)}, u32[]{:S(2)}) collective-permute-start(bf16[1152,128]{1,0:T(8,128)(2,1)S(1)} %get-tuple-element.49.across_ref), channel_id=1, source_target_pairs={{0,1},{1,0},{2,3},{3,2},{4,5},{5,4},{6,7},{7,6},{8,9},{9,8},{10,11... | collective-permute-start | bytes 884744 | tf_op jit(solution)/shard_map/ppermute | solution.py:23
  14.3 2.7 %collective-permute-start.1 = (bf16[640,128]{1,0:T(8,128)(2,1)}, bf16[640,128]{1,0:T(8,128)(2,1)S(1)}, u32[]{:S(2)}, u32[]{:S(2)}) collective-permute-start(bf16[640,128]{1,0:T(8,128)(2,1)} %get-tuple-element.48), channel_id=1, source_target_pairs={{0,1},{1,0},{2,3},{3,2},{4,5},{5,4},{6,7},{7,6},{8,9},{9,8},{10,11... | collective-permute-start | bytes 491528 | tf_op jit(solution)/shard_map/ppermute | solution.py:23
  17.3 6.1 %collective-permute-start.8 = (bf16[4,112,128]{2,1,0:T(8,128)(2,1)S(1)}, bf16[4,112,128]{2,1,0:T(8,128)(2,1)S(1)}, u32[]{:S(2)}, u32[]{:S(2)}) collective-permute-start(bf16[4,112,128]{2,1,0:T(8,128)(2,1)S(1)} %get-tuple-element.57.h_ref), channel_id=1, source_target_pairs={{0,2},{1,3},{2,0},{3,1},{4,6},{5,7},{6,4},{7,5},{8,10},{9,11},{10,... | collective-permute-start | bytes 344072 | tf_op jit(solution)/shard_map/ppermute | solution.py:23
  18.4 10.0 %collective-permute-start.11 = (bf16[4,288,128]{2,1,0:T(8,128)(2,1)S(1)}, bf16[4,288,128]{2,1,0:T(8,128)(2,1)S(1)}, u32[]{:S(2)}, u32[]{:S(2)}) collective-permute-start(bf16[4,288,128]{2,1,0:T(8,128)(2,1)S(1)} %get-tuple-element.59.h_ref), channel_id=1, source_target_pairs={{0,2},{1,3},{2,0},{3,1},{4,6},{5,7},{6,4},{7,5},{8,10},{9,11},{10,... | collective-permute-start | bytes 884744 | tf_op jit(solution)/shard_map/ppermute | solution.py:23
  19.4 4.9 %collective-permute-start.6 = (bf16[496,128]{1,0:T(8,128)(2,1)S(1)}, bf16[496,128]{1,0:T(8,128)(2,1)S(1)}, u32[]{:S(2)}, u32[]{:S(2)}) collective-permute-start(bf16[496,128]{1,0:T(8,128)(2,1)S(1)} %get-tuple-element.54), channel_id=1, source_target_pairs={{0,4},{1,5},{2,6},{3,7},{4,0},{5,1},{6,2},{7,3},{8,12},{9,13},{10,... | collective-permute-start | bytes 380936 | tf_op jit(solution)/shard_map/ppermute | solution.py:23
  21.3 3.1 %collective-permute-start.7 = (bf16[496,128]{1,0:T(8,128)(2,1)S(1)}, bf16[496,128]{1,0:T(8,128)(2,1)S(1)}, u32[]{:S(2)}, u32[]{:S(2)}) collective-permute-start(bf16[496,128]{1,0:T(8,128)(2,1)S(1)} %get-tuple-element.55), channel_id=1, source_target_pairs={{0,1},{1,0},{2,3},{3,2},{4,8},{5,9},{6,10},{7,11},{8,4},{9,5},{10,... | collective-permute-start | bytes 380936 | tf_op jit(solution)/shard_map/ppermute | solution.py:34
  21.3 2.1 %collective-permute-start.9 = (bf16[4,112,128]{2,1,0:T(8,128)(2,1)S(1)}, bf16[4,112,128]{2,1,0:T(8,128)(2,1)S(1)}, u32[]{:S(2)}, u32[]{:S(2)}) collective-permute-start(bf16[4,112,128]{2,1,0:T(8,128)(2,1)S(1)} %get-tuple-element.57.h_ref), channel_id=1, source_target_pairs={{0,1},{1,0},{2,3},{3,2},{4,5},{5,4},{6,7},{7,6},{8,9},{9,8},{10,11... | collective-permute-start | bytes 344072 | tf_op jit(solution)/shard_map/ppermute | solution.py:23
  23.4 1.3 %collective-permute-start.10 = (bf16[4,112,128]{2,1,0:T(8,128)(2,1)S(1)}, bf16[4,112,128]{2,1,0:T(8,128)(2,1)S(1)}, u32[]{:S(2)}, u32[]{:S(2)}) collective-permute-start(bf16[4,112,128]{2,1,0:T(8,128)(2,1)S(1)} %collective-permute-done.8.hy_ref), channel_id=1, source_target_pairs={{0,1},{1,0},{2,3},{3,2},{4,5},{5,4},{6,7},{7,6},{8,9},{9,8},{10,11... | collective-permute-start | bytes 344072 | tf_op jit(solution)/shard_map/ppermute | solution.py:23
  23.4 6.1 %collective-permute-start.12 = (bf16[4,288,128]{2,1,0:T(8,128)(2,1)S(1)}, bf16[4,288,128]{2,1,0:T(8,128)(2,1)S(1)}, u32[]{:S(2)}, u32[]{:S(2)}) collective-permute-start(bf16[4,288,128]{2,1,0:T(8,128)(2,1)S(1)} %get-tuple-element.59.h_ref), channel_id=1, source_target_pairs={{0,1},{1,0},{2,3},{3,2},{4,5},{5,4},{6,7},{7,6},{8,9},{9,8},{10,11... | collective-permute-start | bytes 884744 | tf_op jit(solution)/shard_map/ppermute | solution.py:23
  28.4 1.6 %collective-permute-start.13 = (bf16[4,288,128]{2,1,0:T(8,128)(2,1)S(1)}, bf16[4,288,128]{2,1,0:T(8,128)(2,1)S(1)}, u32[]{:S(2)}, u32[]{:S(2)}) collective-permute-start(bf16[4,288,128]{2,1,0:T(8,128)(2,1)S(1)} %after.1.hy_ref), channel_id=1, source_target_pairs={{0,1},{1,0},{2,3},{3,2},{4,5},{5,4},{6,7},{7,6},{8,9},{9,8},{10,11... | collective-permute-start | bytes 884744 | tf_op jit(solution)/shard_map/ppermute | solution.py:23
  32.2 2.1 %collective-permute-start.14 = (bf16[2,4,32,1152]{3,2,1,0:T(8,128)(2,1)S(1)}, bf16[2,4,32,1152]{3,2,1,0:T(8,128)(2,1)S(1)}, u32[]{:S(2)}, u32[]{:S(2)}) collective-permute-start(bf16[2,4,32,1152]{3,2,1,0:T(8,128)(2,1)S(1)} %get-tuple-element.67), channel_id=1, source_target_pairs={{0,1},{1,0},{2,3},{3,2},{4,5},{5,4},{6,7},{7,6},{8,9},{9,8},{10,11... | collective-permute-start | bytes 1769480 | tf_op jit(solution)/shard_map/ppermute | solution.py:23
  34.3 9.1 %collective-permute-start.15 = (bf16[4,32,1152]{2,1,0:T(8,128)(2,1)S(1)}, bf16[4,32,1152]{2,1,0:T(8,128)(2,1)S(1)}, u32[]{:S(2)}, u32[]{:S(2)}) collective-permute-start(bf16[4,32,1152]{2,1,0:T(8,128)(2,1)S(1)} %get-tuple-element.70), channel_id=1, source_target_pairs={{0,2},{1,3},{2,0},{3,1},{4,6},{5,7},{6,4},{7,5},{8,10},{9,11},{10,... | collective-permute-start | bytes 884744 | tf_op jit(solution)/shard_map/ppermute | solution.py:23
  37.0 1.6 %collective-permute-start.19 = (bf16[4,2,8,1728]{3,2,1,0:T(8,128)(2,1)S(1)}, bf16[4,2,8,1728]{3,2,1,0:T(8,128)(2,1)S(1)}, u32[]{:S(2)}, u32[]{:S(2)}) collective-permute-start(bf16[4,2,8,1728]{3,2,1,0:T(8,128)(2,1)S(1)} %get-tuple-element.80), channel_id=1, source_target_pairs={{0,1},{1,0},{2,3},{3,2},{4,5},{5,4},{6,7},{7,6},{8,9},{9,8},{10,11... | collective-permute-start | bytes 663560 | tf_op jit(solution)/shard_map/ppermute | solution.py:23
  38.6 8.7 %collective-permute-start.20 = (bf16[2,8,1728]{2,1,0:T(8,128)(2,1)S(1)}, bf16[2,8,1728]{2,1,0:T(8,128)(2,1)S(1)}, u32[]{:S(2)}, u32[]{:S(2)}) collective-permute-start(bf16[2,8,1728]{2,1,0:T(8,128)(2,1)S(1)} %get-tuple-element.82), channel_id=1, source_target_pairs={{0,12},{1,13},{2,14},{3,15},{4,8},{5,9},{6,10},{7,11},{8,4},{9,5},... | collective-permute-start | bytes 165896 | tf_op jit(solution)/shard_map/ppermute | solution.py:23
  42.3 6.3 %collective-permute-start.21 = (bf16[2,8,1728]{2,1,0:T(8,128)(2,1)S(1)}, bf16[2,8,1728]{2,1,0:T(8,128)(2,1)S(1)}, u32[]{:S(2)}, u32[]{:S(2)}) collective-permute-start(bf16[2,8,1728]{2,1,0:T(8,128)(2,1)S(1)} %get-tuple-element.83), channel_id=1, source_target_pairs={{0,8},{1,9},{2,10},{3,11},{4,12},{5,13},{6,14},{7,15},{8,0},{9,1},... | collective-permute-start | bytes 165896 | tf_op jit(solution)/shard_map/ppermute | solution.py:23
  42.3 6.3 %collective-permute-start.22 = (bf16[2,8,1728]{2,1,0:T(8,128)(2,1)S(1)}, bf16[2,8,1728]{2,1,0:T(8,128)(2,1)S(1)}, u32[]{:S(2)}, u32[]{:S(2)}) collective-permute-start(bf16[2,8,1728]{2,1,0:T(8,128)(2,1)S(1)} %get-tuple-element.84), channel_id=1, source_target_pairs={{0,4},{1,5},{2,6},{3,7},{4,0},{5,1},{6,2},{7,3},{8,12},{9,13},{10,... | collective-permute-start | bytes 165896 | tf_op jit(solution)/shard_map/ppermute | solution.py:23
  43.5 9.0 %collective-permute-start.16 = (bf16[32,1152]{1,0:T(8,128)(2,1)S(1)}, bf16[32,1152]{1,0:T(8,128)(2,1)S(1)}, u32[]{:S(2)}, u32[]{:S(2)}) collective-permute-start(bf16[32,1152]{1,0:T(8,128)(2,1)S(1)} %get-tuple-element.72), channel_id=1, source_target_pairs={{0,12},{1,13},{2,14},{3,15},{4,8},{5,9},{6,10},{7,11},{8,4},{9,5},... | collective-permute-start | bytes 221192 | tf_op jit(solution)/shard_map/ppermute | solution.py:23
  47.2 6.7 %collective-permute-start.17 = (bf16[32,1152]{1,0:T(8,128)(2,1)S(1)}, bf16[32,1152]{1,0:T(8,128)(2,1)S(1)}, u32[]{:S(2)}, u32[]{:S(2)}) collective-permute-start(bf16[32,1152]{1,0:T(8,128)(2,1)S(1)} %get-tuple-element.73), channel_id=1, source_target_pairs={{0,8},{1,9},{2,10},{3,11},{4,12},{5,13},{6,14},{7,15},{8,0},{9,1},... | collective-permute-start | bytes 221192 | tf_op jit(solution)/shard_map/ppermute | solution.py:23
  47.4 6.6 %collective-permute-start.18 = (bf16[32,1152]{1,0:T(8,128)(2,1)S(1)}, bf16[32,1152]{1,0:T(8,128)(2,1)S(1)}, u32[]{:S(2)}, u32[]{:S(2)}) collective-permute-start(bf16[32,1152]{1,0:T(8,128)(2,1)S(1)} %get-tuple-element.74), channel_id=1, source_target_pairs={{0,4},{1,5},{2,6},{3,7},{4,0},{5,1},{6,2},{7,3},{8,12},{9,13},{10,... | collective-permute-start | bytes 221192 | tf_op jit(solution)/shard_map/ppermute | solution.py:23
  48.6 3.9 %collective-permute-start.23 = (bf16[8,1728]{1,0:T(8,128)(2,1)S(1)}, bf16[8,1728]{1,0:T(8,128)(2,1)S(1)}, u32[]{:S(2)}, u32[]{:S(2)}) collective-permute-start(bf16[8,1728]{1,0:T(8,128)(2,1)S(1)} %get-tuple-element.86), channel_id=1, source_target_pairs={{0,2},{1,3},{2,0},{3,1},{4,6},{5,7},{6,4},{7,5},{8,10},{9,11},{10,... | collective-permute-start | bytes 82952 | tf_op jit(solution)/shard_map/ppermute | solution.py:23

commit v7 on v6

--- a/solution.py
+++ b/solution.py
@@ -184,7 +184,7 @@
     )
 
 
-def hold_kernel(own_ref, across_ref, held_ref, same_ref):
+def hold_kernel(own_ref, far_ref, held_ref, same_ref):
     held_ref[...] = own_ref[...]
 
 
@@ -207,14 +207,10 @@
     near_ref,
     across_ref,
     diagonal_ref,
-    last_ref,
-    small_ref,
     x_ref,
     teacher_ref,
     edge_a_ref,
     edge_b_ref,
-    same_last_ref,
-    same_small_ref,
 ):
     depth, channels = x_ref.shape[1], teacher_ref.shape[1]
     low = position(BLOCKS)[1]
@@ -578,18 +574,32 @@
     far = {k: swap(shard, 4 * k * fold) for k in (1, 2, 3)}
     near = swap(near, 1)
     anywhere = pl.BlockSpec(memory_space=pl.ANY)
-    held, across = call(
+
+    def behind(value, first):
+        return call(
+            after_kernel,
+            "after",
+            (value, first),
+            [(value.shape, value.dtype)],
+            [],
+            1_000_000,
+            {0: anywhere, 1: anywhere},
+            out_spaces={0: anywhere},
+            aliases={0: 0},
+        )[0]
+
+    diagonal = swap(across, 1)
+    held, far[1] = call(
         hold_kernel,
         "hold",
-        (own_class, across),
-        [(own_class.shape, bf16), (across.shape, bf16)],
+        (own_class, far[1]),
+        [(own_class.shape, bf16), (shard.shape, bf16)],
         [],
         1_000_000,
         {1: anywhere},
         out_spaces={1: anywhere},
         aliases={1: 1},
     )
-    diagonal = swap(across, 1)
     edge_t, edge_x = HALO_SLOPE * rows, HALO_X * rows
     edge = edge_t * len(tiles(channels)) + edge_x - edge_t
     part_last = r_last * len(tiles(9 * hidden))
@@ -601,23 +611,18 @@
         [],
         STACK_COST,
     )
-    x_band, t_band, edge_a, edge_b, held_last, held_small = call(
+    x_band, t_band, edge_a, edge_b = call(
         functools.partial(collect_kernel, cells, edge_t, edge_x),
         "collect",
-        (held, near, across, diagonal, held_last, held_small),
+        (held, near, across, diagonal),
         [
             ((own * rows, in_depth), bf16),
             ((own * rows, channels), bf16),
             ((edge, LANES), bf16),
             ((edge, LANES), bf16),
-            (held_last.shape, bf16),
-            (held_small.shape, bf16),
         ],
         [],
         1_000_000,
-        {4: anywhere, 5: anywhere},
-        out_spaces={4: anywhere, 5: anywhere},
-        aliases={4: 4, 5: 5},
     )
 
     small_y = swap(held_small, 2 * fold)
@@ -643,17 +648,7 @@
         [((BLOCKS, 2 * r_small, 9 * hidden), f32)],
         EARLY_COST,
     )
-    (last_y,) = call(
-        after_kernel,
-        "after",
-        (last_y, patch_last),
-        [(last_y.shape, bf16)],
-        [],
-        1_000_000,
-        {0: anywhere, 1: anywhere},
-        out_spaces={0: anywhere},
-        aliases={0: 0},
-    )
+    last_y = behind(last_y, patch_last)
     half = channels // 2
     last_c, last_yc = swap(held_last, fold), swap(last_y, fold)
     w_own, student_own, target = call(
@@ -730,7 +725,7 @@
     out_first, out_middle, out_last = call(
         finish_kernel,
         "finish",
-        (last[0], last_got[3], last_got[2], last_got[1], small_kept, small_got),
+        (last[0], last_got[2], last_got[3], last_got[1], small_kept, small_got),
         [(w.shape, f32) for w in (w_first, w_middle, w_last)],
         [],
         1_000_000,

time: 54.8 us -> 53.7 us (0.980)
  starting transfers between devices: 24.7 us -> 23.9 us
    ppermute x23, starting transfers between devices: 24.7 us -> 23.9 us  [swap(): return lax.ppermute(array, 'cols', [(i, i ^ mask) for i in range(size)])]
  transfers between devices with their start and end apart: 24 -> 24, of which waited for: 14 -> 12; matrix products, arithmetic and copies ran while one was open for 0% -> 0% of each run, Pallas kernels for 11% -> 12%
where the time goes in v7:
time: 53.7 us; the launch traced here: 53.6 us
  starting transfers between devices  23.9 us (45%)
  waiting for transfers between devices  16.3 us (30%)
  Pallas kernels  11.7 us (22%)
  local copies, waits for them, and re-layouts  0.95 us (2%)
  between operations  0.77 us (1%)
    ppermute x23, starting transfers between devices, swap(): return lax.ppermute(array, 'cols', [(i, i ^ mask) for i in range(size)])  23.9 us
    ppermute x23, waiting for transfers between devices, swap(): return lax.ppermute(array, 'cols', [(i, i ^ mask) for i in range(size)])  16.3 us
    pallas_call x15, Pallas kernels, call(): pl.pallas_call(kernel, in_specs=[spaces.get(i, vmem) for i in range(len(i...  11.7 us
  transfers between devices with their start and end apart: 24, of which 12 were waited for; matrix products, arithmetic and copies ran while one was open for 0% of the time, Pallas kernels for 12%

profile of v7, /device:TPU:0, one launch (start us, length us, event | category | flops | bytes accessed | tf_op | source)
XLA Modules:
  0.0 53.6 jit_solution(1134963386954728180)
XLA Ops:
  0.6 2.4 %deal.1 = (bf16[1040,128]{1,0:T(8,128)(2,1)}, bf16[640,128]{1,0:T(8,128)(2,1)}, bf16[1152,128]{1,0:T(8,128)(2,1)}, bf16[400,128]{1,0:T(8,128)(2,1)}) custom-call(bf16[32,1024]{1,0:T(8,128)(2,1)} %x_hbm.1, bf16[32,16,512]{2,1,0:T(8,128)(2,1)} %teacher_hbm.1, bf16[8,576]{1,0:T(8,128)(2,1)} %w_first_hbm.1, bf16[8,1152]{1,0:T(8,128)(2,1)} %w_middle_hbm.1, ...), custom_call_target="tpu_custom_call" | custom-call | flops 600000000 | bytes 1000000 | tf_op jit(solution)/shard_map/deal/pallas_call | solution.py:522
  3.0 3.0 %collective-permute-start.2 = (bf16[1152,128]{1,0:T(8,128)(2,1)}, bf16[1152,128]{1,0:T(8,128)(2,1)S(1)}, u32[]{:S(2)}, u32[]{:S(2)}) collective-permute-start(bf16[1152,128]{1,0:T(8,128)(2,1)} %get-tuple-element.47), channel_id=1, source_target_pairs={{0,2},{1,3},{2,0},{3,1},{4,6},{5,7},{6,4},{7,5},{8,10},{9,11},{10,... | collective-permute-start | bytes 884744 | tf_op jit(solution)/shard_map/ppermute | solution.py:23
  6.1 1.6 %collective-permute-start = (bf16[400,128]{1,0:T(8,128)(2,1)}, bf16[400,128]{1,0:T(8,128)(2,1)S(1)}, u32[]{:S(2)}, u32[]{:S(2)}) collective-permute-start(bf16[400,128]{1,0:T(8,128)(2,1)} %get-tuple-element.44), channel_id=1, source_target_pairs={{0,4},{1,5},{2,6},{3,7},{4,0},{5,1},{6,2},{7,3},{8,12},{9,13},{10,... | collective-permute-start | bytes 307208 | tf_op jit(solution)/shard_map/ppermute | solution.py:23
  7.6 2.6 %collective-permute-start.7 = (bf16[400,128]{1,0:T(8,128)(2,1)}, bf16[400,128]{1,0:T(8,128)(2,1)S(1)}, u32[]{:S(2)}, u32[]{:S(2)}) collective-permute-start(bf16[400,128]{1,0:T(8,128)(2,1)} %get-tuple-element.44), channel_id=1, source_target_pairs={{0,8},{1,9},{2,10},{3,11},{4,12},{5,13},{6,14},{7,15},{8,0},{9,1},... | collective-permute-start | bytes 307208 | tf_op jit(solution)/shard_map/ppermute | solution.py:23
  10.5 1.5 %collective-permute-done.far_ref = bf16[400,128]{1,0:T(8,128)(2,1)S(1)} collective-permute-done((bf16[400,128]{1,0:T(8,128)(2,1)}, bf16[400,128]{1,0:T(8,128)(2,1)S(1)}, u32[]{:S(2)}, u32[]{:S(2)}) %collective-permute-start) | collective-permute-done | bytes 102432 | tf_op jit(solution)/shard_map/ppermute | solution.py:23
  12.0 0.9 %copy-done = bf16[1040,128]{1,0:T(8,128)(2,1)S(1)} copy-done((bf16[1040,128]{1,0:T(8,128)(2,1)S(1)}, bf16[1040,128]{1,0:T(8,128)(2,1)}, u32[]{:S(2)}) %copy-start) | copy-done | bytes 266264
  13.3 5.0 %collective-permute-done.7.far2_ref = bf16[400,128]{1,0:T(8,128)(2,1)S(1)} collective-permute-done((bf16[400,128]{1,0:T(8,128)(2,1)}, bf16[400,128]{1,0:T(8,128)(2,1)S(1)}, u32[]{:S(2)}, u32[]{:S(2)}) %collective-permute-start.7) | collective-permute-done | bytes 102432 | tf_op jit(solution)/shard_map/ppermute | solution.py:23
  18.4 0.6 %collective-permute-start.8 = (bf16[4,112,128]{2,1,0:T(8,128)(2,1)S(1)}, bf16[4,112,128]{2,1,0:T(8,128)(2,1)S(1)}, u32[]{:S(2)}, u32[]{:S(2)}) collective-permute-start(bf16[4,112,128]{2,1,0:T(8,128)(2,1)S(1)} %get-tuple-element.53.h_ref), channel_id=1, source_target_pairs={{0,2},{1,3},{2,0},{3,1},{4,6},{5,7},{6,4},{7,5},{8,10},{9,11},{10,... | collective-permute-start | bytes 344072 | tf_op jit(solution)/shard_map/ppermute | solution.py:23
  18.9 1.5 %collective-permute-start.11 = (bf16[4,288,128]{2,1,0:T(8,128)(2,1)S(1)}, bf16[4,288,128]{2,1,0:T(8,128)(2,1)S(1)}, u32[]{:S(2)}, u32[]{:S(2)}) collective-permute-start(bf16[4,288,128]{2,1,0:T(8,128)(2,1)S(1)} %get-tuple-element.55.h_ref), channel_id=1, source_target_pairs={{0,2},{1,3},{2,0},{3,1},{4,6},{5,7},{6,4},{7,5},{8,10},{9,11},{10,... | collective-permute-start | bytes 884744 | tf_op jit(solution)/shard_map/ppermute | solution.py:23
  20.7 1.7 %collective-permute-start.4 = (bf16[496,128]{1,0:T(8,128)(2,1)S(1)}, bf16[496,128]{1,0:T(8,128)(2,1)S(1)}, u32[]{:S(2)}, u32[]{:S(2)}) collective-permute-start(bf16[496,128]{1,0:T(8,128)(2,1)S(1)} %get-tuple-element.49), channel_id=1, source_target_pairs={{0,4},{1,5},{2,6},{3,7},{4,0},{5,1},{6,2},{7,3},{8,12},{9,13},{10,... | collective-permute-start | bytes 380936 | tf_op jit(solution)/shard_map/ppermute | solution.py:23
  22.4 0.5 collective-permute-start.9
  22.9 1.5 %collective-permute-done.8.hy_ref = bf16[4,112,128]{2,1,0:T(8,128)(2,1)S(1)} collective-permute-done((bf16[4,112,128]{2,1,0:T(8,128)(2,1)S(1)}, bf16[4,112,128]{2,1,0:T(8,128)(2,1)S(1)}, u32[]{:S(2)}, u32[]{:S(2)}) %collective-permute-start.8) | collective-permute-done | bytes 114720 | tf_op jit(solution)/shard_map/ppermute | solution.py:23
  24.4 0.5 collective-permute-start.12
  24.9 0.8 %collective-permute-done.10.hyc_ref = bf16[4,112,128]{2,1,0:T(8,128)(2,1)S(1)} collective-permute-done((bf16[4,112,128]{2,1,0:T(8,128)(2,1)S(1)}, bf16[4,112,128]{2,1,0:T(8,128)(2,1)S(1)}, u32[]{:S(2)}, u32[]{:S(2)}) %collective-permute-start.10) | collective-permute-done | bytes 114720 | tf_op jit(solution)/shard_map/ppermute | solution.py:23
  25.8 2.2 %early.1 = (f32[512,128]{1,0:T(8,128)S(1)}, f32[576,128]{1,0:T(8,128)S(1)}, bf16[896,576]{1,0:T(8,128)(2,1)S(1)}, bf16[832,1152]{1,0:T(8,128)(2,1)S(1)}, bf16[70...) custom-call(bf16[512,64]{1,0:T(8,128)(2,1)S(1)} %get-tuple-element.51.x_ref, ...), custom_call_target="tpu_custom_call" | custom-call | flops 1500000000 | bytes 1000000 | tf_op jit(solution)/shard_map/early/pallas_call | solution.py:522
  28.2 1.1 %half.1 = (bf16[256,1152]{1,0:T(8,128)(2,1)S(1)}, f32[704,256]{1,0:T(8,128)S(1)}, bf16[704,512]{1,0:T(8,128)(2,1)S(1)}) custom-call(bf16[512,512]{1,0:T(8,128)(2,1)S(1)} %get-tuple-element.48.teacher_ref, bf16[496,128]{1,0:T(8,128)(2,1)S(1)} %collective-permute-done.4.edge_a_ref, bf16[496,128]{1,0:T(8,128)(2,1)S(1)} %collective-permute-done.5.edge_b_ref, ...), custom_call_target="tpu_custom_call" | custom-call | flops 1500000000 | bytes 1000000 | tf_op jit(solution)/shard_map/half/pallas_call | solution.py:522
  29.7 2.2 %front.1 = (bf16[2,4,32,1152]{3,2,1,0:T(8,128)(2,1)S(1)}, bf16[704,512]{1,0:T(8,128)(2,1)S(1)}, bf16[256,1152]{1,0:T(8,128)(2,1)S(1)}) custom-call(bf16[704,512]{1,0:T(8,128)(2,1)S(1)} %get-tuple-element.56.target_ref, bf16[704,1152]{1,0:T(8,128)(2,1)S(1)} %get-tuple-element.54.first_ref.patch_last_ref, f32[704,256]{1,0:T(8,128)S(1)} %get-tuple-element.57.student_own_ref, ...), custom_call_target="tpu_custom_call" | custom-call | flops 6000000000 | bytes 1000000 | tf_op jit(solution)/shard_map/front/pallas_call | solution.py:522
  32.1 1.5 %back.1 = (f32[2,4,32,1152]{3,2,1,0:T(8,128)S(1)}, bf16[576,128]{1,0:T(8,128)(2,1)S(1)}) custom-call(bf16[704,512]{1,0:T(8,128)(2,1)S(1)} %get-tuple-element.58.slope_ref, f32[576,128]{1,0:T(8,128)S(1)} %get-tuple-element.59.tilt_second_ref, bf16[256,1152]{1,0:T(8,128)(2,1)S(1)} %get-tuple-element.60.w_own_ref, ...), custom_call_target="tpu_custom_call" | custom-call | flops 4000000000 | bytes 1000000 | tf_op jit(solution)/shard_map/back/pallas_call | solution.py:522
  33.5 0.4 collective-permute-done.14.got_ref
  34.0 0.6 %collective-permute-start.15 = (bf16[4,32,1152]{2,1,0:T(8,128)(2,1)S(1)}, bf16[4,32,1152]{2,1,0:T(8,128)(2,1)S(1)}, u32[]{:S(2)}, u32[]{:S(2)}) collective-permute-start(bf16[4,32,1152]{2,1,0:T(8,128)(2,1)S(1)} %get-tuple-element.66), channel_id=1, source_target_pairs={{0,2},{1,3},{2,0},{3,1},{4,6},{5,7},{6,4},{7,5},{8,10},{9,11},{10,... | collective-permute-start | bytes 884744 | tf_op jit(solution)/shard_map/ppermute | solution.py:23
  34.6 1.1 %first.1 = (f32[4,2,8,1728]{3,2,1,0:T(8,128)S(1)}, bf16[4,2,8,1728]{3,2,1,0:T(8,128)(2,1)S(1)}) custom-call(bf16[576,128]{1,0:T(8,128)(2,1)S(1)} %get-tuple-element.64.tie_ref.slope_second_ref, f32[512,128]{1,0:T(8,128)S(1)} %get-tuple-element.71.tilt_first_ref, bf16[896,576]{1,0:T(8,128)(2,1)S(1)} %get-tuple-element.72.patch_first_ref, ...), custom_call_target="tpu_custom_call" | custom-call | flops 2000000000 | bytes 1000000 | tf_op jit(solution)/shard_map/first/pallas_call | solution.py:522
  35.8 1.5 %collective-permute-done.19.got_ref = bf16[4,2,8,1728]{3,2,1,0:T(8,128)(2,1)S(1)} collective-permute-done((bf16[4,2,8,1728]{3,2,1,0:T(8,128)(2,1)S(1)}, bf16[4,2,8,1728]{3,2,1,0:T(8,128)(2,1)S(1)}, u32[]{:S(2)}, u32[]{:S(2)}) %collective-permute-start.19) | collective-permute-done | bytes 221216 | tf_op jit(solution)/shard_map/ppermute | solution.py:23
  37.4 2.6 %collective-permute-start.20 = (bf16[2,8,1728]{2,1,0:T(8,128)(2,1)S(1)}, bf16[2,8,1728]{2,1,0:T(8,128)(2,1)S(1)}, u32[]{:S(2)}, u32[]{:S(2)}) collective-permute-start(bf16[2,8,1728]{2,1,0:T(8,128)(2,1)S(1)} %get-tuple-element.78), channel_id=1, source_target_pairs={{0,12},{1,13},{2,14},{3,15},{4,8},{5,9},{6,10},{7,11},{8,4},{9,5},... | collective-permute-start | bytes 165896 | tf_op jit(solution)/shard_map/ppermute | solution.py:23
  39.9 1.0 %collective-permute-start.21 = (bf16[2,8,1728]{2,1,0:T(8,128)(2,1)S(1)}, bf16[2,8,1728]{2,1,0:T(8,128)(2,1)S(1)}, u32[]{:S(2)}, u32[]{:S(2)}) collective-permute-start(bf16[2,8,1728]{2,1,0:T(8,128)(2,1)S(1)} %get-tuple-element.79), channel_id=1, source_target_pairs={{0,8},{1,9},{2,10},{3,11},{4,12},{5,13},{6,14},{7,15},{8,0},{9,1},... | collective-permute-start | bytes 165896 | tf_op jit(solution)/shard_map/ppermute | solution.py:23
  40.9 0.9 %collective-permute-start.22 = (bf16[2,8,1728]{2,1,0:T(8,128)(2,1)S(1)}, bf16[2,8,1728]{2,1,0:T(8,128)(2,1)S(1)}, u32[]{:S(2)}, u32[]{:S(2)}) collective-permute-start(bf16[2,8,1728]{2,1,0:T(8,128)(2,1)S(1)} %get-tuple-element.80), channel_id=1, source_target_pairs={{0,4},{1,5},{2,6},{3,7},{4,0},{5,1},{6,2},{7,3},{8,12},{9,13},{10,... | collective-permute-start | bytes 165896 | tf_op jit(solution)/shard_map/ppermute | solution.py:23
  41.8 1.3 %collective-permute-done.15.got_ref = bf16[4,32,1152]{2,1,0:T(8,128)(2,1)S(1)} collective-permute-done((bf16[4,32,1152]{2,1,0:T(8,128)(2,1)S(1)}, bf16[4,32,1152]{2,1,0:T(8,128)(2,1)S(1)}, u32[]{:S(2)}, u32[]{:S(2)}) %collective-permute-start.15) | collective-permute-done | bytes 294944 | tf_op jit(solution)/shard_map/ppermute | solution.py:23
  43.2 3.0 %collective-permute-start.16 = (bf16[32,1152]{1,0:T(8,128)(2,1)S(1)}, bf16[32,1152]{1,0:T(8,128)(2,1)S(1)}, u32[]{:S(2)}, u32[]{:S(2)}) collective-permute-start(bf16[32,1152]{1,0:T(8,128)(2,1)S(1)} %get-tuple-element.68), channel_id=1, source_target_pairs={{0,8},{1,9},{2,10},{3,11},{4,12},{5,13},{6,14},{7,15},{8,0},{9,1},... | collective-permute-start | bytes 221192 | tf_op jit(solution)/shard_map/ppermute | solution.py:23
  46.2 1.5 %collective-permute-start.17 = (bf16[32,1152]{1,0:T(8,128)(2,1)S(1)}, bf16[32,1152]{1,0:T(8,128)(2,1)S(1)}, u32[]{:S(2)}, u32[]{:S(2)}) collective-permute-start(bf16[32,1152]{1,0:T(8,128)(2,1)S(1)} %get-tuple-element.69), channel_id=1, source_target_pairs={{0,12},{1,13},{2,14},{3,15},{4,8},{5,9},{6,10},{7,11},{8,4},{9,5},... | collective-permute-start | bytes 221192 | tf_op jit(solution)/shard_map/ppermute | solution.py:23
  47.7 1.6 %collective-permute-start.23 = (bf16[8,1728]{1,0:T(8,128)(2,1)S(1)}, bf16[8,1728]{1,0:T(8,128)(2,1)S(1)}, u32[]{:S(2)}, u32[]{:S(2)}) collective-permute-start(bf16[8,1728]{1,0:T(8,128)(2,1)S(1)} %get-tuple-element.82), channel_id=1, source_target_pairs={{0,2},{1,3},{2,0},{3,1},{4,6},{5,7},{6,4},{7,5},{8,10},{9,11},{10,... | collective-permute-start | bytes 82952 | tf_op jit(solution)/shard_map/ppermute | solution.py:23
  49.3 2.3 %collective-permute-done.23.got_ref = bf16[8,1728]{1,0:T(8,128)(2,1)S(1)} collective-permute-done((bf16[8,1728]{1,0:T(8,128)(2,1)S(1)}, bf16[8,1728]{1,0:T(8,128)(2,1)S(1)}, u32[]{:S(2)}, u32[]{:S(2)}) %collective-permute-start.23) | collective-permute-done | bytes 27680 | tf_op jit(solution)/shard_map/ppermute | solution.py:23
  51.6 0.9 %collective-permute-done.17.got2_ref = bf16[32,1152]{1,0:T(8,128)(2,1)S(1)} collective-permute-done((bf16[32,1152]{1,0:T(8,128)(2,1)S(1)}, bf16[32,1152]{1,0:T(8,128)(2,1)S(1)}, u32[]{:S(2)}, u32[]{:S(2)}) %collective-permute-start.17) | collective-permute-done | bytes 73760 | tf_op jit(solution)/shard_map/ppermute | solution.py:23
  52.9 0.7 %finish.1 = (f32[8,576]{1,0:T(8,128)}, f32[8,1152]{1,0:T(8,128)}, f32[32,1152]{1,0:T(8,128)}) custom-call(f32[32,1152]{1,0:T(8,128)S(1)} %get-tuple-element.67.last_ref, bf16[32,1152]{1,0:T(8,128)(2,1)S(1)} %collective-permute-done.16.got1_ref, bf16[32,1152]{1,0:T(8,128)(2,1)S(1)} %collective-permute-done.17.got2_ref, ...), custom_call_target="tpu_custom_call" | custom-call | flops 1000000 | bytes 1000000 | tf_op jit(solution)/shard_map/finish/pallas_call | solution.py:522
  (33 shorter events, 2.3 us)
Async XLA Ops:
  3.0 10.3 %collective-permute-start.2 = (bf16[1152,128]{1,0:T(8,128)(2,1)}, bf16[1152,128]{1,0:T(8,128)(2,1)S(1)}, u32[]{:S(2)}, u32[]{:S(2)}) collective-permute-start(bf16[1152,128]{1,0:T(8,128)(2,1)} %get-tuple-element.47), channel_id=1, source_target_pairs={{0,2},{1,3},{2,0},{3,1},{4,6},{5,7},{6,4},{7,5},{8,10},{9,11},{10,... | collective-permute-start | bytes 884744 | tf_op jit(solution)/shard_map/ppermute | solution.py:23
  6.1 5.9 %collective-permute-start = (bf16[400,128]{1,0:T(8,128)(2,1)}, bf16[400,128]{1,0:T(8,128)(2,1)S(1)}, u32[]{:S(2)}, u32[]{:S(2)}) collective-permute-start(bf16[400,128]{1,0:T(8,128)(2,1)} %get-tuple-element.44), channel_id=1, source_target_pairs={{0,4},{1,5},{2,6},{3,7},{4,0},{5,1},{6,2},{7,3},{8,12},{9,13},{10,... | collective-permute-start | bytes 307208 | tf_op jit(solution)/shard_map/ppermute | solution.py:23
  7.6 10.7 %collective-permute-start.7 = (bf16[400,128]{1,0:T(8,128)(2,1)}, bf16[400,128]{1,0:T(8,128)(2,1)S(1)}, u32[]{:S(2)}, u32[]{:S(2)}) collective-permute-start(bf16[400,128]{1,0:T(8,128)(2,1)} %get-tuple-element.44), channel_id=1, source_target_pairs={{0,8},{1,9},{2,10},{3,11},{4,12},{5,13},{6,14},{7,15},{8,0},{9,1},... | collective-permute-start | bytes 307208 | tf_op jit(solution)/shard_map/ppermute | solution.py:23
  10.2 8.1 %collective-permute-start.6 = (bf16[400,128]{1,0:T(8,128)(2,1)}, bf16[400,128]{1,0:T(8,128)(2,1)S(1)}, u32[]{:S(2)}, u32[]{:S(2)}) collective-permute-start(bf16[400,128]{1,0:T(8,128)(2,1)} %get-tuple-element.44), channel_id=1, source_target_pairs={{0,12},{1,13},{2,14},{3,15},{4,8},{5,9},{6,10},{7,11},{8,4},{9,5},... | collective-permute-start | bytes 307208 | tf_op jit(solution)/shard_map/ppermute | solution.py:23
  10.5 10.0 %collective-permute-start.1 = (bf16[640,128]{1,0:T(8,128)(2,1)}, bf16[640,128]{1,0:T(8,128)(2,1)S(1)}, u32[]{:S(2)}, u32[]{:S(2)}) collective-permute-start(bf16[640,128]{1,0:T(8,128)(2,1)} %get-tuple-element.46), channel_id=1, source_target_pairs={{0,1},{1,0},{2,3},{3,2},{4,5},{5,4},{6,7},{7,6},{8,9},{9,8},{10,11... | collective-permute-start | bytes 491528 | tf_op jit(solution)/shard_map/ppermute | solution.py:23
  11.9 1.0 %copy-start = (bf16[1040,128]{1,0:T(8,128)(2,1)S(1)}, bf16[1040,128]{1,0:T(8,128)(2,1)}, u32[]{:S(2)}) copy-start(bf16[1040,128]{1,0:T(8,128)(2,1)} %get-tuple-element.43.own_ref) | copy-start | bytes 798724
  13.3 7.2 %collective-permute-start.3 = (bf16[1152,128]{1,0:T(8,128)(2,1)S(1)}, bf16[1152,128]{1,0:T(8,128)(2,1)S(1)}, u32[]{:S(2)}, u32[]{:S(2)}) collective-permute-start(bf16[1152,128]{1,0:T(8,128)(2,1)S(1)} %collective-permute-done.2.across_ref), channel_id=1, source_target_pairs={{0,1},{1,0},{2,3},{3,2},{4,5},{5,4},{6,7},{7,6},{8,9},{9,8},{10,11... | collective-permute-start | bytes 884744 | tf_op jit(solution)/shard_map/ppermute | solution.py:23
  18.4 6.1 %collective-permute-start.8 = (bf16[4,112,128]{2,1,0:T(8,128)(2,1)S(1)}, bf16[4,112,128]{2,1,0:T(8,128)(2,1)S(1)}, u32[]{:S(2)}, u32[]{:S(2)}) collective-permute-start(bf16[4,112,128]{2,1,0:T(8,128)(2,1)S(1)} %get-tuple-element.53.h_ref), channel_id=1, source_target_pairs={{0,2},{1,3},{2,0},{3,1},{4,6},{5,7},{6,4},{7,5},{8,10},{9,11},{10,... | collective-permute-start | bytes 344072 | tf_op jit(solution)/shard_map/ppermute | solution.py:23
  18.9 9.1 %collective-permute-start.11 = (bf16[4,288,128]{2,1,0:T(8,128)(2,1)S(1)}, bf16[4,288,128]{2,1,0:T(8,128)(2,1)S(1)}, u32[]{:S(2)}, u32[]{:S(2)}) collective-permute-start(bf16[4,288,128]{2,1,0:T(8,128)(2,1)S(1)} %get-tuple-element.55.h_ref), channel_id=1, source_target_pairs={{0,2},{1,3},{2,0},{3,1},{4,6},{5,7},{6,4},{7,5},{8,10},{9,11},{10,... | collective-permute-start | bytes 884744 | tf_op jit(solution)/shard_map/ppermute | solution.py:23
  20.7 5.1 %collective-permute-start.4 = (bf16[496,128]{1,0:T(8,128)(2,1)S(1)}, bf16[496,128]{1,0:T(8,128)(2,1)S(1)}, u32[]{:S(2)}, u32[]{:S(2)}) collective-permute-start(bf16[496,128]{1,0:T(8,128)(2,1)S(1)} %get-tuple-element.49), channel_id=1, source_target_pairs={{0,4},{1,5},{2,6},{3,7},{4,0},{5,1},{6,2},{7,3},{8,12},{9,13},{10,... | collective-permute-start | bytes 380936 | tf_op jit(solution)/shard_map/ppermute | solution.py:23
  22.4 3.3 %collective-permute-start.5 = (bf16[496,128]{1,0:T(8,128)(2,1)S(1)}, bf16[496,128]{1,0:T(8,128)(2,1)S(1)}, u32[]{:S(2)}, u32[]{:S(2)}) collective-permute-start(bf16[496,128]{1,0:T(8,128)(2,1)S(1)} %get-tuple-element.50), channel_id=1, source_target_pairs={{0,1},{1,0},{2,3},{3,2},{4,8},{5,9},{6,10},{7,11},{8,4},{9,5},{10,... | collective-permute-start | bytes 380936 | tf_op jit(solution)/shard_map/ppermute | solution.py:34
  22.4 2.0 %collective-permute-start.9 = (bf16[4,112,128]{2,1,0:T(8,128)(2,1)S(1)}, bf16[4,112,128]{2,1,0:T(8,128)(2,1)S(1)}, u32[]{:S(2)}, u32[]{:S(2)}) collective-permute-start(bf16[4,112,128]{2,1,0:T(8,128)(2,1)S(1)} %get-tuple-element.53.h_ref), channel_id=1, source_target_pairs={{0,1},{1,0},{2,3},{3,2},{4,5},{5,4},{6,7},{7,6},{8,9},{9,8},{10,11... | collective-permute-start | bytes 344072 | tf_op jit(solution)/shard_map/ppermute | solution.py:23
  24.4 1.3 %collective-permute-start.10 = (bf16[4,112,128]{2,1,0:T(8,128)(2,1)S(1)}, bf16[4,112,128]{2,1,0:T(8,128)(2,1)S(1)}, u32[]{:S(2)}, u32[]{:S(2)}) collective-permute-start(bf16[4,112,128]{2,1,0:T(8,128)(2,1)S(1)} %collective-permute-done.8.hy_ref), channel_id=1, source_target_pairs={{0,1},{1,0},{2,3},{3,2},{4,5},{5,4},{6,7},{7,6},{8,9},{9,8},{10,11... | collective-permute-start | bytes 344072 | tf_op jit(solution)/shard_map/ppermute | solution.py:23
  24.4 4.9 %collective-permute-start.12 = (bf16[4,288,128]{2,1,0:T(8,128)(2,1)S(1)}, bf16[4,288,128]{2,1,0:T(8,128)(2,1)S(1)}, u32[]{:S(2)}, u32[]{:S(2)}) collective-permute-start(bf16[4,288,128]{2,1,0:T(8,128)(2,1)S(1)} %get-tuple-element.55.h_ref), channel_id=1, source_target_pairs={{0,1},{1,0},{2,3},{3,2},{4,5},{5,4},{6,7},{7,6},{8,9},{9,8},{10,11... | collective-permute-start | bytes 884744 | tf_op jit(solution)/shard_map/ppermute | solution.py:23
  28.0 1.6 %collective-permute-start.13 = (bf16[4,288,128]{2,1,0:T(8,128)(2,1)S(1)}, bf16[4,288,128]{2,1,0:T(8,128)(2,1)S(1)}, u32[]{:S(2)}, u32[]{:S(2)}) collective-permute-start(bf16[4,288,128]{2,1,0:T(8,128)(2,1)S(1)} %after.1.hy_ref), channel_id=1, source_target_pairs={{0,1},{1,0},{2,3},{3,2},{4,5},{5,4},{6,7},{7,6},{8,9},{9,8},{10,11... | collective-permute-start | bytes 884744 | tf_op jit(solution)/shard_map/ppermute | solution.py:23
  31.8 2.1 %collective-permute-start.14 = (bf16[2,4,32,1152]{3,2,1,0:T(8,128)(2,1)S(1)}, bf16[2,4,32,1152]{3,2,1,0:T(8,128)(2,1)S(1)}, u32[]{:S(2)}, u32[]{:S(2)}) collective-permute-start(bf16[2,4,32,1152]{3,2,1,0:T(8,128)(2,1)S(1)} %get-tuple-element.63), channel_id=1, source_target_pairs={{0,1},{1,0},{2,3},{3,2},{4,5},{5,4},{6,7},{7,6},{8,9},{9,8},{10,11... | collective-permute-start | bytes 1769480 | tf_op jit(solution)/shard_map/ppermute | solution.py:23
  34.0 9.1 %collective-permute-start.15 = (bf16[4,32,1152]{2,1,0:T(8,128)(2,1)S(1)}, bf16[4,32,1152]{2,1,0:T(8,128)(2,1)S(1)}, u32[]{:S(2)}, u32[]{:S(2)}) collective-permute-start(bf16[4,32,1152]{2,1,0:T(8,128)(2,1)S(1)} %get-tuple-element.66), channel_id=1, source_target_pairs={{0,2},{1,3},{2,0},{3,1},{4,6},{5,7},{6,4},{7,5},{8,10},{9,11},{10,... | collective-permute-start | bytes 884744 | tf_op jit(solution)/shard_map/ppermute | solution.py:23
  35.8 1.6 %collective-permute-start.19 = (bf16[4,2,8,1728]{3,2,1,0:T(8,128)(2,1)S(1)}, bf16[4,2,8,1728]{3,2,1,0:T(8,128)(2,1)S(1)}, u32[]{:S(2)}, u32[]{:S(2)}) collective-permute-start(bf16[4,2,8,1728]{3,2,1,0:T(8,128)(2,1)S(1)} %get-tuple-element.76), channel_id=1, source_target_pairs={{0,1},{1,0},{2,3},{3,2},{4,5},{5,4},{6,7},{7,6},{8,9},{9,8},{10,11... | collective-permute-start | bytes 663560 | tf_op jit(solution)/shard_map/ppermute | solution.py:23
  37.4 10.3 %collective-permute-start.20 = (bf16[2,8,1728]{2,1,0:T(8,128)(2,1)S(1)}, bf16[2,8,1728]{2,1,0:T(8,128)(2,1)S(1)}, u32[]{:S(2)}, u32[]{:S(2)}) collective-permute-start(bf16[2,8,1728]{2,1,0:T(8,128)(2,1)S(1)} %get-tuple-element.78), channel_id=1, source_target_pairs={{0,12},{1,13},{2,14},{3,15},{4,8},{5,9},{6,10},{7,11},{8,4},{9,5},... | collective-permute-start | bytes 165896 | tf_op jit(solution)/shard_map/ppermute | solution.py:23
  39.9 7.7 %collective-permute-start.21 = (bf16[2,8,1728]{2,1,0:T(8,128)(2,1)S(1)}, bf16[2,8,1728]{2,1,0:T(8,128)(2,1)S(1)}, u32[]{:S(2)}, u32[]{:S(2)}) collective-permute-start(bf16[2,8,1728]{2,1,0:T(8,128)(2,1)S(1)} %get-tuple-element.79), channel_id=1, source_target_pairs={{0,8},{1,9},{2,10},{3,11},{4,12},{5,13},{6,14},{7,15},{8,0},{9,1},... | collective-permute-start | bytes 165896 | tf_op jit(solution)/shard_map/ppermute | solution.py:23
  40.9 6.7 %collective-permute-start.22 = (bf16[2,8,1728]{2,1,0:T(8,128)(2,1)S(1)}, bf16[2,8,1728]{2,1,0:T(8,128)(2,1)S(1)}, u32[]{:S(2)}, u32[]{:S(2)}) collective-permute-start(bf16[2,8,1728]{2,1,0:T(8,128)(2,1)S(1)} %get-tuple-element.80), channel_id=1, source_target_pairs={{0,4},{1,5},{2,6},{3,7},{4,0},{5,1},{6,2},{7,3},{8,12},{9,13},{10,... | collective-permute-start | bytes 165896 | tf_op jit(solution)/shard_map/ppermute | solution.py:23
  43.2 8.4 %collective-permute-start.16 = (bf16[32,1152]{1,0:T(8,128)(2,1)S(1)}, bf16[32,1152]{1,0:T(8,128)(2,1)S(1)}, u32[]{:S(2)}, u32[]{:S(2)}) collective-permute-start(bf16[32,1152]{1,0:T(8,128)(2,1)S(1)} %get-tuple-element.68), channel_id=1, source_target_pairs={{0,8},{1,9},{2,10},{3,11},{4,12},{5,13},{6,14},{7,15},{8,0},{9,1},... | collective-permute-start | bytes 221192 | tf_op jit(solution)/shard_map/ppermute | solution.py:23
  46.2 6.4 %collective-permute-start.17 = (bf16[32,1152]{1,0:T(8,128)(2,1)S(1)}, bf16[32,1152]{1,0:T(8,128)(2,1)S(1)}, u32[]{:S(2)}, u32[]{:S(2)}) collective-permute-start(bf16[32,1152]{1,0:T(8,128)(2,1)S(1)} %get-tuple-element.69), channel_id=1, source_target_pairs={{0,12},{1,13},{2,14},{3,15},{4,8},{5,9},{6,10},{7,11},{8,4},{9,5},... | collective-permute-start | bytes 221192 | tf_op jit(solution)/shard_map/ppermute | solution.py:23
  47.7 5.2 %collective-permute-start.18 = (bf16[32,1152]{1,0:T(8,128)(2,1)S(1)}, bf16[32,1152]{1,0:T(8,128)(2,1)S(1)}, u32[]{:S(2)}, u32[]{:S(2)}) collective-permute-start(bf16[32,1152]{1,0:T(8,128)(2,1)S(1)} %get-tuple-element.70), channel_id=1, source_target_pairs={{0,4},{1,5},{2,6},{3,7},{4,0},{5,1},{6,2},{7,3},{8,12},{9,13},{10,... | collective-permute-start | bytes 221192 | tf_op jit(solution)/shard_map/ppermute | solution.py:23
  47.7 3.9 %collective-permute-start.23 = (bf16[8,1728]{1,0:T(8,128)(2,1)S(1)}, bf16[8,1728]{1,0:T(8,128)(2,1)S(1)}, u32[]{:S(2)}, u32[]{:S(2)}) collective-permute-start(bf16[8,1728]{1,0:T(8,128)(2,1)S(1)} %get-tuple-element.82), channel_id=1, source_target_pairs={{0,2},{1,3},{2,0},{3,1},{4,6},{5,7},{6,4},{7,5},{8,10},{9,11},{10,... | collective-permute-start | bytes 82952 | tf_op jit(solution)/shard_map/ppermute | solution.py:23

commit v8 on v7

--- a/solution.py
+++ b/solution.py
@@ -262,8 +262,8 @@
     channels,
     edge_t,
     x_ref,
+    edge_b_ref,
     edge_a_ref,
-    edge_b_ref,
     h_ref,
     hy_ref,
     hc_ref,
@@ -389,6 +389,7 @@
     hc_ref,
     hyc_ref,
     send_ref,
+    send_y_ref,
     slope_ref,
     w_other_ref,
     student_ref,
@@ -424,7 +425,9 @@
     terms = dot(
         slope_ref[lo : lo + n_own, half:], patch_last_ref[lo : lo + n_own, :], ((0,), (0,))
     )
-    send_ref[...] = terms.astype(bf16).reshape(send_ref.shape)
+    terms = terms.astype(bf16).reshape((2,) + send_ref.shape)
+    send_ref[...] = terms[0]
+    send_y_ref[...] = terms[1]
 
 
 def back_kernel(
@@ -436,6 +439,7 @@
     w_other_ref,
     patch_last_ref,
     keep_ref,
+    keep_y_ref,
     slope_second_ref,
     parts_ref,
 ):
@@ -444,7 +448,9 @@
     terms = dot(
         slope_ref[lo : lo + n_own, :half], patch_last_ref[lo : lo + n_own, :], ((0,), (0,))
     )
-    keep_ref[...] = terms.reshape(keep_ref.shape)
+    terms = terms.reshape((2,) + keep_ref.shape)
+    keep_ref[...] = terms[0]
+    keep_y_ref[...] = terms[1]
     parts_ref[...] = dot(slope_ref[:, :half], w_own_ref[...], ((1,), (0,))) + dot(
         slope_ref[:, half:], w_other_ref[...], ((1,), (0,))
     )
@@ -487,13 +493,17 @@
             send_ref[far, ry] = terms_ref[at ^ 1].astype(bf16)
 
 
-def tied_split_kernel(keep_ref, got_ref, tie_ref, *out_refs):
-    split_kernel(keep_ref, got_ref, *out_refs)
-
-
-def split_kernel(keep_ref, got_ref, kept_ref, *send_refs):
-    for i, ref in enumerate((kept_ref,) + send_refs):
-        ref[...] = (keep_ref[i] + got_ref[i].astype(f32)).astype(ref.dtype)
+def join_kernel(keep_ref, got_ref, sent_ref):
+    sent_ref[...] = (keep_ref[...] + got_ref[...].astype(f32)).astype(sent_ref.dtype)
+
+
+def split_kernel(keep_ref, *refs):
+    got_refs, out_refs = refs[:-FAR], refs[-FAR:]
+    for i, ref in enumerate(out_refs):
+        total = keep_ref[i]
+        for got_ref in got_refs:
+            total = total + got_ref[i].astype(f32)
+        ref[...] = total.astype(ref.dtype)
 
 
 def add_kernel(keep_ref, got1_ref, got2_ref, got3_ref, kept_ref, send_ref):
@@ -636,7 +646,7 @@
     tilt_first, tilt_second, patch_first, patch_middle, patch_last, all_middle = call(
         functools.partial(early_kernel, own, rows, total, channels, edge_t),
         "early",
-        (x_band, edge_a, edge_b, *all_small),
+        (x_band, edge_b, edge_a, *all_small),
         [
             ((own * rows, hidden), f32),
             ((n_back, hidden), f32),
@@ -663,24 +673,25 @@
         [],
         HALF_COST,
     )
-    send, slope, w_other = call(
+    send, send_y, slope, w_other = call(
         functools.partial(front_kernel, own, rows, total),
         "front",
         (target, patch_last, student_own, last_c, last_yc),
         [
-            ((2, FAR, r_last, 9 * hidden), bf16),
+            ((FAR, r_last, 9 * hidden), bf16),
+            ((FAR, r_last, 9 * hidden), bf16),
             ((n_slope, channels), bf16),
             ((half, 9 * hidden), bf16),
         ],
         [((n_slope, half), f32)],
         6_000_000_000,
     )
-    got = swap(send, fold)
-    keep, slope_second = call(
+    got_y, got = swap(send_y, fold), swap(send, fold)
+    keep, keep_y, slope_second = call(
         functools.partial(back_kernel, own, rows),
         "back",
         (slope, tilt_second, w_own, w_other, patch_last),
-        [((2, FAR, r_last, 9 * hidden), f32), ((n_back, hidden), bf16)],
+        [((FAR, r_last, 9 * hidden), f32)] * 2 + [((n_back, hidden), bf16)],
         [((n_slope, 9 * hidden), f32)],
         4_000_000_000,
     )
@@ -694,24 +705,16 @@
         2_000_000_000,
     )
 
-    def split(keep, got, count):
+    def split(keep, *got):
         shape = keep.shape[1:]
-        outs = [(shape, f32)] + [(shape, bf16)] * (count - 1)
-        return call(split_kernel, "split", (keep, got), outs, [], 1_000_000)
-
-    last_kept, last_sent = call(
-        tied_split_kernel,
-        "split",
-        (keep, got, slope_second),
-        [(keep.shape[1:], f32), (keep.shape[1:], bf16)],
-        [],
-        1_000_000,
-        {2: anywhere},
-    )
+        outs = [(shape, f32)] + [(shape, bf16)] * (FAR - 1)
+        return call(split_kernel, "split", (keep, *got), outs, [], 1_000_000)
+
+    (last_sent,) = call(join_kernel, "join", (keep_y, got_y), [(keep.shape, bf16)], [], 1_000_000)
     last_got = swap(last_sent, 2 * fold)
-    parts = split(small_keep, swap(small_send, fold), FAR)
+    parts = split(small_keep, swap(small_send, fold))
     small_got = {k: swap(parts[k], 4 * k * fold) for k in (1, 2, 3)}
-    last = split(last_kept, last_got, FAR)
+    last = split(keep, got, last_got)
     last_got = {k: swap(last[k], 4 * k * fold) for k in (1, 2, 3)}
     small_kept, small_sent = call(
         add_kernel,
@@ -725,7 +728,7 @@
     out_first, out_middle, out_last = call(
         finish_kernel,
         "finish",
-        (last[0], last_got[2], last_got[3], last_got[1], small_kept, small_got),
+        (last[0], last_got[2], last_got[1], last_got[3], small_kept, small_got),
         [(w.shape, f32) for w in (w_first, w_middle, w_last)],
         [],
         1_000_000,

time: 53.7 us -> 53.3 us (level)
  waiting for transfers between devices: 16.3 us -> 15.4 us
    ppermute x23 -> x24, waiting for transfers between devices: 16.3 us -> 15.4 us  [swap(): return lax.ppermute(array, 'cols', [(i, i ^ mask) for i in range(size)])]
    ppermute x23 -> x24, starting transfers between devices: 23.9 us -> 24.3 us  [swap(): return lax.ppermute(array, 'cols', [(i, i ^ mask) for i in range(size)])]
  transfers between devices with their start and end apart: 24 -> 25, of which waited for: 12 -> 10; matrix products, arithmetic and copies ran while one was open for 0% -> 0% of each run, Pallas kernels for 12% -> 12%
where the time goes in v8:
time: 53.3 us; the launch traced here: 53.2 us
  starting transfers between devices  24.3 us (46%)
  waiting for transfers between devices  15.4 us (29%)
  Pallas kernels  11.7 us (22%)
  local copies, waits for them, and re-layouts  0.95 us (2%)
  between operations  0.76 us (1%)
    ppermute x24, starting transfers between devices, swap(): return lax.ppermute(array, 'cols', [(i, i ^ mask) for i in range(size)])  24.3 us
    ppermute x24, waiting for transfers between devices, swap(): return lax.ppermute(array, 'cols', [(i, i ^ mask) for i in range(size)])  15.4 us
    pallas_call x15, Pallas kernels, call(): pl.pallas_call(kernel, in_specs=[spaces.get(i, vmem) for i in range(len(i...  11.7 us
  transfers between devices with their start and end apart: 25, of which 10 were waited for; matrix products, arithmetic and copies ran while one was open for 0% of the time, Pallas kernels for 12%

profile of v8, /device:TPU:0, one launch (start us, length us, event | category | flops | bytes accessed | tf_op | source)
XLA Modules:
  0.0 53.2 jit_solution(1440833518089919456)
XLA Ops:
  0.6 2.4 %deal.1 = (bf16[1040,128]{1,0:T(8,128)(2,1)}, bf16[640,128]{1,0:T(8,128)(2,1)}, bf16[1152,128]{1,0:T(8,128)(2,1)}, bf16[400,128]{1,0:T(8,128)(2,1)}) custom-call(bf16[32,1024]{1,0:T(8,128)(2,1)} %x_hbm.1, bf16[32,16,512]{2,1,0:T(8,128)(2,1)} %teacher_hbm.1, bf16[8,576]{1,0:T(8,128)(2,1)} %w_first_hbm.1, bf16[8,1152]{1,0:T(8,128)(2,1)} %w_middle_hbm.1, ...), custom_call_target="tpu_custom_call" | custom-call | flops 600000000 | bytes 1000000 | tf_op jit(solution)/shard_map/deal/pallas_call | solution.py:532
  3.0 3.0 %collective-permute-start.2 = (bf16[1152,128]{1,0:T(8,128)(2,1)}, bf16[1152,128]{1,0:T(8,128)(2,1)S(1)}, u32[]{:S(2)}, u32[]{:S(2)}) collective-permute-start(bf16[1152,128]{1,0:T(8,128)(2,1)} %get-tuple-element.47), channel_id=1, source_target_pairs={{0,2},{1,3},{2,0},{3,1},{4,6},{5,7},{6,4},{7,5},{8,10},{9,11},{10,... | collective-permute-start | bytes 884744 | tf_op jit(solution)/shard_map/ppermute | solution.py:23
  6.1 1.6 %collective-permute-start = (bf16[400,128]{1,0:T(8,128)(2,1)}, bf16[400,128]{1,0:T(8,128)(2,1)S(1)}, u32[]{:S(2)}, u32[]{:S(2)}) collective-permute-start(bf16[400,128]{1,0:T(8,128)(2,1)} %get-tuple-element.44), channel_id=1, source_target_pairs={{0,4},{1,5},{2,6},{3,7},{4,0},{5,1},{6,2},{7,3},{8,12},{9,13},{10,... | collective-permute-start | bytes 307208 | tf_op jit(solution)/shard_map/ppermute | solution.py:23
  7.6 2.6 %collective-permute-start.7 = (bf16[400,128]{1,0:T(8,128)(2,1)}, bf16[400,128]{1,0:T(8,128)(2,1)S(1)}, u32[]{:S(2)}, u32[]{:S(2)}) collective-permute-start(bf16[400,128]{1,0:T(8,128)(2,1)} %get-tuple-element.44), channel_id=1, source_target_pairs={{0,8},{1,9},{2,10},{3,11},{4,12},{5,13},{6,14},{7,15},{8,0},{9,1},... | collective-permute-start | bytes 307208 | tf_op jit(solution)/shard_map/ppermute | solution.py:23
  10.5 1.5 %collective-permute-done.far_ref = bf16[400,128]{1,0:T(8,128)(2,1)S(1)} collective-permute-done((bf16[400,128]{1,0:T(8,128)(2,1)}, bf16[400,128]{1,0:T(8,128)(2,1)S(1)}, u32[]{:S(2)}, u32[]{:S(2)}) %collective-permute-start) | collective-permute-done | bytes 102432 | tf_op jit(solution)/shard_map/ppermute | solution.py:23
  12.0 0.9 %copy-done = bf16[1040,128]{1,0:T(8,128)(2,1)S(1)} copy-done((bf16[1040,128]{1,0:T(8,128)(2,1)S(1)}, bf16[1040,128]{1,0:T(8,128)(2,1)}, u32[]{:S(2)}) %copy-start) | copy-done | bytes 266264
  12.9 0.4 collective-permute-done.2.across_ref
  13.3 5.0 %collective-permute-done.7.far2_ref = bf16[400,128]{1,0:T(8,128)(2,1)S(1)} collective-permute-done((bf16[400,128]{1,0:T(8,128)(2,1)}, bf16[400,128]{1,0:T(8,128)(2,1)S(1)}, u32[]{:S(2)}, u32[]{:S(2)}) %collective-permute-start.7) | collective-permute-done | bytes 102432 | tf_op jit(solution)/shard_map/ppermute | solution.py:23
  18.4 0.6 %collective-permute-start.8 = (bf16[4,112,128]{2,1,0:T(8,128)(2,1)S(1)}, bf16[4,112,128]{2,1,0:T(8,128)(2,1)S(1)}, u32[]{:S(2)}, u32[]{:S(2)}) collective-permute-start(bf16[4,112,128]{2,1,0:T(8,128)(2,1)S(1)} %get-tuple-element.53.h_ref), channel_id=1, source_target_pairs={{0,2},{1,3},{2,0},{3,1},{4,6},{5,7},{6,4},{7,5},{8,10},{9,11},{10,... | collective-permute-start | bytes 344072 | tf_op jit(solution)/shard_map/ppermute | solution.py:23
  18.9 1.5 %collective-permute-start.11 = (bf16[4,288,128]{2,1,0:T(8,128)(2,1)S(1)}, bf16[4,288,128]{2,1,0:T(8,128)(2,1)S(1)}, u32[]{:S(2)}, u32[]{:S(2)}) collective-permute-start(bf16[4,288,128]{2,1,0:T(8,128)(2,1)S(1)} %get-tuple-element.55.h_ref), channel_id=1, source_target_pairs={{0,2},{1,3},{2,0},{3,1},{4,6},{5,7},{6,4},{7,5},{8,10},{9,11},{10,... | collective-permute-start | bytes 884744 | tf_op jit(solution)/shard_map/ppermute | solution.py:23
  20.7 1.7 %collective-permute-start.4 = (bf16[496,128]{1,0:T(8,128)(2,1)S(1)}, bf16[496,128]{1,0:T(8,128)(2,1)S(1)}, u32[]{:S(2)}, u32[]{:S(2)}) collective-permute-start(bf16[496,128]{1,0:T(8,128)(2,1)S(1)} %get-tuple-element.49), channel_id=1, source_target_pairs={{0,4},{1,5},{2,6},{3,7},{4,0},{5,1},{6,2},{7,3},{8,12},{9,13},{10,... | collective-permute-start | bytes 380936 | tf_op jit(solution)/shard_map/ppermute | solution.py:23
  22.4 0.5 collective-permute-start.9
  22.9 1.5 %collective-permute-done.8.hy_ref = bf16[4,112,128]{2,1,0:T(8,128)(2,1)S(1)} collective-permute-done((bf16[4,112,128]{2,1,0:T(8,128)(2,1)S(1)}, bf16[4,112,128]{2,1,0:T(8,128)(2,1)S(1)}, u32[]{:S(2)}, u32[]{:S(2)}) %collective-permute-start.8) | collective-permute-done | bytes 114720 | tf_op jit(solution)/shard_map/ppermute | solution.py:23
  24.4 0.5 collective-permute-start.12
  24.9 0.8 %collective-permute-done.10.hyc_ref = bf16[4,112,128]{2,1,0:T(8,128)(2,1)S(1)} collective-permute-done((bf16[4,112,128]{2,1,0:T(8,128)(2,1)S(1)}, bf16[4,112,128]{2,1,0:T(8,128)(2,1)S(1)}, u32[]{:S(2)}, u32[]{:S(2)}) %collective-permute-start.10) | collective-permute-done | bytes 114720 | tf_op jit(solution)/shard_map/ppermute | solution.py:23
  25.8 2.2 %early.1 = (f32[512,128]{1,0:T(8,128)S(1)}, f32[576,128]{1,0:T(8,128)S(1)}, bf16[896,576]{1,0:T(8,128)(2,1)S(1)}, bf16[832,1152]{1,0:T(8,128)(2,1)S(1)}, bf16[70...) custom-call(bf16[512,64]{1,0:T(8,128)(2,1)S(1)} %get-tuple-element.51.x_ref, ...), custom_call_target="tpu_custom_call" | custom-call | flops 1500000000 | bytes 1000000 | tf_op jit(solution)/shard_map/early/pallas_call | solution.py:532
  28.2 1.1 %half.1 = (bf16[256,1152]{1,0:T(8,128)(2,1)S(1)}, f32[704,256]{1,0:T(8,128)S(1)}, bf16[704,512]{1,0:T(8,128)(2,1)S(1)}) custom-call(bf16[512,512]{1,0:T(8,128)(2,1)S(1)} %get-tuple-element.48.teacher_ref, bf16[496,128]{1,0:T(8,128)(2,1)S(1)} %collective-permute-done.4.edge_a_ref, bf16[496,128]{1,0:T(8,128)(2,1)S(1)} %collective-permute-done.5.edge_b_ref, ...), custom_call_target="tpu_custom_call" | custom-call | flops 1500000000 | bytes 1000000 | tf_op jit(solution)/shard_map/half/pallas_call | solution.py:532
  29.7 2.2 %front.1 = (bf16[4,32,1152]{2,1,0:T(8,128)(2,1)S(1)}, bf16[4,32,1152]{2,1,0:T(8,128)(2,1)S(1)}, bf16[704,512]{1,0:T(8,128)(2,1)S(1)}, bf16[256,1152]{1,0:T(8,128)(2,1)S(1)}) custom-call(bf16[704,512]{1,0:T(8,128)(2,1)S(1)} %get-tuple-element.56.target_ref, bf16[704,1152]{1,0:T(8,128)(2,1)S(1)} %get-tuple-element.54.first_ref.patch_last_ref, ...), custom_call_target="tpu_custom_call" | custom-call | flops 6000000000 | bytes 1000000 | tf_op jit(solution)/shard_map/front/pallas_call | solution.py:532
  32.5 1.5 %back.1 = (f32[4,32,1152]{2,1,0:T(8,128)S(1)}, f32[4,32,1152]{2,1,0:T(8,128)S(1)}, bf16[576,128]{1,0:T(8,128)(2,1)S(1)}) custom-call(bf16[704,512]{1,0:T(8,128)(2,1)S(1)} %get-tuple-element.58.slope_ref, f32[576,128]{1,0:T(8,128)S(1)} %get-tuple-element.59.tilt_second_ref, bf16[256,1152]{1,0:T(8,128)(2,1)S(1)} %get-tuple-element.60.w_own_ref, ...), custom_call_target="tpu_custom_call" | custom-call | flops 4000000000 | bytes 1000000 | tf_op jit(solution)/shard_map/back/pallas_call | solution.py:532
  34.0 0.6 %collective-permute-start.16 = (bf16[4,32,1152]{2,1,0:T(8,128)(2,1)S(1)}, bf16[4,32,1152]{2,1,0:T(8,128)(2,1)S(1)}, u32[]{:S(2)}, u32[]{:S(2)}) collective-permute-start(bf16[4,32,1152]{2,1,0:T(8,128)(2,1)S(1)} %join.1), channel_id=1, source_target_pairs={{0,2},{1,3},{2,0},{3,1},{4,6},{5,7},{6,4},{7,5},{8,10},{9,11},{10,... | collective-permute-start | bytes 884744 | tf_op jit(solution)/shard_map/ppermute | solution.py:23
  34.6 1.1 %first.1 = (f32[4,2,8,1728]{3,2,1,0:T(8,128)S(1)}, bf16[4,2,8,1728]{3,2,1,0:T(8,128)(2,1)S(1)}) custom-call(bf16[576,128]{1,0:T(8,128)(2,1)S(1)} %get-tuple-element.70.slope_second_ref, f32[512,128]{1,0:T(8,128)S(1)} %get-tuple-element.71.tilt_first_ref, bf16[896,576]{1,0:T(8,128)(2,1)S(1)} %get-tuple-element.72.patch_first_ref, ...), custom_call_target="tpu_custom_call" | custom-call | flops 2000000000 | bytes 1000000 | tf_op jit(solution)/shard_map/first/pallas_call | solution.py:532
  35.8 1.5 %collective-permute-done.20.refs_0_ = bf16[4,2,8,1728]{3,2,1,0:T(8,128)(2,1)S(1)} collective-permute-done((bf16[4,2,8,1728]{3,2,1,0:T(8,128)(2,1)S(1)}, bf16[4,2,8,1728]{3,2,1,0:T(8,128)(2,1)S(1)}, u32[]{:S(2)}, u32[]{:S(2)}) %collective-permute-start.20) | collective-permute-done | bytes 221216 | tf_op jit(solution)/shard_map/ppermute | solution.py:23
  37.3 2.6 %collective-permute-start.21 = (bf16[2,8,1728]{2,1,0:T(8,128)(2,1)S(1)}, bf16[2,8,1728]{2,1,0:T(8,128)(2,1)S(1)}, u32[]{:S(2)}, u32[]{:S(2)}) collective-permute-start(bf16[2,8,1728]{2,1,0:T(8,128)(2,1)S(1)} %get-tuple-element.78), channel_id=1, source_target_pairs={{0,12},{1,13},{2,14},{3,15},{4,8},{5,9},{6,10},{7,11},{8,4},{9,5},... | collective-permute-start | bytes 165896 | tf_op jit(solution)/shard_map/ppermute | solution.py:23
  39.9 1.0 %collective-permute-start.22 = (bf16[2,8,1728]{2,1,0:T(8,128)(2,1)S(1)}, bf16[2,8,1728]{2,1,0:T(8,128)(2,1)S(1)}, u32[]{:S(2)}, u32[]{:S(2)}) collective-permute-start(bf16[2,8,1728]{2,1,0:T(8,128)(2,1)S(1)} %get-tuple-element.79), channel_id=1, source_target_pairs={{0,8},{1,9},{2,10},{3,11},{4,12},{5,13},{6,14},{7,15},{8,0},{9,1},... | collective-permute-start | bytes 165896 | tf_op jit(solution)/shard_map/ppermute | solution.py:23
  40.9 0.9 %collective-permute-start.23 = (bf16[2,8,1728]{2,1,0:T(8,128)(2,1)S(1)}, bf16[2,8,1728]{2,1,0:T(8,128)(2,1)S(1)}, u32[]{:S(2)}, u32[]{:S(2)}) collective-permute-start(bf16[2,8,1728]{2,1,0:T(8,128)(2,1)S(1)} %get-tuple-element.80), channel_id=1, source_target_pairs={{0,4},{1,5},{2,6},{3,7},{4,0},{5,1},{6,2},{7,3},{8,12},{9,13},{10,... | collective-permute-start | bytes 165896 | tf_op jit(solution)/shard_map/ppermute | solution.py:23
  41.8 1.3 %collective-permute-done.16.refs_1_ = bf16[4,32,1152]{2,1,0:T(8,128)(2,1)S(1)} collective-permute-done((bf16[4,32,1152]{2,1,0:T(8,128)(2,1)S(1)}, bf16[4,32,1152]{2,1,0:T(8,128)(2,1)S(1)}, u32[]{:S(2)}, u32[]{:S(2)}) %collective-permute-start.16) | collective-permute-done | bytes 294944 | tf_op jit(solution)/shard_map/ppermute | solution.py:23
  43.2 3.0 %collective-permute-start.17 = (bf16[32,1152]{1,0:T(8,128)(2,1)S(1)}, bf16[32,1152]{1,0:T(8,128)(2,1)S(1)}, u32[]{:S(2)}, u32[]{:S(2)}) collective-permute-start(bf16[32,1152]{1,0:T(8,128)(2,1)S(1)} %get-tuple-element.67), channel_id=1, source_target_pairs={{0,8},{1,9},{2,10},{3,11},{4,12},{5,13},{6,14},{7,15},{8,0},{9,1},... | collective-permute-start | bytes 221192 | tf_op jit(solution)/shard_map/ppermute | solution.py:23
  46.2 1.5 %collective-permute-start.19 = (bf16[32,1152]{1,0:T(8,128)(2,1)S(1)}, bf16[32,1152]{1,0:T(8,128)(2,1)S(1)}, u32[]{:S(2)}, u32[]{:S(2)}) collective-permute-start(bf16[32,1152]{1,0:T(8,128)(2,1)S(1)} %get-tuple-element.69), channel_id=1, source_target_pairs={{0,12},{1,13},{2,14},{3,15},{4,8},{5,9},{6,10},{7,11},{8,4},{9,5},... | collective-permute-start | bytes 221192 | tf_op jit(solution)/shard_map/ppermute | solution.py:23
  47.8 1.6 %collective-permute-start.24 = (bf16[8,1728]{1,0:T(8,128)(2,1)S(1)}, bf16[8,1728]{1,0:T(8,128)(2,1)S(1)}, u32[]{:S(2)}, u32[]{:S(2)}) collective-permute-start(bf16[8,1728]{1,0:T(8,128)(2,1)S(1)} %get-tuple-element.82), channel_id=1, source_target_pairs={{0,2},{1,3},{2,0},{3,1},{4,6},{5,7},{6,4},{7,5},{8,10},{9,11},{10,... | collective-permute-start | bytes 82952 | tf_op jit(solution)/shard_map/ppermute | solution.py:23
  49.4 2.3 %collective-permute-done.24.got_ref = bf16[8,1728]{1,0:T(8,128)(2,1)S(1)} collective-permute-done((bf16[8,1728]{1,0:T(8,128)(2,1)S(1)}, bf16[8,1728]{1,0:T(8,128)(2,1)S(1)}, u32[]{:S(2)}, u32[]{:S(2)}) %collective-permute-start.24) | collective-permute-done | bytes 27680 | tf_op jit(solution)/shard_map/ppermute | solution.py:23
  51.8 0.7 %collective-permute-done.19.got3_ref = bf16[32,1152]{1,0:T(8,128)(2,1)S(1)} collective-permute-done((bf16[32,1152]{1,0:T(8,128)(2,1)S(1)}, bf16[32,1152]{1,0:T(8,128)(2,1)S(1)}, u32[]{:S(2)}, u32[]{:S(2)}) %collective-permute-start.19) | collective-permute-done | bytes 73760 | tf_op jit(solution)/shard_map/ppermute | solution.py:23
  52.5 0.7 %finish.1 = (f32[8,576]{1,0:T(8,128)}, f32[8,1152]{1,0:T(8,128)}, f32[32,1152]{1,0:T(8,128)}) custom-call(f32[32,1152]{1,0:T(8,128)S(1)} %get-tuple-element.66.last_ref, bf16[32,1152]{1,0:T(8,128)(2,1)S(1)} %collective-permute-done.17.got1_ref, bf16[32,1152]{1,0:T(8,128)(2,1)S(1)} %collective-permute-done.18.got2_ref, ...), custom_call_target="tpu_custom_call" | custom-call | flops 1000000 | bytes 1000000 | tf_op jit(solution)/shard_map/finish/pallas_call | solution.py:532
  (35 shorter events, 2.0 us)
Async XLA Ops:
  3.0 10.3 %collective-permute-start.2 = (bf16[1152,128]{1,0:T(8,128)(2,1)}, bf16[1152,128]{1,0:T(8,128)(2,1)S(1)}, u32[]{:S(2)}, u32[]{:S(2)}) collective-permute-start(bf16[1152,128]{1,0:T(8,128)(2,1)} %get-tuple-element.47), channel_id=1, source_target_pairs={{0,2},{1,3},{2,0},{3,1},{4,6},{5,7},{6,4},{7,5},{8,10},{9,11},{10,... | collective-permute-start | bytes 884744 | tf_op jit(solution)/shard_map/ppermute | solution.py:23
  6.1 5.9 %collective-permute-start = (bf16[400,128]{1,0:T(8,128)(2,1)}, bf16[400,128]{1,0:T(8,128)(2,1)S(1)}, u32[]{:S(2)}, u32[]{:S(2)}) collective-permute-start(bf16[400,128]{1,0:T(8,128)(2,1)} %get-tuple-element.44), channel_id=1, source_target_pairs={{0,4},{1,5},{2,6},{3,7},{4,0},{5,1},{6,2},{7,3},{8,12},{9,13},{10,... | collective-permute-start | bytes 307208 | tf_op jit(solution)/shard_map/ppermute | solution.py:23
  7.6 10.7 %collective-permute-start.7 = (bf16[400,128]{1,0:T(8,128)(2,1)}, bf16[400,128]{1,0:T(8,128)(2,1)S(1)}, u32[]{:S(2)}, u32[]{:S(2)}) collective-permute-start(bf16[400,128]{1,0:T(8,128)(2,1)} %get-tuple-element.44), channel_id=1, source_target_pairs={{0,8},{1,9},{2,10},{3,11},{4,12},{5,13},{6,14},{7,15},{8,0},{9,1},... | collective-permute-start | bytes 307208 | tf_op jit(solution)/shard_map/ppermute | solution.py:23
  10.2 8.1 %collective-permute-start.6 = (bf16[400,128]{1,0:T(8,128)(2,1)}, bf16[400,128]{1,0:T(8,128)(2,1)S(1)}, u32[]{:S(2)}, u32[]{:S(2)}) collective-permute-start(bf16[400,128]{1,0:T(8,128)(2,1)} %get-tuple-element.44), channel_id=1, source_target_pairs={{0,12},{1,13},{2,14},{3,15},{4,8},{5,9},{6,10},{7,11},{8,4},{9,5},... | collective-permute-start | bytes 307208 | tf_op jit(solution)/shard_map/ppermute | solution.py:23
  10.5 10.0 %collective-permute-start.1 = (bf16[640,128]{1,0:T(8,128)(2,1)}, bf16[640,128]{1,0:T(8,128)(2,1)S(1)}, u32[]{:S(2)}, u32[]{:S(2)}) collective-permute-start(bf16[640,128]{1,0:T(8,128)(2,1)} %get-tuple-element.46), channel_id=1, source_target_pairs={{0,1},{1,0},{2,3},{3,2},{4,5},{5,4},{6,7},{7,6},{8,9},{9,8},{10,11... | collective-permute-start | bytes 491528 | tf_op jit(solution)/shard_map/ppermute | solution.py:23
  11.9 1.0 %copy-start = (bf16[1040,128]{1,0:T(8,128)(2,1)S(1)}, bf16[1040,128]{1,0:T(8,128)(2,1)}, u32[]{:S(2)}) copy-start(bf16[1040,128]{1,0:T(8,128)(2,1)} %get-tuple-element.43.own_ref) | copy-start | bytes 798724
  13.3 7.2 %collective-permute-start.3 = (bf16[1152,128]{1,0:T(8,128)(2,1)S(1)}, bf16[1152,128]{1,0:T(8,128)(2,1)S(1)}, u32[]{:S(2)}, u32[]{:S(2)}) collective-permute-start(bf16[1152,128]{1,0:T(8,128)(2,1)S(1)} %collective-permute-done.2.across_ref), channel_id=1, source_target_pairs={{0,1},{1,0},{2,3},{3,2},{4,5},{5,4},{6,7},{7,6},{8,9},{9,8},{10,11... | collective-permute-start | bytes 884744 | tf_op jit(solution)/shard_map/ppermute | solution.py:23
  18.4 6.1 %collective-permute-start.8 = (bf16[4,112,128]{2,1,0:T(8,128)(2,1)S(1)}, bf16[4,112,128]{2,1,0:T(8,128)(2,1)S(1)}, u32[]{:S(2)}, u32[]{:S(2)}) collective-permute-start(bf16[4,112,128]{2,1,0:T(8,128)(2,1)S(1)} %get-tuple-element.53.h_ref), channel_id=1, source_target_pairs={{0,2},{1,3},{2,0},{3,1},{4,6},{5,7},{6,4},{7,5},{8,10},{9,11},{10,... | collective-permute-start | bytes 344072 | tf_op jit(solution)/shard_map/ppermute | solution.py:23
  18.9 9.1 %collective-permute-start.11 = (bf16[4,288,128]{2,1,0:T(8,128)(2,1)S(1)}, bf16[4,288,128]{2,1,0:T(8,128)(2,1)S(1)}, u32[]{:S(2)}, u32[]{:S(2)}) collective-permute-start(bf16[4,288,128]{2,1,0:T(8,128)(2,1)S(1)} %get-tuple-element.55.h_ref), channel_id=1, source_target_pairs={{0,2},{1,3},{2,0},{3,1},{4,6},{5,7},{6,4},{7,5},{8,10},{9,11},{10,... | collective-permute-start | bytes 884744 | tf_op jit(solution)/shard_map/ppermute | solution.py:23
  20.7 5.1 %collective-permute-start.4 = (bf16[496,128]{1,0:T(8,128)(2,1)S(1)}, bf16[496,128]{1,0:T(8,128)(2,1)S(1)}, u32[]{:S(2)}, u32[]{:S(2)}) collective-permute-start(bf16[496,128]{1,0:T(8,128)(2,1)S(1)} %get-tuple-element.49), channel_id=1, source_target_pairs={{0,4},{1,5},{2,6},{3,7},{4,0},{5,1},{6,2},{7,3},{8,12},{9,13},{10,... | collective-permute-start | bytes 380936 | tf_op jit(solution)/shard_map/ppermute | solution.py:23
  22.4 3.3 %collective-permute-start.5 = (bf16[496,128]{1,0:T(8,128)(2,1)S(1)}, bf16[496,128]{1,0:T(8,128)(2,1)S(1)}, u32[]{:S(2)}, u32[]{:S(2)}) collective-permute-start(bf16[496,128]{1,0:T(8,128)(2,1)S(1)} %get-tuple-element.50), channel_id=1, source_target_pairs={{0,1},{1,0},{2,3},{3,2},{4,8},{5,9},{6,10},{7,11},{8,4},{9,5},{10,... | collective-permute-start | bytes 380936 | tf_op jit(solution)/shard_map/ppermute | solution.py:34
  22.4 2.0 %collective-permute-start.9 = (bf16[4,112,128]{2,1,0:T(8,128)(2,1)S(1)}, bf16[4,112,128]{2,1,0:T(8,128)(2,1)S(1)}, u32[]{:S(2)}, u32[]{:S(2)}) collective-permute-start(bf16[4,112,128]{2,1,0:T(8,128)(2,1)S(1)} %get-tuple-element.53.h_ref), channel_id=1, source_target_pairs={{0,1},{1,0},{2,3},{3,2},{4,5},{5,4},{6,7},{7,6},{8,9},{9,8},{10,11... | collective-permute-start | bytes 344072 | tf_op jit(solution)/shard_map/ppermute | solution.py:23
  24.4 1.3 %collective-permute-start.10 = (bf16[4,112,128]{2,1,0:T(8,128)(2,1)S(1)}, bf16[4,112,128]{2,1,0:T(8,128)(2,1)S(1)}, u32[]{:S(2)}, u32[]{:S(2)}) collective-permute-start(bf16[4,112,128]{2,1,0:T(8,128)(2,1)S(1)} %collective-permute-done.8.hy_ref), channel_id=1, source_target_pairs={{0,1},{1,0},{2,3},{3,2},{4,5},{5,4},{6,7},{7,6},{8,9},{9,8},{10,11... | collective-permute-start | bytes 344072 | tf_op jit(solution)/shard_map/ppermute | solution.py:23
  24.4 4.9 %collective-permute-start.12 = (bf16[4,288,128]{2,1,0:T(8,128)(2,1)S(1)}, bf16[4,288,128]{2,1,0:T(8,128)(2,1)S(1)}, u32[]{:S(2)}, u32[]{:S(2)}) collective-permute-start(bf16[4,288,128]{2,1,0:T(8,128)(2,1)S(1)} %get-tuple-element.55.h_ref), channel_id=1, source_target_pairs={{0,1},{1,0},{2,3},{3,2},{4,5},{5,4},{6,7},{7,6},{8,9},{9,8},{10,11... | collective-permute-start | bytes 884744 | tf_op jit(solution)/shard_map/ppermute | solution.py:23
  28.0 1.6 %collective-permute-start.13 = (bf16[4,288,128]{2,1,0:T(8,128)(2,1)S(1)}, bf16[4,288,128]{2,1,0:T(8,128)(2,1)S(1)}, u32[]{:S(2)}, u32[]{:S(2)}) collective-permute-start(bf16[4,288,128]{2,1,0:T(8,128)(2,1)S(1)} %after.1.hy_ref), channel_id=1, source_target_pairs={{0,1},{1,0},{2,3},{3,2},{4,5},{5,4},{6,7},{7,6},{8,9},{9,8},{10,11... | collective-permute-start | bytes 884744 | tf_op jit(solution)/shard_map/ppermute | solution.py:23
  31.9 9.9 %collective-permute-start.14 = (bf16[4,32,1152]{2,1,0:T(8,128)(2,1)S(1)}, bf16[4,32,1152]{2,1,0:T(8,128)(2,1)S(1)}, u32[]{:S(2)}, u32[]{:S(2)}) collective-permute-start(bf16[4,32,1152]{2,1,0:T(8,128)(2,1)S(1)} %get-tuple-element.63), channel_id=1, source_target_pairs={{0,1},{1,0},{2,3},{3,2},{4,5},{5,4},{6,7},{7,6},{8,9},{9,8},{10,11... | collective-permute-start | bytes 884744 | tf_op jit(solution)/shard_map/ppermute | solution.py:23
  32.1 1.9 %collective-permute-start.15 = (bf16[4,32,1152]{2,1,0:T(8,128)(2,1)S(1)}, bf16[4,32,1152]{2,1,0:T(8,128)(2,1)S(1)}, u32[]{:S(2)}, u32[]{:S(2)}) collective-permute-start(bf16[4,32,1152]{2,1,0:T(8,128)(2,1)S(1)} %get-tuple-element.65), channel_id=1, source_target_pairs={{0,1},{1,0},{2,3},{3,2},{4,5},{5,4},{6,7},{7,6},{8,9},{9,8},{10,11... | collective-permute-start | bytes 884744 | tf_op jit(solution)/shard_map/ppermute | solution.py:23
  34.0 9.1 %collective-permute-start.16 = (bf16[4,32,1152]{2,1,0:T(8,128)(2,1)S(1)}, bf16[4,32,1152]{2,1,0:T(8,128)(2,1)S(1)}, u32[]{:S(2)}, u32[]{:S(2)}) collective-permute-start(bf16[4,32,1152]{2,1,0:T(8,128)(2,1)S(1)} %join.1), channel_id=1, source_target_pairs={{0,2},{1,3},{2,0},{3,1},{4,6},{5,7},{6,4},{7,5},{8,10},{9,11},{10,... | collective-permute-start | bytes 884744 | tf_op jit(solution)/shard_map/ppermute | solution.py:23
  35.7 1.6 %collective-permute-start.20 = (bf16[4,2,8,1728]{3,2,1,0:T(8,128)(2,1)S(1)}, bf16[4,2,8,1728]{3,2,1,0:T(8,128)(2,1)S(1)}, u32[]{:S(2)}, u32[]{:S(2)}) collective-permute-start(bf16[4,2,8,1728]{3,2,1,0:T(8,128)(2,1)S(1)} %get-tuple-element.76), channel_id=1, source_target_pairs={{0,1},{1,0},{2,3},{3,2},{4,5},{5,4},{6,7},{7,6},{8,9},{9,8},{10,11... | collective-permute-start | bytes 663560 | tf_op jit(solution)/shard_map/ppermute | solution.py:23
  37.3 8.9 %collective-permute-start.21 = (bf16[2,8,1728]{2,1,0:T(8,128)(2,1)S(1)}, bf16[2,8,1728]{2,1,0:T(8,128)(2,1)S(1)}, u32[]{:S(2)}, u32[]{:S(2)}) collective-permute-start(bf16[2,8,1728]{2,1,0:T(8,128)(2,1)S(1)} %get-tuple-element.78), channel_id=1, source_target_pairs={{0,12},{1,13},{2,14},{3,15},{4,8},{5,9},{6,10},{7,11},{8,4},{9,5},... | collective-permute-start | bytes 165896 | tf_op jit(solution)/shard_map/ppermute | solution.py:23
  39.9 7.8 %collective-permute-start.22 = (bf16[2,8,1728]{2,1,0:T(8,128)(2,1)S(1)}, bf16[2,8,1728]{2,1,0:T(8,128)(2,1)S(1)}, u32[]{:S(2)}, u32[]{:S(2)}) collective-permute-start(bf16[2,8,1728]{2,1,0:T(8,128)(2,1)S(1)} %get-tuple-element.79), channel_id=1, source_target_pairs={{0,8},{1,9},{2,10},{3,11},{4,12},{5,13},{6,14},{7,15},{8,0},{9,1},... | collective-permute-start | bytes 165896 | tf_op jit(solution)/shard_map/ppermute | solution.py:23
  40.9 6.9 %collective-permute-start.23 = (bf16[2,8,1728]{2,1,0:T(8,128)(2,1)S(1)}, bf16[2,8,1728]{2,1,0:T(8,128)(2,1)S(1)}, u32[]{:S(2)}, u32[]{:S(2)}) collective-permute-start(bf16[2,8,1728]{2,1,0:T(8,128)(2,1)S(1)} %get-tuple-element.80), channel_id=1, source_target_pairs={{0,4},{1,5},{2,6},{3,7},{4,0},{5,1},{6,2},{7,3},{8,12},{9,13},{10,... | collective-permute-start | bytes 165896 | tf_op jit(solution)/shard_map/ppermute | solution.py:23
  43.2 8.5 %collective-permute-start.17 = (bf16[32,1152]{1,0:T(8,128)(2,1)S(1)}, bf16[32,1152]{1,0:T(8,128)(2,1)S(1)}, u32[]{:S(2)}, u32[]{:S(2)}) collective-permute-start(bf16[32,1152]{1,0:T(8,128)(2,1)S(1)} %get-tuple-element.67), channel_id=1, source_target_pairs={{0,8},{1,9},{2,10},{3,11},{4,12},{5,13},{6,14},{7,15},{8,0},{9,1},... | collective-permute-start | bytes 221192 | tf_op jit(solution)/shard_map/ppermute | solution.py:23
  46.2 5.5 %collective-permute-start.18 = (bf16[32,1152]{1,0:T(8,128)(2,1)S(1)}, bf16[32,1152]{1,0:T(8,128)(2,1)S(1)}, u32[]{:S(2)}, u32[]{:S(2)}) collective-permute-start(bf16[32,1152]{1,0:T(8,128)(2,1)S(1)} %get-tuple-element.68), channel_id=1, source_target_pairs={{0,4},{1,5},{2,6},{3,7},{4,0},{5,1},{6,2},{7,3},{8,12},{9,13},{10,... | collective-permute-start | bytes 221192 | tf_op jit(solution)/shard_map/ppermute | solution.py:23
  46.2 6.2 %collective-permute-start.19 = (bf16[32,1152]{1,0:T(8,128)(2,1)S(1)}, bf16[32,1152]{1,0:T(8,128)(2,1)S(1)}, u32[]{:S(2)}, u32[]{:S(2)}) collective-permute-start(bf16[32,1152]{1,0:T(8,128)(2,1)S(1)} %get-tuple-element.69), channel_id=1, source_target_pairs={{0,12},{1,13},{2,14},{3,15},{4,8},{5,9},{6,10},{7,11},{8,4},{9,5},... | collective-permute-start | bytes 221192 | tf_op jit(solution)/shard_map/ppermute | solution.py:23
  47.8 3.9 %collective-permute-start.24 = (bf16[8,1728]{1,0:T(8,128)(2,1)S(1)}, bf16[8,1728]{1,0:T(8,128)(2,1)S(1)}, u32[]{:S(2)}, u32[]{:S(2)}) collective-permute-start(bf16[8,1728]{1,0:T(8,128)(2,1)S(1)} %get-tuple-element.82), channel_id=1, source_target_pairs={{0,2},{1,3},{2,0},{3,1},{4,6},{5,7},{6,4},{7,5},{8,10},{9,11},{10,... | collective-permute-start | bytes 82952 | tf_op jit(solution)/shard_map/ppermute | solution.py:23

commit v9 on v8

--- a/solution.py
+++ b/solution.py
@@ -388,7 +388,6 @@
     student_own_ref,
     hc_ref,
     hyc_ref,
-    send_ref,
     send_y_ref,
     slope_ref,
     w_other_ref,
@@ -422,12 +421,32 @@
             slope_ref[at, lane : lane + half] = (student * s_part - target * t_part).astype(bf16)
 
     lo, n_own = HALO_SLOPE * rows, own * rows
+    first = half + half // 2
     terms = dot(
-        slope_ref[lo : lo + n_own, half:], patch_last_ref[lo : lo + n_own, :], ((0,), (0,))
-    )
-    terms = terms.astype(bf16).reshape((2,) + send_ref.shape)
-    send_ref[...] = terms[0]
-    send_y_ref[...] = terms[1]
+        slope_ref[lo : lo + n_own, first:], patch_last_ref[lo : lo + n_own, :], ((0,), (0,))
+    )
+    send_y_ref[...] = terms.astype(bf16).reshape(send_y_ref.shape)
+
+
+def beside_kernel(own, rows, slope_ref, patch_last_ref, keep_y_ref):
+    half, lo, n_own = slope_ref.shape[1] // 2, HALO_SLOPE * rows, own * rows
+    terms = dot(
+        slope_ref[lo : lo + n_own, half // 2 : half],
+        patch_last_ref[lo : lo + n_own, :],
+        ((0,), (0,)),
+    )
+    keep_y_ref[...] = terms.reshape(keep_y_ref.shape)
+
+
+def stay_kernel(own, rows, slope_ref, patch_last_ref, keep_ref, send_ref):
+    half, lo, n_own = slope_ref.shape[1] // 2, HALO_SLOPE * rows, own * rows
+    stays = jnp.concatenate(
+        [slope_ref[lo : lo + n_own, first : first + half // 2] for first in (0, half)], 1
+    )
+    terms = dot(stays, patch_last_ref[lo : lo + n_own, :], ((0,), (0,)))
+    terms = terms.reshape((2,) + keep_ref.shape)
+    keep_ref[...] = terms[0]
+    send_ref[...] = terms[1].astype(bf16)
 
 
 def back_kernel(
@@ -437,20 +456,11 @@
     tilt_second_ref,
     w_own_ref,
     w_other_ref,
-    patch_last_ref,
-    keep_ref,
-    keep_y_ref,
+    tie_ref,
     slope_second_ref,
     parts_ref,
 ):
     half = w_own_ref.shape[0]
-    lo, n_own = HALO_SLOPE * rows, own * rows
-    terms = dot(
-        slope_ref[lo : lo + n_own, :half], patch_last_ref[lo : lo + n_own, :], ((0,), (0,))
-    )
-    terms = terms.reshape((2,) + keep_ref.shape)
-    keep_ref[...] = terms[0]
-    keep_y_ref[...] = terms[1]
     parts_ref[...] = dot(slope_ref[:, :half], w_own_ref[...], ((1,), (0,))) + dot(
         slope_ref[:, half:], w_other_ref[...], ((1,), (0,))
     )
@@ -673,12 +683,11 @@
         [],
         HALF_COST,
     )
-    send, send_y, slope, w_other = call(
+    send_y, slope, w_other = call(
         functools.partial(front_kernel, own, rows, total),
         "front",
         (target, patch_last, student_own, last_c, last_yc),
         [
-            ((FAR, r_last, 9 * hidden), bf16),
             ((FAR, r_last, 9 * hidden), bf16),
             ((n_slope, channels), bf16),
             ((half, 9 * hidden), bf16),
@@ -686,14 +695,26 @@
         [((n_slope, half), f32)],
         6_000_000_000,
     )
-    got_y, got = swap(send_y, fold), swap(send, fold)
-    keep, keep_y, slope_second = call(
+    got_y = swap(send_y, fold)
+    quarter = (FAR, r_last, 9 * hidden)
+    (keep_y,) = call(
+        functools.partial(beside_kernel, own, rows),
+        "beside",
+        (slope, patch_last),
+        [(quarter, f32)],
+        [],
+        1_000_000_000,
+    )
+    (last_sent,) = call(join_kernel, "join", (keep_y, got_y), [(quarter, bf16)], [], 1_000_000)
+    last_got = swap(last_sent, 2 * fold)
+    (slope_second,) = call(
         functools.partial(back_kernel, own, rows),
         "back",
-        (slope, tilt_second, w_own, w_other, patch_last),
-        [((FAR, r_last, 9 * hidden), f32)] * 2 + [((n_back, hidden), bf16)],
+        (slope, tilt_second, w_own, w_other, last_sent),
+        [((n_back, hidden), bf16)],
         [((n_slope, 9 * hidden), f32)],
         4_000_000_000,
+        {4: anywhere},
     )
     both = 9 * (hidden + in_depth)
     small_keep, small_send = call(
@@ -705,13 +726,21 @@
         2_000_000_000,
     )
 
+    keep, send = call(
+        functools.partial(stay_kernel, own, rows),
+        "stay",
+        (slope, patch_last),
+        [(quarter, f32), (quarter, bf16)],
+        [],
+        1_000_000,
+    )
+    got = swap(send, fold)
+
     def split(keep, *got):
         shape = keep.shape[1:]
         outs = [(shape, f32)] + [(shape, bf16)] * (FAR - 1)
         return call(split_kernel, "split", (keep, *got), outs, [], 1_000_000)
 
-    (last_sent,) = call(join_kernel, "join", (keep_y, got_y), [(keep.shape, bf16)], [], 1_000_000)
-    last_got = swap(last_sent, 2 * fold)
     parts = split(small_keep, swap(small_send, fold))
     small_got = {k: swap(parts[k], 4 * k * fold) for k in (1, 2, 3)}
     last = split(keep, got, last_got)

time: 53.3 us -> 52.8 us (level)
  waiting for transfers between devices: 15.4 us -> 14.5 us
    ppermute x24, waiting for transfers between devices: 15.4 us -> 14.5 us  [swap(): return lax.ppermute(array, 'cols', [(i, i ^ mask) for i in range(size)])]
    pallas_call x15 -> x17, Pallas kernels: 11.7 us -> 11.7 us  [call(): pl.pallas_call(kernel, in_specs=[spaces.get(i, vmem) for i in range(len(i...]
  transfers between devices with their start and end apart: 25 -> 25, of which waited for: 10 -> 11; matrix products, arithmetic and copies ran while one was open for 0% -> 0% of each run, Pallas kernels for 12% -> 13%
where the time goes in v9:
time: 52.8 us; the launch traced here: 52.6 us
  starting transfers between devices  24.8 us (47%)
  waiting for transfers between devices  14.5 us (27%)
  Pallas kernels  11.7 us (22%)
  local copies, waits for them, and re-layouts  0.95 us (2%)
  between operations  0.77 us (1%)
    ppermute x24, starting transfers between devices, swap(): return lax.ppermute(array, 'cols', [(i, i ^ mask) for i in range(size)])  24.8 us
    ppermute x24, waiting for transfers between devices, swap(): return lax.ppermute(array, 'cols', [(i, i ^ mask) for i in range(size)])  14.5 us
    pallas_call x17, Pallas kernels, call(): pl.pallas_call(kernel, in_specs=[spaces.get(i, vmem) for i in range(len(i...  11.7 us
  transfers between devices with their start and end apart: 25, of which 11 were waited for; matrix products, arithmetic and copies ran while one was open for 0% of the time, Pallas kernels for 13%

profile of v9, /device:TPU:0, one launch (start us, length us, event | category | flops | bytes accessed | tf_op | source)
XLA Modules:
  0.0 52.6 jit_solution(2626517125423067103)
XLA Ops:
  0.6 2.4 %deal.1 = (bf16[1040,128]{1,0:T(8,128)(2,1)}, bf16[640,128]{1,0:T(8,128)(2,1)}, bf16[1152,128]{1,0:T(8,128)(2,1)}, bf16[400,128]{1,0:T(8,128)(2,1)}) custom-call(bf16[32,1024]{1,0:T(8,128)(2,1)} %x_hbm.1, bf16[32,16,512]{2,1,0:T(8,128)(2,1)} %teacher_hbm.1, bf16[8,576]{1,0:T(8,128)(2,1)} %w_first_hbm.1, bf16[8,1152]{1,0:T(8,128)(2,1)} %w_middle_hbm.1, ...), custom_call_target="tpu_custom_call" | custom-call | flops 600000000 | bytes 1000000 | tf_op jit(solution)/shard_map/deal/pallas_call | solution.py:542
  3.0 3.0 %collective-permute-start.2 = (bf16[1152,128]{1,0:T(8,128)(2,1)}, bf16[1152,128]{1,0:T(8,128)(2,1)S(1)}, u32[]{:S(2)}, u32[]{:S(2)}) collective-permute-start(bf16[1152,128]{1,0:T(8,128)(2,1)} %get-tuple-element.45), channel_id=1, source_target_pairs={{0,2},{1,3},{2,0},{3,1},{4,6},{5,7},{6,4},{7,5},{8,10},{9,11},{10,... | collective-permute-start | bytes 884744 | tf_op jit(solution)/shard_map/ppermute | solution.py:23
  6.1 1.6 %collective-permute-start = (bf16[400,128]{1,0:T(8,128)(2,1)}, bf16[400,128]{1,0:T(8,128)(2,1)S(1)}, u32[]{:S(2)}, u32[]{:S(2)}) collective-permute-start(bf16[400,128]{1,0:T(8,128)(2,1)} %get-tuple-element.42), channel_id=1, source_target_pairs={{0,4},{1,5},{2,6},{3,7},{4,0},{5,1},{6,2},{7,3},{8,12},{9,13},{10,... | collective-permute-start | bytes 307208 | tf_op jit(solution)/shard_map/ppermute | solution.py:23
  7.6 2.6 %collective-permute-start.7 = (bf16[400,128]{1,0:T(8,128)(2,1)}, bf16[400,128]{1,0:T(8,128)(2,1)S(1)}, u32[]{:S(2)}, u32[]{:S(2)}) collective-permute-start(bf16[400,128]{1,0:T(8,128)(2,1)} %get-tuple-element.42), channel_id=1, source_target_pairs={{0,8},{1,9},{2,10},{3,11},{4,12},{5,13},{6,14},{7,15},{8,0},{9,1},... | collective-permute-start | bytes 307208 | tf_op jit(solution)/shard_map/ppermute | solution.py:23
  10.5 1.5 %collective-permute-done.far_ref = bf16[400,128]{1,0:T(8,128)(2,1)S(1)} collective-permute-done((bf16[400,128]{1,0:T(8,128)(2,1)}, bf16[400,128]{1,0:T(8,128)(2,1)S(1)}, u32[]{:S(2)}, u32[]{:S(2)}) %collective-permute-start) | collective-permute-done | bytes 102432 | tf_op jit(solution)/shard_map/ppermute | solution.py:23
  12.0 0.9 %copy-done = bf16[1040,128]{1,0:T(8,128)(2,1)S(1)} copy-done((bf16[1040,128]{1,0:T(8,128)(2,1)S(1)}, bf16[1040,128]{1,0:T(8,128)(2,1)}, u32[]{:S(2)}) %copy-start) | copy-done | bytes 266264
  13.3 5.0 %collective-permute-done.7.far2_ref = bf16[400,128]{1,0:T(8,128)(2,1)S(1)} collective-permute-done((bf16[400,128]{1,0:T(8,128)(2,1)}, bf16[400,128]{1,0:T(8,128)(2,1)S(1)}, u32[]{:S(2)}, u32[]{:S(2)}) %collective-permute-start.7) | collective-permute-done | bytes 102432 | tf_op jit(solution)/shard_map/ppermute | solution.py:23
  18.4 0.6 %collective-permute-start.8 = (bf16[4,112,128]{2,1,0:T(8,128)(2,1)S(1)}, bf16[4,112,128]{2,1,0:T(8,128)(2,1)S(1)}, u32[]{:S(2)}, u32[]{:S(2)}) collective-permute-start(bf16[4,112,128]{2,1,0:T(8,128)(2,1)S(1)} %get-tuple-element.51.h_ref), channel_id=1, source_target_pairs={{0,2},{1,3},{2,0},{3,1},{4,6},{5,7},{6,4},{7,5},{8,10},{9,11},{10,... | collective-permute-start | bytes 344072 | tf_op jit(solution)/shard_map/ppermute | solution.py:23
  18.9 1.5 %collective-permute-start.11 = (bf16[4,288,128]{2,1,0:T(8,128)(2,1)S(1)}, bf16[4,288,128]{2,1,0:T(8,128)(2,1)S(1)}, u32[]{:S(2)}, u32[]{:S(2)}) collective-permute-start(bf16[4,288,128]{2,1,0:T(8,128)(2,1)S(1)} %get-tuple-element.53.h_ref), channel_id=1, source_target_pairs={{0,2},{1,3},{2,0},{3,1},{4,6},{5,7},{6,4},{7,5},{8,10},{9,11},{10,... | collective-permute-start | bytes 884744 | tf_op jit(solution)/shard_map/ppermute | solution.py:23
  20.7 1.7 %collective-permute-start.4 = (bf16[496,128]{1,0:T(8,128)(2,1)S(1)}, bf16[496,128]{1,0:T(8,128)(2,1)S(1)}, u32[]{:S(2)}, u32[]{:S(2)}) collective-permute-start(bf16[496,128]{1,0:T(8,128)(2,1)S(1)} %get-tuple-element.47), channel_id=1, source_target_pairs={{0,4},{1,5},{2,6},{3,7},{4,0},{5,1},{6,2},{7,3},{8,12},{9,13},{10,... | collective-permute-start | bytes 380936 | tf_op jit(solution)/shard_map/ppermute | solution.py:23
  22.4 0.5 collective-permute-start.9
  22.9 1.5 %collective-permute-done.8.hy_ref = bf16[4,112,128]{2,1,0:T(8,128)(2,1)S(1)} collective-permute-done((bf16[4,112,128]{2,1,0:T(8,128)(2,1)S(1)}, bf16[4,112,128]{2,1,0:T(8,128)(2,1)S(1)}, u32[]{:S(2)}, u32[]{:S(2)}) %collective-permute-start.8) | collective-permute-done | bytes 114720 | tf_op jit(solution)/shard_map/ppermute | solution.py:23
  24.4 0.5 collective-permute-start.12
  24.9 0.8 %collective-permute-done.10.hyc_ref = bf16[4,112,128]{2,1,0:T(8,128)(2,1)S(1)} collective-permute-done((bf16[4,112,128]{2,1,0:T(8,128)(2,1)S(1)}, bf16[4,112,128]{2,1,0:T(8,128)(2,1)S(1)}, u32[]{:S(2)}, u32[]{:S(2)}) %collective-permute-start.10) | collective-permute-done | bytes 114720 | tf_op jit(solution)/shard_map/ppermute | solution.py:23
  25.8 2.2 %early.1 = (f32[512,128]{1,0:T(8,128)S(1)}, f32[576,128]{1,0:T(8,128)S(1)}, bf16[896,576]{1,0:T(8,128)(2,1)S(1)}, bf16[832,1152]{1,0:T(8,128)(2,1)S(1)}, bf16[70...) custom-call(bf16[512,64]{1,0:T(8,128)(2,1)S(1)} %get-tuple-element.49.x_ref, ...), custom_call_target="tpu_custom_call" | custom-call | flops 1500000000 | bytes 1000000 | tf_op jit(solution)/shard_map/early/pallas_call | solution.py:542
  28.2 1.1 %half.1 = (bf16[256,1152]{1,0:T(8,128)(2,1)S(1)}, f32[704,256]{1,0:T(8,128)S(1)}, bf16[704,512]{1,0:T(8,128)(2,1)S(1)}) custom-call(bf16[512,512]{1,0:T(8,128)(2,1)S(1)} %get-tuple-element.46.teacher_ref, bf16[496,128]{1,0:T(8,128)(2,1)S(1)} %collective-permute-done.4.edge_a_ref, bf16[496,128]{1,0:T(8,128)(2,1)S(1)} %collective-permute-done.5.edge_b_ref, ...), custom_call_target="tpu_custom_call" | custom-call | flops 1500000000 | bytes 1000000 | tf_op jit(solution)/shard_map/half/pallas_call | solution.py:542
  29.7 1.7 %front.1 = (bf16[4,32,1152]{2,1,0:T(8,128)(2,1)S(1)}, bf16[704,512]{1,0:T(8,128)(2,1)S(1)}, bf16[256,1152]{1,0:T(8,128)(2,1)S(1)}) custom-call(bf16[704,512]{1,0:T(8,128)(2,1)S(1)} %get-tuple-element.54.target_ref, bf16[704,1152]{1,0:T(8,128)(2,1)S(1)} %get-tuple-element.52.first_ref.patch_last_ref, f32[704,256]{1,0:T(8,128)S(1)} %get-tuple-element.55.student_own_ref, ...), custom_call_target="tpu_custom_call" | custom-call | flops 6000000000 | bytes 1000000 | tf_op jit(solution)/shard_map/front/pallas_call | solution.py:542
  31.5 0.5 stay.1
  32.1 0.4 collective-permute-start.14
  33.0 0.6 %collective-permute-start.16 = (bf16[4,32,1152]{2,1,0:T(8,128)(2,1)S(1)}, bf16[4,32,1152]{2,1,0:T(8,128)(2,1)S(1)}, u32[]{:S(2)}, u32[]{:S(2)}) collective-permute-start(bf16[4,32,1152]{2,1,0:T(8,128)(2,1)S(1)} %join.1.tie_ref), channel_id=1, source_target_pairs={{0,2},{1,3},{2,0},{3,1},{4,6},{5,7},{6,4},{7,5},{8,10},{9,11},{10,... | collective-permute-start | bytes 884744 | tf_op jit(solution)/shard_map/ppermute | solution.py:23
  33.6 1.1 %back.1.slope_second_ref = bf16[576,128]{1,0:T(8,128)(2,1)S(1)} custom-call(bf16[704,512]{1,0:T(8,128)(2,1)S(1)} %get-tuple-element.56.slope_ref, f32[576,128]{1,0:T(8,128)S(1)} %get-tuple-element.64.tilt_second_ref, bf16[256,1152]{1,0:T(8,128)(2,1)S(1)} %get-tuple-element.65.w_own_ref, bf16[256,1152]{1,0:T(8,128)(2,1)S(1)} %get-tuple-element.66.w_other_ref, ...), custom_call_target="tpu_custom_call" | custom-call | flops 4000000000 | bytes 1000000 | tf_op jit(solution)/shard_map/back/pallas_call | solution.py:542
  34.7 1.1 %first.1 = (f32[4,2,8,1728]{3,2,1,0:T(8,128)S(1)}, bf16[4,2,8,1728]{3,2,1,0:T(8,128)(2,1)S(1)}) custom-call(bf16[576,128]{1,0:T(8,128)(2,1)S(1)} %back.1.slope_second_ref, f32[512,128]{1,0:T(8,128)S(1)} %get-tuple-element.67.tilt_first_ref, bf16[896,576]{1,0:T(8,128)(2,1)S(1)} %get-tuple-element.68.patch_first_ref, ...), custom_call_target="tpu_custom_call" | custom-call | flops 2000000000 | bytes 1000000 | tf_op jit(solution)/shard_map/first/pallas_call | solution.py:542
  36.0 1.5 %collective-permute-done.20.refs_0_ = bf16[4,2,8,1728]{3,2,1,0:T(8,128)(2,1)S(1)} collective-permute-done((bf16[4,2,8,1728]{3,2,1,0:T(8,128)(2,1)S(1)}, bf16[4,2,8,1728]{3,2,1,0:T(8,128)(2,1)S(1)}, u32[]{:S(2)}, u32[]{:S(2)}) %collective-permute-start.20) | collective-permute-done | bytes 221216 | tf_op jit(solution)/shard_map/ppermute | solution.py:23
  37.5 2.6 %collective-permute-start.21 = (bf16[2,8,1728]{2,1,0:T(8,128)(2,1)S(1)}, bf16[2,8,1728]{2,1,0:T(8,128)(2,1)S(1)}, u32[]{:S(2)}, u32[]{:S(2)}) collective-permute-start(bf16[2,8,1728]{2,1,0:T(8,128)(2,1)S(1)} %get-tuple-element.74), channel_id=1, source_target_pairs={{0,12},{1,13},{2,14},{3,15},{4,8},{5,9},{6,10},{7,11},{8,4},{9,5},... | collective-permute-start | bytes 165896 | tf_op jit(solution)/shard_map/ppermute | solution.py:23
  40.1 1.0 %collective-permute-start.22 = (bf16[2,8,1728]{2,1,0:T(8,128)(2,1)S(1)}, bf16[2,8,1728]{2,1,0:T(8,128)(2,1)S(1)}, u32[]{:S(2)}, u32[]{:S(2)}) collective-permute-start(bf16[2,8,1728]{2,1,0:T(8,128)(2,1)S(1)} %get-tuple-element.75), channel_id=1, source_target_pairs={{0,8},{1,9},{2,10},{3,11},{4,12},{5,13},{6,14},{7,15},{8,0},{9,1},... | collective-permute-start | bytes 165896 | tf_op jit(solution)/shard_map/ppermute | solution.py:23
  41.0 0.9 %collective-permute-start.23 = (bf16[2,8,1728]{2,1,0:T(8,128)(2,1)S(1)}, bf16[2,8,1728]{2,1,0:T(8,128)(2,1)S(1)}, u32[]{:S(2)}, u32[]{:S(2)}) collective-permute-start(bf16[2,8,1728]{2,1,0:T(8,128)(2,1)S(1)} %get-tuple-element.76), channel_id=1, source_target_pairs={{0,4},{1,5},{2,6},{3,7},{4,0},{5,1},{6,2},{7,3},{8,12},{9,13},{10,... | collective-permute-start | bytes 165896 | tf_op jit(solution)/shard_map/ppermute | solution.py:23
  42.2 3.0 %collective-permute-start.17 = (bf16[32,1152]{1,0:T(8,128)(2,1)S(1)}, bf16[32,1152]{1,0:T(8,128)(2,1)S(1)}, u32[]{:S(2)}, u32[]{:S(2)}) collective-permute-start(bf16[32,1152]{1,0:T(8,128)(2,1)S(1)} %get-tuple-element.61), channel_id=1, source_target_pairs={{0,8},{1,9},{2,10},{3,11},{4,12},{5,13},{6,14},{7,15},{8,0},{9,1},... | collective-permute-start | bytes 221192 | tf_op jit(solution)/shard_map/ppermute | solution.py:23
  45.2 1.5 %collective-permute-start.19 = (bf16[32,1152]{1,0:T(8,128)(2,1)S(1)}, bf16[32,1152]{1,0:T(8,128)(2,1)S(1)}, u32[]{:S(2)}, u32[]{:S(2)}) collective-permute-start(bf16[32,1152]{1,0:T(8,128)(2,1)S(1)} %get-tuple-element.63), channel_id=1, source_target_pairs={{0,12},{1,13},{2,14},{3,15},{4,8},{5,9},{6,10},{7,11},{8,4},{9,5},... | collective-permute-start | bytes 221192 | tf_op jit(solution)/shard_map/ppermute | solution.py:23
  46.8 1.2 %collective-permute-done.22.got2_ref = bf16[2,8,1728]{2,1,0:T(8,128)(2,1)S(1)} collective-permute-done((bf16[2,8,1728]{2,1,0:T(8,128)(2,1)S(1)}, bf16[2,8,1728]{2,1,0:T(8,128)(2,1)S(1)}, u32[]{:S(2)}, u32[]{:S(2)}) %collective-permute-start.22) | collective-permute-done | bytes 55328 | tf_op jit(solution)/shard_map/ppermute | solution.py:23
  48.0 2.0 %collective-permute-start.24 = (bf16[8,1728]{1,0:T(8,128)(2,1)S(1)}, bf16[8,1728]{1,0:T(8,128)(2,1)S(1)}, u32[]{:S(2)}, u32[]{:S(2)}) collective-permute-start(bf16[8,1728]{1,0:T(8,128)(2,1)S(1)} %get-tuple-element.78), channel_id=1, source_target_pairs={{0,2},{1,3},{2,0},{3,1},{4,6},{5,7},{6,4},{7,5},{8,10},{9,11},{10,... | collective-permute-start | bytes 82952 | tf_op jit(solution)/shard_map/ppermute | solution.py:23
  50.0 1.9 %collective-permute-done.24.got_ref = bf16[8,1728]{1,0:T(8,128)(2,1)S(1)} collective-permute-done((bf16[8,1728]{1,0:T(8,128)(2,1)S(1)}, bf16[8,1728]{1,0:T(8,128)(2,1)S(1)}, u32[]{:S(2)}, u32[]{:S(2)}) %collective-permute-start.24) | collective-permute-done | bytes 27680 | tf_op jit(solution)/shard_map/ppermute | solution.py:23
  51.9 0.7 %finish.1 = (f32[8,576]{1,0:T(8,128)}, f32[8,1152]{1,0:T(8,128)}, f32[32,1152]{1,0:T(8,128)}) custom-call(f32[32,1152]{1,0:T(8,128)S(1)} %get-tuple-element.60.last_ref, bf16[32,1152]{1,0:T(8,128)(2,1)S(1)} %collective-permute-done.17.got1_ref, bf16[32,1152]{1,0:T(8,128)(2,1)S(1)} %collective-permute-done.18.got2_ref, ...), custom_call_target="tpu_custom_call" | custom-call | flops 1000000 | bytes 1000000 | tf_op jit(solution)/shard_map/finish/pallas_call | solution.py:542
  (37 shorter events, 2.7 us)
Async XLA Ops:
  3.0 10.3 %collective-permute-start.2 = (bf16[1152,128]{1,0:T(8,128)(2,1)}, bf16[1152,128]{1,0:T(8,128)(2,1)S(1)}, u32[]{:S(2)}, u32[]{:S(2)}) collective-permute-start(bf16[1152,128]{1,0:T(8,128)(2,1)} %get-tuple-element.45), channel_id=1, source_target_pairs={{0,2},{1,3},{2,0},{3,1},{4,6},{5,7},{6,4},{7,5},{8,10},{9,11},{10,... | collective-permute-start | bytes 884744 | tf_op jit(solution)/shard_map/ppermute | solution.py:23
  6.1 5.9 %collective-permute-start = (bf16[400,128]{1,0:T(8,128)(2,1)}, bf16[400,128]{1,0:T(8,128)(2,1)S(1)}, u32[]{:S(2)}, u32[]{:S(2)}) collective-permute-start(bf16[400,128]{1,0:T(8,128)(2,1)} %get-tuple-element.42), channel_id=1, source_target_pairs={{0,4},{1,5},{2,6},{3,7},{4,0},{5,1},{6,2},{7,3},{8,12},{9,13},{10,... | collective-permute-start | bytes 307208 | tf_op jit(solution)/shard_map/ppermute | solution.py:23
  7.6 10.7 %collective-permute-start.7 = (bf16[400,128]{1,0:T(8,128)(2,1)}, bf16[400,128]{1,0:T(8,128)(2,1)S(1)}, u32[]{:S(2)}, u32[]{:S(2)}) collective-permute-start(bf16[400,128]{1,0:T(8,128)(2,1)} %get-tuple-element.42), channel_id=1, source_target_pairs={{0,8},{1,9},{2,10},{3,11},{4,12},{5,13},{6,14},{7,15},{8,0},{9,1},... | collective-permute-start | bytes 307208 | tf_op jit(solution)/shard_map/ppermute | solution.py:23
  10.2 8.1 %collective-permute-start.6 = (bf16[400,128]{1,0:T(8,128)(2,1)}, bf16[400,128]{1,0:T(8,128)(2,1)S(1)}, u32[]{:S(2)}, u32[]{:S(2)}) collective-permute-start(bf16[400,128]{1,0:T(8,128)(2,1)} %get-tuple-element.42), channel_id=1, source_target_pairs={{0,12},{1,13},{2,14},{3,15},{4,8},{5,9},{6,10},{7,11},{8,4},{9,5},... | collective-permute-start | bytes 307208 | tf_op jit(solution)/shard_map/ppermute | solution.py:23
  10.5 10.0 %collective-permute-start.1 = (bf16[640,128]{1,0:T(8,128)(2,1)}, bf16[640,128]{1,0:T(8,128)(2,1)S(1)}, u32[]{:S(2)}, u32[]{:S(2)}) collective-permute-start(bf16[640,128]{1,0:T(8,128)(2,1)} %get-tuple-element.44), channel_id=1, source_target_pairs={{0,1},{1,0},{2,3},{3,2},{4,5},{5,4},{6,7},{7,6},{8,9},{9,8},{10,11... | collective-permute-start | bytes 491528 | tf_op jit(solution)/shard_map/ppermute | solution.py:23
  11.9 1.0 %copy-start = (bf16[1040,128]{1,0:T(8,128)(2,1)S(1)}, bf16[1040,128]{1,0:T(8,128)(2,1)}, u32[]{:S(2)}) copy-start(bf16[1040,128]{1,0:T(8,128)(2,1)} %get-tuple-element.41.own_ref) | copy-start | bytes 798724
  13.3 7.2 %collective-permute-start.3 = (bf16[1152,128]{1,0:T(8,128)(2,1)S(1)}, bf16[1152,128]{1,0:T(8,128)(2,1)S(1)}, u32[]{:S(2)}, u32[]{:S(2)}) collective-permute-start(bf16[1152,128]{1,0:T(8,128)(2,1)S(1)} %collective-permute-done.2.across_ref), channel_id=1, source_target_pairs={{0,1},{1,0},{2,3},{3,2},{4,5},{5,4},{6,7},{7,6},{8,9},{9,8},{10,11... | collective-permute-start | bytes 884744 | tf_op jit(solution)/shard_map/ppermute | solution.py:23
  18.4 6.1 %collective-permute-start.8 = (bf16[4,112,128]{2,1,0:T(8,128)(2,1)S(1)}, bf16[4,112,128]{2,1,0:T(8,128)(2,1)S(1)}, u32[]{:S(2)}, u32[]{:S(2)}) collective-permute-start(bf16[4,112,128]{2,1,0:T(8,128)(2,1)S(1)} %get-tuple-element.51.h_ref), channel_id=1, source_target_pairs={{0,2},{1,3},{2,0},{3,1},{4,6},{5,7},{6,4},{7,5},{8,10},{9,11},{10,... | collective-permute-start | bytes 344072 | tf_op jit(solution)/shard_map/ppermute | solution.py:23
  18.9 9.1 %collective-permute-start.11 = (bf16[4,288,128]{2,1,0:T(8,128)(2,1)S(1)}, bf16[4,288,128]{2,1,0:T(8,128)(2,1)S(1)}, u32[]{:S(2)}, u32[]{:S(2)}) collective-permute-start(bf16[4,288,128]{2,1,0:T(8,128)(2,1)S(1)} %get-tuple-element.53.h_ref), channel_id=1, source_target_pairs={{0,2},{1,3},{2,0},{3,1},{4,6},{5,7},{6,4},{7,5},{8,10},{9,11},{10,... | collective-permute-start | bytes 884744 | tf_op jit(solution)/shard_map/ppermute | solution.py:23
  20.7 5.1 %collective-permute-start.4 = (bf16[496,128]{1,0:T(8,128)(2,1)S(1)}, bf16[496,128]{1,0:T(8,128)(2,1)S(1)}, u32[]{:S(2)}, u32[]{:S(2)}) collective-permute-start(bf16[496,128]{1,0:T(8,128)(2,1)S(1)} %get-tuple-element.47), channel_id=1, source_target_pairs={{0,4},{1,5},{2,6},{3,7},{4,0},{5,1},{6,2},{7,3},{8,12},{9,13},{10,... | collective-permute-start | bytes 380936 | tf_op jit(solution)/shard_map/ppermute | solution.py:23
  22.4 3.3 %collective-permute-start.5 = (bf16[496,128]{1,0:T(8,128)(2,1)S(1)}, bf16[496,128]{1,0:T(8,128)(2,1)S(1)}, u32[]{:S(2)}, u32[]{:S(2)}) collective-permute-start(bf16[496,128]{1,0:T(8,128)(2,1)S(1)} %get-tuple-element.48), channel_id=1, source_target_pairs={{0,1},{1,0},{2,3},{3,2},{4,8},{5,9},{6,10},{7,11},{8,4},{9,5},{10,... | collective-permute-start | bytes 380936 | tf_op jit(solution)/shard_map/ppermute | solution.py:34
  22.4 2.0 %collective-permute-start.9 = (bf16[4,112,128]{2,1,0:T(8,128)(2,1)S(1)}, bf16[4,112,128]{2,1,0:T(8,128)(2,1)S(1)}, u32[]{:S(2)}, u32[]{:S(2)}) collective-permute-start(bf16[4,112,128]{2,1,0:T(8,128)(2,1)S(1)} %get-tuple-element.51.h_ref), channel_id=1, source_target_pairs={{0,1},{1,0},{2,3},{3,2},{4,5},{5,4},{6,7},{7,6},{8,9},{9,8},{10,11... | collective-permute-start | bytes 344072 | tf_op jit(solution)/shard_map/ppermute | solution.py:23
  24.4 1.3 %collective-permute-start.10 = (bf16[4,112,128]{2,1,0:T(8,128)(2,1)S(1)}, bf16[4,112,128]{2,1,0:T(8,128)(2,1)S(1)}, u32[]{:S(2)}, u32[]{:S(2)}) collective-permute-start(bf16[4,112,128]{2,1,0:T(8,128)(2,1)S(1)} %collective-permute-done.8.hy_ref), channel_id=1, source_target_pairs={{0,1},{1,0},{2,3},{3,2},{4,5},{5,4},{6,7},{7,6},{8,9},{9,8},{10,11... | collective-permute-start | bytes 344072 | tf_op jit(solution)/shard_map/ppermute | solution.py:23
  24.4 4.9 %collective-permute-start.12 = (bf16[4,288,128]{2,1,0:T(8,128)(2,1)S(1)}, bf16[4,288,128]{2,1,0:T(8,128)(2,1)S(1)}, u32[]{:S(2)}, u32[]{:S(2)}) collective-permute-start(bf16[4,288,128]{2,1,0:T(8,128)(2,1)S(1)} %get-tuple-element.53.h_ref), channel_id=1, source_target_pairs={{0,1},{1,0},{2,3},{3,2},{4,5},{5,4},{6,7},{7,6},{8,9},{9,8},{10,11... | collective-permute-start | bytes 884744 | tf_op jit(solution)/shard_map/ppermute | solution.py:23
  28.0 1.6 %collective-permute-start.13 = (bf16[4,288,128]{2,1,0:T(8,128)(2,1)S(1)}, bf16[4,288,128]{2,1,0:T(8,128)(2,1)S(1)}, u32[]{:S(2)}, u32[]{:S(2)}) collective-permute-start(bf16[4,288,128]{2,1,0:T(8,128)(2,1)S(1)} %after.1.hy_ref), channel_id=1, source_target_pairs={{0,1},{1,0},{2,3},{3,2},{4,5},{5,4},{6,7},{7,6},{8,9},{9,8},{10,11... | collective-permute-start | bytes 884744 | tf_op jit(solution)/shard_map/ppermute | solution.py:23
  31.3 1.6 %collective-permute-start.15 = (bf16[4,32,1152]{2,1,0:T(8,128)(2,1)S(1)}, bf16[4,32,1152]{2,1,0:T(8,128)(2,1)S(1)}, u32[]{:S(2)}, u32[]{:S(2)}) collective-permute-start(bf16[4,32,1152]{2,1,0:T(8,128)(2,1)S(1)} %get-tuple-element.59), channel_id=1, source_target_pairs={{0,1},{1,0},{2,3},{3,2},{4,5},{5,4},{6,7},{7,6},{8,9},{9,8},{10,11... | collective-permute-start | bytes 884744 | tf_op jit(solution)/shard_map/ppermute | solution.py:23
  32.1 9.9 %collective-permute-start.14 = (bf16[4,32,1152]{2,1,0:T(8,128)(2,1)S(1)}, bf16[4,32,1152]{2,1,0:T(8,128)(2,1)S(1)}, u32[]{:S(2)}, u32[]{:S(2)}) collective-permute-start(bf16[4,32,1152]{2,1,0:T(8,128)(2,1)S(1)} %get-tuple-element.58), channel_id=1, source_target_pairs={{0,1},{1,0},{2,3},{3,2},{4,5},{5,4},{6,7},{7,6},{8,9},{9,8},{10,11... | collective-permute-start | bytes 884744 | tf_op jit(solution)/shard_map/ppermute | solution.py:23
  33.0 9.1 %collective-permute-start.16 = (bf16[4,32,1152]{2,1,0:T(8,128)(2,1)S(1)}, bf16[4,32,1152]{2,1,0:T(8,128)(2,1)S(1)}, u32[]{:S(2)}, u32[]{:S(2)}) collective-permute-start(bf16[4,32,1152]{2,1,0:T(8,128)(2,1)S(1)} %join.1.tie_ref), channel_id=1, source_target_pairs={{0,2},{1,3},{2,0},{3,1},{4,6},{5,7},{6,4},{7,5},{8,10},{9,11},{10,... | collective-permute-start | bytes 884744 | tf_op jit(solution)/shard_map/ppermute | solution.py:23
  35.9 1.6 %collective-permute-start.20 = (bf16[4,2,8,1728]{3,2,1,0:T(8,128)(2,1)S(1)}, bf16[4,2,8,1728]{3,2,1,0:T(8,128)(2,1)S(1)}, u32[]{:S(2)}, u32[]{:S(2)}) collective-permute-start(bf16[4,2,8,1728]{3,2,1,0:T(8,128)(2,1)S(1)} %get-tuple-element.72), channel_id=1, source_target_pairs={{0,1},{1,0},{2,3},{3,2},{4,5},{5,4},{6,7},{7,6},{8,9},{9,8},{10,11... | collective-permute-start | bytes 663560 | tf_op jit(solution)/shard_map/ppermute | solution.py:23
  37.5 7.8 %collective-permute-start.21 = (bf16[2,8,1728]{2,1,0:T(8,128)(2,1)S(1)}, bf16[2,8,1728]{2,1,0:T(8,128)(2,1)S(1)}, u32[]{:S(2)}, u32[]{:S(2)}) collective-permute-start(bf16[2,8,1728]{2,1,0:T(8,128)(2,1)S(1)} %get-tuple-element.74), channel_id=1, source_target_pairs={{0,12},{1,13},{2,14},{3,15},{4,8},{5,9},{6,10},{7,11},{8,4},{9,5},... | collective-permute-start | bytes 165896 | tf_op jit(solution)/shard_map/ppermute | solution.py:23
  40.1 7.9 %collective-permute-start.22 = (bf16[2,8,1728]{2,1,0:T(8,128)(2,1)S(1)}, bf16[2,8,1728]{2,1,0:T(8,128)(2,1)S(1)}, u32[]{:S(2)}, u32[]{:S(2)}) collective-permute-start(bf16[2,8,1728]{2,1,0:T(8,128)(2,1)S(1)} %get-tuple-element.75), channel_id=1, source_target_pairs={{0,8},{1,9},{2,10},{3,11},{4,12},{5,13},{6,14},{7,15},{8,0},{9,1},... | collective-permute-start | bytes 165896 | tf_op jit(solution)/shard_map/ppermute | solution.py:23
  41.0 6.9 %collective-permute-start.23 = (bf16[2,8,1728]{2,1,0:T(8,128)(2,1)S(1)}, bf16[2,8,1728]{2,1,0:T(8,128)(2,1)S(1)}, u32[]{:S(2)}, u32[]{:S(2)}) collective-permute-start(bf16[2,8,1728]{2,1,0:T(8,128)(2,1)S(1)} %get-tuple-element.76), channel_id=1, source_target_pairs={{0,4},{1,5},{2,6},{3,7},{4,0},{5,1},{6,2},{7,3},{8,12},{9,13},{10,... | collective-permute-start | bytes 165896 | tf_op jit(solution)/shard_map/ppermute | solution.py:23
  42.2 9.7 %collective-permute-start.17 = (bf16[32,1152]{1,0:T(8,128)(2,1)S(1)}, bf16[32,1152]{1,0:T(8,128)(2,1)S(1)}, u32[]{:S(2)}, u32[]{:S(2)}) collective-permute-start(bf16[32,1152]{1,0:T(8,128)(2,1)S(1)} %get-tuple-element.61), channel_id=1, source_target_pairs={{0,8},{1,9},{2,10},{3,11},{4,12},{5,13},{6,14},{7,15},{8,0},{9,1},... | collective-permute-start | bytes 221192 | tf_op jit(solution)/shard_map/ppermute | solution.py:23
  45.2 6.7 %collective-permute-start.18 = (bf16[32,1152]{1,0:T(8,128)(2,1)S(1)}, bf16[32,1152]{1,0:T(8,128)(2,1)S(1)}, u32[]{:S(2)}, u32[]{:S(2)}) collective-permute-start(bf16[32,1152]{1,0:T(8,128)(2,1)S(1)} %get-tuple-element.62), channel_id=1, source_target_pairs={{0,4},{1,5},{2,6},{3,7},{4,0},{5,1},{6,2},{7,3},{8,12},{9,13},{10,... | collective-permute-start | bytes 221192 | tf_op jit(solution)/shard_map/ppermute | solution.py:23
  45.2 6.7 %collective-permute-start.19 = (bf16[32,1152]{1,0:T(8,128)(2,1)S(1)}, bf16[32,1152]{1,0:T(8,128)(2,1)S(1)}, u32[]{:S(2)}, u32[]{:S(2)}) collective-permute-start(bf16[32,1152]{1,0:T(8,128)(2,1)S(1)} %get-tuple-element.63), channel_id=1, source_target_pairs={{0,12},{1,13},{2,14},{3,15},{4,8},{5,9},{6,10},{7,11},{8,4},{9,5},... | collective-permute-start | bytes 221192 | tf_op jit(solution)/shard_map/ppermute | solution.py:23
  48.0 3.9 %collective-permute-start.24 = (bf16[8,1728]{1,0:T(8,128)(2,1)S(1)}, bf16[8,1728]{1,0:T(8,128)(2,1)S(1)}, u32[]{:S(2)}, u32[]{:S(2)}) collective-permute-start(bf16[8,1728]{1,0:T(8,128)(2,1)S(1)} %get-tuple-element.78), channel_id=1, source_target_pairs={{0,2},{1,3},{2,0},{3,1},{4,6},{5,7},{6,4},{7,5},{8,10},{9,11},{10,... | collective-permute-start | bytes 82952 | tf_op jit(solution)/shard_map/ppermute | solution.py:23

commit v10 on v9

--- a/solution.py
+++ b/solution.py
@@ -13,7 +13,7 @@
 HALO_X, HALO_FIRST, HALO_SECOND, HALO_SLOPE, HALO_BACK = 13, 12, 10, 6, 2
 BLOCKS, FAR = 16, 4
 LANES = 128
-STACK_COST = 3_000_000_000
+STACK_COST = 2_000_000_000
 EARLY_COST = 1_500_000_000
 HALF_COST = 1_500_000_000
 

time: 52.8 us -> 52.8 us (level)
  waiting for transfers between devices: 14.5 us -> 13.1 us
  starting transfers between devices: 24.8 us -> 26.1 us
    ppermute x24, waiting for transfers between devices: 14.5 us -> 13.1 us  [swap(): return lax.ppermute(array, 'cols', [(i, i ^ mask) for i in range(size)])]
    ppermute x24, starting transfers between devices: 24.8 us -> 26.1 us  [swap(): return lax.ppermute(array, 'cols', [(i, i ^ mask) for i in range(size)])]
where the time goes in v10:
time: 52.8 us; the launch traced here: 52.6 us
  starting transfers between devices  26.1 us (49%)
  waiting for transfers between devices  13.1 us (25%)
  Pallas kernels  11.7 us (22%)
  local copies, waits for them, and re-layouts  0.95 us (2%)
  between operations  0.77 us (1%)
    ppermute x24, starting transfers between devices, swap(): return lax.ppermute(array, 'cols', [(i, i ^ mask) for i in range(size)])  26.1 us
    ppermute x24, waiting for transfers between devices, swap(): return lax.ppermute(array, 'cols', [(i, i ^ mask) for i in range(size)])  13.1 us
    pallas_call x17, Pallas kernels, call(): pl.pallas_call(kernel, in_specs=[spaces.get(i, vmem) for i in range(len(i...  11.7 us
  transfers between devices with their start and end apart: 25, of which 11 were waited for; matrix products, arithmetic and copies ran while one was open for 0% of the time, Pallas kernels for 13%

profile of v10, /device:TPU:0, one launch (start us, length us, event | category | flops | bytes accessed | tf_op | source)
XLA Modules:
  0.0 52.6 jit_solution(10203651893969162513)
XLA Ops:
  0.6 2.4 %deal.1 = (bf16[1040,128]{1,0:T(8,128)(2,1)}, bf16[640,128]{1,0:T(8,128)(2,1)}, bf16[1152,128]{1,0:T(8,128)(2,1)}, bf16[400,128]{1,0:T(8,128)(2,1)}) custom-call(bf16[32,1024]{1,0:T(8,128)(2,1)} %x_hbm.1, bf16[32,16,512]{2,1,0:T(8,128)(2,1)} %teacher_hbm.1, bf16[8,576]{1,0:T(8,128)(2,1)} %w_first_hbm.1, bf16[8,1152]{1,0:T(8,128)(2,1)} %w_middle_hbm.1, ...), custom_call_target="tpu_custom_call" | custom-call | flops 600000000 | bytes 1000000 | tf_op jit(solution)/shard_map/deal/pallas_call | solution.py:542
  3.0 3.0 %collective-permute-start.2 = (bf16[1152,128]{1,0:T(8,128)(2,1)}, bf16[1152,128]{1,0:T(8,128)(2,1)S(1)}, u32[]{:S(2)}, u32[]{:S(2)}) collective-permute-start(bf16[1152,128]{1,0:T(8,128)(2,1)} %get-tuple-element.45), channel_id=1, source_target_pairs={{0,2},{1,3},{2,0},{3,1},{4,6},{5,7},{6,4},{7,5},{8,10},{9,11},{10,... | collective-permute-start | bytes 884744 | tf_op jit(solution)/shard_map/ppermute | solution.py:23
  6.1 1.6 %collective-permute-start = (bf16[400,128]{1,0:T(8,128)(2,1)}, bf16[400,128]{1,0:T(8,128)(2,1)S(1)}, u32[]{:S(2)}, u32[]{:S(2)}) collective-permute-start(bf16[400,128]{1,0:T(8,128)(2,1)} %get-tuple-element.42), channel_id=1, source_target_pairs={{0,4},{1,5},{2,6},{3,7},{4,0},{5,1},{6,2},{7,3},{8,12},{9,13},{10,... | collective-permute-start | bytes 307208 | tf_op jit(solution)/shard_map/ppermute | solution.py:23
  7.6 2.6 %collective-permute-start.7 = (bf16[400,128]{1,0:T(8,128)(2,1)}, bf16[400,128]{1,0:T(8,128)(2,1)S(1)}, u32[]{:S(2)}, u32[]{:S(2)}) collective-permute-start(bf16[400,128]{1,0:T(8,128)(2,1)} %get-tuple-element.42), channel_id=1, source_target_pairs={{0,8},{1,9},{2,10},{3,11},{4,12},{5,13},{6,14},{7,15},{8,0},{9,1},... | collective-permute-start | bytes 307208 | tf_op jit(solution)/shard_map/ppermute | solution.py:23
  10.5 2.8 %collective-permute-done.2.across_ref = bf16[1152,128]{1,0:T(8,128)(2,1)S(1)} collective-permute-done((bf16[1152,128]{1,0:T(8,128)(2,1)}, bf16[1152,128]{1,0:T(8,128)(2,1)S(1)}, u32[]{:S(2)}, u32[]{:S(2)}) %collective-permute-start.2) | collective-permute-done | bytes 294944 | tf_op jit(solution)/shard_map/ppermute | solution.py:23
  13.3 0.5 collective-permute-start.1
  13.8 1.0 %copy-done = bf16[1040,128]{1,0:T(8,128)(2,1)S(1)} copy-done((bf16[1040,128]{1,0:T(8,128)(2,1)S(1)}, bf16[1040,128]{1,0:T(8,128)(2,1)}, u32[]{:S(2)}) %copy-start) | copy-done | bytes 266264
  14.8 3.5 %collective-permute-done.7.far2_ref = bf16[400,128]{1,0:T(8,128)(2,1)S(1)} collective-permute-done((bf16[400,128]{1,0:T(8,128)(2,1)}, bf16[400,128]{1,0:T(8,128)(2,1)S(1)}, u32[]{:S(2)}, u32[]{:S(2)}) %collective-permute-start.7) | collective-permute-done | bytes 102432 | tf_op jit(solution)/shard_map/ppermute | solution.py:23
  18.4 0.6 %collective-permute-start.8 = (bf16[4,112,128]{2,1,0:T(8,128)(2,1)S(1)}, bf16[4,112,128]{2,1,0:T(8,128)(2,1)S(1)}, u32[]{:S(2)}, u32[]{:S(2)}) collective-permute-start(bf16[4,112,128]{2,1,0:T(8,128)(2,1)S(1)} %get-tuple-element.51.h_ref), channel_id=1, source_target_pairs={{0,2},{1,3},{2,0},{3,1},{4,6},{5,7},{6,4},{7,5},{8,10},{9,11},{10,... | collective-permute-start | bytes 344072 | tf_op jit(solution)/shard_map/ppermute | solution.py:23
  18.9 1.5 %collective-permute-start.11 = (bf16[4,288,128]{2,1,0:T(8,128)(2,1)S(1)}, bf16[4,288,128]{2,1,0:T(8,128)(2,1)S(1)}, u32[]{:S(2)}, u32[]{:S(2)}) collective-permute-start(bf16[4,288,128]{2,1,0:T(8,128)(2,1)S(1)} %get-tuple-element.53.h_ref), channel_id=1, source_target_pairs={{0,2},{1,3},{2,0},{3,1},{4,6},{5,7},{6,4},{7,5},{8,10},{9,11},{10,... | collective-permute-start | bytes 884744 | tf_op jit(solution)/shard_map/ppermute | solution.py:23
  20.7 1.7 %collective-permute-start.4 = (bf16[496,128]{1,0:T(8,128)(2,1)S(1)}, bf16[496,128]{1,0:T(8,128)(2,1)S(1)}, u32[]{:S(2)}, u32[]{:S(2)}) collective-permute-start(bf16[496,128]{1,0:T(8,128)(2,1)S(1)} %get-tuple-element.47), channel_id=1, source_target_pairs={{0,4},{1,5},{2,6},{3,7},{4,0},{5,1},{6,2},{7,3},{8,12},{9,13},{10,... | collective-permute-start | bytes 380936 | tf_op jit(solution)/shard_map/ppermute | solution.py:23
  22.4 0.5 collective-permute-start.9
  22.9 1.5 %collective-permute-done.8.hy_ref = bf16[4,112,128]{2,1,0:T(8,128)(2,1)S(1)} collective-permute-done((bf16[4,112,128]{2,1,0:T(8,128)(2,1)S(1)}, bf16[4,112,128]{2,1,0:T(8,128)(2,1)S(1)}, u32[]{:S(2)}, u32[]{:S(2)}) %collective-permute-start.8) | collective-permute-done | bytes 114720 | tf_op jit(solution)/shard_map/ppermute | solution.py:23
  24.4 0.5 collective-permute-start.12
  24.9 0.8 %collective-permute-done.10.hyc_ref = bf16[4,112,128]{2,1,0:T(8,128)(2,1)S(1)} collective-permute-done((bf16[4,112,128]{2,1,0:T(8,128)(2,1)S(1)}, bf16[4,112,128]{2,1,0:T(8,128)(2,1)S(1)}, u32[]{:S(2)}, u32[]{:S(2)}) %collective-permute-start.10) | collective-permute-done | bytes 114720 | tf_op jit(solution)/shard_map/ppermute | solution.py:23
  25.8 2.2 %early.1 = (f32[512,128]{1,0:T(8,128)S(1)}, f32[576,128]{1,0:T(8,128)S(1)}, bf16[896,576]{1,0:T(8,128)(2,1)S(1)}, bf16[832,1152]{1,0:T(8,128)(2,1)S(1)}, bf16[70...) custom-call(bf16[512,64]{1,0:T(8,128)(2,1)S(1)} %get-tuple-element.49.x_ref, ...), custom_call_target="tpu_custom_call" | custom-call | flops 1500000000 | bytes 1000000 | tf_op jit(solution)/shard_map/early/pallas_call | solution.py:542
  28.2 1.1 %half.1 = (bf16[256,1152]{1,0:T(8,128)(2,1)S(1)}, f32[704,256]{1,0:T(8,128)S(1)}, bf16[704,512]{1,0:T(8,128)(2,1)S(1)}) custom-call(bf16[512,512]{1,0:T(8,128)(2,1)S(1)} %get-tuple-element.46.teacher_ref, bf16[496,128]{1,0:T(8,128)(2,1)S(1)} %collective-permute-done.4.edge_a_ref, bf16[496,128]{1,0:T(8,128)(2,1)S(1)} %collective-permute-done.5.edge_b_ref, ...), custom_call_target="tpu_custom_call" | custom-call | flops 1500000000 | bytes 1000000 | tf_op jit(solution)/shard_map/half/pallas_call | solution.py:542
  29.7 1.7 %front.1 = (bf16[4,32,1152]{2,1,0:T(8,128)(2,1)S(1)}, bf16[704,512]{1,0:T(8,128)(2,1)S(1)}, bf16[256,1152]{1,0:T(8,128)(2,1)S(1)}) custom-call(bf16[704,512]{1,0:T(8,128)(2,1)S(1)} %get-tuple-element.54.target_ref, bf16[704,1152]{1,0:T(8,128)(2,1)S(1)} %get-tuple-element.52.first_ref.patch_last_ref, f32[704,256]{1,0:T(8,128)S(1)} %get-tuple-element.55.student_own_ref, ...), custom_call_target="tpu_custom_call" | custom-call | flops 6000000000 | bytes 1000000 | tf_op jit(solution)/shard_map/front/pallas_call | solution.py:542
  31.5 0.5 stay.1
  33.0 0.6 %collective-permute-start.16 = (bf16[4,32,1152]{2,1,0:T(8,128)(2,1)S(1)}, bf16[4,32,1152]{2,1,0:T(8,128)(2,1)S(1)}, u32[]{:S(2)}, u32[]{:S(2)}) collective-permute-start(bf16[4,32,1152]{2,1,0:T(8,128)(2,1)S(1)} %join.1.tie_ref), channel_id=1, source_target_pairs={{0,2},{1,3},{2,0},{3,1},{4,6},{5,7},{6,4},{7,5},{8,10},{9,11},{10,... | collective-permute-start | bytes 884744 | tf_op jit(solution)/shard_map/ppermute | solution.py:23
  33.6 1.1 %back.1.slope_second_ref = bf16[576,128]{1,0:T(8,128)(2,1)S(1)} custom-call(bf16[704,512]{1,0:T(8,128)(2,1)S(1)} %get-tuple-element.56.slope_ref, f32[576,128]{1,0:T(8,128)S(1)} %get-tuple-element.64.tilt_second_ref, bf16[256,1152]{1,0:T(8,128)(2,1)S(1)} %get-tuple-element.65.w_own_ref, bf16[256,1152]{1,0:T(8,128)(2,1)S(1)} %get-tuple-element.66.w_other_ref, ...), custom_call_target="tpu_custom_call" | custom-call | flops 4000000000 | bytes 1000000 | tf_op jit(solution)/shard_map/back/pallas_call | solution.py:542
  34.7 1.1 %first.1 = (f32[4,2,8,1728]{3,2,1,0:T(8,128)S(1)}, bf16[4,2,8,1728]{3,2,1,0:T(8,128)(2,1)S(1)}) custom-call(bf16[576,128]{1,0:T(8,128)(2,1)S(1)} %back.1.slope_second_ref, f32[512,128]{1,0:T(8,128)S(1)} %get-tuple-element.67.tilt_first_ref, bf16[896,576]{1,0:T(8,128)(2,1)S(1)} %get-tuple-element.68.patch_first_ref, ...), custom_call_target="tpu_custom_call" | custom-call | flops 2000000000 | bytes 1000000 | tf_op jit(solution)/shard_map/first/pallas_call | solution.py:542
  36.0 1.5 %collective-permute-done.20.refs_0_ = bf16[4,2,8,1728]{3,2,1,0:T(8,128)(2,1)S(1)} collective-permute-done((bf16[4,2,8,1728]{3,2,1,0:T(8,128)(2,1)S(1)}, bf16[4,2,8,1728]{3,2,1,0:T(8,128)(2,1)S(1)}, u32[]{:S(2)}, u32[]{:S(2)}) %collective-permute-start.20) | collective-permute-done | bytes 221216 | tf_op jit(solution)/shard_map/ppermute | solution.py:23
  37.5 3.1 %collective-permute-start.21 = (bf16[2,8,1728]{2,1,0:T(8,128)(2,1)S(1)}, bf16[2,8,1728]{2,1,0:T(8,128)(2,1)S(1)}, u32[]{:S(2)}, u32[]{:S(2)}) collective-permute-start(bf16[2,8,1728]{2,1,0:T(8,128)(2,1)S(1)} %get-tuple-element.74), channel_id=1, source_target_pairs={{0,12},{1,13},{2,14},{3,15},{4,8},{5,9},{6,10},{7,11},{8,4},{9,5},... | collective-permute-start | bytes 165896 | tf_op jit(solution)/shard_map/ppermute | solution.py:23
  40.6 0.5 collective-permute-start.22
  41.0 0.9 %collective-permute-start.23 = (bf16[2,8,1728]{2,1,0:T(8,128)(2,1)S(1)}, bf16[2,8,1728]{2,1,0:T(8,128)(2,1)S(1)}, u32[]{:S(2)}, u32[]{:S(2)}) collective-permute-start(bf16[2,8,1728]{2,1,0:T(8,128)(2,1)S(1)} %get-tuple-element.76), channel_id=1, source_target_pairs={{0,4},{1,5},{2,6},{3,7},{4,0},{5,1},{6,2},{7,3},{8,12},{9,13},{10,... | collective-permute-start | bytes 165896 | tf_op jit(solution)/shard_map/ppermute | solution.py:23
  42.2 3.0 %collective-permute-start.17 = (bf16[32,1152]{1,0:T(8,128)(2,1)S(1)}, bf16[32,1152]{1,0:T(8,128)(2,1)S(1)}, u32[]{:S(2)}, u32[]{:S(2)}) collective-permute-start(bf16[32,1152]{1,0:T(8,128)(2,1)S(1)} %get-tuple-element.61), channel_id=1, source_target_pairs={{0,8},{1,9},{2,10},{3,11},{4,12},{5,13},{6,14},{7,15},{8,0},{9,1},... | collective-permute-start | bytes 221192 | tf_op jit(solution)/shard_map/ppermute | solution.py:23
  45.2 0.5 collective-permute-start.18
  45.7 1.5 %collective-permute-start.19 = (bf16[32,1152]{1,0:T(8,128)(2,1)S(1)}, bf16[32,1152]{1,0:T(8,128)(2,1)S(1)}, u32[]{:S(2)}, u32[]{:S(2)}) collective-permute-start(bf16[32,1152]{1,0:T(8,128)(2,1)S(1)} %get-tuple-element.63), channel_id=1, source_target_pairs={{0,12},{1,13},{2,14},{3,15},{4,8},{5,9},{6,10},{7,11},{8,4},{9,5},... | collective-permute-start | bytes 221192 | tf_op jit(solution)/shard_map/ppermute | solution.py:23
  47.5 2.4 %collective-permute-start.24 = (bf16[8,1728]{1,0:T(8,128)(2,1)S(1)}, bf16[8,1728]{1,0:T(8,128)(2,1)S(1)}, u32[]{:S(2)}, u32[]{:S(2)}) collective-permute-start(bf16[8,1728]{1,0:T(8,128)(2,1)S(1)} %get-tuple-element.78), channel_id=1, source_target_pairs={{0,2},{1,3},{2,0},{3,1},{4,6},{5,7},{6,4},{7,5},{8,10},{9,11},{10,... | collective-permute-start | bytes 82952 | tf_op jit(solution)/shard_map/ppermute | solution.py:23
  49.9 1.9 %collective-permute-done.24.got_ref = bf16[8,1728]{1,0:T(8,128)(2,1)S(1)} collective-permute-done((bf16[8,1728]{1,0:T(8,128)(2,1)S(1)}, bf16[8,1728]{1,0:T(8,128)(2,1)S(1)}, u32[]{:S(2)}, u32[]{:S(2)}) %collective-permute-start.24) | collective-permute-done | bytes 27680 | tf_op jit(solution)/shard_map/ppermute | solution.py:23
  51.9 0.7 %finish.1 = (f32[8,576]{1,0:T(8,128)}, f32[8,1152]{1,0:T(8,128)}, f32[32,1152]{1,0:T(8,128)}) custom-call(f32[32,1152]{1,0:T(8,128)S(1)} %get-tuple-element.60.last_ref, bf16[32,1152]{1,0:T(8,128)(2,1)S(1)} %collective-permute-done.17.got1_ref, bf16[32,1152]{1,0:T(8,128)(2,1)S(1)} %collective-permute-done.18.got2_ref, ...), custom_call_target="tpu_custom_call" | custom-call | flops 1000000 | bytes 1000000 | tf_op jit(solution)/shard_map/finish/pallas_call | solution.py:542
  (37 shorter events, 3.1 us)
Async XLA Ops:
  3.0 10.3 %collective-permute-start.2 = (bf16[1152,128]{1,0:T(8,128)(2,1)}, bf16[1152,128]{1,0:T(8,128)(2,1)S(1)}, u32[]{:S(2)}, u32[]{:S(2)}) collective-permute-start(bf16[1152,128]{1,0:T(8,128)(2,1)} %get-tuple-element.45), channel_id=1, source_target_pairs={{0,2},{1,3},{2,0},{3,1},{4,6},{5,7},{6,4},{7,5},{8,10},{9,11},{10,... | collective-permute-start | bytes 884744 | tf_op jit(solution)/shard_map/ppermute | solution.py:23
  6.1 7.7 %collective-permute-start = (bf16[400,128]{1,0:T(8,128)(2,1)}, bf16[400,128]{1,0:T(8,128)(2,1)S(1)}, u32[]{:S(2)}, u32[]{:S(2)}) collective-permute-start(bf16[400,128]{1,0:T(8,128)(2,1)} %get-tuple-element.42), channel_id=1, source_target_pairs={{0,4},{1,5},{2,6},{3,7},{4,0},{5,1},{6,2},{7,3},{8,12},{9,13},{10,... | collective-permute-start | bytes 307208 | tf_op jit(solution)/shard_map/ppermute | solution.py:23
  7.6 10.7 %collective-permute-start.7 = (bf16[400,128]{1,0:T(8,128)(2,1)}, bf16[400,128]{1,0:T(8,128)(2,1)S(1)}, u32[]{:S(2)}, u32[]{:S(2)}) collective-permute-start(bf16[400,128]{1,0:T(8,128)(2,1)} %get-tuple-element.42), channel_id=1, source_target_pairs={{0,8},{1,9},{2,10},{3,11},{4,12},{5,13},{6,14},{7,15},{8,0},{9,1},... | collective-permute-start | bytes 307208 | tf_op jit(solution)/shard_map/ppermute | solution.py:23
  10.2 8.1 %collective-permute-start.6 = (bf16[400,128]{1,0:T(8,128)(2,1)}, bf16[400,128]{1,0:T(8,128)(2,1)S(1)}, u32[]{:S(2)}, u32[]{:S(2)}) collective-permute-start(bf16[400,128]{1,0:T(8,128)(2,1)} %get-tuple-element.42), channel_id=1, source_target_pairs={{0,12},{1,13},{2,14},{3,15},{4,8},{5,9},{6,10},{7,11},{8,4},{9,5},... | collective-permute-start | bytes 307208 | tf_op jit(solution)/shard_map/ppermute | solution.py:23
  13.3 7.2 %collective-permute-start.3 = (bf16[1152,128]{1,0:T(8,128)(2,1)S(1)}, bf16[1152,128]{1,0:T(8,128)(2,1)S(1)}, u32[]{:S(2)}, u32[]{:S(2)}) collective-permute-start(bf16[1152,128]{1,0:T(8,128)(2,1)S(1)} %collective-permute-done.2.across_ref), channel_id=1, source_target_pairs={{0,1},{1,0},{2,3},{3,2},{4,5},{5,4},{6,7},{7,6},{8,9},{9,8},{10,11... | collective-permute-start | bytes 884744 | tf_op jit(solution)/shard_map/ppermute | solution.py:23
  13.3 7.2 %collective-permute-start.1 = (bf16[640,128]{1,0:T(8,128)(2,1)}, bf16[640,128]{1,0:T(8,128)(2,1)S(1)}, u32[]{:S(2)}, u32[]{:S(2)}) collective-permute-start(bf16[640,128]{1,0:T(8,128)(2,1)} %get-tuple-element.44), channel_id=1, source_target_pairs={{0,1},{1,0},{2,3},{3,2},{4,5},{5,4},{6,7},{7,6},{8,9},{9,8},{10,11... | collective-permute-start | bytes 491528 | tf_op jit(solution)/shard_map/ppermute | solution.py:23
  13.8 1.0 %copy-start = (bf16[1040,128]{1,0:T(8,128)(2,1)S(1)}, bf16[1040,128]{1,0:T(8,128)(2,1)}, u32[]{:S(2)}) copy-start(bf16[1040,128]{1,0:T(8,128)(2,1)} %get-tuple-element.41.own_ref) | copy-start | bytes 798724
  18.4 6.1 %collective-permute-start.8 = (bf16[4,112,128]{2,1,0:T(8,128)(2,1)S(1)}, bf16[4,112,128]{2,1,0:T(8,128)(2,1)S(1)}, u32[]{:S(2)}, u32[]{:S(2)}) collective-permute-start(bf16[4,112,128]{2,1,0:T(8,128)(2,1)S(1)} %get-tuple-element.51.h_ref), channel_id=1, source_target_pairs={{0,2},{1,3},{2,0},{3,1},{4,6},{5,7},{6,4},{7,5},{8,10},{9,11},{10,... | collective-permute-start | bytes 344072 | tf_op jit(solution)/shard_map/ppermute | solution.py:23
  18.9 9.1 %collective-permute-start.11 = (bf16[4,288,128]{2,1,0:T(8,128)(2,1)S(1)}, bf16[4,288,128]{2,1,0:T(8,128)(2,1)S(1)}, u32[]{:S(2)}, u32[]{:S(2)}) collective-permute-start(bf16[4,288,128]{2,1,0:T(8,128)(2,1)S(1)} %get-tuple-element.53.h_ref), channel_id=1, source_target_pairs={{0,2},{1,3},{2,0},{3,1},{4,6},{5,7},{6,4},{7,5},{8,10},{9,11},{10,... | collective-permute-start | bytes 884744 | tf_op jit(solution)/shard_map/ppermute | solution.py:23
  20.7 5.1 %collective-permute-start.4 = (bf16[496,128]{1,0:T(8,128)(2,1)S(1)}, bf16[496,128]{1,0:T(8,128)(2,1)S(1)}, u32[]{:S(2)}, u32[]{:S(2)}) collective-permute-start(bf16[496,128]{1,0:T(8,128)(2,1)S(1)} %get-tuple-element.47), channel_id=1, source_target_pairs={{0,4},{1,5},{2,6},{3,7},{4,0},{5,1},{6,2},{7,3},{8,12},{9,13},{10,... | collective-permute-start | bytes 380936 | tf_op jit(solution)/shard_map/ppermute | solution.py:23
  22.4 3.3 %collective-permute-start.5 = (bf16[496,128]{1,0:T(8,128)(2,1)S(1)}, bf16[496,128]{1,0:T(8,128)(2,1)S(1)}, u32[]{:S(2)}, u32[]{:S(2)}) collective-permute-start(bf16[496,128]{1,0:T(8,128)(2,1)S(1)} %get-tuple-element.48), channel_id=1, source_target_pairs={{0,1},{1,0},{2,3},{3,2},{4,8},{5,9},{6,10},{7,11},{8,4},{9,5},{10,... | collective-permute-start | bytes 380936 | tf_op jit(solution)/shard_map/ppermute | solution.py:34
  22.4 2.0 %collective-permute-start.9 = (bf16[4,112,128]{2,1,0:T(8,128)(2,1)S(1)}, bf16[4,112,128]{2,1,0:T(8,128)(2,1)S(1)}, u32[]{:S(2)}, u32[]{:S(2)}) collective-permute-start(bf16[4,112,128]{2,1,0:T(8,128)(2,1)S(1)} %get-tuple-element.51.h_ref), channel_id=1, source_target_pairs={{0,1},{1,0},{2,3},{3,2},{4,5},{5,4},{6,7},{7,6},{8,9},{9,8},{10,11... | collective-permute-start | bytes 344072 | tf_op jit(solution)/shard_map/ppermute | solution.py:23
  24.4 1.3 %collective-permute-start.10 = (bf16[4,112,128]{2,1,0:T(8,128)(2,1)S(1)}, bf16[4,112,128]{2,1,0:T(8,128)(2,1)S(1)}, u32[]{:S(2)}, u32[]{:S(2)}) collective-permute-start(bf16[4,112,128]{2,1,0:T(8,128)(2,1)S(1)} %collective-permute-done.8.hy_ref), channel_id=1, source_target_pairs={{0,1},{1,0},{2,3},{3,2},{4,5},{5,4},{6,7},{7,6},{8,9},{9,8},{10,11... | collective-permute-start | bytes 344072 | tf_op jit(solution)/shard_map/ppermute | solution.py:23
  24.4 4.9 %collective-permute-start.12 = (bf16[4,288,128]{2,1,0:T(8,128)(2,1)S(1)}, bf16[4,288,128]{2,1,0:T(8,128)(2,1)S(1)}, u32[]{:S(2)}, u32[]{:S(2)}) collective-permute-start(bf16[4,288,128]{2,1,0:T(8,128)(2,1)S(1)} %get-tuple-element.53.h_ref), channel_id=1, source_target_pairs={{0,1},{1,0},{2,3},{3,2},{4,5},{5,4},{6,7},{7,6},{8,9},{9,8},{10,11... | collective-permute-start | bytes 884744 | tf_op jit(solution)/shard_map/ppermute | solution.py:23
  28.0 1.6 %collective-permute-start.13 = (bf16[4,288,128]{2,1,0:T(8,128)(2,1)S(1)}, bf16[4,288,128]{2,1,0:T(8,128)(2,1)S(1)}, u32[]{:S(2)}, u32[]{:S(2)}) collective-permute-start(bf16[4,288,128]{2,1,0:T(8,128)(2,1)S(1)} %after.1.hy_ref), channel_id=1, source_target_pairs={{0,1},{1,0},{2,3},{3,2},{4,5},{5,4},{6,7},{7,6},{8,9},{9,8},{10,11... | collective-permute-start | bytes 884744 | tf_op jit(solution)/shard_map/ppermute | solution.py:23
  31.3 1.6 %collective-permute-start.15 = (bf16[4,32,1152]{2,1,0:T(8,128)(2,1)S(1)}, bf16[4,32,1152]{2,1,0:T(8,128)(2,1)S(1)}, u32[]{:S(2)}, u32[]{:S(2)}) collective-permute-start(bf16[4,32,1152]{2,1,0:T(8,128)(2,1)S(1)} %get-tuple-element.59), channel_id=1, source_target_pairs={{0,1},{1,0},{2,3},{3,2},{4,5},{5,4},{6,7},{7,6},{8,9},{9,8},{10,11... | collective-permute-start | bytes 884744 | tf_op jit(solution)/shard_map/ppermute | solution.py:23
  32.1 9.9 %collective-permute-start.14 = (bf16[4,32,1152]{2,1,0:T(8,128)(2,1)S(1)}, bf16[4,32,1152]{2,1,0:T(8,128)(2,1)S(1)}, u32[]{:S(2)}, u32[]{:S(2)}) collective-permute-start(bf16[4,32,1152]{2,1,0:T(8,128)(2,1)S(1)} %get-tuple-element.58), channel_id=1, source_target_pairs={{0,1},{1,0},{2,3},{3,2},{4,5},{5,4},{6,7},{7,6},{8,9},{9,8},{10,11... | collective-permute-start | bytes 884744 | tf_op jit(solution)/shard_map/ppermute | solution.py:23
  33.0 9.1 %collective-permute-start.16 = (bf16[4,32,1152]{2,1,0:T(8,128)(2,1)S(1)}, bf16[4,32,1152]{2,1,0:T(8,128)(2,1)S(1)}, u32[]{:S(2)}, u32[]{:S(2)}) collective-permute-start(bf16[4,32,1152]{2,1,0:T(8,128)(2,1)S(1)} %join.1.tie_ref), channel_id=1, source_target_pairs={{0,2},{1,3},{2,0},{3,1},{4,6},{5,7},{6,4},{7,5},{8,10},{9,11},{10,... | collective-permute-start | bytes 884744 | tf_op jit(solution)/shard_map/ppermute | solution.py:23
  35.9 1.6 %collective-permute-start.20 = (bf16[4,2,8,1728]{3,2,1,0:T(8,128)(2,1)S(1)}, bf16[4,2,8,1728]{3,2,1,0:T(8,128)(2,1)S(1)}, u32[]{:S(2)}, u32[]{:S(2)}) collective-permute-start(bf16[4,2,8,1728]{3,2,1,0:T(8,128)(2,1)S(1)} %get-tuple-element.72), channel_id=1, source_target_pairs={{0,1},{1,0},{2,3},{3,2},{4,5},{5,4},{6,7},{7,6},{8,9},{9,8},{10,11... | collective-permute-start | bytes 663560 | tf_op jit(solution)/shard_map/ppermute | solution.py:23
  37.5 8.2 %collective-permute-start.21 = (bf16[2,8,1728]{2,1,0:T(8,128)(2,1)S(1)}, bf16[2,8,1728]{2,1,0:T(8,128)(2,1)S(1)}, u32[]{:S(2)}, u32[]{:S(2)}) collective-permute-start(bf16[2,8,1728]{2,1,0:T(8,128)(2,1)S(1)} %get-tuple-element.74), channel_id=1, source_target_pairs={{0,12},{1,13},{2,14},{3,15},{4,8},{5,9},{6,10},{7,11},{8,4},{9,5},... | collective-permute-start | bytes 165896 | tf_op jit(solution)/shard_map/ppermute | solution.py:23
  40.6 6.9 %collective-permute-start.22 = (bf16[2,8,1728]{2,1,0:T(8,128)(2,1)S(1)}, bf16[2,8,1728]{2,1,0:T(8,128)(2,1)S(1)}, u32[]{:S(2)}, u32[]{:S(2)}) collective-permute-start(bf16[2,8,1728]{2,1,0:T(8,128)(2,1)S(1)} %get-tuple-element.75), channel_id=1, source_target_pairs={{0,8},{1,9},{2,10},{3,11},{4,12},{5,13},{6,14},{7,15},{8,0},{9,1},... | collective-permute-start | bytes 165896 | tf_op jit(solution)/shard_map/ppermute | solution.py:23
  41.0 6.4 %collective-permute-start.23 = (bf16[2,8,1728]{2,1,0:T(8,128)(2,1)S(1)}, bf16[2,8,1728]{2,1,0:T(8,128)(2,1)S(1)}, u32[]{:S(2)}, u32[]{:S(2)}) collective-permute-start(bf16[2,8,1728]{2,1,0:T(8,128)(2,1)S(1)} %get-tuple-element.76), channel_id=1, source_target_pairs={{0,4},{1,5},{2,6},{3,7},{4,0},{5,1},{6,2},{7,3},{8,12},{9,13},{10,... | collective-permute-start | bytes 165896 | tf_op jit(solution)/shard_map/ppermute | solution.py:23
  42.2 9.5 %collective-permute-start.17 = (bf16[32,1152]{1,0:T(8,128)(2,1)S(1)}, bf16[32,1152]{1,0:T(8,128)(2,1)S(1)}, u32[]{:S(2)}, u32[]{:S(2)}) collective-permute-start(bf16[32,1152]{1,0:T(8,128)(2,1)S(1)} %get-tuple-element.61), channel_id=1, source_target_pairs={{0,8},{1,9},{2,10},{3,11},{4,12},{5,13},{6,14},{7,15},{8,0},{9,1},... | collective-permute-start | bytes 221192 | tf_op jit(solution)/shard_map/ppermute | solution.py:23
  45.2 6.5 %collective-permute-start.18 = (bf16[32,1152]{1,0:T(8,128)(2,1)S(1)}, bf16[32,1152]{1,0:T(8,128)(2,1)S(1)}, u32[]{:S(2)}, u32[]{:S(2)}) collective-permute-start(bf16[32,1152]{1,0:T(8,128)(2,1)S(1)} %get-tuple-element.62), channel_id=1, source_target_pairs={{0,4},{1,5},{2,6},{3,7},{4,0},{5,1},{6,2},{7,3},{8,12},{9,13},{10,... | collective-permute-start | bytes 221192 | tf_op jit(solution)/shard_map/ppermute | solution.py:23
  45.7 6.2 %collective-permute-start.19 = (bf16[32,1152]{1,0:T(8,128)(2,1)S(1)}, bf16[32,1152]{1,0:T(8,128)(2,1)S(1)}, u32[]{:S(2)}, u32[]{:S(2)}) collective-permute-start(bf16[32,1152]{1,0:T(8,128)(2,1)S(1)} %get-tuple-element.63), channel_id=1, source_target_pairs={{0,12},{1,13},{2,14},{3,15},{4,8},{5,9},{6,10},{7,11},{8,4},{9,5},... | collective-permute-start | bytes 221192 | tf_op jit(solution)/shard_map/ppermute | solution.py:23
  47.5 4.3 %collective-permute-start.24 = (bf16[8,1728]{1,0:T(8,128)(2,1)S(1)}, bf16[8,1728]{1,0:T(8,128)(2,1)S(1)}, u32[]{:S(2)}, u32[]{:S(2)}) collective-permute-start(bf16[8,1728]{1,0:T(8,128)(2,1)S(1)} %get-tuple-element.78), channel_id=1, source_target_pairs={{0,2},{1,3},{2,0},{3,1},{4,6},{5,7},{6,4},{7,5},{8,10},{9,11},{10,... | collective-permute-start | bytes 82952 | tf_op jit(solution)/shard_map/ppermute | solution.py:23
